TPU v7x, 32 devices: a whole 2x2x4 slice. The times are simulated.
32 devices in a mesh: prompt: 4 (over x, core), response: 4 (over z), tensor: 2 (over y).
Axes of the slice: x: 2, y: 2, z: 4, core: 2. Of those that a mesh axis runs over, the one named last changes fastest.
Arguments:
- queries: bfloat16 [4, 512, 8192], P('prompt', 'response', 'tensor'), may hold values from -30 to 30
- keys: bfloat16 [4, 512, 1024], P('prompt', 'response', 'tensor'), may hold values from -6 to 6
- values: bfloat16 [4, 512, 1024], P('prompt', 'response', 'tensor'), may hold values from -36 to 36
- prefix_keys: bfloat16 [4, 512, 1024], P('prompt', ('response', 'tensor')), may hold values from -6 to 6
- prefix_values: bfloat16 [4, 512, 1024], P('prompt', ('response', 'tensor')), may hold values from -36 to 36
- lengths: int32 [4, 4], P('prompt', 'response'), may hold values from 1 to 128, as said below
- out_grad: bfloat16 [4, 512, 8192], P('prompt', 'response', 'tensor'), may hold values from -36 to 36
Outputs:
- output: bfloat16 [4, 512, 8192], P('prompt', 'response', 'tensor')
- query_grad: bfloat16 [4, 512, 8192], P('prompt', 'response', 'tensor')
- key_grad: bfloat16 [4, 512, 1024], P('prompt', 'response', 'tensor')
- value_grad: bfloat16 [4, 512, 1024], P('prompt', 'response', 'tensor')
- prefix_key_grad: bfloat16 [4, 512, 1024], P('prompt', ('response', 'tensor'))
- prefix_value_grad: bfloat16 [4, 512, 1024], P('prompt', ('response', 'tensor'))
Inputs may be any that keep to these rules, and one draw needn't show every extreme that they name: `lengths`: number of live tokens of response r of prompt p; they fill its first slots.
All inputs are finite; a program needn't handle non-finite values.
Results may differ from a plain program's by a relative error of at most 0.023.
Values may be sent and summed in bfloat16 or wider, within the bound.
No kernel may reach another device: no remote copies, remote signals or barrier semaphores. Data moves between devices by JAX's collectives and lax.ppermute only.
A program may use at most 192 MiB of HBM per device.

v0:
```python
import math

import jax
import jax.numpy as jnp
from jax import lax
from jax.sharding import PartitionSpec as P

HD = 128
GROUP = 8


def attend_head(head_queries, own_keys, own_values, pre_keys, pre_values, live_rows, scaled_grad):
    row_count = head_queries.shape[0]
    prefix_len = pre_keys.shape[0]
    all_keys = jnp.concatenate([pre_keys, own_keys], axis=0)
    all_values = jnp.concatenate([pre_values, own_values], axis=0)
    factor = 1.0 / math.sqrt(head_queries.shape[2])
    scores = (
        jnp.einsum("rgd,kd->grk", head_queries, all_keys, preferred_element_type=jnp.float32)
        * factor
    )
    row_pos = jnp.arange(row_count, dtype=jnp.int32)[:, None]
    key_pos = jnp.arange(prefix_len + row_count, dtype=jnp.int32)[None, :] - prefix_len
    allowed = key_pos <= row_pos
    scores = jnp.where(allowed[None], scores, -1e30)
    row_max = jnp.max(scores, axis=2, keepdims=True)
    exponent = jnp.exp(scores - row_max)
    probs = exponent / jnp.sum(exponent, axis=2, keepdims=True)
    rounded = probs.astype(jnp.bfloat16)
    attended = jnp.einsum("grk,kd->rgd", rounded, all_values, preferred_element_type=jnp.float32)
    output = (attended * live_rows[:, None, None]).astype(jnp.bfloat16)
    grad_probs = jnp.einsum(
        "rgd,kd->grk", scaled_grad, all_values, preferred_element_type=jnp.float32
    )
    centre = jnp.sum(scaled_grad.astype(jnp.float32) * attended, axis=2)
    score_grad = (probs * (grad_probs - jnp.transpose(centre)[:, :, None]) * factor).astype(
        jnp.bfloat16
    )
    query_grad = jnp.einsum("grk,kd->rgd", score_grad, all_keys, preferred_element_type=jnp.float32)
    key_grad = jnp.einsum(
        "grk,rgd->kd", score_grad, head_queries, preferred_element_type=jnp.float32
    )
    value_grad = jnp.einsum("grk,rgd->kd", rounded, scaled_grad, preferred_element_type=jnp.float32)
    return (
        output,
        query_grad,
        key_grad[:prefix_len],
        key_grad[prefix_len:],
        value_grad[:prefix_len],
        value_grad[prefix_len:],
    )


def body(queries, keys, values, prefix_keys, prefix_values, lengths, out_grad):
    row_count = queries.shape[1]
    kv_cols = keys.shape[2]
    head_count = kv_cols // HD
    tensor_rank = lax.axis_index("tensor")
    full_keys, full_values = (
        lax.all_gather(prefix_keys, ("response", "tensor"), axis=1, tiled=True),
        lax.all_gather(prefix_values, ("response", "tensor"), axis=1, tiled=True),
    )
    pre_keys = lax.dynamic_slice_in_dim(full_keys, tensor_rank * kv_cols, kv_cols, 2)
    pre_values = lax.dynamic_slice_in_dim(full_values, tensor_rank * kv_cols, kv_cols, 2)
    length = lengths[0, 0]
    live_total = lax.psum(length.astype(jnp.float32), ("prompt", "response"))
    slots = row_count * lax.axis_size("prompt") * lax.axis_size("response")
    weight = slots / live_total
    live_rows = (jnp.arange(row_count, dtype=jnp.int32) < length).astype(jnp.float32)
    scaled = (out_grad[0].astype(jnp.float32) * live_rows[:, None] * weight).astype(jnp.bfloat16)
    outputs, query_grads, key_grads, value_grads, pre_kgs, pre_vgs = ([], [], [], [], [], [])
    for kv_head in range(head_count):
        qstart = kv_head * GROUP * HD
        kstart = kv_head * HD
        block_queries = queries[0, :, qstart : qstart + GROUP * HD].reshape(row_count, GROUP, HD)
        block_grad = scaled[:, qstart : qstart + GROUP * HD].reshape(row_count, GROUP, HD)
        results = attend_head(
            block_queries,
            keys[0, :, kstart : kstart + HD],
            values[0, :, kstart : kstart + HD],
            pre_keys[0, :, kstart : kstart + HD],
            pre_values[0, :, kstart : kstart + HD],
            live_rows,
            block_grad,
        )
        outputs.append(results[0].reshape(row_count, GROUP * HD))
        query_grads.append(results[1].reshape(row_count, GROUP * HD))
        pre_kgs.append(results[2])
        key_grads.append(results[3])
        pre_vgs.append(results[4])
        value_grads.append(results[5])
    output = jnp.concatenate(outputs, axis=1)[None]
    query_grad = jnp.concatenate(query_grads, axis=1).astype(jnp.bfloat16)[None]
    key_grad = jnp.concatenate(key_grads, axis=1).astype(jnp.bfloat16)[None]
    value_grad = jnp.concatenate(value_grads, axis=1).astype(jnp.bfloat16)[None]
    prefix_kterm = jnp.concatenate(pre_kgs, axis=1)[None]
    prefix_vterm = jnp.concatenate(pre_vgs, axis=1)[None]
    all_cols = kv_cols * lax.axis_size("tensor")
    empty = jnp.zeros((1, prefix_kterm.shape[1], all_cols), jnp.float32)
    placed_keys = lax.dynamic_update_slice_in_dim(empty, prefix_kterm, tensor_rank * kv_cols, 2)
    placed_values = lax.dynamic_update_slice_in_dim(empty, prefix_vterm, tensor_rank * kv_cols, 2)
    summed = (
        lax.psum_scatter(
            placed_keys.astype(jnp.bfloat16),
            ("response", "tensor"),
            scatter_dimension=1,
            tiled=True,
        ).astype(jnp.float32),
        lax.psum_scatter(
            placed_values.astype(jnp.bfloat16),
            ("response", "tensor"),
            scatter_dimension=1,
            tiled=True,
        ).astype(jnp.float32),
    )
    prefix_key_grad = summed[0].astype(jnp.bfloat16)
    prefix_value_grad = summed[1].astype(jnp.bfloat16)
    return (output, query_grad, key_grad, value_grad, prefix_key_grad, prefix_value_grad)


def solution(mesh):
    in_specs = (
        P("prompt", "response", "tensor"),
        P("prompt", "response", "tensor"),
        P("prompt", "response", "tensor"),
        P("prompt", ("response", "tensor"), None),
        P("prompt", ("response", "tensor"), None),
        P("prompt", "response"),
        P("prompt", "response", "tensor"),
    )
    out_specs = (
        P("prompt", "response", "tensor"),
        P("prompt", "response", "tensor"),
        P("prompt", "response", "tensor"),
        P("prompt", "response", "tensor"),
        P("prompt", ("response", "tensor"), None),
        P("prompt", ("response", "tensor"), None),
    )
    return jax.shard_map(body, mesh=mesh, in_specs=in_specs, out_specs=out_specs, check_vma=False)
```

profile of v0, /device:TPU:0, one launch (start us, length us, event | category | flops | bytes accessed | tf_op | source)
XLA Modules:
  0.0 277.0 jit_solution(16410322066704397054)
XLA Ops:
  7.2 0.7 all-gather.3.cloned.1.call-update
  7.9 0.7 all-gather.5.cloned.1.call-update
  9.3 35.8 %psum.7 = f32[]{:T(128)} all-reduce(f32[]{:T(128)S(6)} %convert_element_type.116), channel_id=1, replica_groups=mesh['prompt'=4,'response'=4,'tensor'=2] {'prompt','response'}, use_global_device_ids=true, to_apply=%region_8.9 | all-reduce | flops 1 | bytes 8 | tf_op jit(solution)/shard_map/psum | solution.py:66
  45.1 0.8 fusion.92
  46.0 0.7 copy.222
  46.7 0.7 copy.228
  47.4 0.7 copy.225
  48.1 0.7 copy.231
  49.5 1.5 fusion.17
  52.4 0.9 copy.223
  53.2 0.8 copy.229
  54.1 0.8 copy.226
  55.3 0.7 slice_bitcast_fusion.3
  55.9 1.2 constant_dynamic-slice_fusion.2
  57.2 0.8 copy.227
  58.0 0.8 copy.224
  58.9 35.3 %all-gather.5.cloned.1.call-done = bf16[1,512,1024]{2,1,0:T(8,128)(2,1)} async-done(((bf16[1,64,1024]{2,1,0:T(8,128)(2,1)}), bf16[1,512,1024]{2,1,0:T(8,128)(2,1)}) %all-gather.5.cloned.1.call-update) | async-done | bytes 1048592 | tf_op jit(solution)/shard_map/all_gather | solution.py:60
  94.2 1.9 dynamic-slice_bitcast_fusion.3
  96.0 2.4 fusion.93
  98.5 2.1 fusion.37
  100.7 1.1 multiply_reduce_fusion
  101.7 1.7 fusion.6
  104.0 0.7 copy-done.30
  104.7 0.7 slice.183
  105.3 3.5 %fusion.95 = (f32[8,128]{1,0:T(8,128)S(1)}, f32[8,128,640]{1,2,0:T(8,128)}) fusion(pred[128,640]{0,1:T(8,128)(4,1)} %copy-done.57, bf16[128,8,128]{0,2,1:T(8,128)(2,1)} %bitcast.288, bf16[128,128]{1,0:T(8,128)(2,1)} %get-tuple-element.53, bf16[512,128]{1,0:T(8,128)(2,1)} %get-tuple-element.34), kind=kOutput, calls=%fused_computation.167 | convolution fusion | flops 170721920 | bytes 3133440 | tf_op jit(solution)/shard_map/sub | solution.py:27
  108.8 2.1 fusion.35
  111.0 1.1 multiply_reduce_fusion.2
  112.7 1.1 copy-done.7
  115.0 0.7 slice.181
  115.7 3.5 %fusion.94 = (f32[8,128]{1,0:T(8,128)S(1)}, f32[8,128,640]{1,2,0:T(8,128)}) fusion(pred[128,640]{0,1:T(8,128)(4,1)} %copy-done.57, bf16[128,8,128]{0,2,1:T(8,128)(2,1)} %bitcast.286, bf16[128,128]{1,0:T(8,128)(2,1)} %get-tuple-element.55, bf16[512,128]{1,0:T(8,128)(2,1)} %get-tuple-element.33), kind=kOutput, calls=%fused_computation.166 | convolution fusion | flops 170721920 | bytes 3133440 | tf_op jit(solution)/shard_map/sub | solution.py:27
  119.2 2.1 fusion.36
  121.3 1.1 multiply_reduce_fusion.1
  124.5 0.7 copy-done.32
  125.1 3.5 %fusion.96 = (f32[8,128]{1,0:T(8,128)S(1)}, f32[8,128,640]{1,2,0:T(8,128)}) fusion(pred[128,640]{0,1:T(8,128)(4,1)} %copy-done.57, bf16[128,8,128]{0,2,1:T(8,128)(2,1)} %bitcast.284, bf16[128,128]{1,0:T(8,128)(2,1)} %get-tuple-element.52, bf16[512,128]{1,0:T(8,128)(2,1)} %get-tuple-element.32), kind=kOutput, calls=%fused_computation.168 | convolution fusion | flops 170721920 | bytes 3133440 | tf_op jit(solution)/shard_map/sub | solution.py:27
  128.6 2.1 fusion.34
  130.8 1.2 multiply_reduce_fusion.3
  132.0 1.6 fusion.15
  135.4 0.8 maximum_bitcast_fusion.1
  136.2 2.2 copy.176
  138.4 1.1 broadcast_in_dim.41.clone
  139.6 1.9 constant_dynamic-update-slice_fusion.1
  141.6 2.5 convolution_convert_fusion
  144.1 1.8 copy.167
  145.9 1.8 copy.143
  147.7 1.5 convolution_bitcast_fusion.4
  149.2 0.7 copy-done.34
  149.8 0.7 slice.187
  150.5 2.4 convolution_convert_fusion.2
  152.9 1.8 copy.165
  154.8 1.8 copy.141
  158.4 0.8 copy.166
  159.2 0.8 copy.142
  161.8 1.9 fusion.56
  163.7 0.9 fusion.54
  164.5 0.8 pad_maximum_fusion.2
  165.3 0.8 copy.179
  166.1 0.8 fusion.52
  166.9 0.8 fusion.50
  167.7 0.8 copy.178
  168.5 1.2 convolution_convert_fusion.3
  170.0 1.0 pad_maximum_fusion
  171.0 1.0 maximum_bitcast_fusion
  172.1 31.7 %reduce-scatter.3.cloned.1.call-done = bf16[1,64,1024]{2,1,0:T(8,128)(2,1)} async-done(((bf16[1,512,1024]{2,1,0:T(8,128)(2,1)}), bf16[1,64,1024]{2,1,0:T(8,128)(2,1)}) %reduce-scatter.3.cloned.1.call-update) | async-done | bytes 131088 | tf_op jit(solution)/shard_map/reduce_scatter | solution.py:103
  203.8 66.7 %reduce-scatter.5.cloned.1.call-done = bf16[1,64,1024]{2,1,0:T(8,128)(2,1)} async-done(((bf16[1,512,1024]{2,1,0:T(8,128)(2,1)}), bf16[1,64,1024]{2,1,0:T(8,128)(2,1)}) %reduce-scatter.5.cloned.1.call-update) | async-done | bytes 131088 | tf_op jit(solution)/shard_map/reduce_scatter | solution.py:109
  (156 shorter events, 11.9 us)
Async XLA Ops:
  7.2 48.8 %all-gather.3.cloned.1.call-start = ((), (), s32[]{:S(2)}) async-start(), calls=%async_computation.2 | async-start | bytes 1179648 | tf_op jit(solution)/shard_map/all_gather | solution.py:61
  7.9 86.3 %all-gather.5.cloned.1.call-start = ((), (), s32[]{:S(2)}) async-start(), calls=%async_computation.3 | async-start | bytes 1179648 | tf_op jit(solution)/shard_map/all_gather | solution.py:60
  8.6 195.1 %reduce-scatter.3.cloned.1.call-start = ((), (), s32[]{:S(2)}) async-start(), calls=%async_computation.4 | async-start | bytes 1179648 | tf_op jit(solution)/shard_map/reduce_scatter | solution.py:103
  51.0 1.2 copy-start.18
  51.5 49.1 %copy-start.15 = (bf16[128,1024]{0,1:T(8,128)(2,1)}, bf16[128,1024]{0,1:T(8,128)(2,1)S(1)}, u32[]{:S(2)}) copy-start(bf16[128,1024]{0,1:T(8,128)(2,1)S(1)} %copy.159) | copy-start | bytes 786436
  51.5 3.8 %copy-start.54 = (bf16[1,128,512]{2,1,0:T(8,128)(2,1)S(1)}, bf16[1,128,512]{2,1,0:T(8,128)(2,1)}, u32[]{:S(2)}) copy-start(bf16[1,128,512]{2,1,0:T(8,128)(2,1)} %param.8) | copy-start | bytes 393220
  55.1 43.4 %copy-start.22 = (bf16[1,128,1024]{1,2,0:T(8,128)(2,1)}, bf16[1,128,1024]{1,2,0:T(8,128)(2,1)S(1)}, u32[]{:S(2)}) copy-start(bf16[1,128,1024]{1,2,0:T(8,128)(2,1)S(1)} %copy.232) | copy-start | bytes 786436
  55.3 43.2 %copy-start.57 = (pred[128,640]{0,1:T(8,128)(4,1)}, pred[128,640]{0,1:T(8,128)(4,1)S(1)}, u32[]{:S(2)}) copy-start(pred[128,640]{0,1:T(8,128)(4,1)S(1)} %iota_compare_fusion) | copy-start | bytes 245764
  55.9 42.5 %copy-start.56 = (bf16[128,128]{1,0:T(8,128)(2,1)}, bf16[128,128]{1,0:T(8,128)(2,1)S(1)}, u32[]{:S(2)}) copy-start(bf16[128,128]{1,0:T(8,128)(2,1)S(1)} %get-tuple-element.54) | copy-start | bytes 98308
  57.2 73.5 %copy-start.39 = (bf16[1,512,128]{1,2,0:T(8,128)(2,1)}, bf16[1,512,128]{1,2,0:T(8,128)(2,1)S(1)}, u32[]{:S(2)}) copy-start(bf16[1,512,128]{1,2,0:T(8,128)(2,1)S(1)} %copy.221) | copy-start | bytes 393220
  58.9 41.8 %copy-start.42 = (bf16[1,512,128]{1,2,0:T(8,128)(2,1)}, bf16[1,512,128]{1,2,0:T(8,128)(2,1)S(1)}, u32[]{:S(2)}) copy-start(bf16[1,512,128]{1,2,0:T(8,128)(2,1)S(1)} %copy.230) | copy-start | bytes 393220
  96.0 4.6 %copy-start.49 = (bf16[512,128]{1,0:T(8,128)(2,1)}, bf16[512,128]{1,0:T(8,128)(2,1)S(1)}, u32[]{:S(2)}) copy-start(bf16[512,128]{1,0:T(8,128)(2,1)S(1)} %get-tuple-element.35) | copy-start | bytes 393220
  98.5 2.2 copy-start.53
  98.5 3.2 %copy-start.12 = (f32[8,128,640]{1,2,0:T(8,128)S(1)}, f32[8,128,640]{1,2,0:T(8,128)}, u32[]{:S(2)}) copy-start(f32[8,128,640]{1,2,0:T(8,128)} %get-tuple-element.57) | copy-start | bytes 7864324
  101.7 1.7 copy-start.23
  103.4 5.4 %copy-start.6 = (bf16[8,128,640]{1,2,0:T(8,128)(2,1)}, bf16[8,128,640]{1,2,0:T(8,128)(2,1)S(1)}, u32[]{:S(2)}) copy-start(bf16[8,128,640]{1,2,0:T(8,128)(2,1)S(1)} %fusion.6) | copy-start | bytes 3932164
  104.0 0.7 copy-start.30
  108.8 2.1 copy-start.41
  108.8 2.1 copy-start.52
  108.8 3.2 %copy-start.13 = (f32[8,128,640]{1,2,0:T(8,128)S(1)}, f32[8,128,640]{1,2,0:T(8,128)}, u32[]{:S(2)}) copy-start(f32[8,128,640]{1,2,0:T(8,128)} %get-tuple-element.61) | copy-start | bytes 7864324
  112.1 1.8 copy-start.21
  112.7 1.1 copy-start.7
  114.4 0.7 copy-start.31
  119.2 2.1 copy-start.40
  119.2 2.1 copy-start.51
  119.2 3.3 %copy-start.14 = (f32[8,128,640]{1,2,0:T(8,128)S(1)}, f32[8,128,640]{1,2,0:T(8,128)}, u32[]{:S(2)}) copy-start(f32[8,128,640]{1,2,0:T(8,128)} %get-tuple-element.59) | copy-start | bytes 7864324
  121.3 1.8 copy-start
  122.4 1.0 copy-start.20
  123.4 1.1 copy-start.8
  124.5 0.7 copy-start.32
  128.6 2.1 copy-start.50
  128.6 3.3 %copy-start.11 = (f32[8,128,640]{1,2,0:T(8,128)S(1)}, f32[8,128,640]{1,2,0:T(8,128)}, u32[]{:S(2)}) copy-start(f32[8,128,640]{1,2,0:T(8,128)} %get-tuple-element.63) | copy-start | bytes 7864324
  130.7 2.9 %copy-start.2 = (bf16[8,128,640]{1,2,0:T(8,128)(2,1)}, bf16[8,128,640]{1,2,0:T(8,128)(2,1)S(1)}, u32[]{:S(2)}) copy-start(bf16[8,128,640]{1,2,0:T(8,128)(2,1)S(1)} %fusion.34) | copy-start | bytes 3932164
  132.0 1.6 copy-start.19
  132.0 3.4 %slice-start = ((bf16[640,128]{0,1:T(8,128)(2,1)}), bf16[512,128]{0,1:T(8,128)(2,1)S(1)}, s32[]{:S(2)}) async-start(bf16[640,128]{0,1:T(8,128)(2,1)} %copy-done.32), calls=%async_computation.6 | async-start | bytes 262144 | tf_op jit(solution)/shard_map/slice | solution.py:47
  132.0 3.4 %copy-start.43 = (bf16[512,128]{0,1:T(8,128)(2,1)S(1)}, bf16[512,128]{0,1:T(8,128)(2,1)}, u32[]{:S(2)}) copy-start(bf16[512,128]{0,1:T(8,128)(2,1)} %slice.183) | copy-start | bytes 393220
  132.0 3.4 %copy-start.44 = (bf16[512,128]{0,1:T(8,128)(2,1)S(1)}, bf16[512,128]{0,1:T(8,128)(2,1)}, u32[]{:S(2)}) copy-start(bf16[512,128]{0,1:T(8,128)(2,1)} %slice.181) | copy-start | bytes 393220
  133.6 1.1 copy-start.4
  134.7 0.7 copy-start.33
  141.5 9.0 %copy-start.48 = (bf16[512,128]{1,0:T(8,128)(2,1)S(1)}, bf16[512,128]{1,0:T(8,128)(2,1)}, u32[]{:S(2)}) copy-start(bf16[512,128]{1,0:T(8,128)(2,1)} %get-tuple-element.34) | copy-start | bytes 393220
  141.5 128.9 %reduce-scatter.5.cloned.1.call-start = ((), (), s32[]{:S(2)}) async-start(), calls=%async_computation.5 | async-start | bytes 1179648 | tf_op jit(solution)/shard_map/reduce_scatter | solution.py:109
  149.2 0.7 copy-start.34
  149.8 7.3 %copy-start.1 = (bf16[8,128,640]{1,2,0:T(8,128)(2,1)S(1)}, bf16[8,128,640]{1,2,0:T(8,128)(2,1)}, u32[]{:S(2)}) copy-start(bf16[8,128,640]{1,2,0:T(8,128)(2,1)} %copy-done) | copy-start | bytes 3932164
  152.9 4.8 %copy-start.47 = (bf16[512,128]{1,0:T(8,128)(2,1)S(1)}, bf16[512,128]{1,0:T(8,128)(2,1)}, u32[]{:S(2)}) copy-start(bf16[512,128]{1,0:T(8,128)(2,1)} %get-tuple-element.33) | copy-start | bytes 393220
  156.6 1.3 copy-start.9
  156.6 1.3 copy-start.55
  157.1 1.2 copy-start.35
  157.1 2.1 copy-start.17
  157.1 2.9 %copy-start.3 = (bf16[8,128,640]{1,2,0:T(8,128)(2,1)S(1)}, bf16[8,128,640]{1,2,0:T(8,128)(2,1)}, u32[]{:S(2)}) copy-start(bf16[8,128,640]{1,2,0:T(8,128)(2,1)} %copy-done.2) | copy-start | bytes 3932164
  157.7 0.7 copy-start.36
  157.7 3.6 %copy-start.45 = (bf16[512,128]{0,1:T(8,128)(2,1)S(1)}, bf16[512,128]{0,1:T(8,128)(2,1)}, u32[]{:S(2)}) copy-start(bf16[512,128]{0,1:T(8,128)(2,1)} %slice.187) | copy-start | bytes 393220
  158.4 2.9 %slice-start.1 = ((bf16[640,128]{0,1:T(8,128)(2,1)}), bf16[512,128]{0,1:T(8,128)(2,1)S(1)}, s32[]{:S(2)}) async-start(bf16[640,128]{0,1:T(8,128)(2,1)} %copy-done.35), calls=%async_computation.7 | async-start | bytes 262144 | tf_op jit(solution)/shard_map/slice | solution.py:49
  158.4 2.9 %slice-start.2 = ((bf16[640,128]{0,1:T(8,128)(2,1)}), bf16[512,128]{0,1:T(8,128)(2,1)S(1)}, s32[]{:S(2)}) async-start(bf16[640,128]{0,1:T(8,128)(2,1)} %copy-done.36), calls=%async_computation.8 | async-start | bytes 262144 | tf_op jit(solution)/shard_map/slice | solution.py:49
  160.6 1.2 copy-start.37
  161.5 6.9 %copy-start.5 = (bf16[8,128,640]{1,2,0:T(8,128)(2,1)S(1)}, bf16[8,128,640]{1,2,0:T(8,128)(2,1)}, u32[]{:S(2)}) copy-start(bf16[8,128,640]{1,2,0:T(8,128)(2,1)} %copy-done.4) | copy-start | bytes 3932164
  161.5 6.9 %copy-start.46 = (bf16[512,128]{1,0:T(8,128)(2,1)S(1)}, bf16[512,128]{1,0:T(8,128)(2,1)}, u32[]{:S(2)}) copy-start(bf16[512,128]{1,0:T(8,128)(2,1)} %get-tuple-element.32) | copy-start | bytes 393220
  161.8 1.9 copy-start.10
  161.8 8.0 %copy-start.16 = (bf16[128,8,128]{0,2,1:T(8,128)(2,1)S(1)}, bf16[128,8,128]{0,2,1:T(8,128)(2,1)}, u32[]{:S(2)}) copy-start(bf16[128,8,128]{0,2,1:T(8,128)(2,1)} %get-tuple-element.41) | copy-start | bytes 786436
  163.7 6.3 %copy-start.25 = (bf16[1,128,1024]{2,1,0:T(8,128)(2,1)S(1)}, bf16[1,128,1024]{2,1,0:T(8,128)(2,1)}, u32[]{:S(2)}) copy-start(bf16[1,128,1024]{2,1,0:T(8,128)(2,1)} %copy.167) | copy-start | bytes 786436
  163.7 6.3 %copy-start.27 = (bf16[1,128,1024]{2,1,0:T(8,128)(2,1)S(1)}, bf16[1,128,1024]{2,1,0:T(8,128)(2,1)}, u32[]{:S(2)}) copy-start(bf16[1,128,1024]{2,1,0:T(8,128)(2,1)} %copy.165) | copy-start | bytes 786436
  163.7 6.3 %copy-start.29 = (bf16[1,128,1024]{2,1,0:T(8,128)(2,1)S(1)}, bf16[1,128,1024]{2,1,0:T(8,128)(2,1)}, u32[]{:S(2)}) copy-start(bf16[1,128,1024]{2,1,0:T(8,128)(2,1)} %copy.166) | copy-start | bytes 786436
  167.7 3.4 %copy-start.24 = (bf16[128,1024]{1,0:T(8,128)(2,1)S(1)}, bf16[128,1024]{1,0:T(8,128)(2,1)}, u32[]{:S(2)}) copy-start(bf16[128,1024]{1,0:T(8,128)(2,1)} %copy.143) | copy-start | bytes 786436
  167.7 3.4 %copy-start.26 = (bf16[128,1024]{1,0:T(8,128)(2,1)S(1)}, bf16[128,1024]{1,0:T(8,128)(2,1)}, u32[]{:S(2)}) copy-start(bf16[128,1024]{1,0:T(8,128)(2,1)} %copy.141) | copy-start | bytes 786436
  167.7 3.3 %copy-start.28 = (bf16[128,1024]{1,0:T(8,128)(2,1)S(1)}, bf16[128,1024]{1,0:T(8,128)(2,1)}, u32[]{:S(2)}) copy-start(bf16[128,1024]{1,0:T(8,128)(2,1)} %copy.142) | copy-start | bytes 786436
  (1 other events, 0.7 us)
Sparse Core Ops, SparseCore 0:
  10.1 42.9 all-gather.2
  55.3 38.8 all-gather.4
  141.6 62.1 reduce-scatter.2
  208.0 62.4 reduce-scatter.4
where the time goes:
time: 278 us; the launch traced here: 277 us
  waiting for transfers between devices  135 us (49%)
  local copies, waits for them, and re-layouts  42.6 us (15%)
  blocking collectives  35.8 us (13%)
  matrix products  33.6 us (12%)
  between operations  15.9 us (6%)
  other arithmetic  13.9 us (5%)
    reduce_scatter x1, waiting for transfers between devices, body(): lax.psum_scatter(placed_values.astype(jnp.bfloat16), ('response', 'tensor...  66.7 us
    psum x1, blocking collectives, body(): live_total = lax.psum(length.astype(jnp.float32), ('prompt', 'response'))  35.8 us
    all_gather x1, waiting for transfers between devices, body(): lax.all_gather(prefix_keys, ('response', 'tensor'), axis=1, tiled=True)  35.3 us
    reduce_scatter x1, waiting for transfers between devices, body(): lax.psum_scatter(placed_keys.astype(jnp.bfloat16), ('response', 'tensor')...  31.7 us
    unnamed x130, local copies, waits for them, and re-layouts  16.1 us
    sub x4, matrix products, attend_head(): exponent = jnp.exp(scores - row_max)  12.9 us
    convert_element_type x4, other arithmetic, attend_head(): rounded = probs.astype(jnp.bfloat16)  8.44 us
    dot_general x4, matrix products, attend_head(): jnp.einsum('grk,kd->rgd', score_grad, all_keys, preferred_element_type=jn...  6.53 us
  transfers between devices with their start and end apart: 4, of which 3 were waited for; matrix products, arithmetic and copies ran while one was open for 15% of the time, Pallas kernels for 0%

commit v1 on v0

v1 whole, which is shorter than its diff:
```python
import functools
import math

import jax
import jax.numpy as jnp
from jax import lax
from jax.experimental import pallas as pl
from jax.experimental.pallas import tpu as pltpu
from jax.sharding import PartitionSpec as P

HD = 128
GROUP = 8
PAIR = 2
VMEM_LIMIT = 48 * 1024 * 1024
NT = (((1,), (1,)), ((), ()))


def heads_down(ref, first, count):
    return jnp.concatenate(
        [ref[:, (first + i) * HD : (first + i + 1) * HD] for i in range(count)], axis=0
    )


def probs_kernel(n_slots, scale, length_ref, q_ref, do_ref, kown_ref, *refs):
    slot_refs = refs[:n_slots]
    p_ref, dvown_ref = refs[n_slots : n_slots + 2]
    dv_refs = refs[n_slots + 2 : 2 * n_slots + 2]
    s_ref = refs[2 * n_slots + 2]
    rows = q_ref.shape[0]
    own = kown_ref.shape[0]
    keys = jnp.concatenate([kown_ref[...]] + [ref[...] for ref in slot_refs], axis=0)
    width = PAIR * rows
    key_pos = lax.broadcasted_iota(jnp.int32, (own, width), 0)
    row_pos = lax.broadcasted_iota(jnp.int32, (own, width), 1) % rows
    allowed = key_pos <= row_pos
    live = (lax.broadcasted_iota(jnp.int32, (1, width), 1) % rows) < length_ref[0]
    for pair in range(GROUP // PAIR):
        here = s_ref.at[pair % 2]
        cols = slice(pair * width, (pair + 1) * width)
        here[...] = lax.dot_general(
            keys, heads_down(q_ref, pair * PAIR, PAIR), NT, preferred_element_type=jnp.float32
        )
        here[:own] = jnp.where(allowed, here[:own], -1e30)
        top = jnp.max(here[...], axis=0, keepdims=True) * scale
        exponent = jnp.exp2(here[...] * scale - top)
        here[...] = exponent
        total = jnp.sum(exponent, axis=0, keepdims=True)
        inverse = jnp.where(live, 1.0 / total, 0.0)
        p_ref[0, :, cols] = (here[...] * inverse).astype(jnp.bfloat16)
    dv = jnp.dot(p_ref[0], heads_down(do_ref, 0, GROUP), preferred_element_type=jnp.float32)
    dvown_ref[...] = dv[:own]
    start = own
    for ref in dv_refs:
        ref[...] = dv[start : start + ref.shape[0]].astype(jnp.bfloat16)
        start += ref.shape[0]


def grads_kernel(n_slots, factor, weight_ref, q_ref, do_ref, p_ref, dv_ref, kown_ref, vown_ref, *refs):
    kslot_refs = refs[:n_slots]
    vslot_refs = refs[n_slots : 2 * n_slots]
    out_ref, dq_ref, dkown_ref, dvown_ref = refs[2 * n_slots : 2 * n_slots + 4]
    dk_refs = refs[2 * n_slots + 4 : 3 * n_slots + 4]
    dp_ref, ds_ref = refs[3 * n_slots + 4 :]
    rows = q_ref.shape[0]
    own = kown_ref.shape[0]
    weight = weight_ref[0]
    keys = jnp.concatenate([kown_ref[...]] + [ref[...] for ref in kslot_refs], axis=0)
    values = jnp.concatenate([vown_ref[...]] + [ref[...] for ref in vslot_refs], axis=0)
    keys_t = keys.T
    values_t = values.T
    width = PAIR * rows
    for pair in range(GROUP // PAIR):
        here = dp_ref.at[pair % 2]
        cols = slice(pair * width, (pair + 1) * width)
        do = heads_down(do_ref, pair * PAIR, PAIR)
        here[...] = lax.dot_general(values, do, NT, preferred_element_type=jnp.float32)
        attended = jnp.dot(values_t, p_ref[0, :, cols], preferred_element_type=jnp.float32)
        centre = jnp.sum(attended * do.astype(jnp.float32).T, axis=0, keepdims=True)
        ds_ref[:, cols] = (
            p_ref[0, :, cols].astype(jnp.float32) * (here[...] - centre)
        ).astype(jnp.bfloat16)
        dq = jnp.dot(keys_t, ds_ref[:, cols], preferred_element_type=jnp.float32) * (factor * weight)
        for i in range(PAIR):
            head = slice((pair * PAIR + i) * HD, (pair * PAIR + i + 1) * HD)
            lanes = slice(i * rows, (i + 1) * rows)
            out_ref[:, head] = attended[:, lanes].T.astype(jnp.bfloat16)
            dq_ref[:, head] = dq[:, lanes].T.astype(jnp.bfloat16)
    dk = jnp.dot(ds_ref[...], heads_down(q_ref, 0, GROUP), preferred_element_type=jnp.float32)
    dkown_ref[...] = (dk[:own] * (factor * weight)).astype(jnp.bfloat16)
    dvown_ref[...] = (dv_ref[...] * weight).astype(jnp.bfloat16)
    start = own
    for ref in dk_refs:
        ref[...] = dk[start : start + ref.shape[0]].astype(jnp.bfloat16)
        start += ref.shape[0]


def column_block(rows, cols):
    return pl.BlockSpec((rows, cols), lambda j: (0, j))


def shift(x, axis, by):
    size = lax.axis_size(axis)
    return lax.ppermute(x, axis, [(i, (i + by) % size) for i in range(size)])


def gather_slots(block):
    parts = lax.axis_size("tensor")
    rank = lax.axis_index("tensor")
    cols = block.shape[1] // parts
    pieces = []
    for s in range(parts):
        piece = lax.dynamic_slice_in_dim(block, ((rank + s) % parts) * cols, cols, 1)
        pieces.append(piece if s == 0 else shift(piece, "tensor", s))
    mine = jnp.concatenate(pieces, axis=0)
    return [mine] + [shift(mine, "response", s) for s in range(1, lax.axis_size("response"))]


def reduce_slots(slots, scale):
    parts = lax.axis_size("tensor")
    rank = lax.axis_index("tensor")
    total = slots[0].astype(jnp.float32)
    for s in range(1, len(slots)):
        total = total + shift(slots[s], "response", -s).astype(jnp.float32)
    total = (total * scale).astype(jnp.bfloat16)
    rows, cols = total.shape[0] // parts, total.shape[1]
    result = jnp.zeros((rows, cols * parts), jnp.bfloat16)
    for s in range(parts):
        piece = total[s * rows : (s + 1) * rows]
        piece = piece if s == 0 else shift(piece, "tensor", -s)
        result = lax.dynamic_update_slice_in_dim(result, piece, ((rank + s) % parts) * cols, 1)
    return result


def sum_over(x, axis):
    size = lax.axis_size(axis)
    if size & (size - 1):
        terms = [x] + [shift(x, axis, s) for s in range(1, size)]
        return functools.reduce(jnp.add, terms)
    step = 1
    while step < size:
        x = x + shift(x, axis, step)
        step *= 2
    return x


def body(queries, keys, values, prefix_keys, prefix_values, lengths, out_grad):
    q, k, v, do = queries[0], keys[0], values[0], out_grad[0]
    rows = q.shape[0]
    heads = k.shape[1] // HD
    bf16 = jnp.bfloat16
    kslots = gather_slots(prefix_keys[0])
    vslots = gather_slots(prefix_values[0])
    n_slots = len(kslots)
    slot_rows = kslots[0].shape[0]
    n_keys = rows + n_slots * slot_rows
    length = lengths[0]
    live_total = sum_over(sum_over(length.astype(jnp.float32), "prompt"), "response")
    slots = rows * lax.axis_size("prompt") * lax.axis_size("response")
    weight = slots / live_total
    factor = 1.0 / math.sqrt(HD)
    smem = pl.BlockSpec(memory_space=pltpu.SMEM)
    wide = column_block(rows, GROUP * HD)
    own = column_block(rows, HD)
    slot = column_block(slot_rows, HD)
    p_block = pl.BlockSpec((1, n_keys, GROUP * rows), lambda j: (j, 0, 0))
    slot_shape = jax.ShapeDtypeStruct((slot_rows, heads * HD), bf16)
    params = pltpu.CompilerParams(vmem_limit_bytes=VMEM_LIMIT)
    pairs_wide = PAIR * rows
    unit = 2 * n_keys * GROUP * rows * HD * heads
    probs, dv_own, *dv_slots = pl.pallas_call(
        functools.partial(probs_kernel, n_slots, factor * math.log2(math.e)),
        grid=(heads,),
        in_specs=[smem, wide, wide, own] + [slot] * n_slots,
        out_specs=[p_block, own] + [slot] * n_slots,
        out_shape=[
            jax.ShapeDtypeStruct((heads, n_keys, GROUP * rows), bf16),
            jax.ShapeDtypeStruct((rows, heads * HD), jnp.float32),
        ]
        + [slot_shape] * n_slots,
        scratch_shapes=[pltpu.VMEM((2, n_keys, pairs_wide), jnp.float32)],
        compiler_params=params,
        cost_estimate=pl.CostEstimate(
            flops=2 * unit, bytes_accessed=2 * heads * n_keys * GROUP * rows, transcendentals=heads * n_keys * GROUP * rows
        ),
        name="probs",
    )(length, q, do, k, *kslots)
    output, query_grad, key_grad, value_grad, *dk_slots = pl.pallas_call(
        functools.partial(grads_kernel, n_slots, factor),
        grid=(heads,),
        in_specs=[smem, wide, wide, p_block, own, own, own] + [slot] * (2 * n_slots),
        out_specs=[wide, wide, own, own] + [slot] * n_slots,
        out_shape=[
            jax.ShapeDtypeStruct(q.shape, bf16),
            jax.ShapeDtypeStruct(q.shape, bf16),
            jax.ShapeDtypeStruct(k.shape, bf16),
            jax.ShapeDtypeStruct(k.shape, bf16),
        ]
        + [slot_shape] * n_slots,
        scratch_shapes=[
            pltpu.VMEM((2, n_keys, pairs_wide), jnp.float32),
            pltpu.VMEM((n_keys, GROUP * rows), bf16),
        ],
        compiler_params=params,
        cost_estimate=pl.CostEstimate(
            flops=4 * unit, bytes_accessed=2 * heads * n_keys * GROUP * rows, transcendentals=0
        ),
        name="grads",
    )(weight, q, do, probs, dv_own, k, v, *kslots, *vslots)
    prefix_value_grad = reduce_slots(dv_slots, weight)
    prefix_key_grad = reduce_slots(dk_slots, weight * factor)
    return tuple(
        x[None]
        for x in (output, query_grad, key_grad, value_grad, prefix_key_grad, prefix_value_grad)
    )


def solution(mesh):
    in_specs = (
        P("prompt", "response", "tensor"),
        P("prompt", "response", "tensor"),
        P("prompt", "response", "tensor"),
        P("prompt", ("response", "tensor"), None),
        P("prompt", ("response", "tensor"), None),
        P("prompt", "response"),
        P("prompt", "response", "tensor"),
    )
    out_specs = (
        P("prompt", "response", "tensor"),
        P("prompt", "response", "tensor"),
        P("prompt", "response", "tensor"),
        P("prompt", "response", "tensor"),
        P("prompt", ("response", "tensor"), None),
        P("prompt", ("response", "tensor"), None),
    )
    return jax.shard_map(body, mesh=mesh, in_specs=in_specs, out_specs=out_specs, check_vma=False)
```

time: 278 us -> 82.4 us (0.30)
  waiting for transfers between devices: 135 us -> 12.1 us
  starting transfers between devices: 0.16 us -> 38.3 us
  local copies, waits for them, and re-layouts: 42.6 us -> 5.88 us
  blocking collectives: 35.8 us -> 0 us
  matrix products: 33.6 us -> 0 us
  Pallas kernels: 0 us -> 21.5 us
  other arithmetic: 13.9 us -> 0.17 us
  between operations: 15.9 us -> 4.07 us
    reduce_scatter x2 -> x0, waiting for transfers between devices: 98.4 us -> none  [the longest x1 66.7 us: body(): lax.psum_scatter(placed_values.astype(jnp.bfloat16), ('response', 'tensor...]
    ppermute x0 -> x20, starting transfers between devices: none -> 38.3 us  [shift(): return lax.ppermute(x, axis, [(i, (i + by) % size) for i in range(size)])]
    psum x1 -> x0, blocking collectives: 35.8 us -> none  [body(): live_total = lax.psum(length.astype(jnp.float32), ('prompt', 'response'))]
    all_gather x2 -> x0, waiting for transfers between devices: 35.3 us -> none  [the longest x1 35.3 us: body(): lax.all_gather(prefix_keys, ('response', 'tensor'), axis=1, tiled=True)]
    pallas_call x0 -> x2, Pallas kernels: none -> 21.5 us  [the longest x1 13 us: body(): pl.pallas_call(functools.partial(grads_kernel, n_slots, factor), grid=(he...]
    dot_general x20 -> x0, matrix products: 20.8 us -> none  [the longest x4 6.53 us: attend_head(): jnp.einsum('grk,kd->rgd', score_grad, all_keys, preferred_element_type=jn...]
    sub x4 -> x0, matrix products: 12.9 us -> none  [attend_head(): exponent = jnp.exp(scores - row_max)]
    ppermute x0 -> x20, waiting for transfers between devices: none -> 12.1 us  [shift(): return lax.ppermute(x, axis, [(i, (i + by) % size) for i in range(size)])]
  transfers between devices with their start and end apart: 4 -> 20, of which waited for: 3 -> 7; matrix products, arithmetic and copies ran while one was open for 15% -> 1% of each run, Pallas kernels for 0% -> 26%
where the time goes in v1:
time: 82.4 us; the launch traced here: 82 us
  starting transfers between devices  38.3 us (46%)
  Pallas kernels  21.5 us (26%)
  waiting for transfers between devices  12.1 us (15%)
  local copies, waits for them, and re-layouts  5.88 us (7%)
  between operations  4.07 us (5%)
    ppermute x20, starting transfers between devices, shift(): return lax.ppermute(x, axis, [(i, (i + by) % size) for i in range(size)])  38.3 us
    pallas_call x1, Pallas kernels, body(): pl.pallas_call(functools.partial(grads_kernel, n_slots, factor), grid=(he...  13 us
    ppermute x20, waiting for transfers between devices, shift(): return lax.ppermute(x, axis, [(i, (i + by) % size) for i in range(size)])  12.1 us
    pallas_call x1, Pallas kernels, body(): pl.pallas_call(functools.partial(probs_kernel, n_slots, factor * math.log...  8.46 us
    unnamed x12, local copies, waits for them, and re-layouts  4 us
    dynamic_slice x2, local copies, waits for them, and re-layouts, gather_slots(): piece = lax.dynamic_slice_in_dim(block, (rank + s) % parts * cols, cols, 1)  1.8 us
  transfers between devices with their start and end apart: 20, of which 7 were waited for; matrix products, arithmetic and copies ran while one was open for 1% of the time, Pallas kernels for 26%

profile of v1, /device:TPU:0, one launch (start us, length us, event | category | flops | bytes accessed | tf_op | source)
XLA Modules:
  0.0 82.0 jit_solution(5140205890655436275)
XLA Ops:
  0.6 0.0 copy-start.3
  0.7 0.9 %dynamic-slice_bitcast_fusion.3 = (bf16[64,512]{1,0:T(8,128)(2,1)S(1)}, bf16[64,512]{1,0:T(8,128)(2,1)S(1)}) fusion(bf16[1,64,1024]{2,1,0:T(8,128)(2,1)} %param.10, s32[]{:T(128)S(6)} %select_n.36, s32[]{:T(128)S(6)} %select_n.38), kind=kLoop, calls=%fused_computation.13 | loop fusion | bytes 262152 | tf_op jit(solution)/shard_map/dynamic_slice | solution.py:112
  1.6 3.0 %collective-permute-start.4 = (bf16[64,512]{1,0:T(8,128)(2,1)S(1)}, bf16[64,512]{1,0:T(8,128)(2,1)S(1)}, u32[]{:S(2)}, u32[]{:S(2)}) collective-permute-start(bf16[64,512]{1,0:T(8,128)(2,1)S(1)} %get-tuple-element.37), channel_id=1, source_target_pairs={{0,1},{1,0},{2,3},{3,2},{4,5},{5,4},{6,7},{7,6},{8,9},{9,8},{10,11... | collective-permute-start | bytes 196616 | tf_op jit(solution)/shard_map/ppermute | solution.py:103
  4.6 0.9 %dynamic-slice_bitcast_fusion.1 = (bf16[64,512]{1,0:T(8,128)(2,1)S(1)}, bf16[64,512]{1,0:T(8,128)(2,1)S(1)}) fusion(bf16[1,64,1024]{2,1,0:T(8,128)(2,1)} %param.11, s32[]{:T(128)S(6)} %select_n.36, s32[]{:T(128)S(6)} %select_n.38), kind=kLoop, calls=%fused_computation.11 | loop fusion | bytes 262152 | tf_op jit(solution)/shard_map/dynamic_slice | solution.py:112
  5.5 0.1 collective-permute-start.8
  5.6 1.4 %collective-permute-done.4 = bf16[64,512]{1,0:T(8,128)(2,1)S(1)} collective-permute-done((bf16[64,512]{1,0:T(8,128)(2,1)S(1)}, bf16[64,512]{1,0:T(8,128)(2,1)S(1)}, u32[]{:S(2)}, u32[]{:S(2)}) %collective-permute-start.4) | collective-permute-done | bytes 65568 | tf_op jit(solution)/shard_map/ppermute | solution.py:103
  7.0 2.1 %collective-permute-start.5 = (bf16[128,512]{1,0:T(8,128)(2,1)S(1)}, bf16[128,512]{1,0:T(8,128)(2,1)S(1)}, u32[]{:S(2)}, u32[]{:S(2)}) collective-permute-start(bf16[128,512]{1,0:T(8,128)(2,1)S(1)} %pad_maximum_fusion.refs_0_), channel_id=1, source_target_pairs={{0,2},{2,4},{4,6},{6,0},{1,3},{3,5},{5,7},{7,1},{8,10},{10,12},{12... | collective-permute-start | bytes 393224 | tf_op jit(solution)/shard_map/ppermute | solution.py:103
  9.0 2.6 %collective-permute-start.6 = (bf16[128,512]{1,0:T(8,128)(2,1)S(1)}, bf16[128,512]{1,0:T(8,128)(2,1)S(1)}, u32[]{:S(2)}, u32[]{:S(2)}) collective-permute-start(bf16[128,512]{1,0:T(8,128)(2,1)S(1)} %pad_maximum_fusion.refs_0_), channel_id=1, source_target_pairs={{0,4},{2,6},{4,0},{6,2},{1,5},{3,7},{5,1},{7,3},{8,12},{10,14},{12... | collective-permute-start | bytes 393224 | tf_op jit(solution)/shard_map/ppermute | solution.py:103
  11.6 1.3 %collective-permute-start.7 = (bf16[128,512]{1,0:T(8,128)(2,1)S(1)}, bf16[128,512]{1,0:T(8,128)(2,1)S(1)}, u32[]{:S(2)}, u32[]{:S(2)}) collective-permute-start(bf16[128,512]{1,0:T(8,128)(2,1)S(1)} %pad_maximum_fusion.refs_0_), channel_id=1, source_target_pairs={{0,6},{2,0},{4,2},{6,4},{1,7},{3,1},{5,3},{7,5},{8,14},{10,8},{12,... | collective-permute-start | bytes 393224 | tf_op jit(solution)/shard_map/ppermute | solution.py:103
  13.6 1.0 %collective-permute-start = (f32[1]{0:T(128)}, f32[1]{0:T(128)}, u32[]{:S(2)}, u32[]{:S(2)}) collective-permute-start(f32[1]{0:T(128)} %convert_element_type.33), channel_id=1, source_target_pairs={{0,8},{8,16},{16,24},{24,0},{1,9},{9,17},{17,25},{25,1},{2,10},{10... | collective-permute-start | bytes 20 | tf_op jit(solution)/shard_map/ppermute | solution.py:103
  14.6 2.1 %collective-permute-done = f32[1]{0:T(128)} collective-permute-done((f32[1]{0:T(128)}, f32[1]{0:T(128)}, u32[]{:S(2)}, u32[]{:S(2)}) %collective-permute-start) | collective-permute-done | bytes 36 | tf_op jit(solution)/shard_map/ppermute | solution.py:103
  17.4 2.9 %collective-permute-start.1 = (f32[1]{0:T(128)}, f32[1]{0:T(128)}, u32[]{:S(2)}, u32[]{:S(2)}) collective-permute-start(f32[1]{0:T(128)} %add.61), channel_id=1, source_target_pairs={{0,16},{8,24},{16,0},{24,8},{1,17},{9,25},{17,1},{25,9},{2,18},{10... | collective-permute-start | bytes 20 | tf_op jit(solution)/shard_map/ppermute | solution.py:103
  20.2 0.9 %collective-permute-done.1 = f32[1]{0:T(128)} collective-permute-done((f32[1]{0:T(128)}, f32[1]{0:T(128)}, u32[]{:S(2)}, u32[]{:S(2)}) %collective-permute-start.1) | collective-permute-done | bytes 36 | tf_op jit(solution)/shard_map/ppermute | solution.py:103
  21.7 2.0 %collective-permute-start.2 = (f32[1]{0:T(128)}, f32[1]{0:T(128)}, u32[]{:S(2)}, u32[]{:S(2)}) collective-permute-start(f32[1]{0:T(128)} %add.62), channel_id=1, source_target_pairs={{0,2},{2,4},{4,6},{6,0},{1,3},{3,5},{5,7},{7,1},{8,10},{10,12},{12... | collective-permute-start | bytes 20 | tf_op jit(solution)/shard_map/ppermute | solution.py:103
  23.7 3.5 %collective-permute-done.2 = f32[1]{0:T(128)} collective-permute-done((f32[1]{0:T(128)}, f32[1]{0:T(128)}, u32[]{:S(2)}, u32[]{:S(2)}) %collective-permute-start.2) | collective-permute-done | bytes 36 | tf_op jit(solution)/shard_map/ppermute | solution.py:103
  27.8 1.4 %collective-permute-start.3 = (f32[1]{0:T(128)}, f32[1]{0:T(128)}, u32[]{:S(2)}, u32[]{:S(2)}) collective-permute-start(f32[1]{0:T(128)} %add.63), channel_id=1, source_target_pairs={{0,4},{2,6},{4,0},{6,2},{1,5},{3,7},{5,1},{7,3},{8,12},{10,14},{12... | collective-permute-start | bytes 20 | tf_op jit(solution)/shard_map/ppermute | solution.py:103
  29.2 0.0 collective-permute-done.8
  29.2 3.0 %collective-permute-start.10 = (bf16[128,512]{1,0:T(8,128)(2,1)S(1)}, bf16[128,512]{1,0:T(8,128)(2,1)S(1)}, u32[]{:S(2)}, u32[]{:S(2)}) collective-permute-start(bf16[128,512]{1,0:T(8,128)(2,1)S(1)} %pad_maximum_fusion.1.refs_4_), channel_id=1, source_target_pairs={{0,4},{2,6},{4,0},{6,2},{1,5},{3,7},{5,1},{7,3},{8,12},{10,14},{12... | collective-permute-start | bytes 393224 | tf_op jit(solution)/shard_map/ppermute | solution.py:103
  32.2 0.3 collective-permute-done.3
  32.5 0.0 collective-permute-start.11
  32.5 0.0 collective-permute-done.5.refs_1_
  32.5 2.0 %collective-permute-start.9 = (bf16[128,512]{1,0:T(8,128)(2,1)S(1)}, bf16[128,512]{1,0:T(8,128)(2,1)S(1)}, u32[]{:S(2)}, u32[]{:S(2)}) collective-permute-start(bf16[128,512]{1,0:T(8,128)(2,1)S(1)} %pad_maximum_fusion.1.refs_4_), channel_id=1, source_target_pairs={{0,2},{2,4},{4,6},{6,0},{1,3},{3,5},{5,7},{7,1},{8,10},{10,12},{12... | collective-permute-start | bytes 393224 | tf_op jit(solution)/shard_map/ppermute | solution.py:103
  35.2 0.0 collective-permute-done.6.refs_2_
  35.2 0.0 collective-permute-done.7.refs_3_
  35.3 0.0 copy-start
  35.3 1.2 %copy-done = bf16[1,128,4096]{2,1,0:T(8,128)(2,1)S(1)} copy-done((bf16[1,128,4096]{2,1,0:T(8,128)(2,1)S(1)}, bf16[1,128,4096]{2,1,0:T(8,128)(2,1)}, u32[]{:S(2)}) %copy-start) | copy-done | bytes 1048600
  36.5 0.0 copy-start.1
  36.5 1.2 %copy-done.1 = bf16[1,128,4096]{2,1,0:T(8,128)(2,1)S(1)} copy-done((bf16[1,128,4096]{2,1,0:T(8,128)(2,1)S(1)}, bf16[1,128,4096]{2,1,0:T(8,128)(2,1)}, u32[]{:S(2)}) %copy-start.1) | copy-done | bytes 1048600
  37.7 0.0 copy-start.2
  37.7 0.9 %copy-done.2 = bf16[1,128,512]{2,1,0:T(8,128)(2,1)S(1)} copy-done((bf16[1,128,512]{2,1,0:T(8,128)(2,1)S(1)}, bf16[1,128,512]{2,1,0:T(8,128)(2,1)}, u32[]{:S(2)}) %copy-start.2) | copy-done | bytes 131096
  38.6 8.5 %probs.1 = (bf16[4,640,1024]{2,1,0:T(8,128)(2,1)}, f32[128,512]{1,0:T(8,128)S(1)}, bf16[128,512]{1,0:T(8,128)(2,1)S(1)}, bf16[128,512]{1,0:T(8,128)(2,1)S(1)}, b...) custom-call(s32[1]{0:T(128)} %bitcast.32.length_ref, bf16[128,4096]{1,0:T(8,128)(2,1)S(1)} %bitcast.33, ...), custom_call_target="tpu_custom_call" | custom-call | flops 1342177280 | bytes 5242880 | tf_op jit(solution)/shard_map/probs/pallas_call | solution.py:170
  47.1 1.8 %collective-permute-start.16 = (bf16[128,512]{1,0:T(8,128)(2,1)S(1)}, bf16[128,512]{1,0:T(8,128)(2,1)S(1)}, u32[]{:S(2)}, u32[]{:S(2)}) collective-permute-start(bf16[128,512]{1,0:T(8,128)(2,1)S(1)} %get-tuple-element.31), channel_id=1, source_target_pairs={{0,6},{2,0},{4,2},{6,4},{1,7},{3,1},{5,3},{7,5},{8,14},{10,8},{12,... | collective-permute-start | bytes 393224 | tf_op jit(solution)/shard_map/ppermute | solution.py:103
  48.9 0.0 collective-permute-start.17
  48.9 0.0 collective-permute-done.10.refs_6_
  48.9 0.6 collective-permute-start.18
  49.4 0.0 collective-permute-done.11.refs_7_
  49.4 0.0 collective-permute-done.9.refs_5_
  49.4 0.0 copy-done.3
  49.5 13.0 %grads.1 = (bf16[128,4096]{1,0:T(8,128)(2,1)}, bf16[128,4096]{1,0:T(8,128)(2,1)}, bf16[128,512]{1,0:T(8,128)(2,1)}, bf16[128,512]{1,0:T(8,128)(2,1)}, bf16[128,5...) custom-call(f32[1]{0:T(128)} %div.3.weight_ref, ...), custom_call_target="tpu_custom_call" | custom-call | flops 2684354560 | bytes 5242880 | tf_op jit(solution)/shard_map/grads/pallas_call | solution.py:187
  62.5 3.3 %collective-permute-start.12 = (bf16[128,512]{1,0:T(8,128)(2,1)S(1)}, bf16[128,512]{1,0:T(8,128)(2,1)S(1)}, u32[]{:S(2)}, u32[]{:S(2)}) collective-permute-start(bf16[128,512]{1,0:T(8,128)(2,1)S(1)} %get-tuple-element.27), channel_id=1, source_target_pairs={{0,6},{2,0},{4,2},{6,4},{1,7},{3,1},{5,3},{7,5},{8,14},{10,8},{12,... | collective-permute-start | bytes 393224 | tf_op jit(solution)/shard_map/ppermute | solution.py:103
  65.7 1.1 %collective-permute-start.13 = (bf16[128,512]{1,0:T(8,128)(2,1)S(1)}, bf16[128,512]{1,0:T(8,128)(2,1)S(1)}, u32[]{:S(2)}, u32[]{:S(2)}) collective-permute-start(bf16[128,512]{1,0:T(8,128)(2,1)S(1)} %get-tuple-element.28), channel_id=1, source_target_pairs={{0,4},{2,6},{4,0},{6,2},{1,5},{3,7},{5,1},{7,3},{8,12},{10,14},{12... | collective-permute-start | bytes 393224 | tf_op jit(solution)/shard_map/ppermute | solution.py:103
  66.9 0.0 collective-permute-done.16
  66.9 0.2 collective-permute-start.14
  67.1 0.0 collective-permute-done.17
  67.1 0.0 collective-permute-done.18
  67.1 0.1 multiply_convert_fusion
  67.2 5.0 %collective-permute-start.19 = (bf16[64,512]{1,0:T(8,128)(2,1)S(1)}, bf16[64,512]{1,0:T(8,128)(2,1)S(1)}, u32[]{:S(2)}, u32[]{:S(2)}) collective-permute-start(bf16[64,512]{1,0:T(8,128)(2,1)S(1)} %slice.19), channel_id=1, source_target_pairs={{0,1},{1,0},{2,3},{3,2},{4,5},{5,4},{6,7},{7,6},{8,9},{9,8},{10,11... | collective-permute-start | bytes 196616 | tf_op jit(solution)/shard_map/ppermute | solution.py:103
  72.2 0.0 collective-permute-done.12
  72.2 1.8 %collective-permute-done.13 = bf16[128,512]{1,0:T(8,128)(2,1)S(1)} collective-permute-done((bf16[128,512]{1,0:T(8,128)(2,1)S(1)}, bf16[128,512]{1,0:T(8,128)(2,1)S(1)}, u32[]{:S(2)}, u32[]{:S(2)}) %collective-permute-start.13) | collective-permute-done | bytes 131104 | tf_op jit(solution)/shard_map/ppermute | solution.py:103
  74.0 0.0 collective-permute-done.14
  74.0 0.1 multiply_convert_fusion.1
  74.1 5.0 %collective-permute-start.15 = (bf16[64,512]{1,0:T(8,128)(2,1)S(1)}, bf16[64,512]{1,0:T(8,128)(2,1)S(1)}, u32[]{:S(2)}, u32[]{:S(2)}) collective-permute-start(bf16[64,512]{1,0:T(8,128)(2,1)S(1)} %slice.17), channel_id=1, source_target_pairs={{0,1},{1,0},{2,3},{3,2},{4,5},{5,4},{6,7},{7,6},{8,9},{9,8},{10,11... | collective-permute-start | bytes 196616 | tf_op jit(solution)/shard_map/ppermute | solution.py:103
  79.1 0.0 collective-permute-done.19
  79.2 0.0 copy-start.5
  79.2 2.2 %collective-permute-done.15 = bf16[64,512]{1,0:T(8,128)(2,1)S(1)} collective-permute-done((bf16[64,512]{1,0:T(8,128)(2,1)S(1)}, bf16[64,512]{1,0:T(8,128)(2,1)S(1)}, u32[]{:S(2)}, u32[]{:S(2)}) %collective-permute-start.15) | collective-permute-done | bytes 65568 | tf_op jit(solution)/shard_map/ppermute | solution.py:103
  81.4 0.0 copy-start.4
  81.4 0.0 copy-done.5
  81.4 0.6 copy-done.4
  (10 shorter events, 0.1 us)
Async XLA Ops:
  0.6 48.8 %copy-start.3 = (bf16[1,128,512]{2,1,0:T(8,128)(2,1)S(1)}, bf16[1,128,512]{2,1,0:T(8,128)(2,1)}, u32[]{:S(2)}) copy-start(bf16[1,128,512]{2,1,0:T(8,128)(2,1)} %param.9) | copy-start | bytes 393220
  1.6 5.4 %collective-permute-start.4 = (bf16[64,512]{1,0:T(8,128)(2,1)S(1)}, bf16[64,512]{1,0:T(8,128)(2,1)S(1)}, u32[]{:S(2)}, u32[]{:S(2)}) collective-permute-start(bf16[64,512]{1,0:T(8,128)(2,1)S(1)} %get-tuple-element.37), channel_id=1, source_target_pairs={{0,1},{1,0},{2,3},{3,2},{4,5},{5,4},{6,7},{7,6},{8,9},{9,8},{10,11... | collective-permute-start | bytes 196616 | tf_op jit(solution)/shard_map/ppermute | solution.py:103
  5.5 23.7 %collective-permute-start.8 = (bf16[64,512]{1,0:T(8,128)(2,1)S(1)}, bf16[64,512]{1,0:T(8,128)(2,1)S(1)}, u32[]{:S(2)}, u32[]{:S(2)}) collective-permute-start(bf16[64,512]{1,0:T(8,128)(2,1)S(1)} %get-tuple-element.35), channel_id=1, source_target_pairs={{0,1},{1,0},{2,3},{3,2},{4,5},{5,4},{6,7},{7,6},{8,9},{9,8},{10,11... | collective-permute-start | bytes 196616 | tf_op jit(solution)/shard_map/ppermute | solution.py:103
  7.0 25.6 %collective-permute-start.5 = (bf16[128,512]{1,0:T(8,128)(2,1)S(1)}, bf16[128,512]{1,0:T(8,128)(2,1)S(1)}, u32[]{:S(2)}, u32[]{:S(2)}) collective-permute-start(bf16[128,512]{1,0:T(8,128)(2,1)S(1)} %pad_maximum_fusion.refs_0_), channel_id=1, source_target_pairs={{0,2},{2,4},{4,6},{6,0},{1,3},{3,5},{5,7},{7,1},{8,10},{10,12},{12... | collective-permute-start | bytes 393224 | tf_op jit(solution)/shard_map/ppermute | solution.py:103
  9.0 26.2 %collective-permute-start.6 = (bf16[128,512]{1,0:T(8,128)(2,1)S(1)}, bf16[128,512]{1,0:T(8,128)(2,1)S(1)}, u32[]{:S(2)}, u32[]{:S(2)}) collective-permute-start(bf16[128,512]{1,0:T(8,128)(2,1)S(1)} %pad_maximum_fusion.refs_0_), channel_id=1, source_target_pairs={{0,4},{2,6},{4,0},{6,2},{1,5},{3,7},{5,1},{7,3},{8,12},{10,14},{12... | collective-permute-start | bytes 393224 | tf_op jit(solution)/shard_map/ppermute | solution.py:103
  11.6 23.6 %collective-permute-start.7 = (bf16[128,512]{1,0:T(8,128)(2,1)S(1)}, bf16[128,512]{1,0:T(8,128)(2,1)S(1)}, u32[]{:S(2)}, u32[]{:S(2)}) collective-permute-start(bf16[128,512]{1,0:T(8,128)(2,1)S(1)} %pad_maximum_fusion.refs_0_), channel_id=1, source_target_pairs={{0,6},{2,0},{4,2},{6,4},{1,7},{3,1},{5,3},{7,5},{8,14},{10,8},{12,... | collective-permute-start | bytes 393224 | tf_op jit(solution)/shard_map/ppermute | solution.py:103
  13.6 3.1 %collective-permute-start = (f32[1]{0:T(128)}, f32[1]{0:T(128)}, u32[]{:S(2)}, u32[]{:S(2)}) collective-permute-start(f32[1]{0:T(128)} %convert_element_type.33), channel_id=1, source_target_pairs={{0,8},{8,16},{16,24},{24,0},{1,9},{9,17},{17,25},{25,1},{2,10},{10... | collective-permute-start | bytes 20 | tf_op jit(solution)/shard_map/ppermute | solution.py:103
  17.4 3.7 %collective-permute-start.1 = (f32[1]{0:T(128)}, f32[1]{0:T(128)}, u32[]{:S(2)}, u32[]{:S(2)}) collective-permute-start(f32[1]{0:T(128)} %add.61), channel_id=1, source_target_pairs={{0,16},{8,24},{16,0},{24,8},{1,17},{9,25},{17,1},{25,9},{2,18},{10... | collective-permute-start | bytes 20 | tf_op jit(solution)/shard_map/ppermute | solution.py:103
  21.7 5.5 %collective-permute-start.2 = (f32[1]{0:T(128)}, f32[1]{0:T(128)}, u32[]{:S(2)}, u32[]{:S(2)}) collective-permute-start(f32[1]{0:T(128)} %add.62), channel_id=1, source_target_pairs={{0,2},{2,4},{4,6},{6,0},{1,3},{3,5},{5,7},{7,1},{8,10},{10,12},{12... | collective-permute-start | bytes 20 | tf_op jit(solution)/shard_map/ppermute | solution.py:103
  27.8 4.7 %collective-permute-start.3 = (f32[1]{0:T(128)}, f32[1]{0:T(128)}, u32[]{:S(2)}, u32[]{:S(2)}) collective-permute-start(f32[1]{0:T(128)} %add.63), channel_id=1, source_target_pairs={{0,4},{2,6},{4,0},{6,2},{1,5},{3,7},{5,1},{7,3},{8,12},{10,14},{12... | collective-permute-start | bytes 20 | tf_op jit(solution)/shard_map/ppermute | solution.py:103
  29.2 19.6 %collective-permute-start.10 = (bf16[128,512]{1,0:T(8,128)(2,1)S(1)}, bf16[128,512]{1,0:T(8,128)(2,1)S(1)}, u32[]{:S(2)}, u32[]{:S(2)}) collective-permute-start(bf16[128,512]{1,0:T(8,128)(2,1)S(1)} %pad_maximum_fusion.1.refs_4_), channel_id=1, source_target_pairs={{0,4},{2,6},{4,0},{6,2},{1,5},{3,7},{5,1},{7,3},{8,12},{10,14},{12... | collective-permute-start | bytes 393224 | tf_op jit(solution)/shard_map/ppermute | solution.py:103
  32.5 16.9 %collective-permute-start.11 = (bf16[128,512]{1,0:T(8,128)(2,1)S(1)}, bf16[128,512]{1,0:T(8,128)(2,1)S(1)}, u32[]{:S(2)}, u32[]{:S(2)}) collective-permute-start(bf16[128,512]{1,0:T(8,128)(2,1)S(1)} %pad_maximum_fusion.1.refs_4_), channel_id=1, source_target_pairs={{0,6},{2,0},{4,2},{6,4},{1,7},{3,1},{5,3},{7,5},{8,14},{10,8},{12,... | collective-permute-start | bytes 393224 | tf_op jit(solution)/shard_map/ppermute | solution.py:103
  32.5 16.9 %collective-permute-start.9 = (bf16[128,512]{1,0:T(8,128)(2,1)S(1)}, bf16[128,512]{1,0:T(8,128)(2,1)S(1)}, u32[]{:S(2)}, u32[]{:S(2)}) collective-permute-start(bf16[128,512]{1,0:T(8,128)(2,1)S(1)} %pad_maximum_fusion.1.refs_4_), channel_id=1, source_target_pairs={{0,2},{2,4},{4,6},{6,0},{1,3},{3,5},{5,7},{7,1},{8,10},{10,12},{12... | collective-permute-start | bytes 393224 | tf_op jit(solution)/shard_map/ppermute | solution.py:103
  35.3 1.2 %copy-start = (bf16[1,128,4096]{2,1,0:T(8,128)(2,1)S(1)}, bf16[1,128,4096]{2,1,0:T(8,128)(2,1)}, u32[]{:S(2)}) copy-start(bf16[1,128,4096]{2,1,0:T(8,128)(2,1)} %param.7) | copy-start | bytes 3145732
  36.5 1.2 %copy-start.1 = (bf16[1,128,4096]{2,1,0:T(8,128)(2,1)S(1)}, bf16[1,128,4096]{2,1,0:T(8,128)(2,1)}, u32[]{:S(2)}) copy-start(bf16[1,128,4096]{2,1,0:T(8,128)(2,1)} %param.13) | copy-start | bytes 3145732
  37.7 0.9 %copy-start.2 = (bf16[1,128,512]{2,1,0:T(8,128)(2,1)S(1)}, bf16[1,128,512]{2,1,0:T(8,128)(2,1)}, u32[]{:S(2)}) copy-start(bf16[1,128,512]{2,1,0:T(8,128)(2,1)} %param.8) | copy-start | bytes 393220
  47.1 19.8 %collective-permute-start.16 = (bf16[128,512]{1,0:T(8,128)(2,1)S(1)}, bf16[128,512]{1,0:T(8,128)(2,1)S(1)}, u32[]{:S(2)}, u32[]{:S(2)}) collective-permute-start(bf16[128,512]{1,0:T(8,128)(2,1)S(1)} %get-tuple-element.31), channel_id=1, source_target_pairs={{0,6},{2,0},{4,2},{6,4},{1,7},{3,1},{5,3},{7,5},{8,14},{10,8},{12,... | collective-permute-start | bytes 393224 | tf_op jit(solution)/shard_map/ppermute | solution.py:103
  48.9 18.2 %collective-permute-start.17 = (bf16[128,512]{1,0:T(8,128)(2,1)S(1)}, bf16[128,512]{1,0:T(8,128)(2,1)S(1)}, u32[]{:S(2)}, u32[]{:S(2)}) collective-permute-start(bf16[128,512]{1,0:T(8,128)(2,1)S(1)} %get-tuple-element.32), channel_id=1, source_target_pairs={{0,4},{2,6},{4,0},{6,2},{1,5},{3,7},{5,1},{7,3},{8,12},{10,14},{12... | collective-permute-start | bytes 393224 | tf_op jit(solution)/shard_map/ppermute | solution.py:103
  48.9 18.2 %collective-permute-start.18 = (bf16[128,512]{1,0:T(8,128)(2,1)S(1)}, bf16[128,512]{1,0:T(8,128)(2,1)S(1)}, u32[]{:S(2)}, u32[]{:S(2)}) collective-permute-start(bf16[128,512]{1,0:T(8,128)(2,1)S(1)} %get-tuple-element.33), channel_id=1, source_target_pairs={{0,2},{2,4},{4,6},{6,0},{1,3},{3,5},{5,7},{7,1},{8,10},{10,12},{12... | collective-permute-start | bytes 393224 | tf_op jit(solution)/shard_map/ppermute | solution.py:103
  62.5 9.7 %collective-permute-start.12 = (bf16[128,512]{1,0:T(8,128)(2,1)S(1)}, bf16[128,512]{1,0:T(8,128)(2,1)S(1)}, u32[]{:S(2)}, u32[]{:S(2)}) collective-permute-start(bf16[128,512]{1,0:T(8,128)(2,1)S(1)} %get-tuple-element.27), channel_id=1, source_target_pairs={{0,6},{2,0},{4,2},{6,4},{1,7},{3,1},{5,3},{7,5},{8,14},{10,8},{12,... | collective-permute-start | bytes 393224 | tf_op jit(solution)/shard_map/ppermute | solution.py:103
  65.7 8.3 %collective-permute-start.13 = (bf16[128,512]{1,0:T(8,128)(2,1)S(1)}, bf16[128,512]{1,0:T(8,128)(2,1)S(1)}, u32[]{:S(2)}, u32[]{:S(2)}) collective-permute-start(bf16[128,512]{1,0:T(8,128)(2,1)S(1)} %get-tuple-element.28), channel_id=1, source_target_pairs={{0,4},{2,6},{4,0},{6,2},{1,5},{3,7},{5,1},{7,3},{8,12},{10,14},{12... | collective-permute-start | bytes 393224 | tf_op jit(solution)/shard_map/ppermute | solution.py:103
  66.9 7.2 %collective-permute-start.14 = (bf16[128,512]{1,0:T(8,128)(2,1)S(1)}, bf16[128,512]{1,0:T(8,128)(2,1)S(1)}, u32[]{:S(2)}, u32[]{:S(2)}) collective-permute-start(bf16[128,512]{1,0:T(8,128)(2,1)S(1)} %get-tuple-element.29), channel_id=1, source_target_pairs={{0,2},{2,4},{4,6},{6,0},{1,3},{3,5},{5,7},{7,1},{8,10},{10,12},{12... | collective-permute-start | bytes 393224 | tf_op jit(solution)/shard_map/ppermute | solution.py:103
  67.2 11.9 %collective-permute-start.19 = (bf16[64,512]{1,0:T(8,128)(2,1)S(1)}, bf16[64,512]{1,0:T(8,128)(2,1)S(1)}, u32[]{:S(2)}, u32[]{:S(2)}) collective-permute-start(bf16[64,512]{1,0:T(8,128)(2,1)S(1)} %slice.19), channel_id=1, source_target_pairs={{0,1},{1,0},{2,3},{3,2},{4,5},{5,4},{6,7},{7,6},{8,9},{9,8},{10,11... | collective-permute-start | bytes 196616 | tf_op jit(solution)/shard_map/ppermute | solution.py:103
  74.1 7.2 %collective-permute-start.15 = (bf16[64,512]{1,0:T(8,128)(2,1)S(1)}, bf16[64,512]{1,0:T(8,128)(2,1)S(1)}, u32[]{:S(2)}, u32[]{:S(2)}) collective-permute-start(bf16[64,512]{1,0:T(8,128)(2,1)S(1)} %slice.17), channel_id=1, source_target_pairs={{0,1},{1,0},{2,3},{3,2},{4,5},{5,4},{6,7},{7,6},{8,9},{9,8},{10,11... | collective-permute-start | bytes 196616 | tf_op jit(solution)/shard_map/ppermute | solution.py:103
  79.2 2.2 %copy-start.5 = (bf16[1,64,1024]{2,1,0:T(8,128)(2,1)}, bf16[1,64,1024]{2,1,0:T(8,128)(2,1)S(1)}, u32[]{:S(2)}) copy-start(bf16[1,64,1024]{2,1,0:T(8,128)(2,1)S(1)} %bitcast_dynamic-update-slice_fusion) | copy-start | bytes 393220
  81.4 0.7 copy-start.4

commit v2 on v1

--- a/solution.py
+++ b/solution.py
@@ -11,7 +11,7 @@
 HD = 128
 GROUP = 8
 PAIR = 2
-VMEM_LIMIT = 48 * 1024 * 1024
+VMEM_LIMIT = 60 * 1024 * 1024
 NT = (((1,), (1,)), ((), ()))
 
 
@@ -103,44 +103,28 @@
     return lax.ppermute(x, axis, [(i, (i + by) % size) for i in range(size)])
 
 
-def gather_slots(block):
+def exchange(x):
+    return lax.all_to_all(x, ("response", "tensor"), split_axis=0, concat_axis=0, tiled=True)
+
+
+def gather_prefix(block):
     parts = lax.axis_size("tensor")
-    rank = lax.axis_index("tensor")
-    cols = block.shape[1] // parts
-    pieces = []
-    for s in range(parts):
-        piece = lax.dynamic_slice_in_dim(block, ((rank + s) % parts) * cols, cols, 1)
-        pieces.append(piece if s == 0 else shift(piece, "tensor", s))
-    mine = jnp.concatenate(pieces, axis=0)
-    return [mine] + [shift(mine, "response", s) for s in range(1, lax.axis_size("response"))]
-
-
-def reduce_slots(slots, scale):
+    cut = jnp.split(block, parts, axis=1)
+    return exchange(jnp.concatenate(cut * lax.axis_size("response"), axis=0))
+
+
+def reduce_prefix(terms, scale):
     parts = lax.axis_size("tensor")
-    rank = lax.axis_index("tensor")
-    total = slots[0].astype(jnp.float32)
-    for s in range(1, len(slots)):
-        total = total + shift(slots[s], "response", -s).astype(jnp.float32)
-    total = (total * scale).astype(jnp.bfloat16)
-    rows, cols = total.shape[0] // parts, total.shape[1]
-    result = jnp.zeros((rows, cols * parts), jnp.bfloat16)
-    for s in range(parts):
-        piece = total[s * rows : (s + 1) * rows]
-        piece = piece if s == 0 else shift(piece, "tensor", -s)
-        result = lax.dynamic_update_slice_in_dim(result, piece, ((rank + s) % parts) * cols, 1)
-    return result
+    cols = terms.shape[1]
+    pieces = exchange(terms).reshape(lax.axis_size("response"), parts, -1, cols)
+    total = jnp.sum(pieces.astype(jnp.float32), axis=0) * scale
+    total = total.astype(jnp.bfloat16)
+    return jnp.concatenate([total[i] for i in range(parts)], axis=1)
 
 
 def sum_over(x, axis):
-    size = lax.axis_size(axis)
-    if size & (size - 1):
-        terms = [x] + [shift(x, axis, s) for s in range(1, size)]
-        return functools.reduce(jnp.add, terms)
-    step = 1
-    while step < size:
-        x = x + shift(x, axis, step)
-        step *= 2
-    return x
+    terms = [x] + [shift(x, axis, s) for s in range(1, lax.axis_size(axis))]
+    return functools.reduce(jnp.add, terms)
 
 
 def body(queries, keys, values, prefix_keys, prefix_values, lengths, out_grad):
@@ -148,8 +132,8 @@
     rows = q.shape[0]
     heads = k.shape[1] // HD
     bf16 = jnp.bfloat16
-    kslots = gather_slots(prefix_keys[0])
-    vslots = gather_slots(prefix_values[0])
+    kslots = [gather_prefix(prefix_keys[0])]
+    vslots = [gather_prefix(prefix_values[0])]
     n_slots = len(kslots)
     slot_rows = kslots[0].shape[0]
     n_keys = rows + n_slots * slot_rows
@@ -206,8 +190,8 @@
         ),
         name="grads",
     )(weight, q, do, probs, dv_own, k, v, *kslots, *vslots)
-    prefix_value_grad = reduce_slots(dv_slots, weight)
-    prefix_key_grad = reduce_slots(dk_slots, weight * factor)
+    prefix_value_grad = reduce_prefix(dv_slots[0], weight)
+    prefix_key_grad = reduce_prefix(dk_slots[0], weight * factor)
     return tuple(
         x[None]
         for x in (output, query_grad, key_grad, value_grad, prefix_key_grad, prefix_value_grad)

time: 82.4 us -> 118 us (1.43)
  local copies, waits for them, and re-layouts: 5.88 us -> 24.4 us
  blocking collectives: 0 us -> 18.1 us
  starting transfers between devices: 38.3 us -> 30.2 us
  waiting for transfers between devices: 12.1 us -> 16.4 us
    ppermute x20 -> x6, starting transfers between devices: 38.3 us -> 15.6 us  [shift(): return lax.ppermute(x, axis, [(i, (i + by) % size) for i in range(size)])]
    all_to_all x0 -> x1, blocking collectives: none -> 18.1 us  [exchange(): lax.all_to_all(x, ('response', 'tensor'), split_axis=0, concat_axis=0, ti...]
    unnamed x12 -> x18, local copies, waits for them, and re-layouts: 4 us -> 21.4 us
    all_to_all x0 -> x3, waiting for transfers between devices: none -> 16.3 us  [exchange(): lax.all_to_all(x, ('response', 'tensor'), split_axis=0, concat_axis=0, ti...]
    all_to_all x0 -> x3, starting transfers between devices: none -> 14.6 us  [exchange(): lax.all_to_all(x, ('response', 'tensor'), split_axis=0, concat_axis=0, ti...]
    ppermute x20 -> x6, waiting for transfers between devices: 12.1 us -> 0.01 us  [shift(): return lax.ppermute(x, axis, [(i, (i + by) % size) for i in range(size)])]
    concatenate x0 -> x2, local copies, waits for them, and re-layouts: none -> 2.94 us  [gather_prefix(): return exchange(jnp.concatenate(cut * lax.axis_size('response'), axis=0))]
    dynamic_slice x2 -> x0, local copies, waits for them, and re-layouts: 1.8 us -> none  [gather_slots(): piece = lax.dynamic_slice_in_dim(block, (rank + s) % parts * cols, cols, 1)]
  transfers between devices with their start and end apart: 20 -> 9, of which waited for: 7 -> 2; matrix products, arithmetic and copies ran while one was open for 1% -> 10% of each run, Pallas kernels for 26% -> 8%
where the time goes in v2:
time: 118 us; the launch traced here: 117 us
  starting transfers between devices  30.2 us (26%)
  local copies, waits for them, and re-layouts  24.4 us (21%)
  Pallas kernels  22.1 us (19%)
  blocking collectives  18.1 us (15%)
  waiting for transfers between devices  16.4 us (14%)
  between operations  5.06 us (4%)
    unnamed x18, local copies, waits for them, and re-layouts  21.4 us
    all_to_all x1, blocking collectives, exchange(): lax.all_to_all(x, ('response', 'tensor'), split_axis=0, concat_axis=0, ti...  18.1 us
    all_to_all x3, waiting for transfers between devices, exchange(): lax.all_to_all(x, ('response', 'tensor'), split_axis=0, concat_axis=0, ti...  16.3 us
    ppermute x6, starting transfers between devices, shift(): return lax.ppermute(x, axis, [(i, (i + by) % size) for i in range(size)])  15.6 us
    all_to_all x3, starting transfers between devices, exchange(): lax.all_to_all(x, ('response', 'tensor'), split_axis=0, concat_axis=0, ti...  14.6 us
    pallas_call x1, Pallas kernels, body(): pl.pallas_call(functools.partial(grads_kernel, n_slots, factor), grid=(he...  13 us
    pallas_call x1, Pallas kernels, body(): pl.pallas_call(functools.partial(probs_kernel, n_slots, factor * math.log...  9.16 us
    concatenate x2, local copies, waits for them, and re-layouts, gather_prefix(): return exchange(jnp.concatenate(cut * lax.axis_size('response'), axis=0))  2.94 us
  transfers between devices with their start and end apart: 9, of which 2 were waited for; matrix products, arithmetic and copies ran while one was open for 10% of the time, Pallas kernels for 8%

profile of v2, /device:TPU:0, one launch (start us, length us, event | category | flops | bytes accessed | tf_op | source)
XLA Modules:
  0.0 117.0 jit_solution(932426157391961681)
XLA Ops:
  0.6 1.5 %slice_dynamic-update-slice_fusion.14 = bf16[512,512]{1,0:T(8,128)(2,1)} fusion(bf16[64,1024]{1,0:T(8,128)(2,1)} %bitcast.37), kind=kLoop, calls=%fused_computation.24 | loop fusion | bytes 131072
  2.1 1.5 %slice_dynamic-update-slice_fusion.10 = bf16[512,512]{1,0:T(8,128)(2,1)} fusion(bf16[512,512]{1,0:T(8,128)(2,1)} %slice_dynamic-update-slice_fusion.14, bf16[64,1024]{1,0:T(8,128)(2,1)} %bitcast.38), kind=kLoop, calls=%fused_computation.20 | loop fusion | bytes 131072
  3.6 1.5 %slice_dynamic-update-slice_fusion.13 = bf16[512,512]{1,0:T(8,128)(2,1)} fusion(bf16[512,512]{1,0:T(8,128)(2,1)} %slice_dynamic-update-slice_fusion.10, bf16[64,1024]{1,0:T(8,128)(2,1)} %bitcast.39), kind=kLoop, calls=%fused_computation.23 | loop fusion | bytes 131072
  5.1 1.5 %slice_dynamic-update-slice_fusion.9 = bf16[512,512]{1,0:T(8,128)(2,1)} fusion(bf16[512,512]{1,0:T(8,128)(2,1)} %slice_dynamic-update-slice_fusion.13, bf16[64,1024]{1,0:T(8,128)(2,1)} %bitcast.40), kind=kLoop, calls=%fused_computation.19 | loop fusion | bytes 131072
  6.5 1.5 %slice_dynamic-update-slice_fusion.12 = bf16[512,512]{1,0:T(8,128)(2,1)} fusion(bf16[512,512]{1,0:T(8,128)(2,1)} %slice_dynamic-update-slice_fusion.9, bf16[64,1024]{1,0:T(8,128)(2,1)} %bitcast.41), kind=kLoop, calls=%fused_computation.22 | loop fusion | bytes 131072
  8.0 1.5 %slice_dynamic-update-slice_fusion.8 = bf16[512,512]{1,0:T(8,128)(2,1)} fusion(bf16[512,512]{1,0:T(8,128)(2,1)} %slice_dynamic-update-slice_fusion.12, bf16[64,1024]{1,0:T(8,128)(2,1)} %bitcast.42), kind=kLoop, calls=%fused_computation.18 | loop fusion | bytes 131072
  9.5 1.5 %slice_dynamic-update-slice_fusion.15 = bf16[512,512]{1,0:T(8,128)(2,1)} fusion(bf16[512,512]{1,0:T(8,128)(2,1)} %slice_dynamic-update-slice_fusion.8, bf16[64,1024]{1,0:T(8,128)(2,1)} %bitcast.43), kind=kLoop, calls=%fused_computation.25 | loop fusion | bytes 131072
  10.9 1.5 %slice_dynamic-update-slice_fusion.11 = bf16[512,512]{1,0:T(8,128)(2,1)} fusion(bf16[512,512]{1,0:T(8,128)(2,1)} %slice_dynamic-update-slice_fusion.15, bf16[64,1024]{1,0:T(8,128)(2,1)} %bitcast.44), kind=kLoop, calls=%fused_computation.21 | loop fusion | bytes 131072 | tf_op jit(solution)/shard_map/concatenate | solution.py:113
  12.4 7.3 %all-to-all-start = ((bf16[8,64,512]{2,1,0:T(8,128)(2,1)}), bf16[8,64,512]{2,1,0:T(8,128)(2,1)S(1)}, u32[]{:S(2)}, u32[]{:S(2)}) async-start(bf16[8,64,512]{2,1,0:T(8,128)(2,1)} %bitcast.5), calls=%async_computation | async-start | bytes 1048576 | tf_op jit(solution)/shard_map/all_to_all | solution.py:107
  19.7 1.5 %slice_dynamic-update-slice_fusion.6 = bf16[512,512]{1,0:T(8,128)(2,1)} fusion(bf16[64,1024]{1,0:T(8,128)(2,1)} %bitcast.45), kind=kLoop, calls=%fused_computation.16 | loop fusion | bytes 131072
  21.2 1.5 %slice_dynamic-update-slice_fusion.2 = bf16[512,512]{1,0:T(8,128)(2,1)} fusion(bf16[512,512]{1,0:T(8,128)(2,1)} %slice_dynamic-update-slice_fusion.6, bf16[64,1024]{1,0:T(8,128)(2,1)} %bitcast.46), kind=kLoop, calls=%fused_computation.12 | loop fusion | bytes 131072
  22.6 1.5 %slice_dynamic-update-slice_fusion.5 = bf16[512,512]{1,0:T(8,128)(2,1)} fusion(bf16[512,512]{1,0:T(8,128)(2,1)} %slice_dynamic-update-slice_fusion.2, bf16[64,1024]{1,0:T(8,128)(2,1)} %bitcast.47), kind=kLoop, calls=%fused_computation.15 | loop fusion | bytes 131072
  24.1 1.5 %slice_dynamic-update-slice_fusion.1 = bf16[512,512]{1,0:T(8,128)(2,1)} fusion(bf16[512,512]{1,0:T(8,128)(2,1)} %slice_dynamic-update-slice_fusion.5, bf16[64,1024]{1,0:T(8,128)(2,1)} %bitcast.48), kind=kLoop, calls=%fused_computation.11 | loop fusion | bytes 131072
  25.6 1.5 %slice_dynamic-update-slice_fusion.4 = bf16[512,512]{1,0:T(8,128)(2,1)} fusion(bf16[512,512]{1,0:T(8,128)(2,1)} %slice_dynamic-update-slice_fusion.1, bf16[64,1024]{1,0:T(8,128)(2,1)} %bitcast.49), kind=kLoop, calls=%fused_computation.14 | loop fusion | bytes 131072
  27.1 1.5 %slice_dynamic-update-slice_fusion = bf16[512,512]{1,0:T(8,128)(2,1)} fusion(bf16[512,512]{1,0:T(8,128)(2,1)} %slice_dynamic-update-slice_fusion.4, bf16[64,1024]{1,0:T(8,128)(2,1)} %bitcast.50), kind=kLoop, calls=%fused_computation.10 | loop fusion | bytes 131072
  28.5 1.5 %slice_dynamic-update-slice_fusion.7 = bf16[512,512]{1,0:T(8,128)(2,1)} fusion(bf16[512,512]{1,0:T(8,128)(2,1)} %slice_dynamic-update-slice_fusion, bf16[64,1024]{1,0:T(8,128)(2,1)} %bitcast.51), kind=kLoop, calls=%fused_computation.17 | loop fusion | bytes 131072
  30.0 1.5 %slice_dynamic-update-slice_fusion.3 = bf16[512,512]{1,0:T(8,128)(2,1)} fusion(bf16[512,512]{1,0:T(8,128)(2,1)} %slice_dynamic-update-slice_fusion.7, bf16[64,1024]{1,0:T(8,128)(2,1)} %bitcast.52), kind=kLoop, calls=%fused_computation.13 | loop fusion | bytes 131072 | tf_op jit(solution)/shard_map/concatenate | solution.py:113
  31.5 2.7 %all-to-all-done = bf16[8,64,512]{2,1,0:T(8,128)(2,1)S(1)} async-done(((bf16[8,64,512]{2,1,0:T(8,128)(2,1)}), bf16[8,64,512]{2,1,0:T(8,128)(2,1)S(1)}, u32[]{:S(2)}, u32[]{:S(2)}) %all-to-all-start) | async-done | bytes 524320 | tf_op jit(solution)/shard_map/all_to_all | solution.py:107
  34.2 0.0 copy-start
  34.2 3.6 %all-to-all-start.1 = ((bf16[8,64,512]{2,1,0:T(8,128)(2,1)}), bf16[8,64,512]{2,1,0:T(8,128)(2,1)S(1)}, u32[]{:S(2)}, u32[]{:S(2)}) async-start(bf16[8,64,512]{2,1,0:T(8,128)(2,1)} %bitcast.9), calls=%async_computation.1 | async-start | bytes 1048576 | tf_op jit(solution)/shard_map/all_to_all | solution.py:107
  38.5 1.0 collective-permute-start
  39.5 2.8 %collective-permute-start.1 = (f32[1]{0:T(128)}, f32[1]{0:T(128)}, u32[]{:S(2)}, u32[]{:S(2)}) collective-permute-start(f32[1]{0:T(128)} %convert_element_type.21), channel_id=1, source_target_pairs={{0,16},{8,24},{16,0},{24,8},{1,17},{9,25},{17,1},{25,9},{2,18},{10... | collective-permute-start | bytes 20 | tf_op jit(solution)/shard_map/ppermute | solution.py:103
  42.3 2.0 %collective-permute-start.2 = (f32[1]{0:T(128)}, f32[1]{0:T(128)}, u32[]{:S(2)}, u32[]{:S(2)}) collective-permute-start(f32[1]{0:T(128)} %convert_element_type.21), channel_id=1, source_target_pairs={{0,24},{8,0},{16,8},{24,16},{1,25},{9,1},{17,9},{25,17},{2,26},{10... | collective-permute-start | bytes 20 | tf_op jit(solution)/shard_map/ppermute | solution.py:103
  44.2 0.0 collective-permute-done
  44.8 0.0 collective-permute-done.1
  45.4 0.0 collective-permute-done.2
  46.1 3.4 %collective-permute-start.3 = (f32[1]{0:T(128)}, f32[1]{0:T(128)}, u32[]{:S(2)}, u32[]{:S(2)}) collective-permute-start(f32[1]{0:T(128)} %add.20), channel_id=1, source_target_pairs={{0,2},{2,4},{4,6},{6,0},{1,3},{3,5},{5,7},{7,1},{8,10},{10,12},{12... | collective-permute-start | bytes 20 | tf_op jit(solution)/shard_map/ppermute | solution.py:103
  49.4 3.7 %collective-permute-start.4 = (f32[1]{0:T(128)}, f32[1]{0:T(128)}, u32[]{:S(2)}, u32[]{:S(2)}) collective-permute-start(f32[1]{0:T(128)} %add.20), channel_id=1, source_target_pairs={{0,4},{2,6},{4,0},{6,2},{1,5},{3,7},{5,1},{7,3},{8,12},{10,14},{12... | collective-permute-start | bytes 20 | tf_op jit(solution)/shard_map/ppermute | solution.py:103
  53.1 2.8 %collective-permute-start.5 = (f32[1]{0:T(128)}, f32[1]{0:T(128)}, u32[]{:S(2)}, u32[]{:S(2)}) collective-permute-start(f32[1]{0:T(128)} %add.20), channel_id=1, source_target_pairs={{0,6},{2,0},{4,2},{6,4},{1,7},{3,1},{5,3},{7,5},{8,14},{10,8},{12,... | collective-permute-start | bytes 20 | tf_op jit(solution)/shard_map/ppermute | solution.py:103
  55.9 0.0 collective-permute-done.3
  56.5 0.0 collective-permute-done.4
  57.1 0.0 collective-permute-done.5
  57.8 0.0 copy-done
  57.8 9.2 %probs.1 = (bf16[4,640,1024]{2,1,0:T(8,128)(2,1)}, f32[128,512]{1,0:T(8,128)}, bf16[512,512]{1,0:T(8,128)(2,1)}) custom-call(s32[1]{0:T(128)} %bitcast.36.length_ref, bf16[128,4096]{1,0:T(8,128)(2,1)} %bitcast.59, bf16[128,4096]{1,0:T(8,128)(2,1)} %bitcast.61, bf16[128,512]{1,0:T(8,128)(2,1)} %bitcast.63, bf16[512,512]{1,0:T(8,128)(2,1)} %bitcast.55), custom_call_target="tpu_custom_call" | custom-call | flops 1342177280 | bytes 5242880 | tf_op jit(solution)/shard_map/probs/pallas_call | solution.py:154
  67.0 0.0 all-to-all-done.1
  67.0 0.0 copy-start.1
  67.0 0.8 copy-done.1
  67.8 13.0 %grads.1 = (bf16[128,4096]{1,0:T(8,128)(2,1)}, bf16[128,4096]{1,0:T(8,128)(2,1)}, bf16[128,512]{1,0:T(8,128)(2,1)}, bf16[128,512]{1,0:T(8,128)(2,1)}, bf16[512,512]{1,0:T(8,128)(2,1)}) custom-call(f32[1]{0:T(128)} %div.3.weight_ref, bf16[128,4096]{1,0:T(8,128)(2,1)} %bitcast.60, bf16[128,4096]{1,0:T(8,128)(2,1)} %bitcast.62, ...), custom_call_target="tpu_custom_call" | custom-call | flops 2684354560 | bytes 5242880 | tf_op jit(solution)/shard_map/grads/pallas_call | solution.py:171
  80.7 18.1 %all_to_all.40 = bf16[8,64,512]{2,1,0:T(8,128)(2,1)S(1)} all-to-all(bf16[8,64,512]{2,1,0:T(8,128)(2,1)} %bitcast.58), channel_id=1, replica_groups=mesh['prompt'=4,'response'=4,'tensor'=2] {'response','tensor'}, dimensions={0} | all-to-all | bytes 1048576 | tf_op jit(solution)/shard_map/all_to_all | solution.py:107
  98.8 3.6 %all-to-all-start.3 = ((bf16[8,64,512]{2,1,0:T(8,128)(2,1)}), bf16[8,64,512]{2,1,0:T(8,128)(2,1)S(1)}, u32[]{:S(2)}, u32[]{:S(2)}) async-start(bf16[8,64,512]{2,1,0:T(8,128)(2,1)} %bitcast.21), calls=%async_computation.3 | async-start | bytes 1048576 | tf_op jit(solution)/shard_map/all_to_all | solution.py:107
  102.4 0.1 convert_reduce_fusion.1
  102.5 13.6 %all-to-all-done.3 = bf16[8,64,512]{2,1,0:T(8,128)(2,1)S(1)} async-done(((bf16[8,64,512]{2,1,0:T(8,128)(2,1)}), bf16[8,64,512]{2,1,0:T(8,128)(2,1)S(1)}, u32[]{:S(2)}, u32[]{:S(2)}) %all-to-all-start.3) | async-done | bytes 524320 | tf_op jit(solution)/shard_map/all_to_all | solution.py:107
  116.2 0.1 convert_reduce_fusion
  116.3 0.7 maximum_bitcast_fusion
  (4 shorter events, 0.1 us)
Async XLA Ops:
  12.4 21.8 %all-to-all-start = ((bf16[8,64,512]{2,1,0:T(8,128)(2,1)}), bf16[8,64,512]{2,1,0:T(8,128)(2,1)S(1)}, u32[]{:S(2)}, u32[]{:S(2)}) async-start(bf16[8,64,512]{2,1,0:T(8,128)(2,1)} %bitcast.5), calls=%async_computation | async-start | bytes 1048576 | tf_op jit(solution)/shard_map/all_to_all | solution.py:107
  34.2 23.6 %copy-start = (bf16[8,64,512]{2,1,0:T(8,128)(2,1)}, bf16[8,64,512]{2,1,0:T(8,128)(2,1)S(1)}, u32[]{:S(2)}) copy-start(bf16[8,64,512]{2,1,0:T(8,128)(2,1)S(1)} %all-to-all-done) | copy-start | bytes 1572868
  34.2 32.8 %all-to-all-start.1 = ((bf16[8,64,512]{2,1,0:T(8,128)(2,1)}), bf16[8,64,512]{2,1,0:T(8,128)(2,1)S(1)}, u32[]{:S(2)}, u32[]{:S(2)}) async-start(bf16[8,64,512]{2,1,0:T(8,128)(2,1)} %bitcast.9), calls=%async_computation.1 | async-start | bytes 1048576 | tf_op jit(solution)/shard_map/all_to_all | solution.py:107
  38.5 5.8 %collective-permute-start = (f32[1]{0:T(128)}, f32[1]{0:T(128)}, u32[]{:S(2)}, u32[]{:S(2)}) collective-permute-start(f32[1]{0:T(128)} %convert_element_type.21), channel_id=1, source_target_pairs={{0,8},{8,16},{16,24},{24,0},{1,9},{9,17},{17,25},{25,1},{2,10},{10... | collective-permute-start | bytes 20 | tf_op jit(solution)/shard_map/ppermute | solution.py:103
  39.5 5.3 %collective-permute-start.1 = (f32[1]{0:T(128)}, f32[1]{0:T(128)}, u32[]{:S(2)}, u32[]{:S(2)}) collective-permute-start(f32[1]{0:T(128)} %convert_element_type.21), channel_id=1, source_target_pairs={{0,16},{8,24},{16,0},{24,8},{1,17},{9,25},{17,1},{25,9},{2,18},{10... | collective-permute-start | bytes 20 | tf_op jit(solution)/shard_map/ppermute | solution.py:103
  42.3 3.2 %collective-permute-start.2 = (f32[1]{0:T(128)}, f32[1]{0:T(128)}, u32[]{:S(2)}, u32[]{:S(2)}) collective-permute-start(f32[1]{0:T(128)} %convert_element_type.21), channel_id=1, source_target_pairs={{0,24},{8,0},{16,8},{24,16},{1,25},{9,1},{17,9},{25,17},{2,26},{10... | collective-permute-start | bytes 20 | tf_op jit(solution)/shard_map/ppermute | solution.py:103
  46.1 9.9 %collective-permute-start.3 = (f32[1]{0:T(128)}, f32[1]{0:T(128)}, u32[]{:S(2)}, u32[]{:S(2)}) collective-permute-start(f32[1]{0:T(128)} %add.20), channel_id=1, source_target_pairs={{0,2},{2,4},{4,6},{6,0},{1,3},{3,5},{5,7},{7,1},{8,10},{10,12},{12... | collective-permute-start | bytes 20 | tf_op jit(solution)/shard_map/ppermute | solution.py:103
  49.4 7.1 %collective-permute-start.4 = (f32[1]{0:T(128)}, f32[1]{0:T(128)}, u32[]{:S(2)}, u32[]{:S(2)}) collective-permute-start(f32[1]{0:T(128)} %add.20), channel_id=1, source_target_pairs={{0,4},{2,6},{4,0},{6,2},{1,5},{3,7},{5,1},{7,3},{8,12},{10,14},{12... | collective-permute-start | bytes 20 | tf_op jit(solution)/shard_map/ppermute | solution.py:103
  53.1 4.0 %collective-permute-start.5 = (f32[1]{0:T(128)}, f32[1]{0:T(128)}, u32[]{:S(2)}, u32[]{:S(2)}) collective-permute-start(f32[1]{0:T(128)} %add.20), channel_id=1, source_target_pairs={{0,6},{2,0},{4,2},{6,4},{1,7},{3,1},{5,3},{7,5},{8,14},{10,8},{12,... | collective-permute-start | bytes 20 | tf_op jit(solution)/shard_map/ppermute | solution.py:103
  67.0 0.8 copy-start.1
  98.8 17.4 %all-to-all-start.3 = ((bf16[8,64,512]{2,1,0:T(8,128)(2,1)}), bf16[8,64,512]{2,1,0:T(8,128)(2,1)S(1)}, u32[]{:S(2)}, u32[]{:S(2)}) async-start(bf16[8,64,512]{2,1,0:T(8,128)(2,1)} %bitcast.21), calls=%async_computation.3 | async-start | bytes 1048576 | tf_op jit(solution)/shard_map/all_to_all | solution.py:107

commit v3 on v0

v3 whole, which is shorter than its diff:
```python
import functools
import math

import jax
import jax.numpy as jnp
from jax import lax
from jax.experimental import pallas as pl
from jax.experimental.pallas import tpu as pltpu
from jax.sharding import PartitionSpec as P

HD = 128
GROUP = 8
PAIR = 2
CHUNKS = 2
VMEM_LIMIT = 48 * 1024 * 1024
NT = (((1,), (1,)), ((), ()))


def heads_down(ref, first, count):
    return jnp.concatenate(
        [ref[:, (first + i) * HD : (first + i + 1) * HD] for i in range(count)], axis=0
    )


def attend_kernel(n_slots, count, first, factor, carried, *refs):
    length_ref, total_ref, q_hbm, do_hbm, kown_hbm, vown_hbm = refs[:6]
    slot_refs = refs[6 : 6 + n_slots]
    refs = refs[6 + n_slots + carried :]
    out_hbm, dq_hbm, dkown_hbm, dvown_hbm = refs[:4]
    dslot_refs = refs[4 : 4 + n_slots]
    refs = refs[4 + n_slots :]
    q_ref, do_ref, kown_ref, vown_ref, out_ref, dq_ref, dkown_ref, dvown_ref = refs[:8]
    s_ref, dp_ref, p_ref, ds_ref, in_sem, out_sem = refs[8:]

    def columns(head, cols):
        return pl.ds((first + head) * cols, cols)

    loads = []
    for head in range(count):
        loads.append(
            [
                pltpu.make_async_copy(
                    hbm.at[:, columns(head, size)], ref.at[head], in_sem.at[head, i]
                )
                for i, (hbm, ref, size) in enumerate(
                    [
                        (kown_hbm, kown_ref, HD),
                        (q_hbm, q_ref, GROUP * HD),
                        (vown_hbm, vown_ref, HD),
                        (do_hbm, do_ref, GROUP * HD),
                    ]
                )
            ]
        )
        for copy in loads[-1]:
            copy.start()
    stores = []

    def store(ref, hbm, head, size, i):
        copy = pltpu.make_async_copy(ref.at[head], hbm.at[:, columns(head, size)], out_sem.at[head, i])
        copy.start()
        stores.append(copy)

    rows = q_ref.shape[1]
    own = kown_ref.shape[1]
    half = slot_refs[0].shape[0] // 2
    weight = total_ref[0]
    scale = factor * math.log2(math.e)
    width = PAIR * rows
    key_pos = lax.broadcasted_iota(jnp.int32, (own, width), 0)
    row_pos = lax.broadcasted_iota(jnp.int32, (own, width), 1) % rows
    allowed = key_pos <= row_pos
    live = (lax.broadcasted_iota(jnp.int32, (1, width), 1) % rows) < length_ref[0]
    for head in range(count):
        for copy in loads[head]:
            copy.wait()
        here = slice(head * HD, (head + 1) * HD)
        keys = jnp.concatenate([kown_ref[head]] + [ref[:half, here] for ref in slot_refs], axis=0)
        values = jnp.concatenate([vown_ref[head]] + [ref[half:, here] for ref in slot_refs], axis=0)
        keys_t = keys.T
        values_t = values.T
        for pair in range(GROUP // PAIR):
            s_now, dp_now = s_ref.at[pair % 2], dp_ref.at[pair % 2]
            cols = slice(pair * width, (pair + 1) * width)
            do = heads_down(do_ref.at[head], pair * PAIR, PAIR)
            s_now[...] = lax.dot_general(
                keys,
                heads_down(q_ref.at[head], pair * PAIR, PAIR),
                NT,
                preferred_element_type=jnp.float32,
            )
            dp_now[...] = lax.dot_general(values, do, NT, preferred_element_type=jnp.float32)
            s_now[:own] = jnp.where(allowed, s_now[:own], -1e30)
            top = jnp.max(s_now[...], axis=0, keepdims=True) * scale
            exponent = jnp.exp2(s_now[...] * scale - top)
            s_now[...] = exponent
            total = jnp.sum(exponent, axis=0, keepdims=True)
            inverse = jnp.where(live, 1.0 / total, 0.0)
            p_ref[:, cols] = (s_now[...] * inverse).astype(jnp.bfloat16)
            attended = jnp.dot(values_t, p_ref[:, cols], preferred_element_type=jnp.float32)
            centre = jnp.sum(attended * do.astype(jnp.float32).T, axis=0, keepdims=True)
            ds_ref[:, cols] = (
                p_ref[:, cols].astype(jnp.float32) * (dp_now[...] - centre)
            ).astype(jnp.bfloat16)
            dq = jnp.dot(keys_t, ds_ref[:, cols], preferred_element_type=jnp.float32)
            dq = dq * (factor * weight)
            for i in range(PAIR):
                lanes = slice(i * rows, (i + 1) * rows)
                place = slice((pair * PAIR + i) * HD, (pair * PAIR + i + 1) * HD)
                out_ref[head, :, place] = attended[:, lanes].T.astype(jnp.bfloat16)
                dq_ref[head, :, place] = dq[:, lanes].T.astype(jnp.bfloat16)
        store(out_ref, out_hbm, head, GROUP * HD, 0)
        store(dq_ref, dq_hbm, head, GROUP * HD, 1)
        dv = jnp.dot(
            p_ref[...], heads_down(do_ref.at[head], 0, GROUP), preferred_element_type=jnp.float32
        )
        dv = (dv * weight).astype(jnp.bfloat16)
        dk = jnp.dot(
            ds_ref[...], heads_down(q_ref.at[head], 0, GROUP), preferred_element_type=jnp.float32
        )
        dk = (dk * (factor * weight)).astype(jnp.bfloat16)
        dkown_ref[head] = dk[:own]
        dvown_ref[head] = dv[:own]
        store(dkown_ref, dkown_hbm, head, HD, 2)
        store(dvown_ref, dvown_hbm, head, HD, 3)
        for slot, ref in enumerate(dslot_refs):
            part = slice(own + slot * half, own + (slot + 1) * half)
            ref[:half, here] = dk[part]
            ref[half:, here] = dv[part]
    for copy in stores:
        copy.wait()


def swap(x, axis, by):
    return lax.ppermute(x, axis, [(i, i ^ by) for i in range(lax.axis_size(axis))])


def inner(axis):
    rank = lax.axis_index(axis)
    return (rank == 1) | (rank == 2)


def line_gather(block, relay, after=None):
    size = lax.axis_size("response")
    if size != 4 or not relay:
        if after is not None:
            block, after = lax.optimization_barrier((block, after))
        return [block] + [swap(block, "response", m) for m in range(1, size)], after
    far = swap(block, "response", 3)
    near = swap(block, "response", 1)
    onward = jnp.where(inner("response"), far, block)
    onward, after = lax.optimization_barrier((onward, after))
    cycle = [(1, 0), (3, 1), (2, 3), (0, 2)]
    return [block, near, lax.ppermute(onward, "response", cycle), far], after


def line_reduce(slots, relay, after):
    size = lax.axis_size("response")
    wide = jnp.float32
    if size != 4 or not relay:
        terms = [slots[0]] + [swap(slots[m], "response", m) for m in range(1, size)]
        return functools.reduce(jnp.add, [term.astype(wide) for term in terms]), after
    across = lax.ppermute(slots[2], "response", [(0, 1), (1, 3), (3, 2), (2, 0)]).astype(wide)
    near = swap(slots[1], "response", 1)
    mid = inner("response")
    onward = (slots[3].astype(wide) + jnp.where(mid, across, 0.0)).astype(slots[3].dtype)
    onward, after = lax.optimization_barrier((onward, after))
    far = swap(onward, "response", 3)
    total = slots[0].astype(wide) + near.astype(wide) + far.astype(wide)
    return total + jnp.where(mid, 0.0, across), after


def own_columns(block, chunk, by):
    cols = block.shape[1] // (lax.axis_size("tensor") * CHUNKS)
    rank = lax.axis_index("tensor") ^ by
    return lax.dynamic_slice_in_dim(block, (rank * CHUNKS + chunk) * cols, cols, 1)


def tensor_gather(blocks, chunk):
    parts = lax.axis_size("tensor")
    pieces = []
    for m in range(parts):
        piece = jnp.concatenate([own_columns(block, chunk, m) for block in blocks], axis=0)
        pieces.append(piece if m == 0 else swap(piece, "tensor", m))
    rows = blocks[0].shape[0]
    return jnp.concatenate(
        [piece[i * rows : (i + 1) * rows] for i in range(len(blocks)) for piece in pieces], axis=0
    )


def tensor_spread(total, n_arrays):
    parts = lax.axis_size("tensor")
    rows = total.shape[0] // (n_arrays * parts)
    pieces = []
    for m in range(parts):
        piece = jnp.concatenate(
            [total[(i * parts + m) * rows : (i * parts + m + 1) * rows] for i in range(n_arrays)],
            axis=0,
        )
        pieces.append(piece if m == 0 else swap(piece, "tensor", m))
    return pieces


def whole_columns(chunk_pieces, array):
    parts = lax.axis_size("tensor")
    rank = lax.axis_index("tensor")
    rows = chunk_pieces[0][0].shape[0] // 2
    by_rank = [
        jnp.concatenate([pieces[m][array * rows : (array + 1) * rows] for pieces in chunk_pieces], axis=1)
        for m in range(parts)
    ]
    ordered = []
    for t in range(parts):
        column = by_rank[0]
        for m in range(1, parts):
            column = jnp.where(rank ^ m == t, by_rank[m], column)
        ordered.append(column)
    return jnp.concatenate(ordered, axis=1)


def sum_over(x, axis):
    return functools.reduce(jnp.add, [x] + [swap(x, axis, m) for m in range(1, lax.axis_size(axis))])


def attend(chunk, heads, slots, length, weight, q, do, k, v, carried):
    rows = q.shape[0]
    n_slots = len(slots)
    slot_rows = slots[0].shape[0] // 2
    n_keys = rows + n_slots * slot_rows
    count = heads // CHUNKS
    first = chunk * count
    bf16 = jnp.bfloat16
    smem = pl.BlockSpec(memory_space=pltpu.SMEM)
    hbm = pl.BlockSpec(memory_space=pltpu.HBM)
    vmem = pl.BlockSpec(memory_space=pltpu.VMEM)
    like = lambda x: jax.ShapeDtypeStruct(x.shape, bf16)
    unit = 2 * n_keys * GROUP * rows * HD * count
    pair_buffer = pltpu.VMEM((2, n_keys, PAIR * rows), jnp.float32)
    group_buffer = pltpu.VMEM((n_keys, GROUP * rows), bf16)
    wide = pltpu.VMEM((count, rows, GROUP * HD), bf16)
    own = pltpu.VMEM((count, rows, HD), bf16)
    return pl.pallas_call(
        functools.partial(
            attend_kernel, n_slots, count, first, 1.0 / math.sqrt(HD), len(carried)
        ),
        in_specs=[smem, smem] + [hbm] * 4 + [vmem] * n_slots + [hbm] * len(carried),
        out_specs=[hbm] * 4 + [vmem] * n_slots,
        out_shape=[like(q), like(q), like(k), like(v)] + [like(x) for x in slots],
        input_output_aliases={6 + n_slots + i: i for i in range(len(carried))},
        scratch_shapes=[wide, wide, own, own, wide, wide, own, own]
        + [pair_buffer, pair_buffer, group_buffer, group_buffer]
        + [pltpu.SemaphoreType.DMA((count, 4))] * 2,
        compiler_params=pltpu.CompilerParams(vmem_limit_bytes=VMEM_LIMIT),
        cost_estimate=pl.CostEstimate(
            flops=24 * unit,
            bytes_accessed=8 * rows * GROUP * HD * count,
            transcendentals=count * n_keys * GROUP * rows,
        ),
        name=f"attend_{chunk}",
    )(length, weight, q, do, k, v, *slots, *carried)


def body(queries, keys, values, prefix_keys, prefix_values, lengths, out_grad):
    q, k, v, do = queries[0], keys[0], values[0], out_grad[0]
    heads = k.shape[1] // HD
    length = lengths[0]
    prefix = (prefix_keys[0], prefix_values[0])
    prompt_total = sum_over(length.astype(jnp.float32), "prompt")
    blocks = [tensor_gather(prefix, chunk) for chunk in range(CHUNKS)]
    slots, (prompt_total, *blocks[1:]) = line_gather(blocks[0], True, (prompt_total, *blocks[1:]))
    live_total = sum_over(prompt_total, "response")
    weight = q.shape[0] * lax.axis_size("prompt") * lax.axis_size("response") / live_total
    chunk_pieces, carried, total = [], [], ()
    for chunk in range(CHUNKS):
        if chunk + 1 < CHUNKS:
            next_slots, _ = line_gather(blocks[chunk + 1], False)
        results = attend(chunk, heads, slots, length, weight, q, do, k, v, carried)
        carried = list(results[:4])
        terms, total = lax.optimization_barrier((results[4:], total))
        last = chunk + 1 == CHUNKS
        new_total, total = line_reduce(terms, last, total)
        if chunk:
            chunk_pieces.append(tensor_spread(total, len(prefix)))
        total = new_total.astype(jnp.bfloat16)
        slots = next_slots
    chunk_pieces.append(tensor_spread(total, len(prefix)))
    grads = [whole_columns(chunk_pieces, array) for array in range(len(prefix))]
    return tuple(x[None] for x in (*carried, *grads))


def solution(mesh):
    in_specs = (
        P("prompt", "response", "tensor"),
        P("prompt", "response", "tensor"),
        P("prompt", "response", "tensor"),
        P("prompt", ("response", "tensor"), None),
        P("prompt", ("response", "tensor"), None),
        P("prompt", "response"),
        P("prompt", "response", "tensor"),
    )
    out_specs = (
        P("prompt", "response", "tensor"),
        P("prompt", "response", "tensor"),
        P("prompt", "response", "tensor"),
        P("prompt", "response", "tensor"),
        P("prompt", ("response", "tensor"), None),
        P("prompt", ("response", "tensor"), None),
    )
    return jax.shard_map(body, mesh=mesh, in_specs=in_specs, out_specs=out_specs, check_vma=False)
```

time: 278 us -> 81 us (0.29)
  waiting for transfers between devices: 135 us -> 13.1 us
  starting transfers between devices: 0.16 us -> 40.8 us
  local copies, waits for them, and re-layouts: 42.6 us -> 2.17 us
  blocking collectives: 35.8 us -> 0 us
  matrix products: 33.6 us -> 0 us
  Pallas kernels: 0 us -> 17.4 us
  other arithmetic: 13.9 us -> 1.65 us
  between operations: 15.9 us -> 5.51 us
    reduce_scatter x2 -> x0, waiting for transfers between devices: 98.4 us -> none  [the longest x1 66.7 us: body(): lax.psum_scatter(placed_values.astype(jnp.bfloat16), ('response', 'tensor...]
    ppermute x0 -> x22, starting transfers between devices: none -> 40.8 us  [the longest x20 38.5 us: swap(): lax.ppermute(x, axis, [(i, i ^ by) for i in range(lax.axis_size(axis))])]
    psum x1 -> x0, blocking collectives: 35.8 us -> none  [body(): live_total = lax.psum(length.astype(jnp.float32), ('prompt', 'response'))]
    all_gather x2 -> x0, waiting for transfers between devices: 35.3 us -> none  [the longest x1 35.3 us: body(): lax.all_gather(prefix_keys, ('response', 'tensor'), axis=1, tiled=True)]
    dot_general x20 -> x0, matrix products: 20.8 us -> none  [the longest x4 6.53 us: attend_head(): jnp.einsum('grk,kd->rgd', score_grad, all_keys, preferred_element_type=jn...]
    pallas_call x0 -> x2, Pallas kernels: none -> 17.4 us  [attend(): pl.pallas_call(functools.partial(attend_kernel, n_slots, count, first, 1....]
    unnamed x130 -> x8, local copies, waits for them, and re-layouts: 16.1 us -> 1.24 us
    ppermute x0 -> x22, waiting for transfers between devices: none -> 13.1 us  [the longest x20 9.73 us: swap(): lax.ppermute(x, axis, [(i, i ^ by) for i in range(lax.axis_size(axis))])]
  transfers between devices with their start and end apart: 4 -> 22, of which waited for: 3 -> 5; matrix products, arithmetic and copies ran while one was open for 15% -> 1% of each run, Pallas kernels for 0% -> 22%
where the time goes in v3:
time: 81 us; the launch traced here: 80.7 us
  starting transfers between devices  40.8 us (50%)
  Pallas kernels  17.4 us (21%)
  waiting for transfers between devices  13.1 us (16%)
  between operations  5.51 us (7%)
  local copies, waits for them, and re-layouts  2.17 us (3%)
  other arithmetic  1.65 us (2%)
    ppermute x20, starting transfers between devices, swap(): lax.ppermute(x, axis, [(i, i ^ by) for i in range(lax.axis_size(axis))])  38.5 us
    pallas_call x2, Pallas kernels, attend(): pl.pallas_call(functools.partial(attend_kernel, n_slots, count, first, 1....  17.4 us
    ppermute x20, waiting for transfers between devices, swap(): lax.ppermute(x, axis, [(i, i ^ by) for i in range(lax.axis_size(axis))])  9.73 us
    ppermute x1, waiting for transfers between devices, line_reduce(): lax.ppermute(slots[2], 'response', [(0, 1), (1, 3), (3, 2), (2, 0)])  3.36 us
    ppermute x1, starting transfers between devices, line_gather(): return ([block, near, lax.ppermute(onward, 'response', cycle), far], after)  1.67 us
  transfers between devices with their start and end apart: 22, of which 5 were waited for; matrix products, arithmetic and copies ran while one was open for 1% of the time, Pallas kernels for 22%

profile of v3, /device:TPU:0, one launch (start us, length us, event | category | flops | bytes accessed | tf_op | source)
XLA Modules:
  0.0 80.7 jit_solution(10294133463886299187)
XLA Ops:
  0.6 0.0 copy-start
  1.4 1.3 %collective-permute-start.2 = (f32[1]{0:T(128)}, f32[1]{0:T(128)}, u32[]{:S(2)}, u32[]{:S(2)}) collective-permute-start(f32[1]{0:T(128)} %convert_element_type.39), channel_id=1, source_target_pairs={{0,8},{8,0},{16,24},{24,16},{1,9},{9,1},{17,25},{25,17},{2,10},{10... | collective-permute-start | bytes 20 | tf_op jit(solution)/shard_map/ppermute | solution.py:135
  2.7 3.8 %collective-permute-start.3 = (f32[1]{0:T(128)}, f32[1]{0:T(128)}, u32[]{:S(2)}, u32[]{:S(2)}) collective-permute-start(f32[1]{0:T(128)} %convert_element_type.39), channel_id=1, source_target_pairs={{0,16},{8,24},{16,0},{24,8},{1,17},{9,25},{17,1},{25,9},{2,18},{10... | collective-permute-start | bytes 20 | tf_op jit(solution)/shard_map/ppermute | solution.py:135
  6.5 1.3 %collective-permute-start.4 = (f32[1]{0:T(128)}, f32[1]{0:T(128)}, u32[]{:S(2)}, u32[]{:S(2)}) collective-permute-start(f32[1]{0:T(128)} %convert_element_type.39), channel_id=1, source_target_pairs={{0,24},{8,16},{16,8},{24,0},{1,25},{9,17},{17,9},{25,1},{2,26},{10... | collective-permute-start | bytes 20 | tf_op jit(solution)/shard_map/ppermute | solution.py:135
  7.8 0.9 %dynamic-slice_bitcast_fusion = (bf16[64,256]{1,0:T(8,128)(2,1)S(1)}, bf16[64,256]{1,0:T(8,128)(2,1)S(1)}, bf16[64,256]{1,0:T(8,128)(2,1)S(1)}, bf16[64,256]{1,0...) fusion(bf16[1,64,1024]{2,1,0:T(8,128)(2,1)} %param.11, ...), kind=kLoop, calls=%fused_computation.24 | loop fusion | bytes 524304 | tf_op jit(solution)/shard_map/dynamic_slice | solution.py:176
  8.7 1.6 %collective-permute-start = (bf16[128,256]{1,0:T(8,128)(2,1)S(1)}, bf16[128,256]{1,0:T(8,128)(2,1)S(1)}, u32[]{:S(2)}, u32[]{:S(2)}) collective-permute-start(bf16[128,256]{1,0:T(8,128)(2,1)S(1)} %pad_maximum_fusion.2), channel_id=1, source_target_pairs={{0,1},{1,0},{2,3},{3,2},{4,5},{5,4},{6,7},{7,6},{8,9},{9,8},{10,11... | collective-permute-start | bytes 196616 | tf_op jit(solution)/shard_map/ppermute | solution.py:135
  10.3 0.5 collective-permute-start.5
  10.8 0.0 collective-permute-done.2
  11.5 0.0 collective-permute-done.3
  12.2 0.0 collective-permute-done.4
  12.8 0.7 collective-permute-done
  13.5 3.7 %collective-permute-start.1 = (bf16[256,256]{1,0:T(8,128)(2,1)S(1)}, bf16[256,256]{1,0:T(8,128)(2,1)S(1)}, u32[]{:S(2)}, u32[]{:S(2)}) collective-permute-start(bf16[256,256]{1,0:T(8,128)(2,1)S(1)} %pad_maximum_fusion.refs_6_), channel_id=1, source_target_pairs={{0,6},{2,4},{4,2},{6,0},{1,7},{3,5},{5,3},{7,1},{8,14},{10,12},{12... | collective-permute-start | bytes 393224 | tf_op jit(solution)/shard_map/ppermute | solution.py:135
  17.2 0.0 collective-permute-start.12
  17.2 0.0 collective-permute-done.5
  17.2 0.0 copy-start.2
  17.2 0.0 copy-start.3
  17.2 4.0 %collective-permute-done.1.refs_9_ = bf16[256,256]{1,0:T(8,128)(2,1)S(1)} collective-permute-done((bf16[256,256]{1,0:T(8,128)(2,1)S(1)}, bf16[256,256]{1,0:T(8,128)(2,1)S(1)}, u32[]{:S(2)}, u32[]{:S(2)}) %collective-permute-start.1) | collective-permute-done | bytes 131104 | tf_op jit(solution)/shard_map/ppermute | solution.py:135
  21.3 1.7 %collective-permute-start.13 = (bf16[256,256]{1,0:T(8,128)(2,1)S(1)}, bf16[256,256]{1,0:T(8,128)(2,1)S(1)}, u32[]{:S(2)}, u32[]{:S(2)}) collective-permute-start(bf16[256,256]{1,0:T(8,128)(2,1)S(1)} %broadcast_select_fusion), channel_id=1, source_target_pairs={{2,0},{6,2},{4,6},{0,4},{3,1},{7,3},{5,7},{1,5},{10,8},{14,10},{12... | collective-permute-start | bytes 393224 | tf_op jit(solution)/shard_map/ppermute | solution.py:154
  22.9 2.6 %collective-permute-start.6 = (f32[1]{0:T(128)}, f32[1]{0:T(128)}, u32[]{:S(2)}, u32[]{:S(2)}) collective-permute-start(f32[1]{0:T(128)} %add.67), channel_id=1, source_target_pairs={{0,2},{2,0},{4,6},{6,4},{1,3},{3,1},{5,7},{7,5},{8,10},{10,8},{12,... | collective-permute-start | bytes 20 | tf_op jit(solution)/shard_map/ppermute | solution.py:135
  25.5 4.4 %collective-permute-start.7 = (f32[1]{0:T(128)}, f32[1]{0:T(128)}, u32[]{:S(2)}, u32[]{:S(2)}) collective-permute-start(f32[1]{0:T(128)} %add.67), channel_id=1, source_target_pairs={{0,4},{2,6},{4,0},{6,2},{1,5},{3,7},{5,1},{7,3},{8,12},{10,14},{12... | collective-permute-start | bytes 20 | tf_op jit(solution)/shard_map/ppermute | solution.py:135
  29.9 1.5 %collective-permute-start.8 = (f32[1]{0:T(128)}, f32[1]{0:T(128)}, u32[]{:S(2)}, u32[]{:S(2)}) collective-permute-start(f32[1]{0:T(128)} %add.67), channel_id=1, source_target_pairs={{0,6},{2,4},{4,2},{6,0},{1,7},{3,5},{5,3},{7,1},{8,14},{10,12},{12... | collective-permute-start | bytes 20 | tf_op jit(solution)/shard_map/ppermute | solution.py:135
  31.4 0.0 collective-permute-done.6
  31.4 2.0 %collective-permute-start.10 = (bf16[256,256]{1,0:T(8,128)(2,1)S(1)}, bf16[256,256]{1,0:T(8,128)(2,1)S(1)}, u32[]{:S(2)}, u32[]{:S(2)}) collective-permute-start(bf16[256,256]{1,0:T(8,128)(2,1)S(1)} %pad_maximum_fusion.1.refs_6_), channel_id=1, source_target_pairs={{0,4},{2,6},{4,0},{6,2},{1,5},{3,7},{5,1},{7,3},{8,12},{10,14},{12... | collective-permute-start | bytes 393224 | tf_op jit(solution)/shard_map/ppermute | solution.py:135
  34.1 0.0 collective-permute-done.7
  34.1 1.7 %collective-permute-start.11 = (bf16[256,256]{1,0:T(8,128)(2,1)S(1)}, bf16[256,256]{1,0:T(8,128)(2,1)S(1)}, u32[]{:S(2)}, u32[]{:S(2)}) collective-permute-start(bf16[256,256]{1,0:T(8,128)(2,1)S(1)} %pad_maximum_fusion.1.refs_6_), channel_id=1, source_target_pairs={{0,6},{2,4},{4,2},{6,0},{1,7},{3,5},{5,3},{7,1},{8,14},{10,12},{12... | collective-permute-start | bytes 393224 | tf_op jit(solution)/shard_map/ppermute | solution.py:135
  36.5 0.0 collective-permute-done.8
  36.5 0.6 collective-permute-start.9
  37.7 0.0 collective-permute-done.12.refs_7_
  37.8 0.0 collective-permute-done.13.refs_8_
  37.8 0.0 copy-done
  37.8 0.0 copy-done.2
  37.8 0.0 copy-done.3
  37.8 0.0 copy-start.1
  37.8 1.2 %copy-done.1 = bf16[1,128,4096]{2,1,0:T(8,128)(2,1)S(1)} copy-done((bf16[1,128,4096]{2,1,0:T(8,128)(2,1)S(1)}, bf16[1,128,4096]{2,1,0:T(8,128)(2,1)}, u32[]{:S(2)}) %copy-start.1) | copy-done | bytes 1048600
  39.0 8.6 %attend_0.1 = (bf16[128,4096]{1,0:T(8,128)(2,1)}, bf16[128,4096]{1,0:T(8,128)(2,1)}, bf16[128,512]{1,0:T(8,128)(2,1)}, bf16[128,512]{1,0:T(8,128)(2,1)}, bf16[25...) custom-call(s32[1]{0:T(128)} %bitcast.30.refs_0_, ...), custom_call_target="tpu_custom_call" | custom-call | flops 8053063680 | bytes 2097152 | tf_op jit(solution)/shard_map/attend_0/pallas_call | solution.py:242
  47.7 1.5 %collective-permute-start.14 = (bf16[256,256]{1,0:T(8,128)(2,1)S(1)}, bf16[256,256]{1,0:T(8,128)(2,1)S(1)}, u32[]{:S(2)}, u32[]{:S(2)}) collective-permute-start(bf16[256,256]{1,0:T(8,128)(2,1)S(1)} %get-tuple-element.56), channel_id=1, source_target_pairs={{0,2},{2,0},{4,6},{6,4},{1,3},{3,1},{5,7},{7,5},{8,10},{10,8},{12,... | collective-permute-start | bytes 393224 | tf_op jit(solution)/shard_map/ppermute | solution.py:135
  49.2 2.0 %collective-permute-start.15 = (bf16[256,256]{1,0:T(8,128)(2,1)S(1)}, bf16[256,256]{1,0:T(8,128)(2,1)S(1)}, u32[]{:S(2)}, u32[]{:S(2)}) collective-permute-start(bf16[256,256]{1,0:T(8,128)(2,1)S(1)} %get-tuple-element.57), channel_id=1, source_target_pairs={{0,4},{2,6},{4,0},{6,2},{1,5},{3,7},{5,1},{7,3},{8,12},{10,14},{12... | collective-permute-start | bytes 393224 | tf_op jit(solution)/shard_map/ppermute | solution.py:135
  51.2 0.0 collective-permute-done.10.refs_8_
  51.2 0.9 %collective-permute-start.16 = (bf16[256,256]{1,0:T(8,128)(2,1)S(1)}, bf16[256,256]{1,0:T(8,128)(2,1)S(1)}, u32[]{:S(2)}, u32[]{:S(2)}) collective-permute-start(bf16[256,256]{1,0:T(8,128)(2,1)S(1)} %get-tuple-element.58), channel_id=1, source_target_pairs={{0,6},{2,4},{4,2},{6,0},{1,7},{3,5},{5,3},{7,1},{8,14},{10,12},{12... | collective-permute-start | bytes 393224 | tf_op jit(solution)/shard_map/ppermute | solution.py:135
  52.1 0.0 collective-permute-done.11.refs_9_
  52.1 0.0 collective-permute-done.9.refs_7_
  52.1 8.8 %attend_1.1 = (bf16[128,4096]{1,0:T(8,128)(2,1)}, bf16[128,4096]{1,0:T(8,128)(2,1)}, bf16[128,512]{1,0:T(8,128)(2,1)}, bf16[128,512]{1,0:T(8,128)(2,1)}, bf16[25...) custom-call(s32[1]{0:T(128)} %bitcast.31.refs_0_, ...), custom_call_target="tpu_custom_call", output_to_operand_aliasing={{0}: (10, {}), {1}: (11, {}), {2}: (12, {}), {3}: (13, {})} | custom-call | flops 8053063680 | bytes 2097152 | tf_op jit(solution)/shard_map/attend_1/pallas_call | solution.py:242
  60.9 0.0 collective-permute-done.14
  61.0 0.0 collective-permute-done.15
  61.0 0.0 collective-permute-done.16
  61.0 0.1 add_convert_fusion
  61.1 0.6 collective-permute-start.17
  61.7 2.9 %collective-permute-start.19 = (bf16[256,256]{1,0:T(8,128)(2,1)S(1)}, bf16[256,256]{1,0:T(8,128)(2,1)S(1)}, u32[]{:S(2)}, u32[]{:S(2)}) collective-permute-start(bf16[256,256]{1,0:T(8,128)(2,1)S(1)} %get-tuple-element.64), channel_id=1, source_target_pairs={{0,2},{2,0},{4,6},{6,4},{1,3},{3,1},{5,7},{7,5},{8,10},{10,8},{12,... | collective-permute-start | bytes 393224 | tf_op jit(solution)/shard_map/ppermute | solution.py:135
  64.6 3.4 %collective-permute-done.17 = bf16[256,256]{1,0:T(8,128)(2,1)S(1)} collective-permute-done((bf16[256,256]{1,0:T(8,128)(2,1)S(1)}, bf16[256,256]{1,0:T(8,128)(2,1)S(1)}, u32[]{:S(2)}, u32[]{:S(2)}) %collective-permute-start.17) | collective-permute-done | bytes 131104 | tf_op jit(solution)/shard_map/ppermute | solution.py:163
  68.0 2.9 %collective-permute-start.20 = (bf16[256,256]{1,0:T(8,128)(2,1)S(1)}, bf16[256,256]{1,0:T(8,128)(2,1)S(1)}, u32[]{:S(2)}, u32[]{:S(2)}) collective-permute-start(bf16[256,256]{1,0:T(8,128)(2,1)S(1)} %fusion.1), channel_id=1, source_target_pairs={{0,6},{2,4},{4,2},{6,0},{1,7},{3,5},{5,3},{7,1},{8,14},{10,12},{12... | collective-permute-start | bytes 393224 | tf_op jit(solution)/shard_map/ppermute | solution.py:135
  70.9 1.6 %collective-permute-start.18 = (bf16[128,256]{1,0:T(8,128)(2,1)S(1)}, bf16[128,256]{1,0:T(8,128)(2,1)S(1)}, u32[]{:S(2)}, u32[]{:S(2)}) collective-permute-start(bf16[128,256]{1,0:T(8,128)(2,1)S(1)} %pad_maximum_fusion.4), channel_id=1, source_target_pairs={{0,1},{1,0},{2,3},{3,2},{4,5},{5,4},{6,7},{7,6},{8,9},{9,8},{10,11... | collective-permute-start | bytes 196616 | tf_op jit(solution)/shard_map/ppermute | solution.py:135
  72.6 0.0 collective-permute-done.19
  72.6 2.3 %collective-permute-done.20 = bf16[256,256]{1,0:T(8,128)(2,1)S(1)} collective-permute-done((bf16[256,256]{1,0:T(8,128)(2,1)S(1)}, bf16[256,256]{1,0:T(8,128)(2,1)S(1)}, u32[]{:S(2)}, u32[]{:S(2)}) %collective-permute-start.20) | collective-permute-done | bytes 131104 | tf_op jit(solution)/shard_map/ppermute | solution.py:135
  74.8 0.1 fusion.3
  74.9 1.6 %collective-permute-start.21 = (bf16[128,256]{1,0:T(8,128)(2,1)S(1)}, bf16[128,256]{1,0:T(8,128)(2,1)S(1)}, u32[]{:S(2)}, u32[]{:S(2)}) collective-permute-start(bf16[128,256]{1,0:T(8,128)(2,1)S(1)} %pad_maximum_fusion.5), channel_id=1, source_target_pairs={{0,1},{1,0},{2,3},{3,2},{4,5},{5,4},{6,7},{7,6},{8,9},{9,8},{10,11... | collective-permute-start | bytes 196616 | tf_op jit(solution)/shard_map/ppermute | solution.py:135
  76.6 0.0 collective-permute-done.18
  76.6 2.7 %collective-permute-done.21 = bf16[128,256]{1,0:T(8,128)(2,1)S(1)} collective-permute-done((bf16[128,256]{1,0:T(8,128)(2,1)S(1)}, bf16[128,256]{1,0:T(8,128)(2,1)S(1)}, u32[]{:S(2)}, u32[]{:S(2)}) %collective-permute-start.21) | collective-permute-done | bytes 65568 | tf_op jit(solution)/shard_map/ppermute | solution.py:135
  79.3 0.7 maximum_bitcast_fusion.1
  80.0 0.7 maximum_bitcast_fusion
  (16 shorter events, 0.2 us)
Async XLA Ops:
  0.6 37.1 %copy-start = (bf16[1,128,4096]{2,1,0:T(8,128)(2,1)S(1)}, bf16[1,128,4096]{2,1,0:T(8,128)(2,1)}, u32[]{:S(2)}) copy-start(bf16[1,128,4096]{2,1,0:T(8,128)(2,1)} %param.7) | copy-start | bytes 3145732
  1.4 9.4 %collective-permute-start.2 = (f32[1]{0:T(128)}, f32[1]{0:T(128)}, u32[]{:S(2)}, u32[]{:S(2)}) collective-permute-start(f32[1]{0:T(128)} %convert_element_type.39), channel_id=1, source_target_pairs={{0,8},{8,0},{16,24},{24,16},{1,9},{9,1},{17,25},{25,17},{2,10},{10... | collective-permute-start | bytes 20 | tf_op jit(solution)/shard_map/ppermute | solution.py:135
  2.7 8.8 %collective-permute-start.3 = (f32[1]{0:T(128)}, f32[1]{0:T(128)}, u32[]{:S(2)}, u32[]{:S(2)}) collective-permute-start(f32[1]{0:T(128)} %convert_element_type.39), channel_id=1, source_target_pairs={{0,16},{8,24},{16,0},{24,8},{1,17},{9,25},{17,1},{25,9},{2,18},{10... | collective-permute-start | bytes 20 | tf_op jit(solution)/shard_map/ppermute | solution.py:135
  6.5 5.7 %collective-permute-start.4 = (f32[1]{0:T(128)}, f32[1]{0:T(128)}, u32[]{:S(2)}, u32[]{:S(2)}) collective-permute-start(f32[1]{0:T(128)} %convert_element_type.39), channel_id=1, source_target_pairs={{0,24},{8,16},{16,8},{24,0},{1,25},{9,17},{17,9},{25,1},{2,26},{10... | collective-permute-start | bytes 20 | tf_op jit(solution)/shard_map/ppermute | solution.py:135
  8.7 4.8 %collective-permute-start = (bf16[128,256]{1,0:T(8,128)(2,1)S(1)}, bf16[128,256]{1,0:T(8,128)(2,1)S(1)}, u32[]{:S(2)}, u32[]{:S(2)}) collective-permute-start(bf16[128,256]{1,0:T(8,128)(2,1)S(1)} %pad_maximum_fusion.2), channel_id=1, source_target_pairs={{0,1},{1,0},{2,3},{3,2},{4,5},{5,4},{6,7},{7,6},{8,9},{9,8},{10,11... | collective-permute-start | bytes 196616 | tf_op jit(solution)/shard_map/ppermute | solution.py:135
  10.3 6.9 %collective-permute-start.5 = (bf16[128,256]{1,0:T(8,128)(2,1)S(1)}, bf16[128,256]{1,0:T(8,128)(2,1)S(1)}, u32[]{:S(2)}, u32[]{:S(2)}) collective-permute-start(bf16[128,256]{1,0:T(8,128)(2,1)S(1)} %pad_maximum_fusion.3), channel_id=1, source_target_pairs={{0,1},{1,0},{2,3},{3,2},{4,5},{5,4},{6,7},{7,6},{8,9},{9,8},{10,11... | collective-permute-start | bytes 196616 | tf_op jit(solution)/shard_map/ppermute | solution.py:135
  13.5 7.7 %collective-permute-start.1 = (bf16[256,256]{1,0:T(8,128)(2,1)S(1)}, bf16[256,256]{1,0:T(8,128)(2,1)S(1)}, u32[]{:S(2)}, u32[]{:S(2)}) collective-permute-start(bf16[256,256]{1,0:T(8,128)(2,1)S(1)} %pad_maximum_fusion.refs_6_), channel_id=1, source_target_pairs={{0,6},{2,4},{4,2},{6,0},{1,7},{3,5},{5,3},{7,1},{8,14},{10,12},{12... | collective-permute-start | bytes 393224 | tf_op jit(solution)/shard_map/ppermute | solution.py:135
  17.2 20.6 %collective-permute-start.12 = (bf16[256,256]{1,0:T(8,128)(2,1)S(1)}, bf16[256,256]{1,0:T(8,128)(2,1)S(1)}, u32[]{:S(2)}, u32[]{:S(2)}) collective-permute-start(bf16[256,256]{1,0:T(8,128)(2,1)S(1)} %pad_maximum_fusion.refs_6_), channel_id=1, source_target_pairs={{0,2},{2,0},{4,6},{6,4},{1,3},{3,1},{5,7},{7,5},{8,10},{10,8},{12,... | collective-permute-start | bytes 393224 | tf_op jit(solution)/shard_map/ppermute | solution.py:135
  17.2 20.6 %copy-start.2 = (bf16[1,128,512]{2,1,0:T(8,128)(2,1)S(1)}, bf16[1,128,512]{2,1,0:T(8,128)(2,1)}, u32[]{:S(2)}) copy-start(bf16[1,128,512]{2,1,0:T(8,128)(2,1)} %param.8) | copy-start | bytes 393220
  17.2 20.6 %copy-start.3 = (bf16[1,128,512]{2,1,0:T(8,128)(2,1)S(1)}, bf16[1,128,512]{2,1,0:T(8,128)(2,1)}, u32[]{:S(2)}) copy-start(bf16[1,128,512]{2,1,0:T(8,128)(2,1)} %param.9) | copy-start | bytes 393220
  21.3 16.5 %collective-permute-start.13 = (bf16[256,256]{1,0:T(8,128)(2,1)S(1)}, bf16[256,256]{1,0:T(8,128)(2,1)S(1)}, u32[]{:S(2)}, u32[]{:S(2)}) collective-permute-start(bf16[256,256]{1,0:T(8,128)(2,1)S(1)} %broadcast_select_fusion), channel_id=1, source_target_pairs={{2,0},{6,2},{4,6},{0,4},{3,1},{7,3},{5,7},{1,5},{10,8},{14,10},{12... | collective-permute-start | bytes 393224 | tf_op jit(solution)/shard_map/ppermute | solution.py:154
  22.9 8.5 %collective-permute-start.6 = (f32[1]{0:T(128)}, f32[1]{0:T(128)}, u32[]{:S(2)}, u32[]{:S(2)}) collective-permute-start(f32[1]{0:T(128)} %add.67), channel_id=1, source_target_pairs={{0,2},{2,0},{4,6},{6,4},{1,3},{3,1},{5,7},{7,5},{8,10},{10,8},{12,... | collective-permute-start | bytes 20 | tf_op jit(solution)/shard_map/ppermute | solution.py:135
  25.5 8.6 %collective-permute-start.7 = (f32[1]{0:T(128)}, f32[1]{0:T(128)}, u32[]{:S(2)}, u32[]{:S(2)}) collective-permute-start(f32[1]{0:T(128)} %add.67), channel_id=1, source_target_pairs={{0,4},{2,6},{4,0},{6,2},{1,5},{3,7},{5,1},{7,3},{8,12},{10,14},{12... | collective-permute-start | bytes 20 | tf_op jit(solution)/shard_map/ppermute | solution.py:135
  29.9 6.6 %collective-permute-start.8 = (f32[1]{0:T(128)}, f32[1]{0:T(128)}, u32[]{:S(2)}, u32[]{:S(2)}) collective-permute-start(f32[1]{0:T(128)} %add.67), channel_id=1, source_target_pairs={{0,6},{2,4},{4,2},{6,0},{1,7},{3,5},{5,3},{7,1},{8,14},{10,12},{12... | collective-permute-start | bytes 20 | tf_op jit(solution)/shard_map/ppermute | solution.py:135
  31.4 19.8 %collective-permute-start.10 = (bf16[256,256]{1,0:T(8,128)(2,1)S(1)}, bf16[256,256]{1,0:T(8,128)(2,1)S(1)}, u32[]{:S(2)}, u32[]{:S(2)}) collective-permute-start(bf16[256,256]{1,0:T(8,128)(2,1)S(1)} %pad_maximum_fusion.1.refs_6_), channel_id=1, source_target_pairs={{0,4},{2,6},{4,0},{6,2},{1,5},{3,7},{5,1},{7,3},{8,12},{10,14},{12... | collective-permute-start | bytes 393224 | tf_op jit(solution)/shard_map/ppermute | solution.py:135
  34.1 18.0 %collective-permute-start.11 = (bf16[256,256]{1,0:T(8,128)(2,1)S(1)}, bf16[256,256]{1,0:T(8,128)(2,1)S(1)}, u32[]{:S(2)}, u32[]{:S(2)}) collective-permute-start(bf16[256,256]{1,0:T(8,128)(2,1)S(1)} %pad_maximum_fusion.1.refs_6_), channel_id=1, source_target_pairs={{0,6},{2,4},{4,2},{6,0},{1,7},{3,5},{5,3},{7,1},{8,14},{10,12},{12... | collective-permute-start | bytes 393224 | tf_op jit(solution)/shard_map/ppermute | solution.py:135
  36.5 15.6 %collective-permute-start.9 = (bf16[256,256]{1,0:T(8,128)(2,1)S(1)}, bf16[256,256]{1,0:T(8,128)(2,1)S(1)}, u32[]{:S(2)}, u32[]{:S(2)}) collective-permute-start(bf16[256,256]{1,0:T(8,128)(2,1)S(1)} %pad_maximum_fusion.1.refs_6_), channel_id=1, source_target_pairs={{0,2},{2,0},{4,6},{6,4},{1,3},{3,1},{5,7},{7,5},{8,10},{10,8},{12,... | collective-permute-start | bytes 393224 | tf_op jit(solution)/shard_map/ppermute | solution.py:135
  37.8 1.2 %copy-start.1 = (bf16[1,128,4096]{2,1,0:T(8,128)(2,1)S(1)}, bf16[1,128,4096]{2,1,0:T(8,128)(2,1)}, u32[]{:S(2)}) copy-start(bf16[1,128,4096]{2,1,0:T(8,128)(2,1)} %param.13) | copy-start | bytes 3145732
  47.7 13.3 %collective-permute-start.14 = (bf16[256,256]{1,0:T(8,128)(2,1)S(1)}, bf16[256,256]{1,0:T(8,128)(2,1)S(1)}, u32[]{:S(2)}, u32[]{:S(2)}) collective-permute-start(bf16[256,256]{1,0:T(8,128)(2,1)S(1)} %get-tuple-element.56), channel_id=1, source_target_pairs={{0,2},{2,0},{4,6},{6,4},{1,3},{3,1},{5,7},{7,5},{8,10},{10,8},{12,... | collective-permute-start | bytes 393224 | tf_op jit(solution)/shard_map/ppermute | solution.py:135
  49.2 11.8 %collective-permute-start.15 = (bf16[256,256]{1,0:T(8,128)(2,1)S(1)}, bf16[256,256]{1,0:T(8,128)(2,1)S(1)}, u32[]{:S(2)}, u32[]{:S(2)}) collective-permute-start(bf16[256,256]{1,0:T(8,128)(2,1)S(1)} %get-tuple-element.57), channel_id=1, source_target_pairs={{0,4},{2,6},{4,0},{6,2},{1,5},{3,7},{5,1},{7,3},{8,12},{10,14},{12... | collective-permute-start | bytes 393224 | tf_op jit(solution)/shard_map/ppermute | solution.py:135
  51.2 9.8 %collective-permute-start.16 = (bf16[256,256]{1,0:T(8,128)(2,1)S(1)}, bf16[256,256]{1,0:T(8,128)(2,1)S(1)}, u32[]{:S(2)}, u32[]{:S(2)}) collective-permute-start(bf16[256,256]{1,0:T(8,128)(2,1)S(1)} %get-tuple-element.58), channel_id=1, source_target_pairs={{0,6},{2,4},{4,2},{6,0},{1,7},{3,5},{5,3},{7,1},{8,14},{10,12},{12... | collective-permute-start | bytes 393224 | tf_op jit(solution)/shard_map/ppermute | solution.py:135
  61.1 6.9 %collective-permute-start.17 = (bf16[256,256]{1,0:T(8,128)(2,1)S(1)}, bf16[256,256]{1,0:T(8,128)(2,1)S(1)}, u32[]{:S(2)}, u32[]{:S(2)}) collective-permute-start(bf16[256,256]{1,0:T(8,128)(2,1)S(1)} %get-tuple-element.60), channel_id=1, source_target_pairs={{0,2},{2,6},{6,4},{4,0},{1,3},{3,7},{7,5},{5,1},{8,10},{10,14},{14... | collective-permute-start | bytes 393224 | tf_op jit(solution)/shard_map/ppermute | solution.py:163
  61.7 10.9 %collective-permute-start.19 = (bf16[256,256]{1,0:T(8,128)(2,1)S(1)}, bf16[256,256]{1,0:T(8,128)(2,1)S(1)}, u32[]{:S(2)}, u32[]{:S(2)}) collective-permute-start(bf16[256,256]{1,0:T(8,128)(2,1)S(1)} %get-tuple-element.64), channel_id=1, source_target_pairs={{0,2},{2,0},{4,6},{6,4},{1,3},{3,1},{5,7},{7,5},{8,10},{10,8},{12,... | collective-permute-start | bytes 393224 | tf_op jit(solution)/shard_map/ppermute | solution.py:135
  68.0 6.8 %collective-permute-start.20 = (bf16[256,256]{1,0:T(8,128)(2,1)S(1)}, bf16[256,256]{1,0:T(8,128)(2,1)S(1)}, u32[]{:S(2)}, u32[]{:S(2)}) collective-permute-start(bf16[256,256]{1,0:T(8,128)(2,1)S(1)} %fusion.1), channel_id=1, source_target_pairs={{0,6},{2,4},{4,2},{6,0},{1,7},{3,5},{5,3},{7,1},{8,14},{10,12},{12... | collective-permute-start | bytes 393224 | tf_op jit(solution)/shard_map/ppermute | solution.py:135
  70.9 5.7 %collective-permute-start.18 = (bf16[128,256]{1,0:T(8,128)(2,1)S(1)}, bf16[128,256]{1,0:T(8,128)(2,1)S(1)}, u32[]{:S(2)}, u32[]{:S(2)}) collective-permute-start(bf16[128,256]{1,0:T(8,128)(2,1)S(1)} %pad_maximum_fusion.4), channel_id=1, source_target_pairs={{0,1},{1,0},{2,3},{3,2},{4,5},{5,4},{6,7},{7,6},{8,9},{9,8},{10,11... | collective-permute-start | bytes 196616 | tf_op jit(solution)/shard_map/ppermute | solution.py:135
  74.9 4.3 %collective-permute-start.21 = (bf16[128,256]{1,0:T(8,128)(2,1)S(1)}, bf16[128,256]{1,0:T(8,128)(2,1)S(1)}, u32[]{:S(2)}, u32[]{:S(2)}) collective-permute-start(bf16[128,256]{1,0:T(8,128)(2,1)S(1)} %pad_maximum_fusion.5), channel_id=1, source_target_pairs={{0,1},{1,0},{2,3},{3,2},{4,5},{5,4},{6,7},{7,6},{8,9},{9,8},{10,11... | collective-permute-start | bytes 196616 | tf_op jit(solution)/shard_map/ppermute | solution.py:135

commit v4 on v3

v4 whole, which is shorter than its diff:
```python
import functools
import math

import jax
import jax.numpy as jnp
from jax import lax
from jax.experimental import pallas as pl
from jax.experimental.pallas import tpu as pltpu
from jax.sharding import PartitionSpec as P

HD = 128
GROUP = 8
PAIR = 2
CHUNKS = 2
EXTRA = 16
VMEM_LIMIT = 52 * 1024 * 1024
NT = (((1,), (1,)), ((), ()))


def heads_down(ref, first, count):
    return jnp.concatenate(
        [ref[:, (first + i) * HD : (first + i + 1) * HD] for i in range(count)], axis=0
    )


def attend_kernel(n_slots, count, chunk, factor, *refs):
    last = chunk + 1 == CHUNKS
    length_ref, q_hbm, do_hbm, kown_hbm, vown_hbm = refs[:5]
    slot_refs, refs = refs[5 : 5 + n_slots], refs[5 + n_slots :]
    if last:
        slots_all, refs = refs[0], refs[1:]
        carried, refs = refs[1:4], refs[4:]
        out_hbm, dq_hbm, dkown_hbm, dvown_hbm, weight_ref = refs[:5]
        refs = refs[5:]
    else:
        out_hbm, dq_ref, dkown_ref, dvown_ref = refs[:4]
        refs = refs[4:]
    term_refs, refs = refs[:n_slots], refs[n_slots:]
    q_ref, do_ref, kown_ref, vown_ref, out_ref, s_ref, dp_ref, p_ref, ds_ref = refs[:9]
    in_sem, out_sem = refs[9:11]
    if last:
        dq_ref, dkown_ref, dvown_ref = refs[11:]
    first = chunk * count

    def columns(head, size):
        return pl.ds(head * size, size)

    loads = []
    for head in range(count):
        loads.append(
            [
                pltpu.make_async_copy(
                    hbm.at[:, columns(first + head, size)],
                    ref.at[:, columns(head, size)],
                    in_sem.at[head, i],
                )
                for i, (hbm, ref, size) in enumerate(
                    [
                        (kown_hbm, kown_ref, HD),
                        (q_hbm, q_ref, GROUP * HD),
                        (vown_hbm, vown_ref, HD),
                        (do_hbm, do_ref, GROUP * HD),
                    ]
                )
            ]
        )
        for copy in loads[-1]:
            copy.start()
    stores = []

    def store(ref, head, hbm, to, size, i):
        copy = pltpu.make_async_copy(
            ref.at[:, columns(head, size)], hbm.at[:, columns(to, size)], out_sem.at[to, i]
        )
        copy.start()
        stores.append(copy)

    rows = q_ref.shape[0]
    own = kown_ref.shape[0]
    held = term_refs[0].shape[0] // 2
    scale = factor * math.log2(math.e)
    weight = jnp.ones((1, 1), jnp.float32)
    if last:
        totals = [ref[2 * held :, :HD].astype(jnp.float32) for ref in slot_refs]
        totals = functools.reduce(jnp.add, totals)
        live_total = totals[:1] * 256 + totals[EXTRA // 2 : EXTRA // 2 + 1]
        weight_row = slots_all[0] / live_total
        weight_ref[...] = jnp.broadcast_to(weight_row, weight_ref.shape)
        weight = weight_row[:, :1]
        for source, ref, hbm, size, i in (
            (carried[0], dq_ref, dq_hbm, GROUP * HD, 1),
            (carried[1], dkown_ref, dkown_hbm, HD, 2),
            (carried[2], dvown_ref, dvown_hbm, HD, 3),
        ):
            for head in range(first):
                cols = slice(head * size, (head + 1) * size)
                ref[:, cols] = (source[:, cols].astype(jnp.float32) * weight).astype(jnp.bfloat16)
                store(ref, head, hbm, head, size, i)
    grad_scale = weight * factor
    base = first if last else 0
    width = PAIR * rows
    key_pos = lax.broadcasted_iota(jnp.int32, (own, width), 0)
    row_pos = lax.broadcasted_iota(jnp.int32, (own, width), 1) % rows
    allowed = key_pos <= row_pos
    live = (lax.broadcasted_iota(jnp.int32, (1, width), 1) % rows) < length_ref[0]
    for head in range(count):
        for copy in loads[head]:
            copy.wait()
        here = slice(head * HD, (head + 1) * HD)
        q_at = head * GROUP
        keys = jnp.concatenate(
            [kown_ref[:, here]] + [ref[:held, here] for ref in slot_refs], axis=0
        )
        values = jnp.concatenate(
            [vown_ref[:, here]] + [ref[held : 2 * held, here] for ref in slot_refs], axis=0
        )
        keys_t = keys.T
        values_t = values.T
        for pair in range(GROUP // PAIR):
            s_now, dp_now = s_ref.at[pair % 2], dp_ref.at[pair % 2]
            cols = slice(pair * width, (pair + 1) * width)
            do = heads_down(do_ref, q_at + pair * PAIR, PAIR)
            s_now[...] = lax.dot_general(
                keys,
                heads_down(q_ref, q_at + pair * PAIR, PAIR),
                NT,
                preferred_element_type=jnp.float32,
            )
            dp_now[...] = lax.dot_general(values, do, NT, preferred_element_type=jnp.float32)
            s_now[:own] = jnp.where(allowed, s_now[:own], -1e30)
            top = jnp.max(s_now[...], axis=0, keepdims=True) * scale
            exponent = jnp.exp2(s_now[...] * scale - top)
            s_now[...] = exponent
            total = jnp.sum(exponent, axis=0, keepdims=True)
            inverse = jnp.where(live, 1.0 / total, 0.0)
            p_ref[:, cols] = (s_now[...] * inverse).astype(jnp.bfloat16)
            attended = jnp.dot(values_t, p_ref[:, cols], preferred_element_type=jnp.float32)
            centre = jnp.sum(attended * do.astype(jnp.float32).T, axis=0, keepdims=True)
            ds_ref[:, cols] = (
                p_ref[:, cols].astype(jnp.float32) * (dp_now[...] - centre)
            ).astype(jnp.bfloat16)
            dq = jnp.dot(keys_t, ds_ref[:, cols], preferred_element_type=jnp.float32) * grad_scale
            for i in range(PAIR):
                lanes = slice(i * rows, (i + 1) * rows)
                at = pair * PAIR + i
                place = slice((q_at + at) * HD, (q_at + at + 1) * HD)
                out_ref[:, place] = attended[:, lanes].T.astype(jnp.bfloat16)
                place = slice((base * GROUP + q_at + at) * HD, (base * GROUP + q_at + at + 1) * HD)
                dq_ref[:, place] = dq[:, lanes].T.astype(jnp.bfloat16)
        store(out_ref, head, out_hbm, first + head, GROUP * HD, 0)
        dv = jnp.dot(
            p_ref[...], heads_down(do_ref, q_at, GROUP), preferred_element_type=jnp.float32
        )
        dk = jnp.dot(
            ds_ref[...], heads_down(q_ref, q_at, GROUP), preferred_element_type=jnp.float32
        )
        place = slice((base + head) * HD, (base + head + 1) * HD)
        dk = (dk * grad_scale).astype(jnp.bfloat16)
        dv = (dv * weight).astype(jnp.bfloat16)
        dkown_ref[:, place] = dk[:own]
        dvown_ref[:, place] = dv[:own]
        if last:
            store(dq_ref, first + head, dq_hbm, first + head, GROUP * HD, 1)
            store(dkown_ref, first + head, dkown_hbm, first + head, HD, 2)
            store(dvown_ref, first + head, dvown_hbm, first + head, HD, 3)
        for i, ref in enumerate(term_refs):
            part = slice(own + i * held, own + (i + 1) * held)
            ref[:held, here] = dk[part]
            ref[held:, here] = dv[part]
    for copy in stores:
        copy.wait()


def swap(x, axis, by):
    return lax.ppermute(x, axis, [(i, i ^ by) for i in range(lax.axis_size(axis))])


def sum_over(x, axis):
    by = 1
    while by < lax.axis_size(axis):
        x = x + swap(x, axis, by)
        by *= 2
    return x


def line_gather(block):
    return [block] + [swap(block, "response", m) for m in range(1, lax.axis_size("response"))]


def line_reduce(slots, scale):
    terms = [slots[0]] + [swap(slots[m], "response", m) for m in range(1, len(slots))]
    total = functools.reduce(jnp.add, [term.astype(jnp.float32) for term in terms])
    return (total * scale).astype(slots[0].dtype)


def own_columns(block, chunk, by):
    cols = block.shape[1] // (lax.axis_size("tensor") * CHUNKS)
    rank = lax.axis_index("tensor") ^ by
    return lax.dynamic_slice_in_dim(block, (rank * CHUNKS + chunk) * cols, cols, 1)


def tensor_gather(blocks, chunk):
    parts = lax.axis_size("tensor")
    pieces = []
    for m in range(parts):
        piece = jnp.concatenate([own_columns(block, chunk, m) for block in blocks], axis=0)
        pieces.append(piece if m == 0 else swap(piece, "tensor", m))
    rows = blocks[0].shape[0]
    return jnp.concatenate(
        [piece[i * rows : (i + 1) * rows] for i in range(len(blocks)) for piece in pieces], axis=0
    )


def tensor_spread(total, n_arrays):
    parts = lax.axis_size("tensor")
    rows = total.shape[0] // (n_arrays * parts)
    pieces = []
    for m in range(parts):
        piece = jnp.concatenate(
            [total[(i * parts + m) * rows : (i * parts + m + 1) * rows] for i in range(n_arrays)],
            axis=0,
        )
        pieces.append(piece if m == 0 else swap(piece, "tensor", m))
    return pieces


def whole_columns(chunk_pieces, array):
    parts = lax.axis_size("tensor")
    rank = lax.axis_index("tensor")
    rows = chunk_pieces[0][0].shape[0] // 2
    by_rank = [
        jnp.concatenate([pieces[m][array * rows : (array + 1) * rows] for pieces in chunk_pieces], axis=1)
        for m in range(parts)
    ]
    ordered = []
    for t in range(parts):
        column = by_rank[0]
        for m in range(1, parts):
            column = jnp.where(rank ^ m == t, by_rank[m], column)
        ordered.append(column)
    return jnp.concatenate(ordered, axis=1)


SMEM = pl.BlockSpec(memory_space=pltpu.SMEM)
HBM = pl.BlockSpec(memory_space=pltpu.HBM)
VMEM = pl.BlockSpec(memory_space=pltpu.VMEM)


def like(x):
    return jax.ShapeDtypeStruct(x.shape, x.dtype)


def attend(chunk, slots, length, q, do, k, v, slots_all, carried):
    rows = q.shape[0]
    heads = k.shape[1] // HD
    count = heads // CHUNKS
    n_slots = len(slots)
    last = chunk + 1 == CHUNKS
    held = (slots[0].shape[0] - EXTRA * last) // 2
    n_keys = rows + n_slots * held
    bf16 = jnp.bfloat16
    unit = 2 * n_keys * GROUP * rows * HD * count
    pair_buffer = pltpu.VMEM((2, n_keys, PAIR * rows), jnp.float32)
    group_buffer = pltpu.VMEM((n_keys, GROUP * rows), bf16)
    wide = pltpu.VMEM((rows, count * GROUP * HD), bf16)
    own = pltpu.VMEM((rows, count * HD), bf16)
    scratch = [wide, wide, own, own, wide, pair_buffer, pair_buffer, group_buffer, group_buffer]
    scratch += [pltpu.SemaphoreType.DMA((count, 4)), pltpu.SemaphoreType.DMA((heads, 4))]
    terms = [jax.ShapeDtypeStruct((2 * held, count * HD), bf16)] * n_slots
    in_specs = [SMEM] + [HBM] * 4 + [VMEM] * n_slots
    if last:
        in_specs += [SMEM, HBM] + [VMEM] * 3
        out_specs = [HBM] * 4 + [VMEM] * (1 + n_slots)
        out_shape = [like(q), like(q), like(k), like(v)]
        out_shape += [jax.ShapeDtypeStruct((8, HD), jnp.float32)] + terms
        scratch += [pltpu.VMEM(x.shape, bf16) for x in (q, k, v)]
        operands = [slots_all, *carried]
    else:
        out_specs = [HBM] + [VMEM] * (3 + n_slots)
        part = lambda x: jax.ShapeDtypeStruct((x.shape[0], x.shape[1] // CHUNKS), bf16)
        out_shape = [like(q), part(q), part(k), part(v)] + terms
        operands = []
    return pl.pallas_call(
        functools.partial(attend_kernel, n_slots, count, chunk, 1.0 / math.sqrt(HD)),
        in_specs=in_specs,
        out_specs=out_specs,
        out_shape=out_shape,
        input_output_aliases={6 + n_slots: 0} if last else {},
        scratch_shapes=scratch,
        compiler_params=pltpu.CompilerParams(vmem_limit_bytes=VMEM_LIMIT),
        cost_estimate=pl.CostEstimate(
            flops=24 * unit,
            bytes_accessed=8 * rows * GROUP * HD * count,
            transcendentals=count * n_keys * GROUP * rows,
        ),
        name=f"attend_{chunk}",
    )(length, q, do, k, v, *slots, *operands)


def total_rows(total, cols):
    high = jnp.floor(total / 256)
    rows = jnp.repeat(jnp.stack([high, total - 256 * high]), EXTRA // 2, axis=0)
    return jnp.broadcast_to(rows, (EXTRA, cols)).astype(jnp.bfloat16)


def body(queries, keys, values, prefix_keys, prefix_values, lengths, out_grad):
    q, k, v, do = queries[0], keys[0], values[0], out_grad[0]
    length = lengths[0]
    prefix = (prefix_keys[0], prefix_values[0])
    slots_all = q.shape[0] * lax.axis_size("prompt") * lax.axis_size("response")
    slots_all = jnp.full((1,), slots_all, jnp.float32)
    first, second = [tensor_gather(prefix, chunk) for chunk in range(CHUNKS)]
    behind = 0 * second[-1, :1].astype(jnp.float32)
    prompt_total = sum_over(length.astype(jnp.float32) + behind, "prompt")
    second = jnp.concatenate([second, total_rows(prompt_total, second.shape[1])], axis=0)
    slots = line_gather(first)
    next_slots = line_gather(second)
    results = attend(0, slots, length, q, do, k, v, slots_all, [])
    carried, terms = results[:4], results[4:]
    results = attend(1, next_slots, length, q, do, k, v, slots_all, carried)
    outs, weight, next_terms = results[:4], results[4][0, 0], results[5:]
    first_sum = line_reduce(terms, weight)
    second_sum = line_reduce(next_terms, 1.0)
    pieces = [tensor_spread(total, len(prefix)) for total in (first_sum, second_sum)]
    grads = [whole_columns(pieces, array) for array in range(len(prefix))]
    return tuple(x[None] for x in (*outs, *grads))


def solution(mesh):
    in_specs = (
        P("prompt", "response", "tensor"),
        P("prompt", "response", "tensor"),
        P("prompt", "response", "tensor"),
        P("prompt", ("response", "tensor"), None),
        P("prompt", ("response", "tensor"), None),
        P("prompt", "response"),
        P("prompt", "response", "tensor"),
    )
    out_specs = (
        P("prompt", "response", "tensor"),
        P("prompt", "response", "tensor"),
        P("prompt", "response", "tensor"),
        P("prompt", "response", "tensor"),
        P("prompt", ("response", "tensor"), None),
        P("prompt", ("response", "tensor"), None),
    )
    return jax.shard_map(body, mesh=mesh, in_specs=in_specs, out_specs=out_specs, check_vma=False)
```

time: 81 us -> 68.2 us (0.84)
  starting transfers between devices: 40.8 us -> 28.3 us
  waiting for transfers between devices: 13.1 us -> 10.6 us
  between operations: 5.51 us -> 3.4 us
  Pallas kernels: 17.4 us -> 19.4 us
  local copies, waits for them, and re-layouts: 2.17 us -> 3.71 us
    ppermute x20 -> x18, starting transfers between devices: 38.5 us -> 28.3 us  [swap(): lax.ppermute(x, axis, [(i, i ^ by) for i in range(lax.axis_size(axis))])]
    ppermute x2 -> x0, waiting for transfers between devices: 3.36 us -> none  [the longest x1 3.36 us: line_reduce(): lax.ppermute(slots[2], 'response', [(0, 1), (1, 3), (3, 2), (2, 0)])]
    ppermute x2 -> x0, starting transfers between devices: 2.29 us -> none  [the longest x1 1.67 us: line_gather(): return ([block, near, lax.ppermute(onward, 'response', cycle), far], after)]
    pallas_call x2, Pallas kernels: 17.4 us -> 19.4 us  [attend(): pl.pallas_call(functools.partial(attend_kernel, n_slots, count, chunk, 1....]
    slice x0 -> x2, local copies, waits for them, and re-layouts: none -> 1.03 us  [the longest x1 0.52 us: body(): behind = 0 * second[-1, :1].astype(jnp.float32)]
    ppermute x20 -> x18, waiting for transfers between devices: 9.73 us -> 10.6 us  [swap(): lax.ppermute(x, axis, [(i, i ^ by) for i in range(lax.axis_size(axis))])]
  transfers between devices with their start and end apart: 22 -> 18, of which waited for: 5 -> 4; matrix products, arithmetic and copies ran while one was open for 1% -> 6% of each run, Pallas kernels for 22% -> 29%
where the time goes in v4:
time: 68.2 us; the launch traced here: 67.8 us
  starting transfers between devices  28.3 us (41%)
  Pallas kernels  19.4 us (28%)
  waiting for transfers between devices  10.6 us (16%)
  local copies, waits for them, and re-layouts  3.71 us (5%)
  between operations  3.4 us (5%)
  other arithmetic  2.3 us (3%)
    ppermute x18, starting transfers between devices, swap(): lax.ppermute(x, axis, [(i, i ^ by) for i in range(lax.axis_size(axis))])  28.3 us
    pallas_call x2, Pallas kernels, attend(): pl.pallas_call(functools.partial(attend_kernel, n_slots, count, chunk, 1....  19.4 us
    ppermute x18, waiting for transfers between devices, swap(): lax.ppermute(x, axis, [(i, i ^ by) for i in range(lax.axis_size(axis))])  10.6 us
    unnamed x8, local copies, waits for them, and re-layouts  1.54 us
  transfers between devices with their start and end apart: 18, of which 4 were waited for; matrix products, arithmetic and copies ran while one was open for 6% of the time, Pallas kernels for 29%

profile of v4, /device:TPU:0, one launch (start us, length us, event | category | flops | bytes accessed | tf_op | source)
XLA Modules:
  0.0 67.8 jit_solution(16664246923141619055)
XLA Ops:
  0.7 0.9 %dynamic-slice_bitcast_fusion = (bf16[64,256]{1,0:T(8,128)(2,1)S(1)}, bf16[64,256]{1,0:T(8,128)(2,1)S(1)}, bf16[64,256]{1,0:T(8,128)(2,1)S(1)}, bf16[64,256]{1,0...) fusion(bf16[1,64,1024]{2,1,0:T(8,128)(2,1)} %param.11, s32[]{:T(128)S(6)} %select_n.40, ...), kind=kLoop, calls=%fused_computation.21 | loop fusion | bytes 393228 | tf_op jit(solution)/shard_map/dynamic_slice | solution.py:199
  1.5 3.0 %collective-permute-start.6 = (bf16[128,256]{1,0:T(8,128)(2,1)S(1)}, bf16[128,256]{1,0:T(8,128)(2,1)S(1)}, u32[]{:S(2)}, u32[]{:S(2)}) collective-permute-start(bf16[128,256]{1,0:T(8,128)(2,1)S(1)} %pad_maximum_fusion.2), channel_id=1, source_target_pairs={{0,1},{1,0},{2,3},{3,2},{4,5},{5,4},{6,7},{7,6},{8,9},{9,8},{10,11... | collective-permute-start | bytes 196616 | tf_op jit(solution)/shard_map/ppermute | solution.py:175
  4.6 0.1 collective-permute-start
  5.3 0.8 %bitcast_dynamic-update-slice_fusion.1 = bf16[272,256]{1,0:T(8,128)(2,1)S(1)} fusion(bf16[1,64,1024]{2,1,0:T(8,128)(2,1)} %param.10, s32[]{:T(128)S(6)} %select_n.38), kind=kLoop, calls=%fused_computation.20 | loop fusion | bytes 65540
  6.1 0.9 %collective-permute-done.6 = bf16[128,256]{1,0:T(8,128)(2,1)S(1)} collective-permute-done((bf16[128,256]{1,0:T(8,128)(2,1)S(1)}, bf16[128,256]{1,0:T(8,128)(2,1)S(1)}, u32[]{:S(2)}, u32[]{:S(2)}) %collective-permute-start.6) | collective-permute-done | bytes 65568 | tf_op jit(solution)/shard_map/ppermute | solution.py:175
  7.0 0.0 copy-start.1
  7.0 0.0 copy-start
  7.0 2.6 %collective-permute-start.7 = (bf16[256,256]{1,0:T(8,128)(2,1)S(1)}, bf16[256,256]{1,0:T(8,128)(2,1)S(1)}, u32[]{:S(2)}, u32[]{:S(2)}) collective-permute-start(bf16[256,256]{1,0:T(8,128)(2,1)S(1)} %pad_maximum_fusion.refs_5_), channel_id=1, source_target_pairs={{0,2},{2,0},{4,6},{6,4},{1,3},{3,1},{5,7},{7,5},{8,10},{10,8},{12,... | collective-permute-start | bytes 393224 | tf_op jit(solution)/shard_map/ppermute | solution.py:175
  9.6 2.6 %collective-permute-start.8 = (bf16[256,256]{1,0:T(8,128)(2,1)S(1)}, bf16[256,256]{1,0:T(8,128)(2,1)S(1)}, u32[]{:S(2)}, u32[]{:S(2)}) collective-permute-start(bf16[256,256]{1,0:T(8,128)(2,1)S(1)} %pad_maximum_fusion.refs_5_), channel_id=1, source_target_pairs={{0,4},{2,6},{4,0},{6,2},{1,5},{3,7},{5,1},{7,3},{8,12},{10,14},{12... | collective-permute-start | bytes 393224 | tf_op jit(solution)/shard_map/ppermute | solution.py:175
  12.2 0.0 collective-permute-start.9
  12.2 0.0 collective-permute-done
  12.2 0.5 slice.75
  13.4 1.0 %collective-permute-start.1 = (f32[1]{0:T(128)}, f32[1]{0:T(128)}, u32[]{:S(2)}, u32[]{:S(2)}) collective-permute-start(f32[1]{0:T(128)} %add.55), channel_id=1, source_target_pairs={{0,8},{8,0},{16,24},{24,16},{1,9},{9,1},{17,25},{25,17},{2,10},{10... | collective-permute-start | bytes 20 | tf_op jit(solution)/shard_map/ppermute | solution.py:175
  14.4 0.8 %bitcast_dynamic-update-slice_fusion = bf16[272,256]{1,0:T(8,128)(2,1)S(1)} fusion(bf16[272,256]{1,0:T(8,128)(2,1)S(1)} %slice_dynamic-update-slice_fusion.1, bf16[1,64,1024]{2,1,0:T(8,128)(2,1)} %param.11, s32[]{:T(128)S(6)} %select_n.38), kind=kLoop, calls=%fused_computation.19 | loop fusion | bytes 65540
  15.1 0.0 collective-permute-done.1
  15.8 3.1 %collective-permute-start.2 = (f32[1]{0:T(128)}, f32[1]{0:T(128)}, u32[]{:S(2)}, u32[]{:S(2)}) collective-permute-start(f32[1]{0:T(128)} %add.56), channel_id=1, source_target_pairs={{0,16},{8,24},{16,0},{24,8},{1,17},{9,25},{17,1},{25,9},{2,18},{10... | collective-permute-start | bytes 20 | tf_op jit(solution)/shard_map/ppermute | solution.py:175
  18.9 0.6 collective-permute-done.2
  20.2 0.1 maximum_bitcast_fusion.2
  20.2 0.1 broadcast_in_dim.26
  20.3 0.1 convert_element_type.49
  20.4 0.1 constant_dynamic-update-slice_fusion.refs_5_
  20.5 0.9 %collective-permute-start.3 = (bf16[272,256]{1,0:T(8,128)(2,1)S(1)}, bf16[272,256]{1,0:T(8,128)(2,1)S(1)}, u32[]{:S(2)}, u32[]{:S(2)}) collective-permute-start(bf16[272,256]{1,0:T(8,128)(2,1)S(1)} %constant_dynamic-update-slice_fusion.refs_5_), channel_id=1, source_target_pairs={{0,2},{2,0},{4,6},{6,4},{1,3},{3,1},{5,7},{7,5},{8,10},{10,8},{12,... | collective-permute-start | bytes 417800 | tf_op jit(solution)/shard_map/ppermute | solution.py:175
  21.4 3.5 %collective-permute-start.4 = (bf16[272,256]{1,0:T(8,128)(2,1)S(1)}, bf16[272,256]{1,0:T(8,128)(2,1)S(1)}, u32[]{:S(2)}, u32[]{:S(2)}) collective-permute-start(bf16[272,256]{1,0:T(8,128)(2,1)S(1)} %constant_dynamic-update-slice_fusion.refs_5_), channel_id=1, source_target_pairs={{0,4},{2,6},{4,0},{6,2},{1,5},{3,7},{5,1},{7,3},{8,12},{10,14},{12... | collective-permute-start | bytes 417800 | tf_op jit(solution)/shard_map/ppermute | solution.py:175
  24.9 0.0 collective-permute-done.7.refs_6_
  24.9 0.0 collective-permute-start.5
  24.9 0.0 collective-permute-done.8.refs_7_
  24.9 0.0 collective-permute-done.9.refs_8_
  24.9 0.0 copy-done.1
  24.9 0.0 copy-done
  24.9 9.6 %attend_0.1 = (bf16[128,4096]{1,0:T(8,128)(2,1)}, bf16[128,2048]{1,0:T(8,128)(2,1)S(1)}, bf16[128,256]{1,0:T(8,128)(2,1)S(1)}, bf16[128,256]{1,0:T(8,128)(2,1)S(...) custom-call(s32[1]{0:T(128)} %bitcast.36.refs_0_, ...), custom_call_target="tpu_custom_call" | custom-call | flops 8053063680 | bytes 2097152 | tf_op jit(solution)/shard_map/attend_0/pallas_call | solution.py:283
  34.5 0.6 collective-permute-start.10
  35.1 3.8 %collective-permute-start.11 = (bf16[256,256]{1,0:T(8,128)(2,1)S(1)}, bf16[256,256]{1,0:T(8,128)(2,1)S(1)}, u32[]{:S(2)}, u32[]{:S(2)}) collective-permute-start(bf16[256,256]{1,0:T(8,128)(2,1)S(1)} %get-tuple-element.33), channel_id=1, source_target_pairs={{0,4},{2,6},{4,0},{6,2},{1,5},{3,7},{5,1},{7,3},{8,12},{10,14},{12... | collective-permute-start | bytes 393224 | tf_op jit(solution)/shard_map/ppermute | solution.py:175
  38.9 0.0 collective-permute-done.3.refs_6_
  38.9 0.0 collective-permute-start.12
  38.9 0.0 collective-permute-done.4.refs_7_
  38.9 0.0 collective-permute-done.5.refs_8_
  38.9 9.8 %attend_1.1 = (bf16[128,4096]{1,0:T(8,128)(2,1)}, bf16[128,4096]{1,0:T(8,128)(2,1)}, bf16[128,512]{1,0:T(8,128)(2,1)}, bf16[128,512]{1,0:T(8,128)(2,1)}, f32[8,1...) custom-call(s32[1]{0:T(128)} %bitcast.37.refs_0_, ...), custom_call_target="tpu_custom_call", output_to_operand_aliasing={{0}: (10, {})} | custom-call | flops 8053063680 | bytes 2097152 | tf_op jit(solution)/shard_map/attend_1/pallas_call | solution.py:283
  48.8 0.5 slice.60
  49.3 0.5 collective-permute-start.14
  49.8 3.8 %collective-permute-start.15 = (bf16[256,256]{1,0:T(8,128)(2,1)S(1)}, bf16[256,256]{1,0:T(8,128)(2,1)S(1)}, u32[]{:S(2)}, u32[]{:S(2)}) collective-permute-start(bf16[256,256]{1,0:T(8,128)(2,1)S(1)} %get-tuple-element.38), channel_id=1, source_target_pairs={{0,4},{2,6},{4,0},{6,2},{1,5},{3,7},{5,1},{7,3},{8,12},{10,14},{12... | collective-permute-start | bytes 393224 | tf_op jit(solution)/shard_map/ppermute | solution.py:175
  53.7 0.0 collective-permute-done.10
  53.7 0.0 collective-permute-start.16
  53.7 0.0 collective-permute-done.11
  53.7 0.0 collective-permute-done.12
  53.7 0.7 %multiply_convert_fusion = bf16[256,256]{1,0:T(8,128)(2,1)S(1)} fusion(bf16[256,256]{1,0:T(8,128)(2,1)S(1)} %collective-permute-done.12, bf16[256,256]{1,0:T(8,128)(2,1)S(1)} %collective-permute-done.11, bf16[256,256]{1,0:T(8,128)(2,1)S(1)} %collective-permute-done.10, bf16[256,256]{1,0:T(8,128)(2,1)S(1)} %get-tuple-element.31, f32[]{:T(128)} %bitcast.21), kind=kLoop, calls=%fused_computation.1 | loop fusion | flops 589824 | bytes 655364 | tf_op jit(solution)/shard_map/convert_element_type | solution.py:193
  54.5 1.5 %collective-permute-start.13 = (bf16[128,256]{1,0:T(8,128)(2,1)S(1)}, bf16[128,256]{1,0:T(8,128)(2,1)S(1)}, u32[]{:S(2)}, u32[]{:S(2)}) collective-permute-start(bf16[128,256]{1,0:T(8,128)(2,1)S(1)} %pad_maximum_fusion.3), channel_id=1, source_target_pairs={{0,1},{1,0},{2,3},{3,2},{4,5},{5,4},{6,7},{7,6},{8,9},{9,8},{10,11... | collective-permute-start | bytes 196616 | tf_op jit(solution)/shard_map/ppermute | solution.py:175
  55.9 0.0 collective-permute-done.14
  55.9 6.0 %collective-permute-done.15 = bf16[256,256]{1,0:T(8,128)(2,1)S(1)} collective-permute-done((bf16[256,256]{1,0:T(8,128)(2,1)S(1)}, bf16[256,256]{1,0:T(8,128)(2,1)S(1)}, u32[]{:S(2)}, u32[]{:S(2)}) %collective-permute-start.15) | collective-permute-done | bytes 131104 | tf_op jit(solution)/shard_map/ppermute | solution.py:175
  61.9 0.0 collective-permute-done.16
  61.9 0.1 add_convert_fusion
  62.0 1.3 %collective-permute-start.17 = (bf16[128,256]{1,0:T(8,128)(2,1)S(1)}, bf16[128,256]{1,0:T(8,128)(2,1)S(1)}, u32[]{:S(2)}, u32[]{:S(2)}) collective-permute-start(bf16[128,256]{1,0:T(8,128)(2,1)S(1)} %pad_maximum_fusion.4), channel_id=1, source_target_pairs={{0,1},{1,0},{2,3},{3,2},{4,5},{5,4},{6,7},{7,6},{8,9},{9,8},{10,11... | collective-permute-start | bytes 196616 | tf_op jit(solution)/shard_map/ppermute | solution.py:175
  63.3 0.0 collective-permute-done.13
  63.3 3.0 %collective-permute-done.17 = bf16[128,256]{1,0:T(8,128)(2,1)S(1)} collective-permute-done((bf16[128,256]{1,0:T(8,128)(2,1)S(1)}, bf16[128,256]{1,0:T(8,128)(2,1)S(1)}, u32[]{:S(2)}, u32[]{:S(2)}) %collective-permute-start.17) | collective-permute-done | bytes 65568 | tf_op jit(solution)/shard_map/ppermute | solution.py:175
  66.4 0.7 maximum_bitcast_fusion.1
  67.1 0.7 maximum_bitcast_fusion
  (14 shorter events, 0.1 us)
Async XLA Ops:
  1.5 5.4 %collective-permute-start.6 = (bf16[128,256]{1,0:T(8,128)(2,1)S(1)}, bf16[128,256]{1,0:T(8,128)(2,1)S(1)}, u32[]{:S(2)}, u32[]{:S(2)}) collective-permute-start(bf16[128,256]{1,0:T(8,128)(2,1)S(1)} %pad_maximum_fusion.2), channel_id=1, source_target_pairs={{0,1},{1,0},{2,3},{3,2},{4,5},{5,4},{6,7},{7,6},{8,9},{9,8},{10,11... | collective-permute-start | bytes 196616 | tf_op jit(solution)/shard_map/ppermute | solution.py:175
  4.6 7.6 %collective-permute-start = (bf16[128,256]{1,0:T(8,128)(2,1)S(1)}, bf16[128,256]{1,0:T(8,128)(2,1)S(1)}, u32[]{:S(2)}, u32[]{:S(2)}) collective-permute-start(bf16[128,256]{1,0:T(8,128)(2,1)S(1)} %pad_maximum_fusion.1), channel_id=1, source_target_pairs={{0,1},{1,0},{2,3},{3,2},{4,5},{5,4},{6,7},{7,6},{8,9},{9,8},{10,11... | collective-permute-start | bytes 196616 | tf_op jit(solution)/shard_map/ppermute | solution.py:175
  7.0 17.9 %copy-start.1 = (bf16[1,128,512]{2,1,0:T(8,128)(2,1)S(1)}, bf16[1,128,512]{2,1,0:T(8,128)(2,1)}, u32[]{:S(2)}) copy-start(bf16[1,128,512]{2,1,0:T(8,128)(2,1)} %param.9) | copy-start | bytes 393220
  7.0 17.9 %copy-start = (bf16[1,128,512]{2,1,0:T(8,128)(2,1)S(1)}, bf16[1,128,512]{2,1,0:T(8,128)(2,1)}, u32[]{:S(2)}) copy-start(bf16[1,128,512]{2,1,0:T(8,128)(2,1)} %param.8) | copy-start | bytes 393220
  7.0 17.9 %collective-permute-start.7 = (bf16[256,256]{1,0:T(8,128)(2,1)S(1)}, bf16[256,256]{1,0:T(8,128)(2,1)S(1)}, u32[]{:S(2)}, u32[]{:S(2)}) collective-permute-start(bf16[256,256]{1,0:T(8,128)(2,1)S(1)} %pad_maximum_fusion.refs_5_), channel_id=1, source_target_pairs={{0,2},{2,0},{4,6},{6,4},{1,3},{3,1},{5,7},{7,5},{8,10},{10,8},{12,... | collective-permute-start | bytes 393224 | tf_op jit(solution)/shard_map/ppermute | solution.py:175
  9.6 15.3 %collective-permute-start.8 = (bf16[256,256]{1,0:T(8,128)(2,1)S(1)}, bf16[256,256]{1,0:T(8,128)(2,1)S(1)}, u32[]{:S(2)}, u32[]{:S(2)}) collective-permute-start(bf16[256,256]{1,0:T(8,128)(2,1)S(1)} %pad_maximum_fusion.refs_5_), channel_id=1, source_target_pairs={{0,4},{2,6},{4,0},{6,2},{1,5},{3,7},{5,1},{7,3},{8,12},{10,14},{12... | collective-permute-start | bytes 393224 | tf_op jit(solution)/shard_map/ppermute | solution.py:175
  12.2 12.7 %collective-permute-start.9 = (bf16[256,256]{1,0:T(8,128)(2,1)S(1)}, bf16[256,256]{1,0:T(8,128)(2,1)S(1)}, u32[]{:S(2)}, u32[]{:S(2)}) collective-permute-start(bf16[256,256]{1,0:T(8,128)(2,1)S(1)} %pad_maximum_fusion.refs_5_), channel_id=1, source_target_pairs={{0,6},{2,4},{4,2},{6,0},{1,7},{3,5},{5,3},{7,1},{8,14},{10,12},{12... | collective-permute-start | bytes 393224 | tf_op jit(solution)/shard_map/ppermute | solution.py:175
  13.4 1.8 %collective-permute-start.1 = (f32[1]{0:T(128)}, f32[1]{0:T(128)}, u32[]{:S(2)}, u32[]{:S(2)}) collective-permute-start(f32[1]{0:T(128)} %add.55), channel_id=1, source_target_pairs={{0,8},{8,0},{16,24},{24,16},{1,9},{9,1},{17,25},{25,17},{2,10},{10... | collective-permute-start | bytes 20 | tf_op jit(solution)/shard_map/ppermute | solution.py:175
  15.8 3.7 %collective-permute-start.2 = (f32[1]{0:T(128)}, f32[1]{0:T(128)}, u32[]{:S(2)}, u32[]{:S(2)}) collective-permute-start(f32[1]{0:T(128)} %add.56), channel_id=1, source_target_pairs={{0,16},{8,24},{16,0},{24,8},{1,17},{9,25},{17,1},{25,9},{2,18},{10... | collective-permute-start | bytes 20 | tf_op jit(solution)/shard_map/ppermute | solution.py:175
  20.5 18.4 %collective-permute-start.3 = (bf16[272,256]{1,0:T(8,128)(2,1)S(1)}, bf16[272,256]{1,0:T(8,128)(2,1)S(1)}, u32[]{:S(2)}, u32[]{:S(2)}) collective-permute-start(bf16[272,256]{1,0:T(8,128)(2,1)S(1)} %constant_dynamic-update-slice_fusion.refs_5_), channel_id=1, source_target_pairs={{0,2},{2,0},{4,6},{6,4},{1,3},{3,1},{5,7},{7,5},{8,10},{10,8},{12,... | collective-permute-start | bytes 417800 | tf_op jit(solution)/shard_map/ppermute | solution.py:175
  21.4 17.6 %collective-permute-start.4 = (bf16[272,256]{1,0:T(8,128)(2,1)S(1)}, bf16[272,256]{1,0:T(8,128)(2,1)S(1)}, u32[]{:S(2)}, u32[]{:S(2)}) collective-permute-start(bf16[272,256]{1,0:T(8,128)(2,1)S(1)} %constant_dynamic-update-slice_fusion.refs_5_), channel_id=1, source_target_pairs={{0,4},{2,6},{4,0},{6,2},{1,5},{3,7},{5,1},{7,3},{8,12},{10,14},{12... | collective-permute-start | bytes 417800 | tf_op jit(solution)/shard_map/ppermute | solution.py:175
  24.9 14.1 %collective-permute-start.5 = (bf16[272,256]{1,0:T(8,128)(2,1)S(1)}, bf16[272,256]{1,0:T(8,128)(2,1)S(1)}, u32[]{:S(2)}, u32[]{:S(2)}) collective-permute-start(bf16[272,256]{1,0:T(8,128)(2,1)S(1)} %constant_dynamic-update-slice_fusion.refs_5_), channel_id=1, source_target_pairs={{0,6},{2,4},{4,2},{6,0},{1,7},{3,5},{5,3},{7,1},{8,14},{10,12},{12... | collective-permute-start | bytes 417800 | tf_op jit(solution)/shard_map/ppermute | solution.py:175
  34.5 19.2 %collective-permute-start.10 = (bf16[256,256]{1,0:T(8,128)(2,1)S(1)}, bf16[256,256]{1,0:T(8,128)(2,1)S(1)}, u32[]{:S(2)}, u32[]{:S(2)}) collective-permute-start(bf16[256,256]{1,0:T(8,128)(2,1)S(1)} %get-tuple-element.32), channel_id=1, source_target_pairs={{0,2},{2,0},{4,6},{6,4},{1,3},{3,1},{5,7},{7,5},{8,10},{10,8},{12,... | collective-permute-start | bytes 393224 | tf_op jit(solution)/shard_map/ppermute | solution.py:175
  35.1 18.6 %collective-permute-start.11 = (bf16[256,256]{1,0:T(8,128)(2,1)S(1)}, bf16[256,256]{1,0:T(8,128)(2,1)S(1)}, u32[]{:S(2)}, u32[]{:S(2)}) collective-permute-start(bf16[256,256]{1,0:T(8,128)(2,1)S(1)} %get-tuple-element.33), channel_id=1, source_target_pairs={{0,4},{2,6},{4,0},{6,2},{1,5},{3,7},{5,1},{7,3},{8,12},{10,14},{12... | collective-permute-start | bytes 393224 | tf_op jit(solution)/shard_map/ppermute | solution.py:175
  38.9 14.8 %collective-permute-start.12 = (bf16[256,256]{1,0:T(8,128)(2,1)S(1)}, bf16[256,256]{1,0:T(8,128)(2,1)S(1)}, u32[]{:S(2)}, u32[]{:S(2)}) collective-permute-start(bf16[256,256]{1,0:T(8,128)(2,1)S(1)} %get-tuple-element.34), channel_id=1, source_target_pairs={{0,6},{2,4},{4,2},{6,0},{1,7},{3,5},{5,3},{7,1},{8,14},{10,12},{12... | collective-permute-start | bytes 393224 | tf_op jit(solution)/shard_map/ppermute | solution.py:175
  49.3 6.6 %collective-permute-start.14 = (bf16[256,256]{1,0:T(8,128)(2,1)S(1)}, bf16[256,256]{1,0:T(8,128)(2,1)S(1)}, u32[]{:S(2)}, u32[]{:S(2)}) collective-permute-start(bf16[256,256]{1,0:T(8,128)(2,1)S(1)} %get-tuple-element.37), channel_id=1, source_target_pairs={{0,2},{2,0},{4,6},{6,4},{1,3},{3,1},{5,7},{7,5},{8,10},{10,8},{12,... | collective-permute-start | bytes 393224 | tf_op jit(solution)/shard_map/ppermute | solution.py:175
  49.8 12.1 %collective-permute-start.15 = (bf16[256,256]{1,0:T(8,128)(2,1)S(1)}, bf16[256,256]{1,0:T(8,128)(2,1)S(1)}, u32[]{:S(2)}, u32[]{:S(2)}) collective-permute-start(bf16[256,256]{1,0:T(8,128)(2,1)S(1)} %get-tuple-element.38), channel_id=1, source_target_pairs={{0,4},{2,6},{4,0},{6,2},{1,5},{3,7},{5,1},{7,3},{8,12},{10,14},{12... | collective-permute-start | bytes 393224 | tf_op jit(solution)/shard_map/ppermute | solution.py:175
  53.7 8.3 %collective-permute-start.16 = (bf16[256,256]{1,0:T(8,128)(2,1)S(1)}, bf16[256,256]{1,0:T(8,128)(2,1)S(1)}, u32[]{:S(2)}, u32[]{:S(2)}) collective-permute-start(bf16[256,256]{1,0:T(8,128)(2,1)S(1)} %get-tuple-element.39), channel_id=1, source_target_pairs={{0,6},{2,4},{4,2},{6,0},{1,7},{3,5},{5,3},{7,1},{8,14},{10,12},{12... | collective-permute-start | bytes 393224 | tf_op jit(solution)/shard_map/ppermute | solution.py:175
  54.5 8.8 %collective-permute-start.13 = (bf16[128,256]{1,0:T(8,128)(2,1)S(1)}, bf16[128,256]{1,0:T(8,128)(2,1)S(1)}, u32[]{:S(2)}, u32[]{:S(2)}) collective-permute-start(bf16[128,256]{1,0:T(8,128)(2,1)S(1)} %pad_maximum_fusion.3), channel_id=1, source_target_pairs={{0,1},{1,0},{2,3},{3,2},{4,5},{5,4},{6,7},{7,6},{8,9},{9,8},{10,11... | collective-permute-start | bytes 196616 | tf_op jit(solution)/shard_map/ppermute | solution.py:175
  62.0 4.3 %collective-permute-start.17 = (bf16[128,256]{1,0:T(8,128)(2,1)S(1)}, bf16[128,256]{1,0:T(8,128)(2,1)S(1)}, u32[]{:S(2)}, u32[]{:S(2)}) collective-permute-start(bf16[128,256]{1,0:T(8,128)(2,1)S(1)} %pad_maximum_fusion.4), channel_id=1, source_target_pairs={{0,1},{1,0},{2,3},{3,2},{4,5},{5,4},{6,7},{7,6},{8,9},{9,8},{10,11... | collective-permute-start | bytes 196616 | tf_op jit(solution)/shard_map/ppermute | solution.py:175

commit v5 on v4

v5 whole, which is shorter than its diff:
```python
import functools
import math

import jax
import jax.numpy as jnp
from jax import lax
from jax.experimental import pallas as pl
from jax.experimental.pallas import tpu as pltpu
from jax.sharding import PartitionSpec as P

HD = 128
GROUP = 8
PAIR = 2
CHUNKS = 2
EXTRA = 16
STEP = 64
VMEM_LIMIT = 52 * 1024 * 1024
NT = (((1,), (1,)), ((), ()))


def heads_down(ref, first, count):
    return jnp.concatenate(
        [ref[:, (first + i) * HD : (first + i + 1) * HD] for i in range(count)], axis=0
    )


def attend_kernel(n_slots, count, chunk, held, factor, *refs):
    last = chunk + 1 == CHUNKS
    length_ref, q_hbm, do_hbm, kown_hbm, vown_hbm = refs[:5]
    slot_refs, refs = refs[5 : 5 + n_slots], refs[5 + n_slots + last :]
    out_hbm, dq_ref, dkown_ref, dvown_ref = refs[:4]
    term_refs, refs = refs[4 : 4 + n_slots], refs[4 + n_slots :]
    if last:
        total_ref, refs = refs[0], refs[1:]
        totals = [ref[2 * held : 2 * held + 8, :HD].astype(jnp.float32) for ref in slot_refs]
        total_ref[...] = functools.reduce(jnp.add, totals)
    q_ref, do_ref, kown_ref, vown_ref, out_ref = refs[:5]
    s_ref, dp_ref, e_ref, ds_ref, dot_ref = refs[5:10]
    keys_ref, keys_t_ref, values_ref, values_t_ref, in_sem, out_sem = refs[10:]
    first = chunk * count
    rows = q_ref.shape[0]
    own = kown_ref.shape[0]
    n_keys = s_ref.shape[1]
    width = PAIR * rows
    pairs = GROUP // PAIR
    scale = factor * math.log2(math.e)

    def columns(head, size):
        return pl.ds(head * size, size)

    loads = []
    for head in range(count):
        loads.append(
            [
                pltpu.make_async_copy(
                    hbm.at[:, columns(first + head, size)],
                    ref.at[:, columns(head, size)],
                    in_sem.at[head, i],
                )
                for i, (hbm, ref, size) in enumerate(
                    [
                        (kown_hbm, kown_ref, HD),
                        (q_hbm, q_ref, GROUP * HD),
                        (do_hbm, do_ref, GROUP * HD),
                        (vown_hbm, vown_ref, HD),
                    ]
                )
            ]
        )
        for copy in loads[-1]:
            copy.start()
    stores = []

    live = (lax.broadcasted_iota(jnp.int32, (1, width), 1) % rows) < length_ref[0]

    def assemble(head, own_ref, slot_start, wide_ref, tall_ref):
        here = slice(head * HD, (head + 1) * HD)
        wide_ref[head, :own] = own_ref[:, here]
        for i, ref in enumerate(slot_refs):
            part = slice(own + i * held, own + (i + 1) * held)
            wide_ref[head, part] = ref[slot_start : slot_start + held, here]
        tall_ref[head] = wide_ref[head].T

    def place(head, pair):
        return slice(pair * width, (pair + 1) * width)

    def scores(head, pair):
        if pair == 0:
            loads[head][0].wait()
            loads[head][1].wait()
            assemble(head, kown_ref, 0, keys_ref, keys_t_ref)
        s_ref[pair % 2] = lax.dot_general(
            keys_ref[head],
            heads_down(q_ref, head * GROUP + pair * PAIR, PAIR),
            NT,
            preferred_element_type=jnp.float32,
        )

    def softmax(head, pair):
        here = s_ref.at[pair % 2]
        cols = place(head, pair)
        fold = lambda x: x.reshape(x.shape[0] // 8, 8, width)
        top = jnp.full((8, width), -1e30, jnp.float32)
        for at in range(0, n_keys, STEP):
            x = here[at : at + STEP]
            if at < own:
                key_pos = lax.broadcasted_iota(jnp.int32, x.shape, 0) + at
                row_pos = lax.broadcasted_iota(jnp.int32, x.shape, 1) % rows
                x = jnp.where(key_pos <= row_pos, x, -1e30)
                here[at : at + STEP] = x
            top = jnp.maximum(top, jnp.max(fold(x), axis=0))
        top = jnp.max(top, axis=0, keepdims=True) * scale
        top = jnp.broadcast_to(top, (8, width))
        total = jnp.zeros((8, width), jnp.float32)
        for at in range(0, n_keys, STEP):
            e = jnp.exp2(fold(here[at : at + STEP]) * scale - top)
            total = total + jnp.sum(e, axis=0)
            e_ref[head % 2, at : at + STEP, cols] = e.reshape(-1, width).astype(jnp.bfloat16)
        total = jnp.sum(total, axis=0, keepdims=True)
        inverse = jnp.where(live, 1.0 / total, 0.0)
        if pair == 0:
            loads[head][2].wait()
        do = heads_down(do_ref, head * GROUP + pair * PAIR, PAIR)
        dot_ref[head % 2, :, cols] = (do.T.astype(jnp.float32) * inverse).astype(jnp.bfloat16)
        return inverse

    def attended(head, pair, inverse):
        cols = place(head, pair)
        if pair == 0:
            loads[head][3].wait()
            assemble(head, vown_ref, held, values_ref, values_t_ref)
        grad = dot_ref[head % 2, :, cols]
        dp_ref[pair % 2] = jnp.dot(values_ref[head], grad, preferred_element_type=jnp.float32)
        out = jnp.dot(
            values_t_ref[head], e_ref[head % 2, :, cols], preferred_element_type=jnp.float32
        )
        out = out * inverse
        turned = out.astype(jnp.bfloat16).T
        for i in range(PAIR):
            at = head * GROUP + pair * PAIR + i
            out_ref[:, at * HD : (at + 1) * HD] = turned[i * rows : (i + 1) * rows]
        return jnp.sum(out * grad.astype(jnp.float32), axis=0, keepdims=True)

    def score_grads(head, pair, centre):
        cols = place(head, pair)
        here = dp_ref.at[pair % 2]
        centre = jnp.broadcast_to(centre, (STEP, width))
        for at in range(0, n_keys, STEP):
            e = e_ref[head % 2, at : at + STEP, cols].astype(jnp.float32)
            grad = e * (here[at : at + STEP] - centre)
            ds_ref[head % 2, at : at + STEP, cols] = grad.astype(jnp.bfloat16)

    def query_grads(head, pair):
        cols = place(head, pair)
        dq = jnp.dot(
            keys_t_ref[head], ds_ref[head % 2, :, cols], preferred_element_type=jnp.float32
        )
        turned = (dq * factor).astype(jnp.bfloat16).T
        for i in range(PAIR):
            at = head * GROUP + pair * PAIR + i
            dq_ref[:, at * HD : (at + 1) * HD] = turned[i * rows : (i + 1) * rows]

    def key_grads(head):
        copy = pltpu.make_async_copy(
            out_ref.at[:, columns(head, GROUP * HD)],
            out_hbm.at[:, columns(first + head, GROUP * HD)],
            out_sem.at[head],
        )
        copy.start()
        stores.append(copy)
        here = slice(head * HD, (head + 1) * HD)
        dv = lax.dot_general(
            e_ref[head % 2], dot_ref[head % 2], NT, preferred_element_type=jnp.float32
        ).astype(jnp.bfloat16)
        dvown_ref[:, here] = dv[:own]
        for i, ref in enumerate(term_refs):
            ref[held:, here] = dv[own + i * held : own + (i + 1) * held]
        dk = jnp.dot(
            ds_ref[head % 2],
            heads_down(q_ref, head * GROUP, GROUP),
            preferred_element_type=jnp.float32,
        )
        dk = (dk * factor).astype(jnp.bfloat16)
        dkown_ref[:, here] = dk[:own]
        for i, ref in enumerate(term_refs):
            ref[:held, here] = dk[own + i * held : own + (i + 1) * held]

    steps = [(head, pair) for head in range(count) for pair in range(pairs)]
    scores(*steps[0])
    inverse = softmax(*steps[0])
    for now, then in zip(steps, steps[1:] + [None]):
        if then:
            scores(*then)
        centre = attended(*now, inverse)
        if then:
            inverse = softmax(*then)
        score_grads(*now, centre)
        query_grads(*now)
        if now[1] + 1 == pairs:
            key_grads(now[0])
    for copy in stores:
        copy.wait()


def scale_kernel(slots_all, total_ref, *refs):
    sources, refs = refs[: 3 * CHUNKS], refs[3 * CHUNKS :]
    outs, held, sem = refs[:3], refs[3:6], refs[6]
    weight = slots_all / total_ref[:1, :1]
    copies = []
    for chunk in range(CHUNKS):
        for i in range(3):
            source = sources[chunk * 3 + i]
            cols = pl.ds(chunk * source.shape[1], source.shape[1])
            scaled = source[...].astype(jnp.float32) * weight
            held[i][:, cols] = scaled.astype(jnp.bfloat16)
            copy = pltpu.make_async_copy(held[i].at[:, cols], outs[i].at[:, cols], sem.at[chunk, i])
            copy.start()
            copies.append(copy)
    for copy in copies:
        copy.wait()


def swap(x, axis, by):
    return lax.ppermute(x, axis, [(i, i ^ by) for i in range(lax.axis_size(axis))])


def sum_over(x, axis):
    by = 1
    while by < lax.axis_size(axis):
        x = x + swap(x, axis, by)
        by *= 2
    return x


def line_gather(block):
    return [block] + [swap(block, "response", m) for m in range(1, lax.axis_size("response"))]


def line_reduce(slots):
    terms = [slots[0]] + [swap(slots[m], "response", m) for m in range(1, len(slots))]
    total = functools.reduce(jnp.add, [term.astype(jnp.float32) for term in terms])
    return total


def own_columns(block, chunk, by):
    cols = block.shape[1] // (lax.axis_size("tensor") * CHUNKS)
    rank = lax.axis_index("tensor") ^ by
    return lax.dynamic_slice_in_dim(block, (rank * CHUNKS + chunk) * cols, cols, 1)


def tensor_gather(blocks, chunk):
    parts = lax.axis_size("tensor")
    pieces = []
    for m in range(parts):
        piece = jnp.concatenate([own_columns(block, chunk, m) for block in blocks], axis=0)
        pieces.append(piece if m == 0 else swap(piece, "tensor", m))
    rows = blocks[0].shape[0]
    return jnp.concatenate(
        [piece[i * rows : (i + 1) * rows] for i in range(len(blocks)) for piece in pieces], axis=0
    )


def tensor_spread(total, n_arrays):
    parts = lax.axis_size("tensor")
    rows = total.shape[0] // (n_arrays * parts)
    pieces = []
    for m in range(parts):
        piece = jnp.concatenate(
            [total[(i * parts + m) * rows : (i * parts + m + 1) * rows] for i in range(n_arrays)],
            axis=0,
        )
        pieces.append(piece if m == 0 else swap(piece, "tensor", m))
    return pieces


def whole_columns(chunk_pieces, array):
    parts = lax.axis_size("tensor")
    rank = lax.axis_index("tensor")
    rows = chunk_pieces[0][0].shape[0] // 2
    by_rank = [
        jnp.concatenate([pieces[m][array * rows : (array + 1) * rows] for pieces in chunk_pieces], axis=1)
        for m in range(parts)
    ]
    ordered = []
    for t in range(parts):
        column = by_rank[0]
        for m in range(1, parts):
            column = jnp.where(rank ^ m == t, by_rank[m], column)
        ordered.append(column)
    return jnp.concatenate(ordered, axis=1)


SMEM = pl.BlockSpec(memory_space=pltpu.SMEM)
HBM = pl.BlockSpec(memory_space=pltpu.HBM)
VMEM = pl.BlockSpec(memory_space=pltpu.VMEM)


def like(x):
    return jax.ShapeDtypeStruct(x.shape, x.dtype)


def attend(chunk, held, slots, length, q, do, k, v, carried):
    rows = q.shape[0]
    count = k.shape[1] // (HD * CHUNKS)
    n_slots = len(slots)
    last = chunk + 1 == CHUNKS
    n_keys = rows + n_slots * held
    bf16 = jnp.bfloat16
    unit = 2 * n_keys * GROUP * rows * HD * count
    step_buffer = pltpu.VMEM((2, n_keys, PAIR * rows), jnp.float32)
    head_buffer = pltpu.VMEM((2, n_keys, GROUP * rows), bf16)
    wide = pltpu.VMEM((rows, count * GROUP * HD), bf16)
    own = pltpu.VMEM((rows, count * HD), bf16)
    down = pltpu.VMEM((count, n_keys, HD), bf16)
    across = pltpu.VMEM((count, HD, n_keys), bf16)
    scratch = [wide, wide, own, own, wide, step_buffer, step_buffer, head_buffer, head_buffer]
    scratch += [pltpu.VMEM((2, HD, GROUP * rows), bf16), down, across, down, across]
    scratch += [pltpu.SemaphoreType.DMA((count, 4)), pltpu.SemaphoreType.DMA((count,))]
    part = lambda x: jax.ShapeDtypeStruct((x.shape[0], x.shape[1] // CHUNKS), bf16)
    terms = [jax.ShapeDtypeStruct((2 * held, count * HD), bf16)] * n_slots
    total = [jax.ShapeDtypeStruct((8, HD), jnp.float32)] * last
    return pl.pallas_call(
        functools.partial(attend_kernel, n_slots, count, chunk, held, 1.0 / math.sqrt(HD)),
        in_specs=[SMEM] + [HBM] * 4 + [VMEM] * n_slots + [HBM] * last,
        out_specs=[HBM] + [VMEM] * (3 + n_slots + last),
        out_shape=[like(q), part(q), part(k), part(v)] + terms + total,
        input_output_aliases={5 + n_slots: 0} if last else {},
        scratch_shapes=scratch,
        compiler_params=pltpu.CompilerParams(vmem_limit_bytes=VMEM_LIMIT),
        cost_estimate=pl.CostEstimate(
            flops=24 * unit,
            bytes_accessed=8 * rows * GROUP * HD * count,
            transcendentals=count * n_keys * GROUP * rows,
        ),
        name=f"attend_{chunk}",
    )(length, q, do, k, v, *slots, *carried)


def scale_all(slots_all, total, chunk_grads, shapes):
    flat = [grad for grads in chunk_grads for grad in grads]
    return pl.pallas_call(
        functools.partial(scale_kernel, slots_all),
        in_specs=[VMEM] * (1 + len(flat)),
        out_specs=[HBM] * len(shapes),
        out_shape=shapes,
        scratch_shapes=[pltpu.VMEM(x.shape, x.dtype) for x in shapes]
        + [pltpu.SemaphoreType.DMA((CHUNKS, len(shapes)))],
        cost_estimate=pl.CostEstimate(
            flops=sum(x.size for x in shapes),
            bytes_accessed=sum(4 * x.size for x in shapes),
            transcendentals=0,
        ),
        name="scale",
    )(total, *flat)


def body(queries, keys, values, prefix_keys, prefix_values, lengths, out_grad):
    q, k, v, do = queries[0], keys[0], values[0], out_grad[0]
    length = lengths[0]
    prefix = (prefix_keys[0], prefix_values[0])
    slots_all = q.shape[0] * lax.axis_size("prompt") * lax.axis_size("response")
    first, second = [tensor_gather(prefix, chunk) for chunk in range(CHUNKS)]
    held = first.shape[0] // 2
    length_rows = jnp.full((EXTRA, second.shape[1]), length[0].astype(second.dtype))
    slots = line_gather(first)
    next_slots = line_gather(jnp.concatenate([second, length_rows], axis=0))
    results = attend(0, held, slots, length, q, do, k, v, [])
    next_results = attend(1, held, next_slots, length, q, do, k, v, results[:1])
    sums = [line_reduce(results[4:]), line_reduce(next_results[4:-1])]
    total = sum_over(next_results[-1] + 0 * sums[0][:8, :HD], "prompt")
    weight = slots_all / total[0, 0]
    scaled = scale_all(
        slots_all, total, [results[1:4], next_results[1:4]], [like(q), like(k), like(v)]
    )
    pieces = [tensor_spread(terms.astype(jnp.bfloat16), len(prefix)) for terms in sums]
    grads = [whole_columns(pieces, array) for array in range(len(prefix))]
    grads = [(grad.astype(jnp.float32) * weight).astype(jnp.bfloat16) for grad in grads]
    return tuple(x[None] for x in (next_results[0], *scaled, *grads))


def solution(mesh):
    in_specs = (
        P("prompt", "response", "tensor"),
        P("prompt", "response", "tensor"),
        P("prompt", "response", "tensor"),
        P("prompt", ("response", "tensor"), None),
        P("prompt", ("response", "tensor"), None),
        P("prompt", "response"),
        P("prompt", "response", "tensor"),
    )
    out_specs = (
        P("prompt", "response", "tensor"),
        P("prompt", "response", "tensor"),
        P("prompt", "response", "tensor"),
        P("prompt", "response", "tensor"),
        P("prompt", ("response", "tensor"), None),
        P("prompt", ("response", "tensor"), None),
    )
    return jax.shard_map(body, mesh=mesh, in_specs=in_specs, out_specs=out_specs, check_vma=False)
```

time: 68.2 us -> 68.4 us (level)
  starting transfers between devices: 28.3 us -> 31.7 us
  waiting for transfers between devices: 10.6 us -> 8.37 us
  local copies, waits for them, and re-layouts: 3.71 us -> 5.04 us
  between operations: 3.4 us -> 2.26 us
    ppermute x18, starting transfers between devices: 28.3 us -> 31.7 us  [swap(): lax.ppermute(x, axis, [(i, i ^ by) for i in range(lax.axis_size(axis))])]
    ppermute x18, waiting for transfers between devices: 10.6 us -> 8.37 us  [swap(): lax.ppermute(x, axis, [(i, i ^ by) for i in range(lax.axis_size(axis))])]
    unnamed x8 -> x22, local copies, waits for them, and re-layouts: 1.54 us -> 3.61 us
    broadcast_in_dim x2 -> x0, other arithmetic: 1.33 us -> none  [body(): return tuple((x[None] for x in (*outs, *grads)))]
    convert_element_type x3 -> x4, other arithmetic: 0.88 us -> 1.51 us  [the longest x2 1.37 us: body(): (grad.astype(jnp.float32) * weight).astype(jnp.bfloat16)]
    pallas_call x2 -> x3, Pallas kernels: 19.4 us -> 19.1 us  [the longest x2 16.5 us: attend(): pl.pallas_call(functools.partial(attend_kernel, n_slots, count, chunk, he...]
  transfers between devices with their start and end apart: 18 -> 18, of which waited for: 4 -> 3; matrix products, arithmetic and copies ran while one was open for 6% -> 3% of each run, Pallas kernels for 29% -> 28%
where the time goes in v5:
time: 68.4 us; the launch traced here: 68 us
  starting transfers between devices  31.7 us (46%)
  Pallas kernels  19.1 us (28%)
  waiting for transfers between devices  8.37 us (12%)
  local copies, waits for them, and re-layouts  5.04 us (7%)
  between operations  2.26 us (3%)
  other arithmetic  1.62 us (2%)
    ppermute x18, starting transfers between devices, swap(): lax.ppermute(x, axis, [(i, i ^ by) for i in range(lax.axis_size(axis))])  31.7 us
    pallas_call x2, Pallas kernels, attend(): pl.pallas_call(functools.partial(attend_kernel, n_slots, count, chunk, he...  16.5 us
    ppermute x18, waiting for transfers between devices, swap(): lax.ppermute(x, axis, [(i, i ^ by) for i in range(lax.axis_size(axis))])  8.37 us
    unnamed x22, local copies, waits for them, and re-layouts  3.61 us
    pallas_call x1, Pallas kernels, scale_all(): pl.pallas_call(functools.partial(scale_kernel, slots_all), in_specs=[VMEM...  2.54 us
    convert_element_type x2, other arithmetic, body(): (grad.astype(jnp.float32) * weight).astype(jnp.bfloat16)  1.37 us
  transfers between devices with their start and end apart: 18, of which 3 were waited for; matrix products, arithmetic and copies ran while one was open for 3% of the time, Pallas kernels for 28%

profile of v5, /device:TPU:0, one launch (start us, length us, event | category | flops | bytes accessed | tf_op | source)
XLA Modules:
  0.0 68.0 jit_solution(16634033524077064936)
XLA Ops:
  0.7 0.9 %dynamic-slice_bitcast_fusion = (bf16[64,256]{1,0:T(8,128)(2,1)S(1)}, bf16[64,256]{1,0:T(8,128)(2,1)S(1)}, bf16[64,256]{1,0:T(8,128)(2,1)S(1)}, bf16[64,256]{1,0...) fusion(bf16[1,64,1024]{2,1,0:T(8,128)(2,1)} %param.11, s32[]{:T(128)S(6)} %select_n.64, ...), kind=kLoop, calls=%fused_computation.21 | loop fusion | bytes 393228 | tf_op jit(solution)/shard_map/dynamic_slice | solution.py:248
  1.5 3.0 %collective-permute-start.4 = (bf16[128,256]{1,0:T(8,128)(2,1)S(1)}, bf16[128,256]{1,0:T(8,128)(2,1)S(1)}, u32[]{:S(2)}, u32[]{:S(2)}) collective-permute-start(bf16[128,256]{1,0:T(8,128)(2,1)S(1)} %pad_maximum_fusion.2), channel_id=1, source_target_pairs={{0,1},{1,0},{2,3},{3,2},{4,5},{5,4},{6,7},{7,6},{8,9},{9,8},{10,11... | collective-permute-start | bytes 196616 | tf_op jit(solution)/shard_map/ppermute | solution.py:224
  4.6 0.1 collective-permute-start
  5.3 0.8 %bitcast_dynamic-update-slice_fusion.1 = bf16[272,256]{1,0:T(8,128)(2,1)S(1)} fusion(bf16[1,64,1024]{2,1,0:T(8,128)(2,1)} %param.10, s32[]{:T(128)S(6)} %select_n.62), kind=kLoop, calls=%fused_computation.20 | loop fusion | bytes 65540
  6.1 0.9 %collective-permute-done.4 = bf16[128,256]{1,0:T(8,128)(2,1)S(1)} collective-permute-done((bf16[128,256]{1,0:T(8,128)(2,1)S(1)}, bf16[128,256]{1,0:T(8,128)(2,1)S(1)}, u32[]{:S(2)}, u32[]{:S(2)}) %collective-permute-start.4) | collective-permute-done | bytes 65568 | tf_op jit(solution)/shard_map/ppermute | solution.py:224
  7.0 0.0 copy-start.7
  7.0 0.0 copy-start.6
  7.0 2.6 %collective-permute-start.5 = (bf16[256,256]{1,0:T(8,128)(2,1)S(1)}, bf16[256,256]{1,0:T(8,128)(2,1)S(1)}, u32[]{:S(2)}, u32[]{:S(2)}) collective-permute-start(bf16[256,256]{1,0:T(8,128)(2,1)S(1)} %pad_maximum_fusion.refs_5_), channel_id=1, source_target_pairs={{0,2},{2,0},{4,6},{6,4},{1,3},{3,1},{5,7},{7,5},{8,10},{10,8},{12,... | collective-permute-start | bytes 393224 | tf_op jit(solution)/shard_map/ppermute | solution.py:224
  9.6 2.6 %collective-permute-start.6 = (bf16[256,256]{1,0:T(8,128)(2,1)S(1)}, bf16[256,256]{1,0:T(8,128)(2,1)S(1)}, u32[]{:S(2)}, u32[]{:S(2)}) collective-permute-start(bf16[256,256]{1,0:T(8,128)(2,1)S(1)} %pad_maximum_fusion.refs_5_), channel_id=1, source_target_pairs={{0,4},{2,6},{4,0},{6,2},{1,5},{3,7},{5,1},{7,3},{8,12},{10,14},{12... | collective-permute-start | bytes 393224 | tf_op jit(solution)/shard_map/ppermute | solution.py:224
  12.2 0.0 collective-permute-start.7
  12.2 0.0 collective-permute-done
  12.2 0.8 %bitcast_dynamic-update-slice_fusion = bf16[272,256]{1,0:T(8,128)(2,1)S(1)} fusion(bf16[272,256]{1,0:T(8,128)(2,1)S(1)} %slice_dynamic-update-slice_fusion.1, bf16[1,64,1024]{2,1,0:T(8,128)(2,1)} %param.11, s32[]{:T(128)S(6)} %select_n.62), kind=kLoop, calls=%fused_computation.19 | loop fusion | bytes 65540
  13.0 1.0 %collective-permute-start.1 = (bf16[272,256]{1,0:T(8,128)(2,1)S(1)}, bf16[272,256]{1,0:T(8,128)(2,1)S(1)}, u32[]{:S(2)}, u32[]{:S(2)}) collective-permute-start(bf16[272,256]{1,0:T(8,128)(2,1)S(1)} %constant_dynamic-update-slice_fusion.refs_5_), channel_id=1, source_target_pairs={{0,2},{2,0},{4,6},{6,4},{1,3},{3,1},{5,7},{7,5},{8,10},{10,8},{12,... | collective-permute-start | bytes 417800 | tf_op jit(solution)/shard_map/ppermute | solution.py:224
  13.9 3.5 %collective-permute-start.2 = (bf16[272,256]{1,0:T(8,128)(2,1)S(1)}, bf16[272,256]{1,0:T(8,128)(2,1)S(1)}, u32[]{:S(2)}, u32[]{:S(2)}) collective-permute-start(bf16[272,256]{1,0:T(8,128)(2,1)S(1)} %constant_dynamic-update-slice_fusion.refs_5_), channel_id=1, source_target_pairs={{0,4},{2,6},{4,0},{6,2},{1,5},{3,7},{5,1},{7,3},{8,12},{10,14},{12... | collective-permute-start | bytes 417800 | tf_op jit(solution)/shard_map/ppermute | solution.py:224
  17.4 0.0 collective-permute-done.5.refs_6_
  17.4 0.4 collective-permute-start.3
  17.8 4.7 %collective-permute-done.6.refs_7_ = bf16[256,256]{1,0:T(8,128)(2,1)S(1)} collective-permute-done((bf16[256,256]{1,0:T(8,128)(2,1)S(1)}, bf16[256,256]{1,0:T(8,128)(2,1)S(1)}, u32[]{:S(2)}, u32[]{:S(2)}) %collective-permute-start.6) | collective-permute-done | bytes 131104 | tf_op jit(solution)/shard_map/ppermute | solution.py:224
  22.4 0.0 collective-permute-done.7.refs_8_
  22.4 0.0 copy-done.7
  22.4 0.0 copy-done.6
  22.4 8.3 %attend_0.1 = (bf16[128,4096]{1,0:T(8,128)(2,1)}, bf16[128,2048]{1,0:T(8,128)(2,1)S(1)}, bf16[128,256]{1,0:T(8,128)(2,1)S(1)}, bf16[128,256]{1,0:T(8,128)(2,1)S(...) custom-call(s32[1]{0:T(128)} %bitcast.35.refs_0_, ...), custom_call_target="tpu_custom_call" | custom-call | flops 8053063680 | bytes 2097152 | tf_op jit(solution)/shard_map/attend_0/pallas_call | solution.py:322
  30.7 0.0 copy-start
  30.7 0.8 %copy-done = bf16[128,2048]{1,0:T(8,128)(2,1)} copy-done((bf16[128,2048]{1,0:T(8,128)(2,1)}, bf16[128,2048]{1,0:T(8,128)(2,1)S(1)}, u32[]{:S(2)}) %copy-start) | copy-done | bytes 524312
  31.5 0.0 copy-start.2
  31.5 0.6 copy-done.2
  32.1 0.0 copy-start.3
  32.1 0.6 copy-done.3
  32.8 2.5 %collective-permute-start.10 = (bf16[256,256]{1,0:T(8,128)(2,1)S(1)}, bf16[256,256]{1,0:T(8,128)(2,1)S(1)}, u32[]{:S(2)}, u32[]{:S(2)}) collective-permute-start(bf16[256,256]{1,0:T(8,128)(2,1)S(1)} %get-tuple-element.32), channel_id=1, source_target_pairs={{0,6},{2,4},{4,2},{6,0},{1,7},{3,5},{5,3},{7,1},{8,14},{10,12},{12... | collective-permute-start | bytes 393224 | tf_op jit(solution)/shard_map/ppermute | solution.py:224
  35.2 7.2 %collective-permute-start.8 = (bf16[256,256]{1,0:T(8,128)(2,1)S(1)}, bf16[256,256]{1,0:T(8,128)(2,1)S(1)}, u32[]{:S(2)}, u32[]{:S(2)}) collective-permute-start(bf16[256,256]{1,0:T(8,128)(2,1)S(1)} %get-tuple-element.30), channel_id=1, source_target_pairs={{0,2},{2,0},{4,6},{6,4},{1,3},{3,1},{5,7},{7,5},{8,10},{10,8},{12,... | collective-permute-start | bytes 393224 | tf_op jit(solution)/shard_map/ppermute | solution.py:224
  42.5 0.0 collective-permute-done.1.refs_6_
  42.5 0.0 collective-permute-start.9
  42.5 0.0 collective-permute-done.2.refs_7_
  42.5 0.0 collective-permute-done.3.refs_8_
  42.5 8.3 %attend_1.1 = (bf16[128,4096]{1,0:T(8,128)(2,1)}, bf16[128,2048]{1,0:T(8,128)(2,1)S(1)}, bf16[128,256]{1,0:T(8,128)(2,1)S(1)}, bf16[128,256]{1,0:T(8,128)(2,1)S(...) custom-call(s32[1]{0:T(128)} %bitcast.36.refs_0_, ...), custom_call_target="tpu_custom_call", output_to_operand_aliasing={{0}: (9, {})} | custom-call | flops 8053063680 | bytes 2097152 | tf_op jit(solution)/shard_map/attend_1/pallas_call | solution.py:322
  50.8 0.0 copy-start.4
  50.8 0.0 copy-start.5
  50.8 0.0 copy-start.1
  50.8 1.9 %collective-permute-start.14 = (bf16[256,256]{1,0:T(8,128)(2,1)S(1)}, bf16[256,256]{1,0:T(8,128)(2,1)S(1)}, u32[]{:S(2)}, u32[]{:S(2)}) collective-permute-start(bf16[256,256]{1,0:T(8,128)(2,1)S(1)} %get-tuple-element.43), channel_id=1, source_target_pairs={{0,2},{2,0},{4,6},{6,4},{1,3},{3,1},{5,7},{7,5},{8,10},{10,8},{12,... | collective-permute-start | bytes 393224 | tf_op jit(solution)/shard_map/ppermute | solution.py:224
  52.7 1.2 %collective-permute-start.15 = (bf16[256,256]{1,0:T(8,128)(2,1)S(1)}, bf16[256,256]{1,0:T(8,128)(2,1)S(1)}, u32[]{:S(2)}, u32[]{:S(2)}) collective-permute-start(bf16[256,256]{1,0:T(8,128)(2,1)S(1)} %get-tuple-element.44), channel_id=1, source_target_pairs={{0,4},{2,6},{4,0},{6,2},{1,5},{3,7},{5,1},{7,3},{8,12},{10,14},{12... | collective-permute-start | bytes 393224 | tf_op jit(solution)/shard_map/ppermute | solution.py:224
  53.9 0.0 collective-permute-done.10
  53.9 1.4 %collective-permute-start.16 = (bf16[256,256]{1,0:T(8,128)(2,1)S(1)}, bf16[256,256]{1,0:T(8,128)(2,1)S(1)}, u32[]{:S(2)}, u32[]{:S(2)}) collective-permute-start(bf16[256,256]{1,0:T(8,128)(2,1)S(1)} %get-tuple-element.45), channel_id=1, source_target_pairs={{0,6},{2,4},{4,2},{6,0},{1,7},{3,5},{5,3},{7,1},{8,14},{10,12},{12... | collective-permute-start | bytes 393224 | tf_op jit(solution)/shard_map/ppermute | solution.py:224
  55.3 0.0 collective-permute-done.8
  55.3 0.0 collective-permute-done.9
  55.3 0.1 fusion.1
  55.3 0.0 copy-done.4
  55.3 0.0 copy-done.5
  55.4 0.0 copy-done.1
  55.4 0.1 collective-permute-start.11
  55.5 1.6 %collective-permute-start.13 = (bf16[128,256]{1,0:T(8,128)(2,1)S(1)}, bf16[128,256]{1,0:T(8,128)(2,1)S(1)}, u32[]{:S(2)}, u32[]{:S(2)}) collective-permute-start(bf16[128,256]{1,0:T(8,128)(2,1)S(1)} %pad_maximum_fusion.3), channel_id=1, source_target_pairs={{0,1},{1,0},{2,3},{3,2},{4,5},{5,4},{6,7},{7,6},{8,9},{9,8},{10,11... | collective-permute-start | bytes 196616 | tf_op jit(solution)/shard_map/ppermute | solution.py:224
  57.0 0.0 collective-permute-done.11
  57.0 1.5 %collective-permute-start.12 = (f32[8,128]{1,0:T(8,128)S(1)}, f32[8,128]{1,0:T(8,128)S(1)}, u32[]{:S(2)}, u32[]{:S(2)}) collective-permute-start(f32[8,128]{1,0:T(8,128)S(1)} %add.61), channel_id=1, source_target_pairs={{0,16},{8,24},{16,0},{24,8},{1,17},{9,25},{17,1},{25,9},{2,18},{10... | collective-permute-start | bytes 12296 | tf_op jit(solution)/shard_map/ppermute | solution.py:224
  58.5 0.0 collective-permute-done.14
  58.5 2.8 %collective-permute-done.15 = bf16[256,256]{1,0:T(8,128)(2,1)S(1)} collective-permute-done((bf16[256,256]{1,0:T(8,128)(2,1)S(1)}, bf16[256,256]{1,0:T(8,128)(2,1)S(1)}, u32[]{:S(2)}, u32[]{:S(2)}) %collective-permute-start.15) | collective-permute-done | bytes 131104 | tf_op jit(solution)/shard_map/ppermute | solution.py:224
  61.3 0.0 collective-permute-done.16
  61.3 0.1 add_convert_fusion
  61.5 1.3 %collective-permute-start.17 = (bf16[128,256]{1,0:T(8,128)(2,1)S(1)}, bf16[128,256]{1,0:T(8,128)(2,1)S(1)}, u32[]{:S(2)}, u32[]{:S(2)}) collective-permute-start(bf16[128,256]{1,0:T(8,128)(2,1)S(1)} %pad_maximum_fusion.4), channel_id=1, source_target_pairs={{0,1},{1,0},{2,3},{3,2},{4,5},{5,4},{6,7},{7,6},{8,9},{9,8},{10,11... | collective-permute-start | bytes 196616 | tf_op jit(solution)/shard_map/ppermute | solution.py:224
  62.8 0.0 collective-permute-done.12
  62.8 0.5 slice.67
  64.0 0.0 copy-done.8
  64.0 2.5 %scale.1 = (bf16[128,4096]{1,0:T(8,128)(2,1)}, bf16[128,512]{1,0:T(8,128)(2,1)}, bf16[128,512]{1,0:T(8,128)(2,1)}) custom-call(f32[8,128]{1,0:T(8,128)} %copy-done.8, bf16[128,2048]{1,0:T(8,128)(2,1)} %copy-done, bf16[128,256]{1,0:T(8,128)(2,1)} %copy-done.2, bf16[128,256]{1,0:T(8,128)(2,1)} %copy-done.3, bf16[128,2048]{1,0:T(8,128)(2,1)} %copy-done.1, ...), custom_call_target="tpu_custom_call" | custom-call | flops 655360 | bytes 2621440 | tf_op jit(solution)/shard_map/scale/pallas_call | solution.py:341
  66.5 0.0 collective-permute-done.13
  66.6 0.0 collective-permute-done.17
  66.6 0.7 %multiply_convert_fusion = bf16[1,64,1024]{2,1,0:T(8,128)(2,1)} fusion(bf16[1,64,512]{2,1,0:T(8,128)(2,1)S(1)} %get-tuple-element.49, bf16[1,64,512]{2,1,0:T(8,128)(2,1)S(1)} %get-tuple-element.48, f32[]{:T(128)} %bitcast.20), kind=kLoop, calls=%fused_computation | loop fusion | flops 393216 | bytes 262148 | tf_op jit(solution)/shard_map/convert_element_type | solution.py:377
  67.3 0.7 %multiply_convert_fusion.1 = bf16[1,64,1024]{2,1,0:T(8,128)(2,1)} fusion(bf16[1,64,512]{2,1,0:T(8,128)(2,1)S(1)} %get-tuple-element.59, bf16[1,64,512]{2,1,0:T(8,128)(2,1)S(1)} %get-tuple-element.58, f32[]{:T(128)} %bitcast.20), kind=kLoop, calls=%fused_computation.1 | loop fusion | flops 393216 | bytes 262148 | tf_op jit(solution)/shard_map/convert_element_type | solution.py:377
  (19 shorter events, 0.2 us)
Async XLA Ops:
  1.5 5.4 %collective-permute-start.4 = (bf16[128,256]{1,0:T(8,128)(2,1)S(1)}, bf16[128,256]{1,0:T(8,128)(2,1)S(1)}, u32[]{:S(2)}, u32[]{:S(2)}) collective-permute-start(bf16[128,256]{1,0:T(8,128)(2,1)S(1)} %pad_maximum_fusion.2), channel_id=1, source_target_pairs={{0,1},{1,0},{2,3},{3,2},{4,5},{5,4},{6,7},{7,6},{8,9},{9,8},{10,11... | collective-permute-start | bytes 196616 | tf_op jit(solution)/shard_map/ppermute | solution.py:224
  4.6 7.6 %collective-permute-start = (bf16[128,256]{1,0:T(8,128)(2,1)S(1)}, bf16[128,256]{1,0:T(8,128)(2,1)S(1)}, u32[]{:S(2)}, u32[]{:S(2)}) collective-permute-start(bf16[128,256]{1,0:T(8,128)(2,1)S(1)} %pad_maximum_fusion.1), channel_id=1, source_target_pairs={{0,1},{1,0},{2,3},{3,2},{4,5},{5,4},{6,7},{7,6},{8,9},{9,8},{10,11... | collective-permute-start | bytes 196616 | tf_op jit(solution)/shard_map/ppermute | solution.py:224
  7.0 15.5 %copy-start.7 = (bf16[1,128,512]{2,1,0:T(8,128)(2,1)S(1)}, bf16[1,128,512]{2,1,0:T(8,128)(2,1)}, u32[]{:S(2)}) copy-start(bf16[1,128,512]{2,1,0:T(8,128)(2,1)} %param.9) | copy-start | bytes 393220
  7.0 15.5 %copy-start.6 = (bf16[1,128,512]{2,1,0:T(8,128)(2,1)S(1)}, bf16[1,128,512]{2,1,0:T(8,128)(2,1)}, u32[]{:S(2)}) copy-start(bf16[1,128,512]{2,1,0:T(8,128)(2,1)} %param.8) | copy-start | bytes 393220
  7.0 10.4 %collective-permute-start.5 = (bf16[256,256]{1,0:T(8,128)(2,1)S(1)}, bf16[256,256]{1,0:T(8,128)(2,1)S(1)}, u32[]{:S(2)}, u32[]{:S(2)}) collective-permute-start(bf16[256,256]{1,0:T(8,128)(2,1)S(1)} %pad_maximum_fusion.refs_5_), channel_id=1, source_target_pairs={{0,2},{2,0},{4,6},{6,4},{1,3},{3,1},{5,7},{7,5},{8,10},{10,8},{12,... | collective-permute-start | bytes 393224 | tf_op jit(solution)/shard_map/ppermute | solution.py:224
  9.6 12.8 %collective-permute-start.6 = (bf16[256,256]{1,0:T(8,128)(2,1)S(1)}, bf16[256,256]{1,0:T(8,128)(2,1)S(1)}, u32[]{:S(2)}, u32[]{:S(2)}) collective-permute-start(bf16[256,256]{1,0:T(8,128)(2,1)S(1)} %pad_maximum_fusion.refs_5_), channel_id=1, source_target_pairs={{0,4},{2,6},{4,0},{6,2},{1,5},{3,7},{5,1},{7,3},{8,12},{10,14},{12... | collective-permute-start | bytes 393224 | tf_op jit(solution)/shard_map/ppermute | solution.py:224
  12.2 10.3 %collective-permute-start.7 = (bf16[256,256]{1,0:T(8,128)(2,1)S(1)}, bf16[256,256]{1,0:T(8,128)(2,1)S(1)}, u32[]{:S(2)}, u32[]{:S(2)}) collective-permute-start(bf16[256,256]{1,0:T(8,128)(2,1)S(1)} %pad_maximum_fusion.refs_5_), channel_id=1, source_target_pairs={{0,6},{2,4},{4,2},{6,0},{1,7},{3,5},{5,3},{7,1},{8,14},{10,12},{12... | collective-permute-start | bytes 393224 | tf_op jit(solution)/shard_map/ppermute | solution.py:224
  13.0 29.5 %collective-permute-start.1 = (bf16[272,256]{1,0:T(8,128)(2,1)S(1)}, bf16[272,256]{1,0:T(8,128)(2,1)S(1)}, u32[]{:S(2)}, u32[]{:S(2)}) collective-permute-start(bf16[272,256]{1,0:T(8,128)(2,1)S(1)} %constant_dynamic-update-slice_fusion.refs_5_), channel_id=1, source_target_pairs={{0,2},{2,0},{4,6},{6,4},{1,3},{3,1},{5,7},{7,5},{8,10},{10,8},{12,... | collective-permute-start | bytes 417800 | tf_op jit(solution)/shard_map/ppermute | solution.py:224
  13.9 28.6 %collective-permute-start.2 = (bf16[272,256]{1,0:T(8,128)(2,1)S(1)}, bf16[272,256]{1,0:T(8,128)(2,1)S(1)}, u32[]{:S(2)}, u32[]{:S(2)}) collective-permute-start(bf16[272,256]{1,0:T(8,128)(2,1)S(1)} %constant_dynamic-update-slice_fusion.refs_5_), channel_id=1, source_target_pairs={{0,4},{2,6},{4,0},{6,2},{1,5},{3,7},{5,1},{7,3},{8,12},{10,14},{12... | collective-permute-start | bytes 417800 | tf_op jit(solution)/shard_map/ppermute | solution.py:224
  17.4 25.1 %collective-permute-start.3 = (bf16[272,256]{1,0:T(8,128)(2,1)S(1)}, bf16[272,256]{1,0:T(8,128)(2,1)S(1)}, u32[]{:S(2)}, u32[]{:S(2)}) collective-permute-start(bf16[272,256]{1,0:T(8,128)(2,1)S(1)} %constant_dynamic-update-slice_fusion.refs_5_), channel_id=1, source_target_pairs={{0,6},{2,4},{4,2},{6,0},{1,7},{3,5},{5,3},{7,1},{8,14},{10,12},{12... | collective-permute-start | bytes 417800 | tf_op jit(solution)/shard_map/ppermute | solution.py:224
  30.7 0.8 %copy-start = (bf16[128,2048]{1,0:T(8,128)(2,1)}, bf16[128,2048]{1,0:T(8,128)(2,1)S(1)}, u32[]{:S(2)}) copy-start(bf16[128,2048]{1,0:T(8,128)(2,1)S(1)} %get-tuple-element.33.refs_0_) | copy-start | bytes 1572868
  31.5 0.6 copy-start.2
  32.1 0.6 copy-start.3
  32.8 21.1 %collective-permute-start.10 = (bf16[256,256]{1,0:T(8,128)(2,1)S(1)}, bf16[256,256]{1,0:T(8,128)(2,1)S(1)}, u32[]{:S(2)}, u32[]{:S(2)}) collective-permute-start(bf16[256,256]{1,0:T(8,128)(2,1)S(1)} %get-tuple-element.32), channel_id=1, source_target_pairs={{0,6},{2,4},{4,2},{6,0},{1,7},{3,5},{5,3},{7,1},{8,14},{10,12},{12... | collective-permute-start | bytes 393224 | tf_op jit(solution)/shard_map/ppermute | solution.py:224
  35.2 20.0 %collective-permute-start.8 = (bf16[256,256]{1,0:T(8,128)(2,1)S(1)}, bf16[256,256]{1,0:T(8,128)(2,1)S(1)}, u32[]{:S(2)}, u32[]{:S(2)}) collective-permute-start(bf16[256,256]{1,0:T(8,128)(2,1)S(1)} %get-tuple-element.30), channel_id=1, source_target_pairs={{0,2},{2,0},{4,6},{6,4},{1,3},{3,1},{5,7},{7,5},{8,10},{10,8},{12,... | collective-permute-start | bytes 393224 | tf_op jit(solution)/shard_map/ppermute | solution.py:224
  42.5 12.8 %collective-permute-start.9 = (bf16[256,256]{1,0:T(8,128)(2,1)S(1)}, bf16[256,256]{1,0:T(8,128)(2,1)S(1)}, u32[]{:S(2)}, u32[]{:S(2)}) collective-permute-start(bf16[256,256]{1,0:T(8,128)(2,1)S(1)} %get-tuple-element.31), channel_id=1, source_target_pairs={{0,4},{2,6},{4,0},{6,2},{1,5},{3,7},{5,1},{7,3},{8,12},{10,14},{12... | collective-permute-start | bytes 393224 | tf_op jit(solution)/shard_map/ppermute | solution.py:224
  50.8 4.6 %copy-start.4 = (bf16[128,256]{1,0:T(8,128)(2,1)}, bf16[128,256]{1,0:T(8,128)(2,1)S(1)}, u32[]{:S(2)}) copy-start(bf16[128,256]{1,0:T(8,128)(2,1)S(1)} %get-tuple-element.37.refs_4_) | copy-start | bytes 196612
  50.8 4.6 %copy-start.5 = (bf16[128,256]{1,0:T(8,128)(2,1)}, bf16[128,256]{1,0:T(8,128)(2,1)S(1)}, u32[]{:S(2)}) copy-start(bf16[128,256]{1,0:T(8,128)(2,1)S(1)} %get-tuple-element.38.refs_5_) | copy-start | bytes 196612
  50.8 4.6 %copy-start.1 = (bf16[128,2048]{1,0:T(8,128)(2,1)}, bf16[128,2048]{1,0:T(8,128)(2,1)S(1)}, u32[]{:S(2)}) copy-start(bf16[128,2048]{1,0:T(8,128)(2,1)S(1)} %get-tuple-element.36.refs_3_) | copy-start | bytes 1572868
  50.8 7.7 %collective-permute-start.14 = (bf16[256,256]{1,0:T(8,128)(2,1)S(1)}, bf16[256,256]{1,0:T(8,128)(2,1)S(1)}, u32[]{:S(2)}, u32[]{:S(2)}) collective-permute-start(bf16[256,256]{1,0:T(8,128)(2,1)S(1)} %get-tuple-element.43), channel_id=1, source_target_pairs={{0,2},{2,0},{4,6},{6,4},{1,3},{3,1},{5,7},{7,5},{8,10},{10,8},{12,... | collective-permute-start | bytes 393224 | tf_op jit(solution)/shard_map/ppermute | solution.py:224
  52.7 8.7 %collective-permute-start.15 = (bf16[256,256]{1,0:T(8,128)(2,1)S(1)}, bf16[256,256]{1,0:T(8,128)(2,1)S(1)}, u32[]{:S(2)}, u32[]{:S(2)}) collective-permute-start(bf16[256,256]{1,0:T(8,128)(2,1)S(1)} %get-tuple-element.44), channel_id=1, source_target_pairs={{0,4},{2,6},{4,0},{6,2},{1,5},{3,7},{5,1},{7,3},{8,12},{10,14},{12... | collective-permute-start | bytes 393224 | tf_op jit(solution)/shard_map/ppermute | solution.py:224
  53.9 7.5 %collective-permute-start.16 = (bf16[256,256]{1,0:T(8,128)(2,1)S(1)}, bf16[256,256]{1,0:T(8,128)(2,1)S(1)}, u32[]{:S(2)}, u32[]{:S(2)}) collective-permute-start(bf16[256,256]{1,0:T(8,128)(2,1)S(1)} %get-tuple-element.45), channel_id=1, source_target_pairs={{0,6},{2,4},{4,2},{6,0},{1,7},{3,5},{5,3},{7,1},{8,14},{10,12},{12... | collective-permute-start | bytes 393224 | tf_op jit(solution)/shard_map/ppermute | solution.py:224
  55.4 1.6 %collective-permute-start.11 = (f32[8,128]{1,0:T(8,128)S(1)}, f32[8,128]{1,0:T(8,128)S(1)}, u32[]{:S(2)}, u32[]{:S(2)}) collective-permute-start(f32[8,128]{1,0:T(8,128)S(1)} %fusion), channel_id=1, source_target_pairs={{0,8},{8,0},{16,24},{24,16},{1,9},{9,1},{17,25},{25,17},{2,10},{10... | collective-permute-start | bytes 12296 | tf_op jit(solution)/shard_map/ppermute | solution.py:224
  55.5 11.1 %collective-permute-start.13 = (bf16[128,256]{1,0:T(8,128)(2,1)S(1)}, bf16[128,256]{1,0:T(8,128)(2,1)S(1)}, u32[]{:S(2)}, u32[]{:S(2)}) collective-permute-start(bf16[128,256]{1,0:T(8,128)(2,1)S(1)} %pad_maximum_fusion.3), channel_id=1, source_target_pairs={{0,1},{1,0},{2,3},{3,2},{4,5},{5,4},{6,7},{7,6},{8,9},{9,8},{10,11... | collective-permute-start | bytes 196616 | tf_op jit(solution)/shard_map/ppermute | solution.py:224
  57.0 5.7 %collective-permute-start.12 = (f32[8,128]{1,0:T(8,128)S(1)}, f32[8,128]{1,0:T(8,128)S(1)}, u32[]{:S(2)}, u32[]{:S(2)}) collective-permute-start(f32[8,128]{1,0:T(8,128)S(1)} %add.61), channel_id=1, source_target_pairs={{0,16},{8,24},{16,0},{24,8},{1,17},{9,25},{17,1},{25,9},{2,18},{10... | collective-permute-start | bytes 12296 | tf_op jit(solution)/shard_map/ppermute | solution.py:224
  61.5 5.1 %collective-permute-start.17 = (bf16[128,256]{1,0:T(8,128)(2,1)S(1)}, bf16[128,256]{1,0:T(8,128)(2,1)S(1)}, u32[]{:S(2)}, u32[]{:S(2)}) collective-permute-start(bf16[128,256]{1,0:T(8,128)(2,1)S(1)} %pad_maximum_fusion.4), channel_id=1, source_target_pairs={{0,1},{1,0},{2,3},{3,2},{4,5},{5,4},{6,7},{7,6},{8,9},{9,8},{10,11... | collective-permute-start | bytes 196616 | tf_op jit(solution)/shard_map/ppermute | solution.py:224
  62.8 1.2 %copy-start.8 = (f32[8,128]{1,0:T(8,128)}, f32[8,128]{1,0:T(8,128)S(1)}, u32[]{:S(2)}) copy-start(f32[8,128]{1,0:T(8,128)S(1)} %add.62.total_ref) | copy-start | bytes 12292

commit v6 on v5

--- a/solution.py
+++ b/solution.py
@@ -232,8 +232,13 @@
     return x
 
 
-def line_gather(block):
-    return [block] + [swap(block, "response", m) for m in range(1, lax.axis_size("response"))]
+def line_gather(block, butterfly):
+    size = lax.axis_size("response")
+    if size != 4 or not butterfly:
+        return [block] + [swap(block, "response", m) for m in range(1, size)]
+    far = swap(block, "response", 3)
+    near = swap(block, "response", 1)
+    return [block, near, swap(far, "response", 1), far]
 
 
 def line_reduce(slots):
@@ -361,9 +366,9 @@
     slots_all = q.shape[0] * lax.axis_size("prompt") * lax.axis_size("response")
     first, second = [tensor_gather(prefix, chunk) for chunk in range(CHUNKS)]
     held = first.shape[0] // 2
-    length_rows = jnp.full((EXTRA, second.shape[1]), length[0].astype(second.dtype))
-    slots = line_gather(first)
-    next_slots = line_gather(jnp.concatenate([second, length_rows], axis=0))
+    slots = line_gather(first, True)
+    length_rows = length[0].astype(second.dtype) + 0 * slots[-1][-EXTRA:]
+    next_slots = line_gather(jnp.concatenate([second, length_rows], axis=0), False)
     results = attend(0, held, slots, length, q, do, k, v, [])
     next_results = attend(1, held, next_slots, length, q, do, k, v, results[:1])
     sums = [line_reduce(results[4:]), line_reduce(next_results[4:-1])]

time: 68.4 us -> 63.5 us (0.928)
  starting transfers between devices: 31.7 us -> 26.8 us
    ppermute x18, starting transfers between devices: 31.7 us -> 26.8 us  [swap(): lax.ppermute(x, axis, [(i, i ^ by) for i in range(lax.axis_size(axis))])]
  transfers between devices with their start and end apart: 18 -> 18, of which waited for: 3 -> 4; matrix products, arithmetic and copies ran while one was open for 3% -> 4% of each run, Pallas kernels for 28% -> 30%
where the time goes in v6:
time: 63.5 us; the launch traced here: 63.1 us
  starting transfers between devices  26.8 us (42%)
  Pallas kernels  19.1 us (30%)
  waiting for transfers between devices  8.37 us (13%)
  local copies, waits for them, and re-layouts  5.03 us (8%)
  between operations  2.25 us (4%)
  other arithmetic  1.61 us (3%)
    ppermute x18, starting transfers between devices, swap(): lax.ppermute(x, axis, [(i, i ^ by) for i in range(lax.axis_size(axis))])  26.8 us
    pallas_call x2, Pallas kernels, attend(): pl.pallas_call(functools.partial(attend_kernel, n_slots, count, chunk, he...  16.5 us
    ppermute x18, waiting for transfers between devices, swap(): lax.ppermute(x, axis, [(i, i ^ by) for i in range(lax.axis_size(axis))])  8.37 us
    unnamed x22, local copies, waits for them, and re-layouts  3.61 us
    pallas_call x1, Pallas kernels, scale_all(): pl.pallas_call(functools.partial(scale_kernel, slots_all), in_specs=[VMEM...  2.54 us
    convert_element_type x2, other arithmetic, body(): (grad.astype(jnp.float32) * weight).astype(jnp.bfloat16)  1.37 us
  transfers between devices with their start and end apart: 18, of which 4 were waited for; matrix products, arithmetic and copies ran while one was open for 4% of the time, Pallas kernels for 30%

profile of v6, /device:TPU:0, one launch (start us, length us, event | category | flops | bytes accessed | tf_op | source)
XLA Modules:
  0.0 63.1 jit_solution(10310750367323331417)
XLA Ops:
  0.7 0.9 %dynamic-slice_bitcast_fusion = (bf16[64,256]{1,0:T(8,128)(2,1)S(1)}, bf16[64,256]{1,0:T(8,128)(2,1)S(1)}, bf16[64,256]{1,0:T(8,128)(2,1)S(1)}, bf16[64,256]{1,0...) fusion(bf16[1,64,1024]{2,1,0:T(8,128)(2,1)} %param.11, s32[]{:T(128)S(6)} %select_n.64, ...), kind=kLoop, calls=%fused_computation.21 | loop fusion | bytes 393228 | tf_op jit(solution)/shard_map/dynamic_slice | solution.py:253
  1.5 3.0 %collective-permute-start.1 = (bf16[128,256]{1,0:T(8,128)(2,1)S(1)}, bf16[128,256]{1,0:T(8,128)(2,1)S(1)}, u32[]{:S(2)}, u32[]{:S(2)}) collective-permute-start(bf16[128,256]{1,0:T(8,128)(2,1)S(1)} %pad_maximum_fusion.2), channel_id=1, source_target_pairs={{0,1},{1,0},{2,3},{3,2},{4,5},{5,4},{6,7},{7,6},{8,9},{9,8},{10,11... | collective-permute-start | bytes 196616 | tf_op jit(solution)/shard_map/ppermute | solution.py:224
  4.6 0.1 collective-permute-start
  5.3 0.8 %bitcast_dynamic-update-slice_fusion.1 = bf16[272,256]{1,0:T(8,128)(2,1)S(1)} fusion(bf16[1,64,1024]{2,1,0:T(8,128)(2,1)} %param.10, s32[]{:T(128)S(6)} %select_n.62), kind=kLoop, calls=%fused_computation.20 | loop fusion | bytes 65540
  6.1 0.9 %collective-permute-done.1 = bf16[128,256]{1,0:T(8,128)(2,1)S(1)} collective-permute-done((bf16[128,256]{1,0:T(8,128)(2,1)S(1)}, bf16[128,256]{1,0:T(8,128)(2,1)S(1)}, u32[]{:S(2)}, u32[]{:S(2)}) %collective-permute-start.1) | collective-permute-done | bytes 65568 | tf_op jit(solution)/shard_map/ppermute | solution.py:224
  7.0 0.0 copy-start.7
  7.0 0.0 copy-start.6
  7.0 4.6 %collective-permute-start.2 = (bf16[256,256]{1,0:T(8,128)(2,1)S(1)}, bf16[256,256]{1,0:T(8,128)(2,1)S(1)}, u32[]{:S(2)}, u32[]{:S(2)}) collective-permute-start(bf16[256,256]{1,0:T(8,128)(2,1)S(1)} %pad_maximum_fusion.refs_5_), channel_id=1, source_target_pairs={{0,6},{2,4},{4,2},{6,0},{1,7},{3,5},{5,3},{7,1},{8,14},{10,12},{12... | collective-permute-start | bytes 393224 | tf_op jit(solution)/shard_map/ppermute | solution.py:224
  11.6 0.0 collective-permute-start.6
  11.6 0.0 collective-permute-done
  11.6 0.8 %bitcast_dynamic-update-slice_fusion = bf16[272,256]{1,0:T(8,128)(2,1)S(1)} fusion(bf16[272,256]{1,0:T(8,128)(2,1)S(1)} %slice_dynamic-update-slice_fusion.1, bf16[1,64,1024]{2,1,0:T(8,128)(2,1)} %param.11, s32[]{:T(128)S(6)} %select_n.62), kind=kLoop, calls=%fused_computation.19 | loop fusion | bytes 65540
  12.4 2.8 %collective-permute-done.2.refs_8_ = bf16[256,256]{1,0:T(8,128)(2,1)S(1)} collective-permute-done((bf16[256,256]{1,0:T(8,128)(2,1)S(1)}, bf16[256,256]{1,0:T(8,128)(2,1)S(1)}, u32[]{:S(2)}, u32[]{:S(2)}) %collective-permute-start.2) | collective-permute-done | bytes 131104 | tf_op jit(solution)/shard_map/ppermute | solution.py:224
  15.2 0.8 %collective-permute-start.7 = (bf16[256,256]{1,0:T(8,128)(2,1)S(1)}, bf16[256,256]{1,0:T(8,128)(2,1)S(1)}, u32[]{:S(2)}, u32[]{:S(2)}) collective-permute-start(bf16[256,256]{1,0:T(8,128)(2,1)S(1)} %collective-permute-done.2.refs_8_), channel_id=1, source_target_pairs={{0,2},{2,0},{4,6},{6,4},{1,3},{3,1},{5,7},{7,5},{8,10},{10,8},{12,... | collective-permute-start | bytes 393224 | tf_op jit(solution)/shard_map/ppermute | solution.py:224
  16.0 1.2 %collective-permute-start.3 = (bf16[272,256]{1,0:T(8,128)(2,1)S(1)}, bf16[272,256]{1,0:T(8,128)(2,1)S(1)}, u32[]{:S(2)}, u32[]{:S(2)}) collective-permute-start(bf16[272,256]{1,0:T(8,128)(2,1)S(1)} %constant_dynamic-update-slice_fusion.refs_5_), channel_id=1, source_target_pairs={{0,2},{2,0},{4,6},{6,4},{1,3},{3,1},{5,7},{7,5},{8,10},{10,8},{12,... | collective-permute-start | bytes 417800 | tf_op jit(solution)/shard_map/ppermute | solution.py:224
  17.2 2.9 %collective-permute-start.4 = (bf16[272,256]{1,0:T(8,128)(2,1)S(1)}, bf16[272,256]{1,0:T(8,128)(2,1)S(1)}, u32[]{:S(2)}, u32[]{:S(2)}) collective-permute-start(bf16[272,256]{1,0:T(8,128)(2,1)S(1)} %constant_dynamic-update-slice_fusion.refs_5_), channel_id=1, source_target_pairs={{0,4},{2,6},{4,0},{6,2},{1,5},{3,7},{5,1},{7,3},{8,12},{10,14},{12... | collective-permute-start | bytes 417800 | tf_op jit(solution)/shard_map/ppermute | solution.py:224
  20.1 1.4 %collective-permute-start.5 = (bf16[272,256]{1,0:T(8,128)(2,1)S(1)}, bf16[272,256]{1,0:T(8,128)(2,1)S(1)}, u32[]{:S(2)}, u32[]{:S(2)}) collective-permute-start(bf16[272,256]{1,0:T(8,128)(2,1)S(1)} %constant_dynamic-update-slice_fusion.refs_5_), channel_id=1, source_target_pairs={{0,6},{2,4},{4,2},{6,0},{1,7},{3,5},{5,3},{7,1},{8,14},{10,12},{12... | collective-permute-start | bytes 417800 | tf_op jit(solution)/shard_map/ppermute | solution.py:224
  21.5 0.0 collective-permute-done.6.refs_6_
  21.5 3.1 %collective-permute-done.7.refs_7_ = bf16[256,256]{1,0:T(8,128)(2,1)S(1)} collective-permute-done((bf16[256,256]{1,0:T(8,128)(2,1)S(1)}, bf16[256,256]{1,0:T(8,128)(2,1)S(1)}, u32[]{:S(2)}, u32[]{:S(2)}) %collective-permute-start.7) | collective-permute-done | bytes 131104 | tf_op jit(solution)/shard_map/ppermute | solution.py:224
  24.6 0.0 copy-done.7
  24.6 0.0 copy-done.6
  24.6 8.2 %attend_0.1 = (bf16[128,4096]{1,0:T(8,128)(2,1)}, bf16[128,2048]{1,0:T(8,128)(2,1)S(1)}, bf16[128,256]{1,0:T(8,128)(2,1)S(1)}, bf16[128,256]{1,0:T(8,128)(2,1)S(...) custom-call(s32[1]{0:T(128)} %bitcast.35.refs_0_, ...), custom_call_target="tpu_custom_call" | custom-call | flops 8053063680 | bytes 2097152 | tf_op jit(solution)/shard_map/attend_0/pallas_call | solution.py:327
  32.9 0.0 copy-start
  32.9 0.8 %copy-done = bf16[128,2048]{1,0:T(8,128)(2,1)} copy-done((bf16[128,2048]{1,0:T(8,128)(2,1)}, bf16[128,2048]{1,0:T(8,128)(2,1)S(1)}, u32[]{:S(2)}) %copy-start) | copy-done | bytes 524312
  33.7 0.6 copy-done.2
  34.3 0.0 copy-start.3
  34.3 0.6 copy-done.3
  35.0 0.0 collective-permute-start.10
  35.0 0.1 collective-permute-start.8
  35.1 0.0 collective-permute-done.3.refs_6_
  35.1 4.3 %collective-permute-start.9 = (bf16[256,256]{1,0:T(8,128)(2,1)S(1)}, bf16[256,256]{1,0:T(8,128)(2,1)S(1)}, u32[]{:S(2)}, u32[]{:S(2)}) collective-permute-start(bf16[256,256]{1,0:T(8,128)(2,1)S(1)} %get-tuple-element.31), channel_id=1, source_target_pairs={{0,4},{2,6},{4,0},{6,2},{1,5},{3,7},{5,1},{7,3},{8,12},{10,14},{12... | collective-permute-start | bytes 393224 | tf_op jit(solution)/shard_map/ppermute | solution.py:224
  39.4 0.0 collective-permute-done.4.refs_7_
  39.4 0.0 collective-permute-done.5.refs_8_
  39.4 8.3 %attend_1.1 = (bf16[128,4096]{1,0:T(8,128)(2,1)}, bf16[128,2048]{1,0:T(8,128)(2,1)S(1)}, bf16[128,256]{1,0:T(8,128)(2,1)S(1)}, bf16[128,256]{1,0:T(8,128)(2,1)S(...) custom-call(s32[1]{0:T(128)} %bitcast.36.refs_0_, ...), custom_call_target="tpu_custom_call", output_to_operand_aliasing={{0}: (9, {})} | custom-call | flops 8053063680 | bytes 2097152 | tf_op jit(solution)/shard_map/attend_1/pallas_call | solution.py:327
  47.6 0.0 copy-start.4
  47.6 0.0 copy-start.5
  47.7 0.0 copy-start.1
  47.7 0.1 collective-permute-start.14
  47.7 0.5 collective-permute-start.15
  48.3 0.0 collective-permute-done.10
  48.3 3.8 %collective-permute-start.16 = (bf16[256,256]{1,0:T(8,128)(2,1)S(1)}, bf16[256,256]{1,0:T(8,128)(2,1)S(1)}, u32[]{:S(2)}, u32[]{:S(2)}) collective-permute-start(bf16[256,256]{1,0:T(8,128)(2,1)S(1)} %get-tuple-element.45), channel_id=1, source_target_pairs={{0,6},{2,4},{4,2},{6,0},{1,7},{3,5},{5,3},{7,1},{8,14},{10,12},{12... | collective-permute-start | bytes 393224 | tf_op jit(solution)/shard_map/ppermute | solution.py:224
  52.1 0.0 collective-permute-done.8
  52.1 0.0 collective-permute-done.9
  52.1 0.1 fusion.2
  52.2 0.0 copy-done.4
  52.2 0.0 copy-done.5
  52.2 0.0 copy-done.1
  52.3 0.1 collective-permute-start.11
  52.4 1.2 %collective-permute-start.13 = (bf16[128,256]{1,0:T(8,128)(2,1)S(1)}, bf16[128,256]{1,0:T(8,128)(2,1)S(1)}, u32[]{:S(2)}, u32[]{:S(2)}) collective-permute-start(bf16[128,256]{1,0:T(8,128)(2,1)S(1)} %pad_maximum_fusion.3), channel_id=1, source_target_pairs={{0,1},{1,0},{2,3},{3,2},{4,5},{5,4},{6,7},{7,6},{8,9},{9,8},{10,11... | collective-permute-start | bytes 196616 | tf_op jit(solution)/shard_map/ppermute | solution.py:224
  53.5 0.0 collective-permute-done.11
  53.5 1.5 %collective-permute-start.12 = (f32[8,128]{1,0:T(8,128)S(1)}, f32[8,128]{1,0:T(8,128)S(1)}, u32[]{:S(2)}, u32[]{:S(2)}) collective-permute-start(f32[8,128]{1,0:T(8,128)S(1)} %add.69), channel_id=1, source_target_pairs={{0,16},{8,24},{16,0},{24,8},{1,17},{9,25},{17,1},{25,9},{2,18},{10... | collective-permute-start | bytes 12296 | tf_op jit(solution)/shard_map/ppermute | solution.py:224
  55.0 0.0 collective-permute-done.14
  55.0 0.0 collective-permute-done.15
  55.0 1.5 %collective-permute-done.16 = bf16[256,256]{1,0:T(8,128)(2,1)S(1)} collective-permute-done((bf16[256,256]{1,0:T(8,128)(2,1)S(1)}, bf16[256,256]{1,0:T(8,128)(2,1)S(1)}, u32[]{:S(2)}, u32[]{:S(2)}) %collective-permute-start.16) | collective-permute-done | bytes 131104 | tf_op jit(solution)/shard_map/ppermute | solution.py:224
  56.6 0.1 add_convert_fusion
  56.7 1.2 %collective-permute-start.17 = (bf16[128,256]{1,0:T(8,128)(2,1)S(1)}, bf16[128,256]{1,0:T(8,128)(2,1)S(1)}, u32[]{:S(2)}, u32[]{:S(2)}) collective-permute-start(bf16[128,256]{1,0:T(8,128)(2,1)S(1)} %pad_maximum_fusion.4), channel_id=1, source_target_pairs={{0,1},{1,0},{2,3},{3,2},{4,5},{5,4},{6,7},{7,6},{8,9},{9,8},{10,11... | collective-permute-start | bytes 196616 | tf_op jit(solution)/shard_map/ppermute | solution.py:224
  57.8 0.0 collective-permute-done.12
  57.8 0.0 copy-start.8
  57.8 0.5 slice.71
  59.0 0.0 copy-done.8
  59.1 2.5 %scale.1 = (bf16[128,4096]{1,0:T(8,128)(2,1)}, bf16[128,512]{1,0:T(8,128)(2,1)}, bf16[128,512]{1,0:T(8,128)(2,1)}) custom-call(f32[8,128]{1,0:T(8,128)} %copy-done.8, bf16[128,2048]{1,0:T(8,128)(2,1)} %copy-done, bf16[128,256]{1,0:T(8,128)(2,1)} %copy-done.2, bf16[128,256]{1,0:T(8,128)(2,1)} %copy-done.3, bf16[128,2048]{1,0:T(8,128)(2,1)} %copy-done.1, ...), custom_call_target="tpu_custom_call" | custom-call | flops 655360 | bytes 2621440 | tf_op jit(solution)/shard_map/scale/pallas_call | solution.py:346
  61.6 0.0 collective-permute-done.13
  61.6 0.0 collective-permute-done.17
  61.7 0.7 %multiply_convert_fusion = bf16[1,64,1024]{2,1,0:T(8,128)(2,1)} fusion(bf16[1,64,512]{2,1,0:T(8,128)(2,1)S(1)} %get-tuple-element.49, bf16[1,64,512]{2,1,0:T(8,128)(2,1)S(1)} %get-tuple-element.48, f32[]{:T(128)} %bitcast.20), kind=kLoop, calls=%fused_computation | loop fusion | flops 393216 | bytes 262148 | tf_op jit(solution)/shard_map/convert_element_type | solution.py:382
  62.4 0.7 %multiply_convert_fusion.1 = bf16[1,64,1024]{2,1,0:T(8,128)(2,1)} fusion(bf16[1,64,512]{2,1,0:T(8,128)(2,1)S(1)} %get-tuple-element.59, bf16[1,64,512]{2,1,0:T(8,128)(2,1)S(1)} %get-tuple-element.58, f32[]{:T(128)} %bitcast.20), kind=kLoop, calls=%fused_computation.1 | loop fusion | flops 393216 | bytes 262148 | tf_op jit(solution)/shard_map/convert_element_type | solution.py:382
  (19 shorter events, 0.2 us)
Async XLA Ops:
  1.5 5.4 %collective-permute-start.1 = (bf16[128,256]{1,0:T(8,128)(2,1)S(1)}, bf16[128,256]{1,0:T(8,128)(2,1)S(1)}, u32[]{:S(2)}, u32[]{:S(2)}) collective-permute-start(bf16[128,256]{1,0:T(8,128)(2,1)S(1)} %pad_maximum_fusion.2), channel_id=1, source_target_pairs={{0,1},{1,0},{2,3},{3,2},{4,5},{5,4},{6,7},{7,6},{8,9},{9,8},{10,11... | collective-permute-start | bytes 196616 | tf_op jit(solution)/shard_map/ppermute | solution.py:224
  4.6 7.0 %collective-permute-start = (bf16[128,256]{1,0:T(8,128)(2,1)S(1)}, bf16[128,256]{1,0:T(8,128)(2,1)S(1)}, u32[]{:S(2)}, u32[]{:S(2)}) collective-permute-start(bf16[128,256]{1,0:T(8,128)(2,1)S(1)} %pad_maximum_fusion.1), channel_id=1, source_target_pairs={{0,1},{1,0},{2,3},{3,2},{4,5},{5,4},{6,7},{7,6},{8,9},{9,8},{10,11... | collective-permute-start | bytes 196616 | tf_op jit(solution)/shard_map/ppermute | solution.py:224
  7.0 17.7 %copy-start.7 = (bf16[1,128,512]{2,1,0:T(8,128)(2,1)S(1)}, bf16[1,128,512]{2,1,0:T(8,128)(2,1)}, u32[]{:S(2)}) copy-start(bf16[1,128,512]{2,1,0:T(8,128)(2,1)} %param.9) | copy-start | bytes 393220
  7.0 17.7 %copy-start.6 = (bf16[1,128,512]{2,1,0:T(8,128)(2,1)S(1)}, bf16[1,128,512]{2,1,0:T(8,128)(2,1)}, u32[]{:S(2)}) copy-start(bf16[1,128,512]{2,1,0:T(8,128)(2,1)} %param.8) | copy-start | bytes 393220
  7.0 8.2 %collective-permute-start.2 = (bf16[256,256]{1,0:T(8,128)(2,1)S(1)}, bf16[256,256]{1,0:T(8,128)(2,1)S(1)}, u32[]{:S(2)}, u32[]{:S(2)}) collective-permute-start(bf16[256,256]{1,0:T(8,128)(2,1)S(1)} %pad_maximum_fusion.refs_5_), channel_id=1, source_target_pairs={{0,6},{2,4},{4,2},{6,0},{1,7},{3,5},{5,3},{7,1},{8,14},{10,12},{12... | collective-permute-start | bytes 393224 | tf_op jit(solution)/shard_map/ppermute | solution.py:224
  11.6 9.9 %collective-permute-start.6 = (bf16[256,256]{1,0:T(8,128)(2,1)S(1)}, bf16[256,256]{1,0:T(8,128)(2,1)S(1)}, u32[]{:S(2)}, u32[]{:S(2)}) collective-permute-start(bf16[256,256]{1,0:T(8,128)(2,1)S(1)} %pad_maximum_fusion.refs_5_), channel_id=1, source_target_pairs={{0,2},{2,0},{4,6},{6,4},{1,3},{3,1},{5,7},{7,5},{8,10},{10,8},{12,... | collective-permute-start | bytes 393224 | tf_op jit(solution)/shard_map/ppermute | solution.py:224
  15.2 9.5 %collective-permute-start.7 = (bf16[256,256]{1,0:T(8,128)(2,1)S(1)}, bf16[256,256]{1,0:T(8,128)(2,1)S(1)}, u32[]{:S(2)}, u32[]{:S(2)}) collective-permute-start(bf16[256,256]{1,0:T(8,128)(2,1)S(1)} %collective-permute-done.2.refs_8_), channel_id=1, source_target_pairs={{0,2},{2,0},{4,6},{6,4},{1,3},{3,1},{5,7},{7,5},{8,10},{10,8},{12,... | collective-permute-start | bytes 393224 | tf_op jit(solution)/shard_map/ppermute | solution.py:224
  16.0 19.1 %collective-permute-start.3 = (bf16[272,256]{1,0:T(8,128)(2,1)S(1)}, bf16[272,256]{1,0:T(8,128)(2,1)S(1)}, u32[]{:S(2)}, u32[]{:S(2)}) collective-permute-start(bf16[272,256]{1,0:T(8,128)(2,1)S(1)} %constant_dynamic-update-slice_fusion.refs_5_), channel_id=1, source_target_pairs={{0,2},{2,0},{4,6},{6,4},{1,3},{3,1},{5,7},{7,5},{8,10},{10,8},{12,... | collective-permute-start | bytes 417800 | tf_op jit(solution)/shard_map/ppermute | solution.py:224
  17.2 22.1 %collective-permute-start.4 = (bf16[272,256]{1,0:T(8,128)(2,1)S(1)}, bf16[272,256]{1,0:T(8,128)(2,1)S(1)}, u32[]{:S(2)}, u32[]{:S(2)}) collective-permute-start(bf16[272,256]{1,0:T(8,128)(2,1)S(1)} %constant_dynamic-update-slice_fusion.refs_5_), channel_id=1, source_target_pairs={{0,4},{2,6},{4,0},{6,2},{1,5},{3,7},{5,1},{7,3},{8,12},{10,14},{12... | collective-permute-start | bytes 417800 | tf_op jit(solution)/shard_map/ppermute | solution.py:224
  20.1 19.3 %collective-permute-start.5 = (bf16[272,256]{1,0:T(8,128)(2,1)S(1)}, bf16[272,256]{1,0:T(8,128)(2,1)S(1)}, u32[]{:S(2)}, u32[]{:S(2)}) collective-permute-start(bf16[272,256]{1,0:T(8,128)(2,1)S(1)} %constant_dynamic-update-slice_fusion.refs_5_), channel_id=1, source_target_pairs={{0,6},{2,4},{4,2},{6,0},{1,7},{3,5},{5,3},{7,1},{8,14},{10,12},{12... | collective-permute-start | bytes 417800 | tf_op jit(solution)/shard_map/ppermute | solution.py:224
  32.9 0.8 %copy-start = (bf16[128,2048]{1,0:T(8,128)(2,1)}, bf16[128,2048]{1,0:T(8,128)(2,1)S(1)}, u32[]{:S(2)}) copy-start(bf16[128,2048]{1,0:T(8,128)(2,1)S(1)} %get-tuple-element.33.refs_0_) | copy-start | bytes 1572868
  33.7 0.6 copy-start.2
  34.3 0.6 copy-start.3
  35.0 13.3 %collective-permute-start.10 = (bf16[256,256]{1,0:T(8,128)(2,1)S(1)}, bf16[256,256]{1,0:T(8,128)(2,1)S(1)}, u32[]{:S(2)}, u32[]{:S(2)}) collective-permute-start(bf16[256,256]{1,0:T(8,128)(2,1)S(1)} %get-tuple-element.32), channel_id=1, source_target_pairs={{0,6},{2,4},{4,2},{6,0},{1,7},{3,5},{5,3},{7,1},{8,14},{10,12},{12... | collective-permute-start | bytes 393224 | tf_op jit(solution)/shard_map/ppermute | solution.py:224
  35.0 17.2 %collective-permute-start.8 = (bf16[256,256]{1,0:T(8,128)(2,1)S(1)}, bf16[256,256]{1,0:T(8,128)(2,1)S(1)}, u32[]{:S(2)}, u32[]{:S(2)}) collective-permute-start(bf16[256,256]{1,0:T(8,128)(2,1)S(1)} %get-tuple-element.30), channel_id=1, source_target_pairs={{0,2},{2,0},{4,6},{6,4},{1,3},{3,1},{5,7},{7,5},{8,10},{10,8},{12,... | collective-permute-start | bytes 393224 | tf_op jit(solution)/shard_map/ppermute | solution.py:224
  35.1 17.1 %collective-permute-start.9 = (bf16[256,256]{1,0:T(8,128)(2,1)S(1)}, bf16[256,256]{1,0:T(8,128)(2,1)S(1)}, u32[]{:S(2)}, u32[]{:S(2)}) collective-permute-start(bf16[256,256]{1,0:T(8,128)(2,1)S(1)} %get-tuple-element.31), channel_id=1, source_target_pairs={{0,4},{2,6},{4,0},{6,2},{1,5},{3,7},{5,1},{7,3},{8,12},{10,14},{12... | collective-permute-start | bytes 393224 | tf_op jit(solution)/shard_map/ppermute | solution.py:224
  47.6 4.6 %copy-start.4 = (bf16[128,256]{1,0:T(8,128)(2,1)}, bf16[128,256]{1,0:T(8,128)(2,1)S(1)}, u32[]{:S(2)}) copy-start(bf16[128,256]{1,0:T(8,128)(2,1)S(1)} %get-tuple-element.37.refs_4_) | copy-start | bytes 196612
  47.6 4.6 %copy-start.5 = (bf16[128,256]{1,0:T(8,128)(2,1)}, bf16[128,256]{1,0:T(8,128)(2,1)S(1)}, u32[]{:S(2)}) copy-start(bf16[128,256]{1,0:T(8,128)(2,1)S(1)} %get-tuple-element.38.refs_5_) | copy-start | bytes 196612
  47.7 4.6 %copy-start.1 = (bf16[128,2048]{1,0:T(8,128)(2,1)}, bf16[128,2048]{1,0:T(8,128)(2,1)S(1)}, u32[]{:S(2)}) copy-start(bf16[128,2048]{1,0:T(8,128)(2,1)S(1)} %get-tuple-element.36.refs_3_) | copy-start | bytes 1572868
  47.7 7.4 %collective-permute-start.14 = (bf16[256,256]{1,0:T(8,128)(2,1)S(1)}, bf16[256,256]{1,0:T(8,128)(2,1)S(1)}, u32[]{:S(2)}, u32[]{:S(2)}) collective-permute-start(bf16[256,256]{1,0:T(8,128)(2,1)S(1)} %get-tuple-element.43), channel_id=1, source_target_pairs={{0,2},{2,0},{4,6},{6,4},{1,3},{3,1},{5,7},{7,5},{8,10},{10,8},{12,... | collective-permute-start | bytes 393224 | tf_op jit(solution)/shard_map/ppermute | solution.py:224
  47.7 7.3 %collective-permute-start.15 = (bf16[256,256]{1,0:T(8,128)(2,1)S(1)}, bf16[256,256]{1,0:T(8,128)(2,1)S(1)}, u32[]{:S(2)}, u32[]{:S(2)}) collective-permute-start(bf16[256,256]{1,0:T(8,128)(2,1)S(1)} %get-tuple-element.44), channel_id=1, source_target_pairs={{0,4},{2,6},{4,0},{6,2},{1,5},{3,7},{5,1},{7,3},{8,12},{10,14},{12... | collective-permute-start | bytes 393224 | tf_op jit(solution)/shard_map/ppermute | solution.py:224
  48.3 8.3 %collective-permute-start.16 = (bf16[256,256]{1,0:T(8,128)(2,1)S(1)}, bf16[256,256]{1,0:T(8,128)(2,1)S(1)}, u32[]{:S(2)}, u32[]{:S(2)}) collective-permute-start(bf16[256,256]{1,0:T(8,128)(2,1)S(1)} %get-tuple-element.45), channel_id=1, source_target_pairs={{0,6},{2,4},{4,2},{6,0},{1,7},{3,5},{5,3},{7,1},{8,14},{10,12},{12... | collective-permute-start | bytes 393224 | tf_op jit(solution)/shard_map/ppermute | solution.py:224
  52.3 1.2 %collective-permute-start.11 = (f32[8,128]{1,0:T(8,128)S(1)}, f32[8,128]{1,0:T(8,128)S(1)}, u32[]{:S(2)}, u32[]{:S(2)}) collective-permute-start(f32[8,128]{1,0:T(8,128)S(1)} %fusion.1), channel_id=1, source_target_pairs={{0,8},{8,0},{16,24},{24,16},{1,9},{9,1},{17,25},{25,17},{2,10},{10... | collective-permute-start | bytes 12296 | tf_op jit(solution)/shard_map/ppermute | solution.py:224
  52.4 9.2 %collective-permute-start.13 = (bf16[128,256]{1,0:T(8,128)(2,1)S(1)}, bf16[128,256]{1,0:T(8,128)(2,1)S(1)}, u32[]{:S(2)}, u32[]{:S(2)}) collective-permute-start(bf16[128,256]{1,0:T(8,128)(2,1)S(1)} %pad_maximum_fusion.3), channel_id=1, source_target_pairs={{0,1},{1,0},{2,3},{3,2},{4,5},{5,4},{6,7},{7,6},{8,9},{9,8},{10,11... | collective-permute-start | bytes 196616 | tf_op jit(solution)/shard_map/ppermute | solution.py:224
  53.5 4.3 %collective-permute-start.12 = (f32[8,128]{1,0:T(8,128)S(1)}, f32[8,128]{1,0:T(8,128)S(1)}, u32[]{:S(2)}, u32[]{:S(2)}) collective-permute-start(f32[8,128]{1,0:T(8,128)S(1)} %add.69), channel_id=1, source_target_pairs={{0,16},{8,24},{16,0},{24,8},{1,17},{9,25},{17,1},{25,9},{2,18},{10... | collective-permute-start | bytes 12296 | tf_op jit(solution)/shard_map/ppermute | solution.py:224
  56.7 5.0 %collective-permute-start.17 = (bf16[128,256]{1,0:T(8,128)(2,1)S(1)}, bf16[128,256]{1,0:T(8,128)(2,1)S(1)}, u32[]{:S(2)}, u32[]{:S(2)}) collective-permute-start(bf16[128,256]{1,0:T(8,128)(2,1)S(1)} %pad_maximum_fusion.4), channel_id=1, source_target_pairs={{0,1},{1,0},{2,3},{3,2},{4,5},{5,4},{6,7},{7,6},{8,9},{9,8},{10,11... | collective-permute-start | bytes 196616 | tf_op jit(solution)/shard_map/ppermute | solution.py:224
  57.8 1.2 %copy-start.8 = (f32[8,128]{1,0:T(8,128)}, f32[8,128]{1,0:T(8,128)S(1)}, u32[]{:S(2)}) copy-start(f32[8,128]{1,0:T(8,128)S(1)} %add.70.total_ref) | copy-start | bytes 12292

commit v7 on v6

--- a/solution.py
+++ b/solution.py
@@ -14,7 +14,7 @@
 CHUNKS = 2
 EXTRA = 16
 STEP = 64
-VMEM_LIMIT = 52 * 1024 * 1024
+VMEM_LIMIT = 40 * 1024 * 1024
 NT = (((1,), (1,)), ((), ()))
 
 
@@ -26,7 +26,7 @@
 
 def attend_kernel(n_slots, count, chunk, held, factor, *refs):
     last = chunk + 1 == CHUNKS
-    length_ref, q_hbm, do_hbm, kown_hbm, vown_hbm = refs[:5]
+    length_ref, q_ref, turned_ref, kown_ref, vown_ref = refs[:5]
     slot_refs, refs = refs[5 : 5 + n_slots], refs[5 + n_slots + last :]
     out_hbm, dq_ref, dkown_ref, dvown_ref = refs[:4]
     term_refs, refs = refs[4 : 4 + n_slots], refs[4 + n_slots :]
@@ -34,9 +34,8 @@
         total_ref, refs = refs[0], refs[1:]
         totals = [ref[2 * held : 2 * held + 8, :HD].astype(jnp.float32) for ref in slot_refs]
         total_ref[...] = functools.reduce(jnp.add, totals)
-    q_ref, do_ref, kown_ref, vown_ref, out_ref = refs[:5]
-    s_ref, dp_ref, e_ref, ds_ref, dot_ref = refs[5:10]
-    keys_ref, keys_t_ref, values_ref, values_t_ref, in_sem, out_sem = refs[10:]
+    out_ref, s_ref, dp_ref, e_ref, ds_ref, dot_ref = refs[:6]
+    keys_ref, keys_t_ref, values_ref, values_t_ref, out_sem = refs[6:]
     first = chunk * count
     rows = q_ref.shape[0]
     own = kown_ref.shape[0]
@@ -48,34 +47,13 @@
     def columns(head, size):
         return pl.ds(head * size, size)
 
-    loads = []
-    for head in range(count):
-        loads.append(
-            [
-                pltpu.make_async_copy(
-                    hbm.at[:, columns(first + head, size)],
-                    ref.at[:, columns(head, size)],
-                    in_sem.at[head, i],
-                )
-                for i, (hbm, ref, size) in enumerate(
-                    [
-                        (kown_hbm, kown_ref, HD),
-                        (q_hbm, q_ref, GROUP * HD),
-                        (do_hbm, do_ref, GROUP * HD),
-                        (vown_hbm, vown_ref, HD),
-                    ]
-                )
-            ]
-        )
-        for copy in loads[-1]:
-            copy.start()
     stores = []
 
     live = (lax.broadcasted_iota(jnp.int32, (1, width), 1) % rows) < length_ref[0]
 
     def assemble(head, own_ref, slot_start, wide_ref, tall_ref):
         here = slice(head * HD, (head + 1) * HD)
-        wide_ref[head, :own] = own_ref[:, here]
+        wide_ref[head, :own] = own_ref[:, (first + head) * HD : (first + head + 1) * HD]
         for i, ref in enumerate(slot_refs):
             part = slice(own + i * held, own + (i + 1) * held)
             wide_ref[head, part] = ref[slot_start : slot_start + held, here]
@@ -86,12 +64,10 @@
 
     def scores(head, pair):
         if pair == 0:
-            loads[head][0].wait()
-            loads[head][1].wait()
             assemble(head, kown_ref, 0, keys_ref, keys_t_ref)
         s_ref[pair % 2] = lax.dot_general(
             keys_ref[head],
-            heads_down(q_ref, head * GROUP + pair * PAIR, PAIR),
+            heads_down(q_ref, (first + head) * GROUP + pair * PAIR, PAIR),
             NT,
             preferred_element_type=jnp.float32,
         )
@@ -118,16 +94,13 @@
             e_ref[head % 2, at : at + STEP, cols] = e.reshape(-1, width).astype(jnp.bfloat16)
         total = jnp.sum(total, axis=0, keepdims=True)
         inverse = jnp.where(live, 1.0 / total, 0.0)
-        if pair == 0:
-            loads[head][2].wait()
-        do = heads_down(do_ref, head * GROUP + pair * PAIR, PAIR)
-        dot_ref[head % 2, :, cols] = (do.T.astype(jnp.float32) * inverse).astype(jnp.bfloat16)
+        grad = turned_ref[first + head, :, cols].astype(jnp.float32) * inverse
+        dot_ref[head % 2, :, cols] = grad.astype(jnp.bfloat16)
         return inverse
 
     def attended(head, pair, inverse):
         cols = place(head, pair)
         if pair == 0:
-            loads[head][3].wait()
             assemble(head, vown_ref, held, values_ref, values_t_ref)
         grad = dot_ref[head % 2, :, cols]
         dp_ref[pair % 2] = jnp.dot(values_ref[head], grad, preferred_element_type=jnp.float32)
@@ -177,7 +150,7 @@
             ref[held:, here] = dv[own + i * held : own + (i + 1) * held]
         dk = jnp.dot(
             ds_ref[head % 2],
-            heads_down(q_ref, head * GROUP, GROUP),
+            heads_down(q_ref, (first + head) * GROUP, GROUP),
             preferred_element_type=jnp.float32,
         )
         dk = (dk * factor).astype(jnp.bfloat16)
@@ -200,6 +173,10 @@
             key_grads(now[0])
     for copy in stores:
         copy.wait()
+
+
+def turn_kernel(do_ref, after_ref, out_ref):
+    out_ref[0] = heads_down(do_ref, 0, GROUP).T
 
 
 def scale_kernel(slots_all, total_ref, *refs):
@@ -304,7 +281,19 @@
     return jax.ShapeDtypeStruct(x.shape, x.dtype)
 
 
-def attend(chunk, held, slots, length, q, do, k, v, carried):
+def turn(do, after):
+    rows, heads = do.shape[0], do.shape[1] // (GROUP * HD)
+    return pl.pallas_call(
+        turn_kernel,
+        grid=(heads,),
+        in_specs=[pl.BlockSpec((rows, GROUP * HD), lambda j: (0, j)), HBM],
+        out_specs=pl.BlockSpec((1, HD, GROUP * rows), lambda j: (j, 0, 0)),
+        out_shape=jax.ShapeDtypeStruct((heads, HD, GROUP * rows), do.dtype),
+        name="turn",
+    )(do, after)
+
+
+def attend(chunk, held, slots, length, q, turned, k, v, carried):
     rows = q.shape[0]
     count = k.shape[1] // (HD * CHUNKS)
     n_slots = len(slots)
@@ -315,18 +304,17 @@
     step_buffer = pltpu.VMEM((2, n_keys, PAIR * rows), jnp.float32)
     head_buffer = pltpu.VMEM((2, n_keys, GROUP * rows), bf16)
     wide = pltpu.VMEM((rows, count * GROUP * HD), bf16)
-    own = pltpu.VMEM((rows, count * HD), bf16)
     down = pltpu.VMEM((count, n_keys, HD), bf16)
     across = pltpu.VMEM((count, HD, n_keys), bf16)
-    scratch = [wide, wide, own, own, wide, step_buffer, step_buffer, head_buffer, head_buffer]
+    scratch = [wide, step_buffer, step_buffer, head_buffer, head_buffer]
     scratch += [pltpu.VMEM((2, HD, GROUP * rows), bf16), down, across, down, across]
-    scratch += [pltpu.SemaphoreType.DMA((count, 4)), pltpu.SemaphoreType.DMA((count,))]
+    scratch += [pltpu.SemaphoreType.DMA((count,))]
     part = lambda x: jax.ShapeDtypeStruct((x.shape[0], x.shape[1] // CHUNKS), bf16)
     terms = [jax.ShapeDtypeStruct((2 * held, count * HD), bf16)] * n_slots
     total = [jax.ShapeDtypeStruct((8, HD), jnp.float32)] * last
     return pl.pallas_call(
         functools.partial(attend_kernel, n_slots, count, chunk, held, 1.0 / math.sqrt(HD)),
-        in_specs=[SMEM] + [HBM] * 4 + [VMEM] * n_slots + [HBM] * last,
+        in_specs=[SMEM] + [VMEM] * (4 + n_slots) + [HBM] * last,
         out_specs=[HBM] + [VMEM] * (3 + n_slots + last),
         out_shape=[like(q), part(q), part(k), part(v)] + terms + total,
         input_output_aliases={5 + n_slots: 0} if last else {},
@@ -338,7 +326,7 @@
             transcendentals=count * n_keys * GROUP * rows,
         ),
         name=f"attend_{chunk}",
-    )(length, q, do, k, v, *slots, *carried)
+    )(length, q, turned, k, v, *slots, *carried)
 
 
 def scale_all(slots_all, total, chunk_grads, shapes):
@@ -369,8 +357,9 @@
     slots = line_gather(first, True)
     length_rows = length[0].astype(second.dtype) + 0 * slots[-1][-EXTRA:]
     next_slots = line_gather(jnp.concatenate([second, length_rows], axis=0), False)
-    results = attend(0, held, slots, length, q, do, k, v, [])
-    next_results = attend(1, held, next_slots, length, q, do, k, v, results[:1])
+    turned = turn(do, first)
+    results = attend(0, held, slots, length, q, turned, k, v, [])
+    next_results = attend(1, held, next_slots, length, q, turned, k, v, results[:1])
     sums = [line_reduce(results[4:]), line_reduce(next_results[4:-1])]
     total = sum_over(next_results[-1] + 0 * sums[0][:8, :HD], "prompt")
     weight = slots_all / total[0, 0]

time: 63.5 us -> 60 us (0.945)
  waiting for transfers between devices: 8.37 us -> 3.15 us
  local copies, waits for them, and re-layouts: 5.03 us -> 6.29 us
  starting transfers between devices: 26.8 us -> 27.6 us
    ppermute x18, waiting for transfers between devices: 8.37 us -> 3.15 us  [swap(): lax.ppermute(x, axis, [(i, i ^ by) for i in range(lax.axis_size(axis))])]
    pallas_call x2, Pallas kernels: 16.5 us -> 12.4 us  [attend(): pl.pallas_call(functools.partial(attend_kernel, n_slots, count, chunk, he...]
    pallas_call x0 -> x1, Pallas kernels: none -> 3.68 us  [turn(): pl.pallas_call(turn_kernel, grid=(heads,), in_specs=[pl.BlockSpec((rows,...]
    unnamed x22 -> x32, local copies, waits for them, and re-layouts: 3.61 us -> 4.87 us
    ppermute x18, starting transfers between devices: 26.8 us -> 27.6 us  [swap(): lax.ppermute(x, axis, [(i, i ^ by) for i in range(lax.axis_size(axis))])]
  transfers between devices with their start and end apart: 18 -> 18, of which waited for: 4 -> 2; matrix products, arithmetic and copies ran while one was open for 4% -> 4% of each run, Pallas kernels for 30% -> 31%
where the time goes in v7:
time: 60 us; the launch traced here: 59.5 us
  starting transfers between devices  27.6 us (46%)
  Pallas kernels  18.6 us (31%)
  local copies, waits for them, and re-layouts  6.29 us (10%)
  waiting for transfers between devices  3.15 us (5%)
  between operations  2.29 us (4%)
  other arithmetic  1.63 us (3%)
    ppermute x18, starting transfers between devices, swap(): lax.ppermute(x, axis, [(i, i ^ by) for i in range(lax.axis_size(axis))])  27.6 us
    pallas_call x2, Pallas kernels, attend(): pl.pallas_call(functools.partial(attend_kernel, n_slots, count, chunk, he...  12.4 us
    unnamed x32, local copies, waits for them, and re-layouts  4.87 us
    pallas_call x1, Pallas kernels, turn(): pl.pallas_call(turn_kernel, grid=(heads,), in_specs=[pl.BlockSpec((rows,...  3.68 us
    ppermute x18, waiting for transfers between devices, swap(): lax.ppermute(x, axis, [(i, i ^ by) for i in range(lax.axis_size(axis))])  3.15 us
    pallas_call x1, Pallas kernels, scale_all(): pl.pallas_call(functools.partial(scale_kernel, slots_all), in_specs=[VMEM...  2.54 us
    convert_element_type x2, other arithmetic, body(): (grad.astype(jnp.float32) * weight).astype(jnp.bfloat16)  1.37 us
  transfers between devices with their start and end apart: 18, of which 2 were waited for; matrix products, arithmetic and copies ran while one was open for 4% of the time, Pallas kernels for 31%

profile of v7, /device:TPU:0, one launch (start us, length us, event | category | flops | bytes accessed | tf_op | source)
XLA Modules:
  0.0 59.5 jit_solution(5479029078394490060)
XLA Ops:
  0.7 0.9 %dynamic-slice_bitcast_fusion = (bf16[64,256]{1,0:T(8,128)(2,1)S(1)}, bf16[64,256]{1,0:T(8,128)(2,1)S(1)}, bf16[64,256]{1,0:T(8,128)(2,1)S(1)}, bf16[64,256]{1,0...) fusion(bf16[1,64,1024]{2,1,0:T(8,128)(2,1)} %param.11, s32[]{:T(128)S(6)} %select_n.65, ...), kind=kLoop, calls=%fused_computation.21 | loop fusion | bytes 393228 | tf_op jit(solution)/shard_map/dynamic_slice | solution.py:230
  1.5 3.0 %collective-permute-start = (bf16[128,256]{1,0:T(8,128)(2,1)S(1)}, bf16[128,256]{1,0:T(8,128)(2,1)S(1)}, u32[]{:S(2)}, u32[]{:S(2)}) collective-permute-start(bf16[128,256]{1,0:T(8,128)(2,1)S(1)} %pad_maximum_fusion.1), channel_id=1, source_target_pairs={{0,1},{1,0},{2,3},{3,2},{4,5},{5,4},{6,7},{7,6},{8,9},{9,8},{10,11... | collective-permute-start | bytes 196616 | tf_op jit(solution)/shard_map/ppermute | solution.py:201
  4.6 0.1 collective-permute-start.1
  5.3 0.8 %bitcast_dynamic-update-slice_fusion.1 = bf16[272,256]{1,0:T(8,128)(2,1)S(1)} fusion(bf16[1,64,1024]{2,1,0:T(8,128)(2,1)} %param.10, s32[]{:T(128)S(6)} %select_n.64), kind=kLoop, calls=%fused_computation.20 | loop fusion | bytes 65540
  6.1 0.9 %collective-permute-done = bf16[128,256]{1,0:T(8,128)(2,1)S(1)} collective-permute-done((bf16[128,256]{1,0:T(8,128)(2,1)S(1)}, bf16[128,256]{1,0:T(8,128)(2,1)S(1)}, u32[]{:S(2)}, u32[]{:S(2)}) %collective-permute-start) | collective-permute-done | bytes 65568 | tf_op jit(solution)/shard_map/ppermute | solution.py:201
  7.0 0.0 copy-start.2
  7.0 4.6 %collective-permute-start.2 = (bf16[256,256]{1,0:T(8,128)(2,1)S(1)}, bf16[256,256]{1,0:T(8,128)(2,1)S(1)}, u32[]{:S(2)}, u32[]{:S(2)}) collective-permute-start(bf16[256,256]{1,0:T(8,128)(2,1)S(1)} %pad_maximum_fusion.after_ref.refs_5_), channel_id=1, source_target_pairs={{0,6},{2,4},{4,2},{6,0},{1,7},{3,5},{5,3},{7,1},{8,14},{10,12},{12... | collective-permute-start | bytes 393224 | tf_op jit(solution)/shard_map/ppermute | solution.py:201
  11.6 0.0 collective-permute-start.6
  11.6 0.0 copy-done.2
  11.6 0.0 copy-start.12
  11.6 3.7 %turn.1.refs_2_ = bf16[4,128,1024]{2,1,0:T(8,128)(2,1)} custom-call(bf16[128,4096]{1,0:T(8,128)(2,1)} %bitcast.43, bf16[256,256]{1,0:T(8,128)(2,1)} %copy-done.2), custom_call_target="tpu_custom_call" | custom-call | tf_op jit(solution)/shard_map/turn/pallas_call | solution.py:286
  15.3 0.0 collective-permute-done.1
  15.3 0.8 %bitcast_dynamic-update-slice_fusion = bf16[272,256]{1,0:T(8,128)(2,1)S(1)} fusion(bf16[272,256]{1,0:T(8,128)(2,1)S(1)} %slice_dynamic-update-slice_fusion.1, bf16[1,64,1024]{2,1,0:T(8,128)(2,1)} %param.11, s32[]{:T(128)S(6)} %select_n.64), kind=kLoop, calls=%fused_computation.19 | loop fusion | bytes 65540
  16.1 0.0 collective-permute-done.2.refs_8_
  16.1 2.1 %collective-permute-start.7 = (bf16[256,256]{1,0:T(8,128)(2,1)S(1)}, bf16[256,256]{1,0:T(8,128)(2,1)S(1)}, u32[]{:S(2)}, u32[]{:S(2)}) collective-permute-start(bf16[256,256]{1,0:T(8,128)(2,1)S(1)} %collective-permute-done.2.refs_8_), channel_id=1, source_target_pairs={{0,2},{2,0},{4,6},{6,4},{1,3},{3,1},{5,7},{7,5},{8,10},{10,8},{12,... | collective-permute-start | bytes 393224 | tf_op jit(solution)/shard_map/ppermute | solution.py:201
  18.2 0.1 collective-permute-start.3
  18.3 0.8 %collective-permute-start.4 = (bf16[272,256]{1,0:T(8,128)(2,1)S(1)}, bf16[272,256]{1,0:T(8,128)(2,1)S(1)}, u32[]{:S(2)}, u32[]{:S(2)}) collective-permute-start(bf16[272,256]{1,0:T(8,128)(2,1)S(1)} %constant_dynamic-update-slice_fusion.refs_5_), channel_id=1, source_target_pairs={{0,4},{2,6},{4,0},{6,2},{1,5},{3,7},{5,1},{7,3},{8,12},{10,14},{12... | collective-permute-start | bytes 417800 | tf_op jit(solution)/shard_map/ppermute | solution.py:201
  19.1 3.5 %collective-permute-start.5 = (bf16[272,256]{1,0:T(8,128)(2,1)S(1)}, bf16[272,256]{1,0:T(8,128)(2,1)S(1)}, u32[]{:S(2)}, u32[]{:S(2)}) collective-permute-start(bf16[272,256]{1,0:T(8,128)(2,1)S(1)} %constant_dynamic-update-slice_fusion.refs_5_), channel_id=1, source_target_pairs={{0,6},{2,4},{4,2},{6,0},{1,7},{3,5},{5,3},{7,1},{8,14},{10,12},{12... | collective-permute-start | bytes 417800 | tf_op jit(solution)/shard_map/ppermute | solution.py:201
  22.6 0.0 collective-permute-done.6.refs_6_
  22.6 0.0 collective-permute-done.7.refs_7_
  22.6 0.0 copy-done.10
  22.6 0.0 copy-done.11
  22.6 0.0 copy-done.12
  22.6 0.0 copy-done.3
  22.6 0.0 copy-start
  22.7 1.2 %copy-done = bf16[4,128,1024]{2,1,0:T(8,128)(2,1)S(1)} copy-done((bf16[4,128,1024]{2,1,0:T(8,128)(2,1)S(1)}, bf16[4,128,1024]{2,1,0:T(8,128)(2,1)}, u32[]{:S(2)}) %copy-start) | copy-done | bytes 1048600
  23.9 6.2 %attend_0.1 = (bf16[128,4096]{1,0:T(8,128)(2,1)}, bf16[128,2048]{1,0:T(8,128)(2,1)S(1)}, bf16[128,256]{1,0:T(8,128)(2,1)S(1)}, bf16[128,256]{1,0:T(8,128)(2,1)S(...) custom-call(s32[1]{0:T(128)} %bitcast.35.refs_0_, ...), custom_call_target="tpu_custom_call" | custom-call | flops 8053063680 | bytes 2097152 | tf_op jit(solution)/shard_map/attend_0/pallas_call | solution.py:315
  30.1 0.0 copy-start.4
  30.1 0.8 %copy-done.4 = bf16[128,2048]{1,0:T(8,128)(2,1)} copy-done((bf16[128,2048]{1,0:T(8,128)(2,1)}, bf16[128,2048]{1,0:T(8,128)(2,1)S(1)}, u32[]{:S(2)}) %copy-start.4) | copy-done | bytes 524312
  30.9 0.6 %copy-done.6 = bf16[128,256]{1,0:T(8,128)(2,1)} copy-done((bf16[128,256]{1,0:T(8,128)(2,1)}, bf16[128,256]{1,0:T(8,128)(2,1)S(1)}, u32[]{:S(2)}) %copy-start.6) | copy-done | bytes 65560
  31.5 0.6 %copy-done.7 = bf16[128,256]{1,0:T(8,128)(2,1)} copy-done((bf16[128,256]{1,0:T(8,128)(2,1)}, bf16[128,256]{1,0:T(8,128)(2,1)S(1)}, u32[]{:S(2)}) %copy-start.7) | copy-done | bytes 65560
  32.1 1.5 %collective-permute-start.10 = (bf16[256,256]{1,0:T(8,128)(2,1)S(1)}, bf16[256,256]{1,0:T(8,128)(2,1)S(1)}, u32[]{:S(2)}, u32[]{:S(2)}) collective-permute-start(bf16[256,256]{1,0:T(8,128)(2,1)S(1)} %get-tuple-element.32), channel_id=1, source_target_pairs={{0,6},{2,4},{4,2},{6,0},{1,7},{3,5},{5,3},{7,1},{8,14},{10,12},{12... | collective-permute-start | bytes 393224 | tf_op jit(solution)/shard_map/ppermute | solution.py:201
  33.6 0.5 collective-permute-start.8
  34.1 0.0 collective-permute-done.3.refs_6_
  34.1 2.4 %collective-permute-start.9 = (bf16[256,256]{1,0:T(8,128)(2,1)S(1)}, bf16[256,256]{1,0:T(8,128)(2,1)S(1)}, u32[]{:S(2)}, u32[]{:S(2)}) collective-permute-start(bf16[256,256]{1,0:T(8,128)(2,1)S(1)} %get-tuple-element.31), channel_id=1, source_target_pairs={{0,4},{2,6},{4,0},{6,2},{1,5},{3,7},{5,1},{7,3},{8,12},{10,14},{12... | collective-permute-start | bytes 393224 | tf_op jit(solution)/shard_map/ppermute | solution.py:201
  36.5 0.0 collective-permute-done.4.refs_7_
  36.5 0.0 collective-permute-done.5.refs_8_
  36.5 6.2 %attend_1.1 = (bf16[128,4096]{1,0:T(8,128)(2,1)}, bf16[128,2048]{1,0:T(8,128)(2,1)S(1)}, bf16[128,256]{1,0:T(8,128)(2,1)S(1)}, bf16[128,256]{1,0:T(8,128)(2,1)S(...) custom-call(s32[1]{0:T(128)} %bitcast.36.refs_0_, ...), custom_call_target="tpu_custom_call", output_to_operand_aliasing={{0}: (9, {})} | custom-call | flops 8053063680 | bytes 2097152 | tf_op jit(solution)/shard_map/attend_1/pallas_call | solution.py:315
  42.7 0.0 copy-start.8
  42.8 0.0 copy-start.9
  42.8 0.0 copy-start.5
  42.8 1.2 %collective-permute-start.14 = (bf16[256,256]{1,0:T(8,128)(2,1)S(1)}, bf16[256,256]{1,0:T(8,128)(2,1)S(1)}, u32[]{:S(2)}, u32[]{:S(2)}) collective-permute-start(bf16[256,256]{1,0:T(8,128)(2,1)S(1)} %get-tuple-element.43), channel_id=1, source_target_pairs={{0,2},{2,0},{4,6},{6,4},{1,3},{3,1},{5,7},{7,5},{8,10},{10,8},{12,... | collective-permute-start | bytes 393224 | tf_op jit(solution)/shard_map/ppermute | solution.py:201
  43.9 1.0 %collective-permute-start.15 = (bf16[256,256]{1,0:T(8,128)(2,1)S(1)}, bf16[256,256]{1,0:T(8,128)(2,1)S(1)}, u32[]{:S(2)}, u32[]{:S(2)}) collective-permute-start(bf16[256,256]{1,0:T(8,128)(2,1)S(1)} %get-tuple-element.44), channel_id=1, source_target_pairs={{0,4},{2,6},{4,0},{6,2},{1,5},{3,7},{5,1},{7,3},{8,12},{10,14},{12... | collective-permute-start | bytes 393224 | tf_op jit(solution)/shard_map/ppermute | solution.py:201
  44.9 0.0 collective-permute-done.10
  44.9 2.3 %collective-permute-start.16 = (bf16[256,256]{1,0:T(8,128)(2,1)S(1)}, bf16[256,256]{1,0:T(8,128)(2,1)S(1)}, u32[]{:S(2)}, u32[]{:S(2)}) collective-permute-start(bf16[256,256]{1,0:T(8,128)(2,1)S(1)} %get-tuple-element.45), channel_id=1, source_target_pairs={{0,6},{2,4},{4,2},{6,0},{1,7},{3,5},{5,3},{7,1},{8,14},{10,12},{12... | collective-permute-start | bytes 393224 | tf_op jit(solution)/shard_map/ppermute | solution.py:201
  47.2 0.0 collective-permute-done.8
  47.2 0.0 collective-permute-done.9
  47.2 0.1 fusion.2
  47.4 0.1 collective-permute-start.11
  47.5 1.4 %collective-permute-start.13 = (bf16[128,256]{1,0:T(8,128)(2,1)S(1)}, bf16[128,256]{1,0:T(8,128)(2,1)S(1)}, u32[]{:S(2)}, u32[]{:S(2)}) collective-permute-start(bf16[128,256]{1,0:T(8,128)(2,1)S(1)} %pad_maximum_fusion.3), channel_id=1, source_target_pairs={{0,1},{1,0},{2,3},{3,2},{4,5},{5,4},{6,7},{7,6},{8,9},{9,8},{10,11... | collective-permute-start | bytes 196616 | tf_op jit(solution)/shard_map/ppermute | solution.py:201
  48.9 0.0 collective-permute-done.11
  48.9 1.5 %collective-permute-start.12 = (f32[8,128]{1,0:T(8,128)S(1)}, f32[8,128]{1,0:T(8,128)S(1)}, u32[]{:S(2)}, u32[]{:S(2)}) collective-permute-start(f32[8,128]{1,0:T(8,128)S(1)} %add.69), channel_id=1, source_target_pairs={{0,16},{8,24},{16,0},{24,8},{1,17},{9,25},{17,1},{25,9},{2,18},{10... | collective-permute-start | bytes 12296 | tf_op jit(solution)/shard_map/ppermute | solution.py:201
  50.4 0.0 collective-permute-done.14
  50.4 2.2 %collective-permute-done.15 = bf16[256,256]{1,0:T(8,128)(2,1)S(1)} collective-permute-done((bf16[256,256]{1,0:T(8,128)(2,1)S(1)}, bf16[256,256]{1,0:T(8,128)(2,1)S(1)}, u32[]{:S(2)}, u32[]{:S(2)}) %collective-permute-start.15) | collective-permute-done | bytes 131104 | tf_op jit(solution)/shard_map/ppermute | solution.py:201
  52.6 0.0 collective-permute-done.16
  52.6 0.1 add_convert_fusion
  52.7 1.5 %collective-permute-start.17 = (bf16[128,256]{1,0:T(8,128)(2,1)S(1)}, bf16[128,256]{1,0:T(8,128)(2,1)S(1)}, u32[]{:S(2)}, u32[]{:S(2)}) collective-permute-start(bf16[128,256]{1,0:T(8,128)(2,1)S(1)} %pad_maximum_fusion.4), channel_id=1, source_target_pairs={{0,1},{1,0},{2,3},{3,2},{4,5},{5,4},{6,7},{7,6},{8,9},{9,8},{10,11... | collective-permute-start | bytes 196616 | tf_op jit(solution)/shard_map/ppermute | solution.py:201
  54.3 0.0 collective-permute-done.12
  54.3 0.5 slice.71
  55.5 2.5 %scale.1 = (bf16[128,4096]{1,0:T(8,128)(2,1)}, bf16[128,512]{1,0:T(8,128)(2,1)}, bf16[128,512]{1,0:T(8,128)(2,1)}) custom-call(f32[8,128]{1,0:T(8,128)} %copy-done.13, bf16[128,2048]{1,0:T(8,128)(2,1)} %copy-done.4, bf16[128,256]{1,0:T(8,128)(2,1)} %copy-done.6, bf16[128,256]{1,0:T(8,128)(2,1)} %copy-done.7, bf16[128,2048]{1,0:T(8,128)(2,1)} %copy-done.5, ...), custom_call_target="tpu_custom_call" | custom-call | flops 655360 | bytes 2621440 | tf_op jit(solution)/shard_map/scale/pallas_call | solution.py:334
  58.1 0.0 collective-permute-done.13
  58.1 0.0 collective-permute-done.17
  58.1 0.7 %multiply_convert_fusion = bf16[1,64,1024]{2,1,0:T(8,128)(2,1)} fusion(bf16[1,64,512]{2,1,0:T(8,128)(2,1)S(1)} %get-tuple-element.49, bf16[1,64,512]{2,1,0:T(8,128)(2,1)S(1)} %get-tuple-element.48, f32[]{:T(128)} %bitcast.20), kind=kLoop, calls=%fused_computation | loop fusion | flops 393216 | bytes 262148 | tf_op jit(solution)/shard_map/convert_element_type | solution.py:371
  58.9 0.7 %multiply_convert_fusion.1 = bf16[1,64,1024]{2,1,0:T(8,128)(2,1)} fusion(bf16[1,64,512]{2,1,0:T(8,128)(2,1)S(1)} %get-tuple-element.59, bf16[1,64,512]{2,1,0:T(8,128)(2,1)S(1)} %get-tuple-element.58, f32[]{:T(128)} %bitcast.20), kind=kLoop, calls=%fused_computation.1 | loop fusion | flops 393216 | bytes 262148 | tf_op jit(solution)/shard_map/convert_element_type | solution.py:371
  (30 shorter events, 0.2 us)
Async XLA Ops:
  1.5 5.4 %collective-permute-start = (bf16[128,256]{1,0:T(8,128)(2,1)S(1)}, bf16[128,256]{1,0:T(8,128)(2,1)S(1)}, u32[]{:S(2)}, u32[]{:S(2)}) collective-permute-start(bf16[128,256]{1,0:T(8,128)(2,1)S(1)} %pad_maximum_fusion.1), channel_id=1, source_target_pairs={{0,1},{1,0},{2,3},{3,2},{4,5},{5,4},{6,7},{7,6},{8,9},{9,8},{10,11... | collective-permute-start | bytes 196616 | tf_op jit(solution)/shard_map/ppermute | solution.py:201
  4.6 10.7 %collective-permute-start.1 = (bf16[128,256]{1,0:T(8,128)(2,1)S(1)}, bf16[128,256]{1,0:T(8,128)(2,1)S(1)}, u32[]{:S(2)}, u32[]{:S(2)}) collective-permute-start(bf16[128,256]{1,0:T(8,128)(2,1)S(1)} %pad_maximum_fusion.2), channel_id=1, source_target_pairs={{0,1},{1,0},{2,3},{3,2},{4,5},{5,4},{6,7},{7,6},{8,9},{9,8},{10,11... | collective-permute-start | bytes 196616 | tf_op jit(solution)/shard_map/ppermute | solution.py:201
  7.0 4.6 %copy-start.2 = (bf16[256,256]{1,0:T(8,128)(2,1)}, bf16[256,256]{1,0:T(8,128)(2,1)S(1)}, u32[]{:S(2)}) copy-start(bf16[256,256]{1,0:T(8,128)(2,1)S(1)} %pad_maximum_fusion.after_ref.refs_5_) | copy-start | bytes 393220
  7.0 9.1 %collective-permute-start.2 = (bf16[256,256]{1,0:T(8,128)(2,1)S(1)}, bf16[256,256]{1,0:T(8,128)(2,1)S(1)}, u32[]{:S(2)}, u32[]{:S(2)}) collective-permute-start(bf16[256,256]{1,0:T(8,128)(2,1)S(1)} %pad_maximum_fusion.after_ref.refs_5_), channel_id=1, source_target_pairs={{0,6},{2,4},{4,2},{6,0},{1,7},{3,5},{5,3},{7,1},{8,14},{10,12},{12... | collective-permute-start | bytes 393224 | tf_op jit(solution)/shard_map/ppermute | solution.py:201
  11.6 11.0 %collective-permute-start.6 = (bf16[256,256]{1,0:T(8,128)(2,1)S(1)}, bf16[256,256]{1,0:T(8,128)(2,1)S(1)}, u32[]{:S(2)}, u32[]{:S(2)}) collective-permute-start(bf16[256,256]{1,0:T(8,128)(2,1)S(1)} %pad_maximum_fusion.after_ref.refs_5_), channel_id=1, source_target_pairs={{0,2},{2,0},{4,6},{6,4},{1,3},{3,1},{5,7},{7,5},{8,10},{10,8},{12,... | collective-permute-start | bytes 393224 | tf_op jit(solution)/shard_map/ppermute | solution.py:201
  11.6 11.0 %copy-start.10 = (bf16[1,128,4096]{2,1,0:T(8,128)(2,1)S(1)}, bf16[1,128,4096]{2,1,0:T(8,128)(2,1)}, u32[]{:S(2)}) copy-start(bf16[1,128,4096]{2,1,0:T(8,128)(2,1)} %param.7) | copy-start | bytes 3145732
  11.6 11.0 %copy-start.11 = (bf16[1,128,512]{2,1,0:T(8,128)(2,1)S(1)}, bf16[1,128,512]{2,1,0:T(8,128)(2,1)}, u32[]{:S(2)}) copy-start(bf16[1,128,512]{2,1,0:T(8,128)(2,1)} %param.8) | copy-start | bytes 393220
  11.6 11.0 %copy-start.12 = (bf16[1,128,512]{2,1,0:T(8,128)(2,1)S(1)}, bf16[1,128,512]{2,1,0:T(8,128)(2,1)}, u32[]{:S(2)}) copy-start(bf16[1,128,512]{2,1,0:T(8,128)(2,1)} %param.9) | copy-start | bytes 393220
  15.3 7.3 %copy-start.3 = (bf16[256,256]{1,0:T(8,128)(2,1)S(1)}, bf16[256,256]{1,0:T(8,128)(2,1)}, u32[]{:S(2)}) copy-start(bf16[256,256]{1,0:T(8,128)(2,1)} %copy-done.2) | copy-start | bytes 393220
  16.1 6.5 %collective-permute-start.7 = (bf16[256,256]{1,0:T(8,128)(2,1)S(1)}, bf16[256,256]{1,0:T(8,128)(2,1)S(1)}, u32[]{:S(2)}, u32[]{:S(2)}) collective-permute-start(bf16[256,256]{1,0:T(8,128)(2,1)S(1)} %collective-permute-done.2.refs_8_), channel_id=1, source_target_pairs={{0,2},{2,0},{4,6},{6,4},{1,3},{3,1},{5,7},{7,5},{8,10},{10,8},{12,... | collective-permute-start | bytes 393224 | tf_op jit(solution)/shard_map/ppermute | solution.py:201
  18.2 15.9 %collective-permute-start.3 = (bf16[272,256]{1,0:T(8,128)(2,1)S(1)}, bf16[272,256]{1,0:T(8,128)(2,1)S(1)}, u32[]{:S(2)}, u32[]{:S(2)}) collective-permute-start(bf16[272,256]{1,0:T(8,128)(2,1)S(1)} %constant_dynamic-update-slice_fusion.refs_5_), channel_id=1, source_target_pairs={{0,2},{2,0},{4,6},{6,4},{1,3},{3,1},{5,7},{7,5},{8,10},{10,8},{12,... | collective-permute-start | bytes 417800 | tf_op jit(solution)/shard_map/ppermute | solution.py:201
  18.3 18.2 %collective-permute-start.4 = (bf16[272,256]{1,0:T(8,128)(2,1)S(1)}, bf16[272,256]{1,0:T(8,128)(2,1)S(1)}, u32[]{:S(2)}, u32[]{:S(2)}) collective-permute-start(bf16[272,256]{1,0:T(8,128)(2,1)S(1)} %constant_dynamic-update-slice_fusion.refs_5_), channel_id=1, source_target_pairs={{0,4},{2,6},{4,0},{6,2},{1,5},{3,7},{5,1},{7,3},{8,12},{10,14},{12... | collective-permute-start | bytes 417800 | tf_op jit(solution)/shard_map/ppermute | solution.py:201
  19.1 17.5 %collective-permute-start.5 = (bf16[272,256]{1,0:T(8,128)(2,1)S(1)}, bf16[272,256]{1,0:T(8,128)(2,1)S(1)}, u32[]{:S(2)}, u32[]{:S(2)}) collective-permute-start(bf16[272,256]{1,0:T(8,128)(2,1)S(1)} %constant_dynamic-update-slice_fusion.refs_5_), channel_id=1, source_target_pairs={{0,6},{2,4},{4,2},{6,0},{1,7},{3,5},{5,3},{7,1},{8,14},{10,12},{12... | collective-permute-start | bytes 417800 | tf_op jit(solution)/shard_map/ppermute | solution.py:201
  22.6 1.2 %copy-start = (bf16[4,128,1024]{2,1,0:T(8,128)(2,1)S(1)}, bf16[4,128,1024]{2,1,0:T(8,128)(2,1)}, u32[]{:S(2)}) copy-start(bf16[4,128,1024]{2,1,0:T(8,128)(2,1)} %turn.1.refs_2_) | copy-start | bytes 3145732
  23.9 12.7 %copy-start.1 = (bf16[4,128,1024]{2,1,0:T(8,128)(2,1)S(1)}, bf16[4,128,1024]{2,1,0:T(8,128)(2,1)}, u32[]{:S(2)}) copy-start(bf16[4,128,1024]{2,1,0:T(8,128)(2,1)} %turn.1.refs_2_) | copy-start | bytes 3145732
  30.1 0.8 %copy-start.4 = (bf16[128,2048]{1,0:T(8,128)(2,1)}, bf16[128,2048]{1,0:T(8,128)(2,1)S(1)}, u32[]{:S(2)}) copy-start(bf16[128,2048]{1,0:T(8,128)(2,1)S(1)} %get-tuple-element.33.refs_0_) | copy-start | bytes 1572868
  30.9 0.6 %copy-start.6 = (bf16[128,256]{1,0:T(8,128)(2,1)}, bf16[128,256]{1,0:T(8,128)(2,1)S(1)}, u32[]{:S(2)}) copy-start(bf16[128,256]{1,0:T(8,128)(2,1)S(1)} %get-tuple-element.34.refs_1_) | copy-start | bytes 196612
  31.5 0.6 %copy-start.7 = (bf16[128,256]{1,0:T(8,128)(2,1)}, bf16[128,256]{1,0:T(8,128)(2,1)S(1)}, u32[]{:S(2)}) copy-start(bf16[128,256]{1,0:T(8,128)(2,1)S(1)} %get-tuple-element.35.refs_2_) | copy-start | bytes 196612
  32.1 12.8 %collective-permute-start.10 = (bf16[256,256]{1,0:T(8,128)(2,1)S(1)}, bf16[256,256]{1,0:T(8,128)(2,1)S(1)}, u32[]{:S(2)}, u32[]{:S(2)}) collective-permute-start(bf16[256,256]{1,0:T(8,128)(2,1)S(1)} %get-tuple-element.32), channel_id=1, source_target_pairs={{0,6},{2,4},{4,2},{6,0},{1,7},{3,5},{5,3},{7,1},{8,14},{10,12},{12... | collective-permute-start | bytes 393224 | tf_op jit(solution)/shard_map/ppermute | solution.py:201
  33.6 13.6 %collective-permute-start.8 = (bf16[256,256]{1,0:T(8,128)(2,1)S(1)}, bf16[256,256]{1,0:T(8,128)(2,1)S(1)}, u32[]{:S(2)}, u32[]{:S(2)}) collective-permute-start(bf16[256,256]{1,0:T(8,128)(2,1)S(1)} %get-tuple-element.30), channel_id=1, source_target_pairs={{0,2},{2,0},{4,6},{6,4},{1,3},{3,1},{5,7},{7,5},{8,10},{10,8},{12,... | collective-permute-start | bytes 393224 | tf_op jit(solution)/shard_map/ppermute | solution.py:201
  34.1 13.1 %collective-permute-start.9 = (bf16[256,256]{1,0:T(8,128)(2,1)S(1)}, bf16[256,256]{1,0:T(8,128)(2,1)S(1)}, u32[]{:S(2)}, u32[]{:S(2)}) collective-permute-start(bf16[256,256]{1,0:T(8,128)(2,1)S(1)} %get-tuple-element.31), channel_id=1, source_target_pairs={{0,4},{2,6},{4,0},{6,2},{1,5},{3,7},{5,1},{7,3},{8,12},{10,14},{12... | collective-permute-start | bytes 393224 | tf_op jit(solution)/shard_map/ppermute | solution.py:201
  42.7 4.6 %copy-start.8 = (bf16[128,256]{1,0:T(8,128)(2,1)}, bf16[128,256]{1,0:T(8,128)(2,1)S(1)}, u32[]{:S(2)}) copy-start(bf16[128,256]{1,0:T(8,128)(2,1)S(1)} %get-tuple-element.37.refs_4_) | copy-start | bytes 196612
  42.8 4.6 %copy-start.9 = (bf16[128,256]{1,0:T(8,128)(2,1)}, bf16[128,256]{1,0:T(8,128)(2,1)S(1)}, u32[]{:S(2)}) copy-start(bf16[128,256]{1,0:T(8,128)(2,1)S(1)} %get-tuple-element.38.refs_5_) | copy-start | bytes 196612
  42.8 4.6 %copy-start.5 = (bf16[128,2048]{1,0:T(8,128)(2,1)}, bf16[128,2048]{1,0:T(8,128)(2,1)S(1)}, u32[]{:S(2)}) copy-start(bf16[128,2048]{1,0:T(8,128)(2,1)S(1)} %get-tuple-element.36.refs_3_) | copy-start | bytes 1572868
  42.8 7.6 %collective-permute-start.14 = (bf16[256,256]{1,0:T(8,128)(2,1)S(1)}, bf16[256,256]{1,0:T(8,128)(2,1)S(1)}, u32[]{:S(2)}, u32[]{:S(2)}) collective-permute-start(bf16[256,256]{1,0:T(8,128)(2,1)S(1)} %get-tuple-element.43), channel_id=1, source_target_pairs={{0,2},{2,0},{4,6},{6,4},{1,3},{3,1},{5,7},{7,5},{8,10},{10,8},{12,... | collective-permute-start | bytes 393224 | tf_op jit(solution)/shard_map/ppermute | solution.py:201
  43.9 8.7 %collective-permute-start.15 = (bf16[256,256]{1,0:T(8,128)(2,1)S(1)}, bf16[256,256]{1,0:T(8,128)(2,1)S(1)}, u32[]{:S(2)}, u32[]{:S(2)}) collective-permute-start(bf16[256,256]{1,0:T(8,128)(2,1)S(1)} %get-tuple-element.44), channel_id=1, source_target_pairs={{0,4},{2,6},{4,0},{6,2},{1,5},{3,7},{5,1},{7,3},{8,12},{10,14},{12... | collective-permute-start | bytes 393224 | tf_op jit(solution)/shard_map/ppermute | solution.py:201
  44.9 7.7 %collective-permute-start.16 = (bf16[256,256]{1,0:T(8,128)(2,1)S(1)}, bf16[256,256]{1,0:T(8,128)(2,1)S(1)}, u32[]{:S(2)}, u32[]{:S(2)}) collective-permute-start(bf16[256,256]{1,0:T(8,128)(2,1)S(1)} %get-tuple-element.45), channel_id=1, source_target_pairs={{0,6},{2,4},{4,2},{6,0},{1,7},{3,5},{5,3},{7,1},{8,14},{10,12},{12... | collective-permute-start | bytes 393224 | tf_op jit(solution)/shard_map/ppermute | solution.py:201
  47.4 1.5 %collective-permute-start.11 = (f32[8,128]{1,0:T(8,128)S(1)}, f32[8,128]{1,0:T(8,128)S(1)}, u32[]{:S(2)}, u32[]{:S(2)}) collective-permute-start(f32[8,128]{1,0:T(8,128)S(1)} %fusion.1), channel_id=1, source_target_pairs={{0,8},{8,0},{16,24},{24,16},{1,9},{9,1},{17,25},{25,17},{2,10},{10... | collective-permute-start | bytes 12296 | tf_op jit(solution)/shard_map/ppermute | solution.py:201
  47.5 10.6 %collective-permute-start.13 = (bf16[128,256]{1,0:T(8,128)(2,1)S(1)}, bf16[128,256]{1,0:T(8,128)(2,1)S(1)}, u32[]{:S(2)}, u32[]{:S(2)}) collective-permute-start(bf16[128,256]{1,0:T(8,128)(2,1)S(1)} %pad_maximum_fusion.3), channel_id=1, source_target_pairs={{0,1},{1,0},{2,3},{3,2},{4,5},{5,4},{6,7},{7,6},{8,9},{9,8},{10,11... | collective-permute-start | bytes 196616 | tf_op jit(solution)/shard_map/ppermute | solution.py:201
  48.9 5.4 %collective-permute-start.12 = (f32[8,128]{1,0:T(8,128)S(1)}, f32[8,128]{1,0:T(8,128)S(1)}, u32[]{:S(2)}, u32[]{:S(2)}) collective-permute-start(f32[8,128]{1,0:T(8,128)S(1)} %add.69), channel_id=1, source_target_pairs={{0,16},{8,24},{16,0},{24,8},{1,17},{9,25},{17,1},{25,9},{2,18},{10... | collective-permute-start | bytes 12296 | tf_op jit(solution)/shard_map/ppermute | solution.py:201
  52.7 5.3 %collective-permute-start.17 = (bf16[128,256]{1,0:T(8,128)(2,1)S(1)}, bf16[128,256]{1,0:T(8,128)(2,1)S(1)}, u32[]{:S(2)}, u32[]{:S(2)}) collective-permute-start(bf16[128,256]{1,0:T(8,128)(2,1)S(1)} %pad_maximum_fusion.4), channel_id=1, source_target_pairs={{0,1},{1,0},{2,3},{3,2},{4,5},{5,4},{6,7},{7,6},{8,9},{9,8},{10,11... | collective-permute-start | bytes 196616 | tf_op jit(solution)/shard_map/ppermute | solution.py:201
  54.3 1.2 %copy-start.13 = (f32[8,128]{1,0:T(8,128)}, f32[8,128]{1,0:T(8,128)S(1)}, u32[]{:S(2)}) copy-start(f32[8,128]{1,0:T(8,128)S(1)} %add.70.total_ref) | copy-start | bytes 12292

commit v8 on v7

--- a/solution.py
+++ b/solution.py
@@ -15,6 +15,7 @@
 EXTRA = 16
 STEP = 64
 VMEM_LIMIT = 40 * 1024 * 1024
+SMALL_LIMIT = 8 * 1024 * 1024
 NT = (((1,), (1,)), ((), ()))
 
 
@@ -289,6 +290,7 @@
         in_specs=[pl.BlockSpec((rows, GROUP * HD), lambda j: (0, j)), HBM],
         out_specs=pl.BlockSpec((1, HD, GROUP * rows), lambda j: (j, 0, 0)),
         out_shape=jax.ShapeDtypeStruct((heads, HD, GROUP * rows), do.dtype),
+        compiler_params=pltpu.CompilerParams(vmem_limit_bytes=SMALL_LIMIT),
         name="turn",
     )(do, after)
 
@@ -338,6 +340,7 @@
         out_shape=shapes,
         scratch_shapes=[pltpu.VMEM(x.shape, x.dtype) for x in shapes]
         + [pltpu.SemaphoreType.DMA((CHUNKS, len(shapes)))],
+        compiler_params=pltpu.CompilerParams(vmem_limit_bytes=SMALL_LIMIT),
         cost_estimate=pl.CostEstimate(
             flops=sum(x.size for x in shapes),
             bytes_accessed=sum(4 * x.size for x in shapes),
@@ -362,7 +365,7 @@
     next_results = attend(1, held, next_slots, length, q, turned, k, v, results[:1])
     sums = [line_reduce(results[4:]), line_reduce(next_results[4:-1])]
     total = sum_over(next_results[-1] + 0 * sums[0][:8, :HD], "prompt")
-    weight = slots_all / total[0, 0]
+    weight = jnp.tile(slots_all / total[:1], (1, prefix[0].shape[1] // HD))
     scaled = scale_all(
         slots_all, total, [results[1:4], next_results[1:4]], [like(q), like(k), like(v)]
     )

time: 60 us -> 57.7 us (0.962)
  waiting for transfers between devices: 3.15 us -> 10.4 us
  Pallas kernels: 18.6 us -> 14.3 us
  local copies, waits for them, and re-layouts: 6.29 us -> 2.55 us
  between operations: 2.29 us -> 1.51 us
  other arithmetic: 1.63 us -> 1.01 us
    ppermute x18, waiting for transfers between devices: 3.15 us -> 10.4 us  [swap(): lax.ppermute(x, axis, [(i, i ^ by) for i in range(lax.axis_size(axis))])]
    unnamed x32 -> x12, local copies, waits for them, and re-layouts: 4.87 us -> 1.56 us
    pallas_call x1, Pallas kernels: 3.68 us -> 0.62 us  [turn(): pl.pallas_call(turn_kernel, grid=(heads,), in_specs=[pl.BlockSpec((rows,...]
    pallas_call x1, Pallas kernels: 2.54 us -> 1.27 us  [scale_all(): pl.pallas_call(functools.partial(scale_kernel, slots_all), in_specs=[VMEM...]
    convert_element_type x2 -> x1, other arithmetic: 1.37 us -> 0.75 us  [body(): (grad.astype(jnp.float32) * weight).astype(jnp.bfloat16)]
  transfers between devices with their start and end apart: 18 -> 18, of which waited for: 2 -> 5; matrix products, arithmetic and copies ran while one was open for 4% -> 3% of each run, Pallas kernels for 31% -> 25%
where the time goes in v8:
time: 57.7 us; the launch traced here: 57.5 us
  starting transfers between devices  27.8 us (48%)
  Pallas kernels  14.3 us (25%)
  waiting for transfers between devices  10.4 us (18%)
  local copies, waits for them, and re-layouts  2.55 us (4%)
  between operations  1.51 us (3%)
  other arithmetic  1.01 us (2%)
    ppermute x18, starting transfers between devices, swap(): lax.ppermute(x, axis, [(i, i ^ by) for i in range(lax.axis_size(axis))])  27.8 us
    pallas_call x2, Pallas kernels, attend(): pl.pallas_call(functools.partial(attend_kernel, n_slots, count, chunk, he...  12.4 us
    ppermute x18, waiting for transfers between devices, swap(): lax.ppermute(x, axis, [(i, i ^ by) for i in range(lax.axis_size(axis))])  10.4 us
    unnamed x12, local copies, waits for them, and re-layouts  1.56 us
    pallas_call x1, Pallas kernels, scale_all(): pl.pallas_call(functools.partial(scale_kernel, slots_all), in_specs=[VMEM...  1.27 us
  transfers between devices with their start and end apart: 18, of which 5 were waited for; matrix products, arithmetic and copies ran while one was open for 3% of the time, Pallas kernels for 25%

profile of v8, /device:TPU:0, one launch (start us, length us, event | category | flops | bytes accessed | tf_op | source)
XLA Modules:
  0.0 57.5 jit_solution(11281672640935661327)
XLA Ops:
  0.6 0.0 copy-start
  0.7 0.9 %dynamic-slice_bitcast_fusion = (bf16[64,256]{1,0:T(8,128)(2,1)S(1)}, bf16[64,256]{1,0:T(8,128)(2,1)S(1)}, bf16[64,256]{1,0:T(8,128)(2,1)S(1)}, bf16[64,256]{1,0...) fusion(bf16[1,64,1024]{2,1,0:T(8,128)(2,1)} %param.11, s32[]{:T(128)S(6)} %select_n.65, ...), kind=kLoop, calls=%fused_computation.21 | loop fusion | bytes 393228 | tf_op jit(solution)/shard_map/dynamic_slice | solution.py:231
  1.6 3.0 %collective-permute-start = (bf16[128,256]{1,0:T(8,128)(2,1)S(1)}, bf16[128,256]{1,0:T(8,128)(2,1)S(1)}, u32[]{:S(2)}, u32[]{:S(2)}) collective-permute-start(bf16[128,256]{1,0:T(8,128)(2,1)S(1)} %pad_maximum_fusion.1), channel_id=1, source_target_pairs={{0,1},{1,0},{2,3},{3,2},{4,5},{5,4},{6,7},{7,6},{8,9},{9,8},{10,11... | collective-permute-start | bytes 196616 | tf_op jit(solution)/shard_map/ppermute | solution.py:202
  4.7 0.1 collective-permute-start.1
  5.4 0.8 %bitcast_dynamic-update-slice_fusion.1 = bf16[272,256]{1,0:T(8,128)(2,1)S(1)} fusion(bf16[1,64,1024]{2,1,0:T(8,128)(2,1)} %param.10, s32[]{:T(128)S(6)} %select_n.64), kind=kLoop, calls=%fused_computation.20 | loop fusion | bytes 65540
  6.2 0.9 %collective-permute-done = bf16[128,256]{1,0:T(8,128)(2,1)S(1)} collective-permute-done((bf16[128,256]{1,0:T(8,128)(2,1)S(1)}, bf16[128,256]{1,0:T(8,128)(2,1)S(1)}, u32[]{:S(2)}, u32[]{:S(2)}) %collective-permute-start) | collective-permute-done | bytes 65568 | tf_op jit(solution)/shard_map/ppermute | solution.py:202
  7.1 4.6 %collective-permute-start.2 = (bf16[256,256]{1,0:T(8,128)(2,1)S(1)}, bf16[256,256]{1,0:T(8,128)(2,1)S(1)}, u32[]{:S(2)}, u32[]{:S(2)}) collective-permute-start(bf16[256,256]{1,0:T(8,128)(2,1)S(1)} %pad_maximum_fusion.after_ref.refs_5_), channel_id=1, source_target_pairs={{0,6},{2,4},{4,2},{6,0},{1,7},{3,5},{5,3},{7,1},{8,14},{10,12},{12... | collective-permute-start | bytes 393224 | tf_op jit(solution)/shard_map/ppermute | solution.py:202
  11.7 0.0 collective-permute-start.6
  11.7 0.0 copy-done
  11.7 0.0 copy-start.1
  11.7 0.0 copy-start.3
  11.7 0.6 %turn.1.refs_2_ = bf16[4,128,1024]{2,1,0:T(8,128)(2,1)S(1)} custom-call(bf16[128,4096]{1,0:T(8,128)(2,1)S(1)} %bitcast.40, bf16[256,256]{1,0:T(8,128)(2,1)S(1)} %pad_maximum_fusion.after_ref.refs_5_), custom_call_target="tpu_custom_call" | custom-call | tf_op jit(solution)/shard_map/turn/pallas_call | solution.py:287
  12.3 0.0 copy-start.2
  12.3 0.0 collective-permute-done.1
  12.4 0.8 %bitcast_dynamic-update-slice_fusion = bf16[272,256]{1,0:T(8,128)(2,1)S(1)} fusion(bf16[272,256]{1,0:T(8,128)(2,1)S(1)} %slice_dynamic-update-slice_fusion.1, bf16[1,64,1024]{2,1,0:T(8,128)(2,1)} %param.11, s32[]{:T(128)S(6)} %select_n.64), kind=kLoop, calls=%fused_computation.19 | loop fusion | bytes 65540
  13.1 2.1 %collective-permute-done.2.refs_8_ = bf16[256,256]{1,0:T(8,128)(2,1)S(1)} collective-permute-done((bf16[256,256]{1,0:T(8,128)(2,1)S(1)}, bf16[256,256]{1,0:T(8,128)(2,1)S(1)}, u32[]{:S(2)}, u32[]{:S(2)}) %collective-permute-start.2) | collective-permute-done | bytes 131104 | tf_op jit(solution)/shard_map/ppermute | solution.py:202
  15.2 0.8 %collective-permute-start.7 = (bf16[256,256]{1,0:T(8,128)(2,1)S(1)}, bf16[256,256]{1,0:T(8,128)(2,1)S(1)}, u32[]{:S(2)}, u32[]{:S(2)}) collective-permute-start(bf16[256,256]{1,0:T(8,128)(2,1)S(1)} %collective-permute-done.2.refs_8_), channel_id=1, source_target_pairs={{0,2},{2,0},{4,6},{6,4},{1,3},{3,1},{5,7},{7,5},{8,10},{10,8},{12,... | collective-permute-start | bytes 393224 | tf_op jit(solution)/shard_map/ppermute | solution.py:202
  16.0 1.2 %collective-permute-start.3 = (bf16[272,256]{1,0:T(8,128)(2,1)S(1)}, bf16[272,256]{1,0:T(8,128)(2,1)S(1)}, u32[]{:S(2)}, u32[]{:S(2)}) collective-permute-start(bf16[272,256]{1,0:T(8,128)(2,1)S(1)} %constant_dynamic-update-slice_fusion.refs_5_), channel_id=1, source_target_pairs={{0,2},{2,0},{4,6},{6,4},{1,3},{3,1},{5,7},{7,5},{8,10},{10,8},{12,... | collective-permute-start | bytes 417800 | tf_op jit(solution)/shard_map/ppermute | solution.py:202
  17.3 2.9 %collective-permute-start.4 = (bf16[272,256]{1,0:T(8,128)(2,1)S(1)}, bf16[272,256]{1,0:T(8,128)(2,1)S(1)}, u32[]{:S(2)}, u32[]{:S(2)}) collective-permute-start(bf16[272,256]{1,0:T(8,128)(2,1)S(1)} %constant_dynamic-update-slice_fusion.refs_5_), channel_id=1, source_target_pairs={{0,4},{2,6},{4,0},{6,2},{1,5},{3,7},{5,1},{7,3},{8,12},{10,14},{12... | collective-permute-start | bytes 417800 | tf_op jit(solution)/shard_map/ppermute | solution.py:202
  20.2 1.4 %collective-permute-start.5 = (bf16[272,256]{1,0:T(8,128)(2,1)S(1)}, bf16[272,256]{1,0:T(8,128)(2,1)S(1)}, u32[]{:S(2)}, u32[]{:S(2)}) collective-permute-start(bf16[272,256]{1,0:T(8,128)(2,1)S(1)} %constant_dynamic-update-slice_fusion.refs_5_), channel_id=1, source_target_pairs={{0,6},{2,4},{4,2},{6,0},{1,7},{3,5},{5,3},{7,1},{8,14},{10,12},{12... | collective-permute-start | bytes 417800 | tf_op jit(solution)/shard_map/ppermute | solution.py:202
  21.6 0.0 collective-permute-done.6.refs_6_
  21.6 3.1 %collective-permute-done.7.refs_7_ = bf16[256,256]{1,0:T(8,128)(2,1)S(1)} collective-permute-done((bf16[256,256]{1,0:T(8,128)(2,1)S(1)}, bf16[256,256]{1,0:T(8,128)(2,1)S(1)}, u32[]{:S(2)}, u32[]{:S(2)}) %collective-permute-start.7) | collective-permute-done | bytes 131104 | tf_op jit(solution)/shard_map/ppermute | solution.py:202
  24.7 0.0 copy-done.1
  24.7 0.0 copy-done.3
  24.7 0.0 copy-done.2
  24.7 6.2 %attend_0.1 = (bf16[128,4096]{1,0:T(8,128)(2,1)}, bf16[128,2048]{1,0:T(8,128)(2,1)S(1)}, bf16[128,256]{1,0:T(8,128)(2,1)S(1)}, bf16[128,256]{1,0:T(8,128)(2,1)S(...) custom-call(s32[1]{0:T(128)} %bitcast.38.refs_0_, ...), custom_call_target="tpu_custom_call" | custom-call | flops 8053063680 | bytes 2097152 | tf_op jit(solution)/shard_map/attend_0/pallas_call | solution.py:317
  30.9 0.1 collective-permute-start.10
  31.0 0.1 collective-permute-start.8
  31.1 0.0 collective-permute-done.3.refs_6_
  31.1 4.3 %collective-permute-start.9 = (bf16[256,256]{1,0:T(8,128)(2,1)S(1)}, bf16[256,256]{1,0:T(8,128)(2,1)S(1)}, u32[]{:S(2)}, u32[]{:S(2)}) collective-permute-start(bf16[256,256]{1,0:T(8,128)(2,1)S(1)} %get-tuple-element.31), channel_id=1, source_target_pairs={{0,4},{2,6},{4,0},{6,2},{1,5},{3,7},{5,1},{7,3},{8,12},{10,14},{12... | collective-permute-start | bytes 393224 | tf_op jit(solution)/shard_map/ppermute | solution.py:202
  35.4 0.0 collective-permute-done.4.refs_7_
  35.4 0.0 collective-permute-done.5.refs_8_
  35.4 6.2 %attend_1.1 = (bf16[128,4096]{1,0:T(8,128)(2,1)}, bf16[128,2048]{1,0:T(8,128)(2,1)S(1)}, bf16[128,256]{1,0:T(8,128)(2,1)S(1)}, bf16[128,256]{1,0:T(8,128)(2,1)S(...) custom-call(s32[1]{0:T(128)} %bitcast.39.refs_0_, ...), custom_call_target="tpu_custom_call", output_to_operand_aliasing={{0}: (9, {})} | custom-call | flops 8053063680 | bytes 2097152 | tf_op jit(solution)/shard_map/attend_1/pallas_call | solution.py:317
  41.6 1.4 %collective-permute-start.14 = (bf16[256,256]{1,0:T(8,128)(2,1)S(1)}, bf16[256,256]{1,0:T(8,128)(2,1)S(1)}, u32[]{:S(2)}, u32[]{:S(2)}) collective-permute-start(bf16[256,256]{1,0:T(8,128)(2,1)S(1)} %get-tuple-element.43), channel_id=1, source_target_pairs={{0,2},{2,0},{4,6},{6,4},{1,3},{3,1},{5,7},{7,5},{8,10},{10,8},{12,... | collective-permute-start | bytes 393224 | tf_op jit(solution)/shard_map/ppermute | solution.py:202
  43.0 2.0 %collective-permute-start.15 = (bf16[256,256]{1,0:T(8,128)(2,1)S(1)}, bf16[256,256]{1,0:T(8,128)(2,1)S(1)}, u32[]{:S(2)}, u32[]{:S(2)}) collective-permute-start(bf16[256,256]{1,0:T(8,128)(2,1)S(1)} %get-tuple-element.44), channel_id=1, source_target_pairs={{0,4},{2,6},{4,0},{6,2},{1,5},{3,7},{5,1},{7,3},{8,12},{10,14},{12... | collective-permute-start | bytes 393224 | tf_op jit(solution)/shard_map/ppermute | solution.py:202
  45.0 0.0 collective-permute-done.10
  45.0 1.4 %collective-permute-start.16 = (bf16[256,256]{1,0:T(8,128)(2,1)S(1)}, bf16[256,256]{1,0:T(8,128)(2,1)S(1)}, u32[]{:S(2)}, u32[]{:S(2)}) collective-permute-start(bf16[256,256]{1,0:T(8,128)(2,1)S(1)} %get-tuple-element.45), channel_id=1, source_target_pairs={{0,6},{2,4},{4,2},{6,0},{1,7},{3,5},{5,3},{7,1},{8,14},{10,12},{12... | collective-permute-start | bytes 393224 | tf_op jit(solution)/shard_map/ppermute | solution.py:202
  46.4 0.0 collective-permute-done.8
  46.4 0.0 collective-permute-done.9
  46.4 0.1 fusion.2
  46.5 0.1 collective-permute-start.11
  46.6 1.5 %collective-permute-start.13 = (bf16[128,256]{1,0:T(8,128)(2,1)S(1)}, bf16[128,256]{1,0:T(8,128)(2,1)S(1)}, u32[]{:S(2)}, u32[]{:S(2)}) collective-permute-start(bf16[128,256]{1,0:T(8,128)(2,1)S(1)} %pad_maximum_fusion.3), channel_id=1, source_target_pairs={{0,1},{1,0},{2,3},{3,2},{4,5},{5,4},{6,7},{7,6},{8,9},{9,8},{10,11... | collective-permute-start | bytes 196616 | tf_op jit(solution)/shard_map/ppermute | solution.py:202
  48.1 0.0 collective-permute-done.11
  48.1 1.5 %collective-permute-start.12 = (f32[8,128]{1,0:T(8,128)S(1)}, f32[8,128]{1,0:T(8,128)S(1)}, u32[]{:S(2)}, u32[]{:S(2)}) collective-permute-start(f32[8,128]{1,0:T(8,128)S(1)} %add.69), channel_id=1, source_target_pairs={{0,16},{8,24},{16,0},{24,8},{1,17},{9,25},{17,1},{25,9},{2,18},{10... | collective-permute-start | bytes 12296 | tf_op jit(solution)/shard_map/ppermute | solution.py:202
  49.6 0.0 collective-permute-done.14
  49.6 0.0 collective-permute-done.15
  49.6 2.7 %collective-permute-done.16 = bf16[256,256]{1,0:T(8,128)(2,1)S(1)} collective-permute-done((bf16[256,256]{1,0:T(8,128)(2,1)S(1)}, bf16[256,256]{1,0:T(8,128)(2,1)S(1)}, u32[]{:S(2)}, u32[]{:S(2)}) %collective-permute-start.16) | collective-permute-done | bytes 131104 | tf_op jit(solution)/shard_map/ppermute | solution.py:202
  52.3 0.1 add_convert_fusion
  52.4 1.5 %collective-permute-start.17 = (bf16[128,256]{1,0:T(8,128)(2,1)S(1)}, bf16[128,256]{1,0:T(8,128)(2,1)S(1)}, u32[]{:S(2)}, u32[]{:S(2)}) collective-permute-start(bf16[128,256]{1,0:T(8,128)(2,1)S(1)} %pad_maximum_fusion.4), channel_id=1, source_target_pairs={{0,1},{1,0},{2,3},{3,2},{4,5},{5,4},{6,7},{7,6},{8,9},{9,8},{10,11... | collective-permute-start | bytes 196616 | tf_op jit(solution)/shard_map/ppermute | solution.py:202
  53.8 0.0 collective-permute-done.12
  53.9 1.3 %scale.1 = (bf16[128,4096]{1,0:T(8,128)(2,1)}, bf16[128,512]{1,0:T(8,128)(2,1)}, bf16[128,512]{1,0:T(8,128)(2,1)}) custom-call(f32[8,128]{1,0:T(8,128)S(1)} %add.70.total_ref, bf16[128,2048]{1,0:T(8,128)(2,1)S(1)} %get-tuple-element.33.refs_0_, bf16[128,256]{1,0:T(8,128)(2,1)S(1)} %get-tuple-element.34.refs_1_, ...), custom_call_target="tpu_custom_call" | custom-call | flops 655360 | bytes 2621440 | tf_op jit(solution)/shard_map/scale/pallas_call | solution.py:336
  55.1 0.0 collective-permute-done.13
  55.2 1.5 %collective-permute-done.17 = bf16[128,256]{1,0:T(8,128)(2,1)S(1)} collective-permute-done((bf16[128,256]{1,0:T(8,128)(2,1)S(1)}, bf16[128,256]{1,0:T(8,128)(2,1)S(1)}, u32[]{:S(2)}, u32[]{:S(2)}) %collective-permute-start.17) | collective-permute-done | bytes 65568 | tf_op jit(solution)/shard_map/ppermute | solution.py:202
  56.8 0.8 %multiply_convert_fusion = (bf16[1,64,1024]{2,1,0:T(8,128)(2,1)}, bf16[1,64,1024]{2,1,0:T(8,128)(2,1)}) fusion(bf16[1,64,512]{2,1,0:T(8,128)(2,1)S(1)} %get-tuple-element.49, bf16[1,64,512]{2,1,0:T(8,128)(2,1)S(1)} %get-tuple-element.48, f32[1024]{0:T(1024)S(1)} %broadcast_bitcast_fusion, bf16[1,64,512]{2,1,0:T(8,128)(2,1)S(1)} %get-tuple-element.59, ...), kind=kLoop, calls=%fused_computation | loop fusion | flops 786432 | bytes 528384 | tf_op jit(solution)/shard_map/convert_element_type | solution.py:374
  (20 shorter events, 0.2 us)
Async XLA Ops:
  0.6 11.0 %copy-start = (bf16[1,128,4096]{2,1,0:T(8,128)(2,1)S(1)}, bf16[1,128,4096]{2,1,0:T(8,128)(2,1)}, u32[]{:S(2)}) copy-start(bf16[1,128,4096]{2,1,0:T(8,128)(2,1)} %param.13) | copy-start | bytes 3145732
  1.6 5.4 %collective-permute-start = (bf16[128,256]{1,0:T(8,128)(2,1)S(1)}, bf16[128,256]{1,0:T(8,128)(2,1)S(1)}, u32[]{:S(2)}, u32[]{:S(2)}) collective-permute-start(bf16[128,256]{1,0:T(8,128)(2,1)S(1)} %pad_maximum_fusion.1), channel_id=1, source_target_pairs={{0,1},{1,0},{2,3},{3,2},{4,5},{5,4},{6,7},{7,6},{8,9},{9,8},{10,11... | collective-permute-start | bytes 196616 | tf_op jit(solution)/shard_map/ppermute | solution.py:202
  4.7 7.7 %collective-permute-start.1 = (bf16[128,256]{1,0:T(8,128)(2,1)S(1)}, bf16[128,256]{1,0:T(8,128)(2,1)S(1)}, u32[]{:S(2)}, u32[]{:S(2)}) collective-permute-start(bf16[128,256]{1,0:T(8,128)(2,1)S(1)} %pad_maximum_fusion.2), channel_id=1, source_target_pairs={{0,1},{1,0},{2,3},{3,2},{4,5},{5,4},{6,7},{7,6},{8,9},{9,8},{10,11... | collective-permute-start | bytes 196616 | tf_op jit(solution)/shard_map/ppermute | solution.py:202
  7.1 8.2 %collective-permute-start.2 = (bf16[256,256]{1,0:T(8,128)(2,1)S(1)}, bf16[256,256]{1,0:T(8,128)(2,1)S(1)}, u32[]{:S(2)}, u32[]{:S(2)}) collective-permute-start(bf16[256,256]{1,0:T(8,128)(2,1)S(1)} %pad_maximum_fusion.after_ref.refs_5_), channel_id=1, source_target_pairs={{0,6},{2,4},{4,2},{6,0},{1,7},{3,5},{5,3},{7,1},{8,14},{10,12},{12... | collective-permute-start | bytes 393224 | tf_op jit(solution)/shard_map/ppermute | solution.py:202
  11.7 9.9 %collective-permute-start.6 = (bf16[256,256]{1,0:T(8,128)(2,1)S(1)}, bf16[256,256]{1,0:T(8,128)(2,1)S(1)}, u32[]{:S(2)}, u32[]{:S(2)}) collective-permute-start(bf16[256,256]{1,0:T(8,128)(2,1)S(1)} %pad_maximum_fusion.after_ref.refs_5_), channel_id=1, source_target_pairs={{0,2},{2,0},{4,6},{6,4},{1,3},{3,1},{5,7},{7,5},{8,10},{10,8},{12,... | collective-permute-start | bytes 393224 | tf_op jit(solution)/shard_map/ppermute | solution.py:202
  11.7 13.0 %copy-start.1 = (bf16[1,128,4096]{2,1,0:T(8,128)(2,1)S(1)}, bf16[1,128,4096]{2,1,0:T(8,128)(2,1)}, u32[]{:S(2)}) copy-start(bf16[1,128,4096]{2,1,0:T(8,128)(2,1)} %param.7) | copy-start | bytes 3145732
  11.7 13.0 %copy-start.3 = (bf16[1,128,512]{2,1,0:T(8,128)(2,1)S(1)}, bf16[1,128,512]{2,1,0:T(8,128)(2,1)}, u32[]{:S(2)}) copy-start(bf16[1,128,512]{2,1,0:T(8,128)(2,1)} %param.9) | copy-start | bytes 393220
  12.3 12.4 %copy-start.2 = (bf16[1,128,512]{2,1,0:T(8,128)(2,1)S(1)}, bf16[1,128,512]{2,1,0:T(8,128)(2,1)}, u32[]{:S(2)}) copy-start(bf16[1,128,512]{2,1,0:T(8,128)(2,1)} %param.8) | copy-start | bytes 393220
  15.2 9.5 %collective-permute-start.7 = (bf16[256,256]{1,0:T(8,128)(2,1)S(1)}, bf16[256,256]{1,0:T(8,128)(2,1)S(1)}, u32[]{:S(2)}, u32[]{:S(2)}) collective-permute-start(bf16[256,256]{1,0:T(8,128)(2,1)S(1)} %collective-permute-done.2.refs_8_), channel_id=1, source_target_pairs={{0,2},{2,0},{4,6},{6,4},{1,3},{3,1},{5,7},{7,5},{8,10},{10,8},{12,... | collective-permute-start | bytes 393224 | tf_op jit(solution)/shard_map/ppermute | solution.py:202
  16.0 15.1 %collective-permute-start.3 = (bf16[272,256]{1,0:T(8,128)(2,1)S(1)}, bf16[272,256]{1,0:T(8,128)(2,1)S(1)}, u32[]{:S(2)}, u32[]{:S(2)}) collective-permute-start(bf16[272,256]{1,0:T(8,128)(2,1)S(1)} %constant_dynamic-update-slice_fusion.refs_5_), channel_id=1, source_target_pairs={{0,2},{2,0},{4,6},{6,4},{1,3},{3,1},{5,7},{7,5},{8,10},{10,8},{12,... | collective-permute-start | bytes 417800 | tf_op jit(solution)/shard_map/ppermute | solution.py:202
  17.3 18.1 %collective-permute-start.4 = (bf16[272,256]{1,0:T(8,128)(2,1)S(1)}, bf16[272,256]{1,0:T(8,128)(2,1)S(1)}, u32[]{:S(2)}, u32[]{:S(2)}) collective-permute-start(bf16[272,256]{1,0:T(8,128)(2,1)S(1)} %constant_dynamic-update-slice_fusion.refs_5_), channel_id=1, source_target_pairs={{0,4},{2,6},{4,0},{6,2},{1,5},{3,7},{5,1},{7,3},{8,12},{10,14},{12... | collective-permute-start | bytes 417800 | tf_op jit(solution)/shard_map/ppermute | solution.py:202
  20.2 15.2 %collective-permute-start.5 = (bf16[272,256]{1,0:T(8,128)(2,1)S(1)}, bf16[272,256]{1,0:T(8,128)(2,1)S(1)}, u32[]{:S(2)}, u32[]{:S(2)}) collective-permute-start(bf16[272,256]{1,0:T(8,128)(2,1)S(1)} %constant_dynamic-update-slice_fusion.refs_5_), channel_id=1, source_target_pairs={{0,6},{2,4},{4,2},{6,0},{1,7},{3,5},{5,3},{7,1},{8,14},{10,12},{12... | collective-permute-start | bytes 417800 | tf_op jit(solution)/shard_map/ppermute | solution.py:202
  30.9 14.1 %collective-permute-start.10 = (bf16[256,256]{1,0:T(8,128)(2,1)S(1)}, bf16[256,256]{1,0:T(8,128)(2,1)S(1)}, u32[]{:S(2)}, u32[]{:S(2)}) collective-permute-start(bf16[256,256]{1,0:T(8,128)(2,1)S(1)} %get-tuple-element.32), channel_id=1, source_target_pairs={{0,6},{2,4},{4,2},{6,0},{1,7},{3,5},{5,3},{7,1},{8,14},{10,12},{12... | collective-permute-start | bytes 393224 | tf_op jit(solution)/shard_map/ppermute | solution.py:202
  31.0 15.4 %collective-permute-start.8 = (bf16[256,256]{1,0:T(8,128)(2,1)S(1)}, bf16[256,256]{1,0:T(8,128)(2,1)S(1)}, u32[]{:S(2)}, u32[]{:S(2)}) collective-permute-start(bf16[256,256]{1,0:T(8,128)(2,1)S(1)} %get-tuple-element.30), channel_id=1, source_target_pairs={{0,2},{2,0},{4,6},{6,4},{1,3},{3,1},{5,7},{7,5},{8,10},{10,8},{12,... | collective-permute-start | bytes 393224 | tf_op jit(solution)/shard_map/ppermute | solution.py:202
  31.1 15.3 %collective-permute-start.9 = (bf16[256,256]{1,0:T(8,128)(2,1)S(1)}, bf16[256,256]{1,0:T(8,128)(2,1)S(1)}, u32[]{:S(2)}, u32[]{:S(2)}) collective-permute-start(bf16[256,256]{1,0:T(8,128)(2,1)S(1)} %get-tuple-element.31), channel_id=1, source_target_pairs={{0,4},{2,6},{4,0},{6,2},{1,5},{3,7},{5,1},{7,3},{8,12},{10,14},{12... | collective-permute-start | bytes 393224 | tf_op jit(solution)/shard_map/ppermute | solution.py:202
  41.6 8.0 %collective-permute-start.14 = (bf16[256,256]{1,0:T(8,128)(2,1)S(1)}, bf16[256,256]{1,0:T(8,128)(2,1)S(1)}, u32[]{:S(2)}, u32[]{:S(2)}) collective-permute-start(bf16[256,256]{1,0:T(8,128)(2,1)S(1)} %get-tuple-element.43), channel_id=1, source_target_pairs={{0,2},{2,0},{4,6},{6,4},{1,3},{3,1},{5,7},{7,5},{8,10},{10,8},{12,... | collective-permute-start | bytes 393224 | tf_op jit(solution)/shard_map/ppermute | solution.py:202
  43.0 6.6 %collective-permute-start.15 = (bf16[256,256]{1,0:T(8,128)(2,1)S(1)}, bf16[256,256]{1,0:T(8,128)(2,1)S(1)}, u32[]{:S(2)}, u32[]{:S(2)}) collective-permute-start(bf16[256,256]{1,0:T(8,128)(2,1)S(1)} %get-tuple-element.44), channel_id=1, source_target_pairs={{0,4},{2,6},{4,0},{6,2},{1,5},{3,7},{5,1},{7,3},{8,12},{10,14},{12... | collective-permute-start | bytes 393224 | tf_op jit(solution)/shard_map/ppermute | solution.py:202
  45.0 7.2 %collective-permute-start.16 = (bf16[256,256]{1,0:T(8,128)(2,1)S(1)}, bf16[256,256]{1,0:T(8,128)(2,1)S(1)}, u32[]{:S(2)}, u32[]{:S(2)}) collective-permute-start(bf16[256,256]{1,0:T(8,128)(2,1)S(1)} %get-tuple-element.45), channel_id=1, source_target_pairs={{0,6},{2,4},{4,2},{6,0},{1,7},{3,5},{5,3},{7,1},{8,14},{10,12},{12... | collective-permute-start | bytes 393224 | tf_op jit(solution)/shard_map/ppermute | solution.py:202
  46.5 1.6 %collective-permute-start.11 = (f32[8,128]{1,0:T(8,128)S(1)}, f32[8,128]{1,0:T(8,128)S(1)}, u32[]{:S(2)}, u32[]{:S(2)}) collective-permute-start(f32[8,128]{1,0:T(8,128)S(1)} %fusion.1), channel_id=1, source_target_pairs={{0,8},{8,0},{16,24},{24,16},{1,9},{9,1},{17,25},{25,17},{2,10},{10... | collective-permute-start | bytes 12296 | tf_op jit(solution)/shard_map/ppermute | solution.py:202
  46.6 8.5 %collective-permute-start.13 = (bf16[128,256]{1,0:T(8,128)(2,1)S(1)}, bf16[128,256]{1,0:T(8,128)(2,1)S(1)}, u32[]{:S(2)}, u32[]{:S(2)}) collective-permute-start(bf16[128,256]{1,0:T(8,128)(2,1)S(1)} %pad_maximum_fusion.3), channel_id=1, source_target_pairs={{0,1},{1,0},{2,3},{3,2},{4,5},{5,4},{6,7},{7,6},{8,9},{9,8},{10,11... | collective-permute-start | bytes 196616 | tf_op jit(solution)/shard_map/ppermute | solution.py:202
  48.1 5.7 %collective-permute-start.12 = (f32[8,128]{1,0:T(8,128)S(1)}, f32[8,128]{1,0:T(8,128)S(1)}, u32[]{:S(2)}, u32[]{:S(2)}) collective-permute-start(f32[8,128]{1,0:T(8,128)S(1)} %add.69), channel_id=1, source_target_pairs={{0,16},{8,24},{16,0},{24,8},{1,17},{9,25},{17,1},{25,9},{2,18},{10... | collective-permute-start | bytes 12296 | tf_op jit(solution)/shard_map/ppermute | solution.py:202
  52.4 4.3 %collective-permute-start.17 = (bf16[128,256]{1,0:T(8,128)(2,1)S(1)}, bf16[128,256]{1,0:T(8,128)(2,1)S(1)}, u32[]{:S(2)}, u32[]{:S(2)}) collective-permute-start(bf16[128,256]{1,0:T(8,128)(2,1)S(1)} %pad_maximum_fusion.4), channel_id=1, source_target_pairs={{0,1},{1,0},{2,3},{3,2},{4,5},{5,4},{6,7},{7,6},{8,9},{9,8},{10,11... | collective-permute-start | bytes 196616 | tf_op jit(solution)/shard_map/ppermute | solution.py:202

commit v9 on v8

--- a/solution.py
+++ b/solution.py
@@ -220,9 +220,8 @@
 
 
 def line_reduce(slots):
-    terms = [slots[0]] + [swap(slots[m], "response", m) for m in range(1, len(slots))]
-    total = functools.reduce(jnp.add, [term.astype(jnp.float32) for term in terms])
-    return total
+    terms = [swap(slots[m], "response", m) for m in range(len(slots) - 1, 0, -1)]
+    return functools.reduce(jnp.add, [term.astype(jnp.float32) for term in [slots[0]] + terms])
 
 
 def own_columns(block, chunk, by):
@@ -358,9 +357,9 @@
     first, second = [tensor_gather(prefix, chunk) for chunk in range(CHUNKS)]
     held = first.shape[0] // 2
     slots = line_gather(first, True)
-    length_rows = length[0].astype(second.dtype) + 0 * slots[-1][-EXTRA:]
+    turned = turn(do, slots[-1])
+    length_rows = length[0].astype(second.dtype) + 0 * turned[0, :EXTRA, : second.shape[1]]
     next_slots = line_gather(jnp.concatenate([second, length_rows], axis=0), False)
-    turned = turn(do, first)
     results = attend(0, held, slots, length, q, turned, k, v, [])
     next_results = attend(1, held, next_slots, length, q, turned, k, v, results[:1])
     sums = [line_reduce(results[4:]), line_reduce(next_results[4:-1])]

time: 57.7 us -> 60.7 us (1.052)
  starting transfers between devices: 27.8 us -> 34.5 us
  waiting for transfers between devices: 10.4 us -> 6.65 us
    ppermute x18, starting transfers between devices: 27.8 us -> 34.5 us  [swap(): lax.ppermute(x, axis, [(i, i ^ by) for i in range(lax.axis_size(axis))])]
    ppermute x18, waiting for transfers between devices: 10.4 us -> 6.65 us  [swap(): lax.ppermute(x, axis, [(i, i ^ by) for i in range(lax.axis_size(axis))])]
  transfers between devices with their start and end apart: 18 -> 18, of which waited for: 5 -> 6; matrix products, arithmetic and copies ran while one was open for 3% -> 3% of each run, Pallas kernels for 25% -> 24%
where the time goes in v9:
time: 60.7 us; the launch traced here: 60.4 us
  starting transfers between devices  34.5 us (57%)
  Pallas kernels  14.3 us (24%)
  waiting for transfers between devices  6.65 us (11%)
  local copies, waits for them, and re-layouts  2.55 us (4%)
  between operations  1.49 us (2%)
  other arithmetic  1.01 us (2%)
    ppermute x18, starting transfers between devices, swap(): lax.ppermute(x, axis, [(i, i ^ by) for i in range(lax.axis_size(axis))])  34.5 us
    pallas_call x2, Pallas kernels, attend(): pl.pallas_call(functools.partial(attend_kernel, n_slots, count, chunk, he...  12.4 us
    ppermute x18, waiting for transfers between devices, swap(): lax.ppermute(x, axis, [(i, i ^ by) for i in range(lax.axis_size(axis))])  6.65 us
    unnamed x12, local copies, waits for them, and re-layouts  1.56 us
    pallas_call x1, Pallas kernels, scale_all(): pl.pallas_call(functools.partial(scale_kernel, slots_all), in_specs=[VMEM...  1.27 us
  transfers between devices with their start and end apart: 18, of which 6 were waited for; matrix products, arithmetic and copies ran while one was open for 3% of the time, Pallas kernels for 24%

profile of v9, /device:TPU:0, one launch (start us, length us, event | category | flops | bytes accessed | tf_op | source)
XLA Modules:
  0.0 60.4 jit_solution(1834545365651729387)
XLA Ops:
  0.6 0.0 copy-start
  0.7 0.9 %dynamic-slice_bitcast_fusion = (bf16[64,256]{1,0:T(8,128)(2,1)S(1)}, bf16[64,256]{1,0:T(8,128)(2,1)S(1)}, bf16[64,256]{1,0:T(8,128)(2,1)S(1)}, bf16[64,256]{1,0...) fusion(bf16[1,64,1024]{2,1,0:T(8,128)(2,1)} %param.11, s32[]{:T(128)S(6)} %select_n.65, ...), kind=kLoop, calls=%fused_computation.21 | loop fusion | bytes 393228 | tf_op jit(solution)/shard_map/dynamic_slice | solution.py:230
  1.6 3.0 %collective-permute-start = (bf16[128,256]{1,0:T(8,128)(2,1)S(1)}, bf16[128,256]{1,0:T(8,128)(2,1)S(1)}, u32[]{:S(2)}, u32[]{:S(2)}) collective-permute-start(bf16[128,256]{1,0:T(8,128)(2,1)S(1)} %pad_maximum_fusion.1), channel_id=1, source_target_pairs={{0,1},{1,0},{2,3},{3,2},{4,5},{5,4},{6,7},{7,6},{8,9},{9,8},{10,11... | collective-permute-start | bytes 196616 | tf_op jit(solution)/shard_map/ppermute | solution.py:202
  4.7 0.1 collective-permute-start.2
  5.4 0.8 %bitcast_dynamic-update-slice_fusion.1 = bf16[272,256]{1,0:T(8,128)(2,1)S(1)} fusion(bf16[1,64,1024]{2,1,0:T(8,128)(2,1)} %param.10, s32[]{:T(128)S(6)} %select_n.64), kind=kLoop, calls=%fused_computation.20 | loop fusion | bytes 65540
  6.2 0.9 %collective-permute-done = bf16[128,256]{1,0:T(8,128)(2,1)S(1)} collective-permute-done((bf16[128,256]{1,0:T(8,128)(2,1)S(1)}, bf16[128,256]{1,0:T(8,128)(2,1)S(1)}, u32[]{:S(2)}, u32[]{:S(2)}) %collective-permute-start) | collective-permute-done | bytes 65568 | tf_op jit(solution)/shard_map/ppermute | solution.py:202
  7.1 4.6 %collective-permute-start.1 = (bf16[256,256]{1,0:T(8,128)(2,1)S(1)}, bf16[256,256]{1,0:T(8,128)(2,1)S(1)}, u32[]{:S(2)}, u32[]{:S(2)}) collective-permute-start(bf16[256,256]{1,0:T(8,128)(2,1)S(1)} %pad_maximum_fusion.refs_5_), channel_id=1, source_target_pairs={{0,6},{2,4},{4,2},{6,0},{1,7},{3,5},{5,3},{7,1},{8,14},{10,12},{12... | collective-permute-start | bytes 393224 | tf_op jit(solution)/shard_map/ppermute | solution.py:202
  11.7 0.0 collective-permute-start.6
  11.7 0.0 collective-permute-done.2
  11.7 0.8 %bitcast_dynamic-update-slice_fusion = bf16[272,256]{1,0:T(8,128)(2,1)S(1)} fusion(bf16[272,256]{1,0:T(8,128)(2,1)S(1)} %slice_dynamic-update-slice_fusion.1, bf16[1,64,1024]{2,1,0:T(8,128)(2,1)} %param.11, s32[]{:T(128)S(6)} %select_n.64), kind=kLoop, calls=%fused_computation.19 | loop fusion | bytes 65540
  12.5 2.8 %collective-permute-done.1.after_ref.refs_8_ = bf16[256,256]{1,0:T(8,128)(2,1)S(1)} collective-permute-done((bf16[256,256]{1,0:T(8,128)(2,1)S(1)}, bf16[256,256]{1,0:T(8,128)(2,1)S(1)}, u32[]{:S(2)}, u32[]{:S(2)}) %collective-permute-start.1) | collective-permute-done | bytes 131104 | tf_op jit(solution)/shard_map/ppermute | solution.py:202
  15.2 0.8 %collective-permute-start.7 = (bf16[256,256]{1,0:T(8,128)(2,1)S(1)}, bf16[256,256]{1,0:T(8,128)(2,1)S(1)}, u32[]{:S(2)}, u32[]{:S(2)}) collective-permute-start(bf16[256,256]{1,0:T(8,128)(2,1)S(1)} %collective-permute-done.1.after_ref.refs_8_), channel_id=1, source_target_pairs={{0,2},{2,0},{4,6},{6,4},{1,3},{3,1},{5,7},{7,5},{8,10},{10,8},{12,... | collective-permute-start | bytes 393224 | tf_op jit(solution)/shard_map/ppermute | solution.py:202
  16.0 0.0 copy-done
  16.0 0.0 copy-start.1
  16.0 0.0 copy-start.2
  16.0 0.0 copy-start.3
  16.0 0.6 %turn.1.refs_2_ = bf16[4,128,1024]{2,1,0:T(8,128)(2,1)S(1)} custom-call(bf16[128,4096]{1,0:T(8,128)(2,1)S(1)} %bitcast.44, bf16[256,256]{1,0:T(8,128)(2,1)S(1)} %collective-permute-done.1.after_ref.refs_8_), custom_call_target="tpu_custom_call" | custom-call | tf_op jit(solution)/shard_map/turn/pallas_call | solution.py:286
  16.7 1.3 %collective-permute-start.3 = (bf16[272,256]{1,0:T(8,128)(2,1)S(1)}, bf16[272,256]{1,0:T(8,128)(2,1)S(1)}, u32[]{:S(2)}, u32[]{:S(2)}) collective-permute-start(bf16[272,256]{1,0:T(8,128)(2,1)S(1)} %constant_dynamic-update-slice_fusion.refs_5_), channel_id=1, source_target_pairs={{0,2},{2,0},{4,6},{6,4},{1,3},{3,1},{5,7},{7,5},{8,10},{10,8},{12,... | collective-permute-start | bytes 417800 | tf_op jit(solution)/shard_map/ppermute | solution.py:202
  18.0 2.9 %collective-permute-start.4 = (bf16[272,256]{1,0:T(8,128)(2,1)S(1)}, bf16[272,256]{1,0:T(8,128)(2,1)S(1)}, u32[]{:S(2)}, u32[]{:S(2)}) collective-permute-start(bf16[272,256]{1,0:T(8,128)(2,1)S(1)} %constant_dynamic-update-slice_fusion.refs_5_), channel_id=1, source_target_pairs={{0,4},{2,6},{4,0},{6,2},{1,5},{3,7},{5,1},{7,3},{8,12},{10,14},{12... | collective-permute-start | bytes 417800 | tf_op jit(solution)/shard_map/ppermute | solution.py:202
  20.9 1.4 %collective-permute-start.5 = (bf16[272,256]{1,0:T(8,128)(2,1)S(1)}, bf16[272,256]{1,0:T(8,128)(2,1)S(1)}, u32[]{:S(2)}, u32[]{:S(2)}) collective-permute-start(bf16[272,256]{1,0:T(8,128)(2,1)S(1)} %constant_dynamic-update-slice_fusion.refs_5_), channel_id=1, source_target_pairs={{0,6},{2,4},{4,2},{6,0},{1,7},{3,5},{5,3},{7,1},{8,14},{10,12},{12... | collective-permute-start | bytes 417800 | tf_op jit(solution)/shard_map/ppermute | solution.py:202
  22.3 0.0 collective-permute-done.6.refs_6_
  22.3 0.2 collective-permute-done.7.refs_7_
  22.5 0.0 copy-done.1
  22.5 0.0 copy-done.2
  22.5 0.0 copy-done.3
  22.5 6.2 %attend_0.1 = (bf16[128,4096]{1,0:T(8,128)(2,1)}, bf16[128,2048]{1,0:T(8,128)(2,1)S(1)}, bf16[128,256]{1,0:T(8,128)(2,1)S(1)}, bf16[128,256]{1,0:T(8,128)(2,1)S(...) custom-call(s32[1]{0:T(128)} %bitcast.42.refs_0_, ...), custom_call_target="tpu_custom_call" | custom-call | flops 8053063680 | bytes 2097152 | tf_op jit(solution)/shard_map/attend_0/pallas_call | solution.py:316
  28.7 0.9 %collective-permute-start.10 = (bf16[256,256]{1,0:T(8,128)(2,1)S(1)}, bf16[256,256]{1,0:T(8,128)(2,1)S(1)}, u32[]{:S(2)}, u32[]{:S(2)}) collective-permute-start(bf16[256,256]{1,0:T(8,128)(2,1)S(1)} %get-tuple-element.32), channel_id=1, source_target_pairs={{0,2},{2,0},{4,6},{6,4},{1,3},{3,1},{5,7},{7,5},{8,10},{10,8},{12,... | collective-permute-start | bytes 393224 | tf_op jit(solution)/shard_map/ppermute | solution.py:202
  29.6 2.6 %collective-permute-start.8 = (bf16[256,256]{1,0:T(8,128)(2,1)S(1)}, bf16[256,256]{1,0:T(8,128)(2,1)S(1)}, u32[]{:S(2)}, u32[]{:S(2)}) collective-permute-start(bf16[256,256]{1,0:T(8,128)(2,1)S(1)} %get-tuple-element.30), channel_id=1, source_target_pairs={{0,6},{2,4},{4,2},{6,0},{1,7},{3,5},{5,3},{7,1},{8,14},{10,12},{12... | collective-permute-start | bytes 393224 | tf_op jit(solution)/shard_map/ppermute | solution.py:202
  32.2 0.0 collective-permute-done.3.refs_6_
  32.2 0.0 collective-permute-start.9
  32.3 0.0 collective-permute-done.4.refs_7_
  32.3 0.0 collective-permute-done.5.refs_8_
  32.3 6.2 %attend_1.1 = (bf16[128,4096]{1,0:T(8,128)(2,1)}, bf16[128,2048]{1,0:T(8,128)(2,1)S(1)}, bf16[128,256]{1,0:T(8,128)(2,1)S(1)}, bf16[128,256]{1,0:T(8,128)(2,1)S(...) custom-call(s32[1]{0:T(128)} %bitcast.43.refs_0_, ...), custom_call_target="tpu_custom_call", output_to_operand_aliasing={{0}: (9, {})} | custom-call | flops 8053063680 | bytes 2097152 | tf_op jit(solution)/shard_map/attend_1/pallas_call | solution.py:316
  38.5 2.3 %collective-permute-start.14 = (bf16[256,256]{1,0:T(8,128)(2,1)S(1)}, bf16[256,256]{1,0:T(8,128)(2,1)S(1)}, u32[]{:S(2)}, u32[]{:S(2)}) collective-permute-start(bf16[256,256]{1,0:T(8,128)(2,1)S(1)} %get-tuple-element.43), channel_id=1, source_target_pairs={{0,6},{2,4},{4,2},{6,0},{1,7},{3,5},{5,3},{7,1},{8,14},{10,12},{12... | collective-permute-start | bytes 393224 | tf_op jit(solution)/shard_map/ppermute | solution.py:202
  40.8 8.7 %collective-permute-start.15 = (bf16[256,256]{1,0:T(8,128)(2,1)S(1)}, bf16[256,256]{1,0:T(8,128)(2,1)S(1)}, u32[]{:S(2)}, u32[]{:S(2)}) collective-permute-start(bf16[256,256]{1,0:T(8,128)(2,1)S(1)} %get-tuple-element.44), channel_id=1, source_target_pairs={{0,4},{2,6},{4,0},{6,2},{1,5},{3,7},{5,1},{7,3},{8,12},{10,14},{12... | collective-permute-start | bytes 393224 | tf_op jit(solution)/shard_map/ppermute | solution.py:202
  49.5 0.0 collective-permute-done.10
  49.5 0.5 collective-permute-start.16
  50.0 0.0 collective-permute-done.8
  50.0 0.0 collective-permute-done.9
  50.0 0.1 fusion.3
  50.1 0.1 collective-permute-start.11
  50.2 1.9 %collective-permute-start.13 = (bf16[128,256]{1,0:T(8,128)(2,1)S(1)}, bf16[128,256]{1,0:T(8,128)(2,1)S(1)}, u32[]{:S(2)}, u32[]{:S(2)}) collective-permute-start(bf16[128,256]{1,0:T(8,128)(2,1)S(1)} %pad_maximum_fusion.3), channel_id=1, source_target_pairs={{0,1},{1,0},{2,3},{3,2},{4,5},{5,4},{6,7},{7,6},{8,9},{9,8},{10,11... | collective-permute-start | bytes 196616 | tf_op jit(solution)/shard_map/ppermute | solution.py:202
  52.1 0.0 collective-permute-done.11
  52.1 1.5 %collective-permute-start.12 = (f32[8,128]{1,0:T(8,128)S(1)}, f32[8,128]{1,0:T(8,128)S(1)}, u32[]{:S(2)}, u32[]{:S(2)}) collective-permute-start(f32[8,128]{1,0:T(8,128)S(1)} %add.73), channel_id=1, source_target_pairs={{0,16},{8,24},{16,0},{24,8},{1,17},{9,25},{17,1},{25,9},{2,18},{10... | collective-permute-start | bytes 12296 | tf_op jit(solution)/shard_map/ppermute | solution.py:202
  53.6 0.0 collective-permute-done.14
  53.6 0.3 collective-permute-done.15
  53.9 1.3 %collective-permute-done.16 = bf16[256,256]{1,0:T(8,128)(2,1)S(1)} collective-permute-done((bf16[256,256]{1,0:T(8,128)(2,1)S(1)}, bf16[256,256]{1,0:T(8,128)(2,1)S(1)}, u32[]{:S(2)}, u32[]{:S(2)}) %collective-permute-start.16) | collective-permute-done | bytes 131104 | tf_op jit(solution)/shard_map/ppermute | solution.py:202
  55.2 0.1 add_convert_fusion
  55.3 1.9 %collective-permute-start.17 = (bf16[128,256]{1,0:T(8,128)(2,1)S(1)}, bf16[128,256]{1,0:T(8,128)(2,1)S(1)}, u32[]{:S(2)}, u32[]{:S(2)}) collective-permute-start(bf16[128,256]{1,0:T(8,128)(2,1)S(1)} %pad_maximum_fusion.4), channel_id=1, source_target_pairs={{0,1},{1,0},{2,3},{3,2},{4,5},{5,4},{6,7},{7,6},{8,9},{9,8},{10,11... | collective-permute-start | bytes 196616 | tf_op jit(solution)/shard_map/ppermute | solution.py:202
  57.2 0.0 collective-permute-done.12
  57.2 1.3 %scale.1 = (bf16[128,4096]{1,0:T(8,128)(2,1)}, bf16[128,512]{1,0:T(8,128)(2,1)}, bf16[128,512]{1,0:T(8,128)(2,1)}) custom-call(f32[8,128]{1,0:T(8,128)S(1)} %add.74.total_ref, bf16[128,2048]{1,0:T(8,128)(2,1)S(1)} %get-tuple-element.33.refs_0_, bf16[128,256]{1,0:T(8,128)(2,1)S(1)} %get-tuple-element.34.refs_1_, ...), custom_call_target="tpu_custom_call" | custom-call | flops 655360 | bytes 2621440 | tf_op jit(solution)/shard_map/scale/pallas_call | solution.py:335
  58.5 0.0 collective-permute-done.13
  58.5 1.1 %collective-permute-done.17 = bf16[128,256]{1,0:T(8,128)(2,1)S(1)} collective-permute-done((bf16[128,256]{1,0:T(8,128)(2,1)S(1)}, bf16[128,256]{1,0:T(8,128)(2,1)S(1)}, u32[]{:S(2)}, u32[]{:S(2)}) %collective-permute-start.17) | collective-permute-done | bytes 65568 | tf_op jit(solution)/shard_map/ppermute | solution.py:202
  59.7 0.8 %multiply_convert_fusion = (bf16[1,64,1024]{2,1,0:T(8,128)(2,1)}, bf16[1,64,1024]{2,1,0:T(8,128)(2,1)}) fusion(bf16[1,64,512]{2,1,0:T(8,128)(2,1)S(1)} %get-tuple-element.49, bf16[1,64,512]{2,1,0:T(8,128)(2,1)S(1)} %get-tuple-element.48, f32[1024]{0:T(1024)S(1)} %broadcast_bitcast_fusion, bf16[1,64,512]{2,1,0:T(8,128)(2,1)S(1)} %get-tuple-element.59, ...), kind=kLoop, calls=%fused_computation | loop fusion | flops 786432 | bytes 528384 | tf_op jit(solution)/shard_map/convert_element_type | solution.py:373
  (20 shorter events, 0.2 us)
Async XLA Ops:
  0.6 15.4 %copy-start = (bf16[1,128,4096]{2,1,0:T(8,128)(2,1)S(1)}, bf16[1,128,4096]{2,1,0:T(8,128)(2,1)}, u32[]{:S(2)}) copy-start(bf16[1,128,4096]{2,1,0:T(8,128)(2,1)} %param.13) | copy-start | bytes 3145732
  1.6 5.4 %collective-permute-start = (bf16[128,256]{1,0:T(8,128)(2,1)S(1)}, bf16[128,256]{1,0:T(8,128)(2,1)S(1)}, u32[]{:S(2)}, u32[]{:S(2)}) collective-permute-start(bf16[128,256]{1,0:T(8,128)(2,1)S(1)} %pad_maximum_fusion.1), channel_id=1, source_target_pairs={{0,1},{1,0},{2,3},{3,2},{4,5},{5,4},{6,7},{7,6},{8,9},{9,8},{10,11... | collective-permute-start | bytes 196616 | tf_op jit(solution)/shard_map/ppermute | solution.py:202
  4.7 7.0 %collective-permute-start.2 = (bf16[128,256]{1,0:T(8,128)(2,1)S(1)}, bf16[128,256]{1,0:T(8,128)(2,1)S(1)}, u32[]{:S(2)}, u32[]{:S(2)}) collective-permute-start(bf16[128,256]{1,0:T(8,128)(2,1)S(1)} %pad_maximum_fusion.2), channel_id=1, source_target_pairs={{0,1},{1,0},{2,3},{3,2},{4,5},{5,4},{6,7},{7,6},{8,9},{9,8},{10,11... | collective-permute-start | bytes 196616 | tf_op jit(solution)/shard_map/ppermute | solution.py:202
  7.1 8.2 %collective-permute-start.1 = (bf16[256,256]{1,0:T(8,128)(2,1)S(1)}, bf16[256,256]{1,0:T(8,128)(2,1)S(1)}, u32[]{:S(2)}, u32[]{:S(2)}) collective-permute-start(bf16[256,256]{1,0:T(8,128)(2,1)S(1)} %pad_maximum_fusion.refs_5_), channel_id=1, source_target_pairs={{0,6},{2,4},{4,2},{6,0},{1,7},{3,5},{5,3},{7,1},{8,14},{10,12},{12... | collective-permute-start | bytes 393224 | tf_op jit(solution)/shard_map/ppermute | solution.py:202
  11.7 10.6 %collective-permute-start.6 = (bf16[256,256]{1,0:T(8,128)(2,1)S(1)}, bf16[256,256]{1,0:T(8,128)(2,1)S(1)}, u32[]{:S(2)}, u32[]{:S(2)}) collective-permute-start(bf16[256,256]{1,0:T(8,128)(2,1)S(1)} %pad_maximum_fusion.refs_5_), channel_id=1, source_target_pairs={{0,2},{2,0},{4,6},{6,4},{1,3},{3,1},{5,7},{7,5},{8,10},{10,8},{12,... | collective-permute-start | bytes 393224 | tf_op jit(solution)/shard_map/ppermute | solution.py:202
  15.2 7.2 %collective-permute-start.7 = (bf16[256,256]{1,0:T(8,128)(2,1)S(1)}, bf16[256,256]{1,0:T(8,128)(2,1)S(1)}, u32[]{:S(2)}, u32[]{:S(2)}) collective-permute-start(bf16[256,256]{1,0:T(8,128)(2,1)S(1)} %collective-permute-done.1.after_ref.refs_8_), channel_id=1, source_target_pairs={{0,2},{2,0},{4,6},{6,4},{1,3},{3,1},{5,7},{7,5},{8,10},{10,8},{12,... | collective-permute-start | bytes 393224 | tf_op jit(solution)/shard_map/ppermute | solution.py:202
  16.0 6.5 %copy-start.1 = (bf16[1,128,4096]{2,1,0:T(8,128)(2,1)S(1)}, bf16[1,128,4096]{2,1,0:T(8,128)(2,1)}, u32[]{:S(2)}) copy-start(bf16[1,128,4096]{2,1,0:T(8,128)(2,1)} %param.7) | copy-start | bytes 3145732
  16.0 6.5 %copy-start.2 = (bf16[1,128,512]{2,1,0:T(8,128)(2,1)S(1)}, bf16[1,128,512]{2,1,0:T(8,128)(2,1)}, u32[]{:S(2)}) copy-start(bf16[1,128,512]{2,1,0:T(8,128)(2,1)} %param.8) | copy-start | bytes 393220
  16.0 6.5 %copy-start.3 = (bf16[1,128,512]{2,1,0:T(8,128)(2,1)S(1)}, bf16[1,128,512]{2,1,0:T(8,128)(2,1)}, u32[]{:S(2)}) copy-start(bf16[1,128,512]{2,1,0:T(8,128)(2,1)} %param.9) | copy-start | bytes 393220
  16.7 15.6 %collective-permute-start.3 = (bf16[272,256]{1,0:T(8,128)(2,1)S(1)}, bf16[272,256]{1,0:T(8,128)(2,1)S(1)}, u32[]{:S(2)}, u32[]{:S(2)}) collective-permute-start(bf16[272,256]{1,0:T(8,128)(2,1)S(1)} %constant_dynamic-update-slice_fusion.refs_5_), channel_id=1, source_target_pairs={{0,2},{2,0},{4,6},{6,4},{1,3},{3,1},{5,7},{7,5},{8,10},{10,8},{12,... | collective-permute-start | bytes 417800 | tf_op jit(solution)/shard_map/ppermute | solution.py:202
  18.0 14.3 %collective-permute-start.4 = (bf16[272,256]{1,0:T(8,128)(2,1)S(1)}, bf16[272,256]{1,0:T(8,128)(2,1)S(1)}, u32[]{:S(2)}, u32[]{:S(2)}) collective-permute-start(bf16[272,256]{1,0:T(8,128)(2,1)S(1)} %constant_dynamic-update-slice_fusion.refs_5_), channel_id=1, source_target_pairs={{0,4},{2,6},{4,0},{6,2},{1,5},{3,7},{5,1},{7,3},{8,12},{10,14},{12... | collective-permute-start | bytes 417800 | tf_op jit(solution)/shard_map/ppermute | solution.py:202
  20.9 11.4 %collective-permute-start.5 = (bf16[272,256]{1,0:T(8,128)(2,1)S(1)}, bf16[272,256]{1,0:T(8,128)(2,1)S(1)}, u32[]{:S(2)}, u32[]{:S(2)}) collective-permute-start(bf16[272,256]{1,0:T(8,128)(2,1)S(1)} %constant_dynamic-update-slice_fusion.refs_5_), channel_id=1, source_target_pairs={{0,6},{2,4},{4,2},{6,0},{1,7},{3,5},{5,3},{7,1},{8,14},{10,12},{12... | collective-permute-start | bytes 417800 | tf_op jit(solution)/shard_map/ppermute | solution.py:202
  28.7 20.8 %collective-permute-start.10 = (bf16[256,256]{1,0:T(8,128)(2,1)S(1)}, bf16[256,256]{1,0:T(8,128)(2,1)S(1)}, u32[]{:S(2)}, u32[]{:S(2)}) collective-permute-start(bf16[256,256]{1,0:T(8,128)(2,1)S(1)} %get-tuple-element.32), channel_id=1, source_target_pairs={{0,2},{2,0},{4,6},{6,4},{1,3},{3,1},{5,7},{7,5},{8,10},{10,8},{12,... | collective-permute-start | bytes 393224 | tf_op jit(solution)/shard_map/ppermute | solution.py:202
  29.6 20.4 %collective-permute-start.8 = (bf16[256,256]{1,0:T(8,128)(2,1)S(1)}, bf16[256,256]{1,0:T(8,128)(2,1)S(1)}, u32[]{:S(2)}, u32[]{:S(2)}) collective-permute-start(bf16[256,256]{1,0:T(8,128)(2,1)S(1)} %get-tuple-element.30), channel_id=1, source_target_pairs={{0,6},{2,4},{4,2},{6,0},{1,7},{3,5},{5,3},{7,1},{8,14},{10,12},{12... | collective-permute-start | bytes 393224 | tf_op jit(solution)/shard_map/ppermute | solution.py:202
  32.2 17.8 %collective-permute-start.9 = (bf16[256,256]{1,0:T(8,128)(2,1)S(1)}, bf16[256,256]{1,0:T(8,128)(2,1)S(1)}, u32[]{:S(2)}, u32[]{:S(2)}) collective-permute-start(bf16[256,256]{1,0:T(8,128)(2,1)S(1)} %get-tuple-element.31), channel_id=1, source_target_pairs={{0,4},{2,6},{4,0},{6,2},{1,5},{3,7},{5,1},{7,3},{8,12},{10,14},{12... | collective-permute-start | bytes 393224 | tf_op jit(solution)/shard_map/ppermute | solution.py:202
  38.5 15.1 %collective-permute-start.14 = (bf16[256,256]{1,0:T(8,128)(2,1)S(1)}, bf16[256,256]{1,0:T(8,128)(2,1)S(1)}, u32[]{:S(2)}, u32[]{:S(2)}) collective-permute-start(bf16[256,256]{1,0:T(8,128)(2,1)S(1)} %get-tuple-element.43), channel_id=1, source_target_pairs={{0,6},{2,4},{4,2},{6,0},{1,7},{3,5},{5,3},{7,1},{8,14},{10,12},{12... | collective-permute-start | bytes 393224 | tf_op jit(solution)/shard_map/ppermute | solution.py:202
  40.8 13.1 %collective-permute-start.15 = (bf16[256,256]{1,0:T(8,128)(2,1)S(1)}, bf16[256,256]{1,0:T(8,128)(2,1)S(1)}, u32[]{:S(2)}, u32[]{:S(2)}) collective-permute-start(bf16[256,256]{1,0:T(8,128)(2,1)S(1)} %get-tuple-element.44), channel_id=1, source_target_pairs={{0,4},{2,6},{4,0},{6,2},{1,5},{3,7},{5,1},{7,3},{8,12},{10,14},{12... | collective-permute-start | bytes 393224 | tf_op jit(solution)/shard_map/ppermute | solution.py:202
  49.5 5.7 %collective-permute-start.16 = (bf16[256,256]{1,0:T(8,128)(2,1)S(1)}, bf16[256,256]{1,0:T(8,128)(2,1)S(1)}, u32[]{:S(2)}, u32[]{:S(2)}) collective-permute-start(bf16[256,256]{1,0:T(8,128)(2,1)S(1)} %get-tuple-element.45), channel_id=1, source_target_pairs={{0,2},{2,0},{4,6},{6,4},{1,3},{3,1},{5,7},{7,5},{8,10},{10,8},{12,... | collective-permute-start | bytes 393224 | tf_op jit(solution)/shard_map/ppermute | solution.py:202
  50.1 2.0 %collective-permute-start.11 = (f32[8,128]{1,0:T(8,128)S(1)}, f32[8,128]{1,0:T(8,128)S(1)}, u32[]{:S(2)}, u32[]{:S(2)}) collective-permute-start(f32[8,128]{1,0:T(8,128)S(1)} %fusion.2), channel_id=1, source_target_pairs={{0,8},{8,0},{16,24},{24,16},{1,9},{9,1},{17,25},{25,17},{2,10},{10... | collective-permute-start | bytes 12296 | tf_op jit(solution)/shard_map/ppermute | solution.py:202
  50.2 8.2 %collective-permute-start.13 = (bf16[128,256]{1,0:T(8,128)(2,1)S(1)}, bf16[128,256]{1,0:T(8,128)(2,1)S(1)}, u32[]{:S(2)}, u32[]{:S(2)}) collective-permute-start(bf16[128,256]{1,0:T(8,128)(2,1)S(1)} %pad_maximum_fusion.3), channel_id=1, source_target_pairs={{0,1},{1,0},{2,3},{3,2},{4,5},{5,4},{6,7},{7,6},{8,9},{9,8},{10,11... | collective-permute-start | bytes 196616 | tf_op jit(solution)/shard_map/ppermute | solution.py:202
  52.1 5.1 %collective-permute-start.12 = (f32[8,128]{1,0:T(8,128)S(1)}, f32[8,128]{1,0:T(8,128)S(1)}, u32[]{:S(2)}, u32[]{:S(2)}) collective-permute-start(f32[8,128]{1,0:T(8,128)S(1)} %add.73), channel_id=1, source_target_pairs={{0,16},{8,24},{16,0},{24,8},{1,17},{9,25},{17,1},{25,9},{2,18},{10... | collective-permute-start | bytes 12296 | tf_op jit(solution)/shard_map/ppermute | solution.py:202
  55.3 4.3 %collective-permute-start.17 = (bf16[128,256]{1,0:T(8,128)(2,1)S(1)}, bf16[128,256]{1,0:T(8,128)(2,1)S(1)}, u32[]{:S(2)}, u32[]{:S(2)}) collective-permute-start(bf16[128,256]{1,0:T(8,128)(2,1)S(1)} %pad_maximum_fusion.4), channel_id=1, source_target_pairs={{0,1},{1,0},{2,3},{3,2},{4,5},{5,4},{6,7},{7,6},{8,9},{9,8},{10,11... | collective-permute-start | bytes 196616 | tf_op jit(solution)/shard_map/ppermute | solution.py:202

commit v10 on v8

--- a/solution.py
+++ b/solution.py
@@ -210,19 +210,22 @@
     return x
 
 
-def line_gather(block, butterfly):
+def far_and_near(block):
     size = lax.axis_size("response")
-    if size != 4 or not butterfly:
-        return [block] + [swap(block, "response", m) for m in range(1, size)]
-    far = swap(block, "response", 3)
-    near = swap(block, "response", 1)
-    return [block, near, swap(far, "response", 1), far]
-
-
-def line_reduce(slots):
-    terms = [slots[0]] + [swap(slots[m], "response", m) for m in range(1, len(slots))]
-    total = functools.reduce(jnp.add, [term.astype(jnp.float32) for term in terms])
-    return total
+    order = (3, 1) if size == 4 else range(1, size)
+    return {m: swap(block, "response", m) for m in order}
+
+
+def line_gather(block, sent):
+    size = lax.axis_size("response")
+    if size == 4:
+        sent = {**sent, 2: swap(sent[3], "response", 1)}
+    return [block] + [sent[m] for m in range(1, size)]
+
+
+def line_reduce(slots, order):
+    terms = [swap(slots[m], "response", m) for m in order]
+    return functools.reduce(jnp.add, [term.astype(jnp.float32) for term in [slots[0]] + terms])
 
 
 def own_columns(block, chunk, by):
@@ -357,19 +360,30 @@
     slots_all = q.shape[0] * lax.axis_size("prompt") * lax.axis_size("response")
     first, second = [tensor_gather(prefix, chunk) for chunk in range(CHUNKS)]
     held = first.shape[0] // 2
-    slots = line_gather(first, True)
+    sent = far_and_near(first)
+    slots = line_gather(first, sent)
     length_rows = length[0].astype(second.dtype) + 0 * slots[-1][-EXTRA:]
-    next_slots = line_gather(jnp.concatenate([second, length_rows], axis=0), False)
+    second = jnp.concatenate([second, length_rows], axis=0)
+    sent = far_and_near(second)
     turned = turn(do, first)
     results = attend(0, held, slots, length, q, turned, k, v, [])
+    if len(slots) == 4:
+        far = sent[3]
+        sent[3] = jnp.concatenate([far[:-EXTRA] + 0 * results[4], far[-EXTRA:]], axis=0)
+    next_slots = line_gather(second, sent)
     next_results = attend(1, held, next_slots, length, q, turned, k, v, results[:1])
-    sums = [line_reduce(results[4:]), line_reduce(next_results[4:-1])]
+    terms, next_terms = results[4:], next_results[4:-1]
+    behind = 0 * next_results[3][:1].astype(jnp.float32)
+    farthest_first = list(range(len(terms) - 1, 0, -1))
+    order = (2, 1, 3) if len(terms) == 4 else farthest_first
+    sums = [line_reduce(terms, order) + behind, line_reduce(next_terms, farthest_first)]
     total = sum_over(next_results[-1] + 0 * sums[0][:8, :HD], "prompt")
     weight = jnp.tile(slots_all / total[:1], (1, prefix[0].shape[1] // HD))
     scaled = scale_all(
-        slots_all, total, [results[1:4], next_results[1:4]], [like(q), like(k), like(v)]
+        slots_all, total + 0 * sums[1][:8, :HD], [results[1:4], next_results[1:4]], [like(q), like(k), like(v)]
     )
-    pieces = [tensor_spread(terms.astype(jnp.bfloat16), len(prefix)) for terms in sums]
+    both = jnp.concatenate([terms.astype(jnp.bfloat16) for terms in sums], axis=1)
+    pieces = [tensor_spread(both, len(prefix))]
     grads = [whole_columns(pieces, array) for array in range(len(prefix))]
     grads = [(grad.astype(jnp.float32) * weight).astype(jnp.bfloat16) for grad in grads]
     return tuple(x[None] for x in (next_results[0], *scaled, *grads))

time: 57.7 us -> 57.6 us (level)
  starting transfers between devices: 27.8 us -> 26 us
  waiting for transfers between devices: 10.4 us -> 12 us
    ppermute x18 -> x17, starting transfers between devices: 27.8 us -> 26 us  [swap(): lax.ppermute(x, axis, [(i, i ^ by) for i in range(lax.axis_size(axis))])]
    ppermute x18 -> x17, waiting for transfers between devices: 10.4 us -> 12 us  [swap(): lax.ppermute(x, axis, [(i, i ^ by) for i in range(lax.axis_size(axis))])]
  transfers between devices with their start and end apart: 18 -> 17, of which waited for: 5 -> 8; matrix products, arithmetic and copies ran while one was open for 3% -> 3% of each run, Pallas kernels for 25% -> 25%
where the time goes in v10:
time: 57.6 us; the launch traced here: 57.3 us
  starting transfers between devices  26 us (45%)
  Pallas kernels  14.3 us (25%)
  waiting for transfers between devices  12 us (21%)
  local copies, waits for them, and re-layouts  2.52 us (4%)
  between operations  1.51 us (3%)
  other arithmetic  1.06 us (2%)
    ppermute x17, starting transfers between devices, swap(): lax.ppermute(x, axis, [(i, i ^ by) for i in range(lax.axis_size(axis))])  26 us
    pallas_call x2, Pallas kernels, attend(): pl.pallas_call(functools.partial(attend_kernel, n_slots, count, chunk, he...  12.4 us
    ppermute x17, waiting for transfers between devices, swap(): lax.ppermute(x, axis, [(i, i ^ by) for i in range(lax.axis_size(axis))])  12 us
    unnamed x12, local copies, waits for them, and re-layouts  1.56 us
    pallas_call x1, Pallas kernels, scale_all(): pl.pallas_call(functools.partial(scale_kernel, slots_all), in_specs=[VMEM...  1.27 us
  transfers between devices with their start and end apart: 17, of which 8 were waited for; matrix products, arithmetic and copies ran while one was open for 3% of the time, Pallas kernels for 25%

profile of v10, /device:TPU:0, one launch (start us, length us, event | category | flops | bytes accessed | tf_op | source)
XLA Modules:
  0.0 57.3 jit_solution(7884253307643881428)
XLA Ops:
  0.6 0.0 copy-start
  0.7 0.9 %dynamic-slice_bitcast_fusion = (bf16[64,256]{1,0:T(8,128)(2,1)S(1)}, bf16[64,256]{1,0:T(8,128)(2,1)S(1)}, bf16[64,256]{1,0:T(8,128)(2,1)S(1)}, bf16[64,256]{1,0...) fusion(bf16[1,64,1024]{2,1,0:T(8,128)(2,1)} %param.11, s32[]{:T(128)S(6)} %select_n.41, ...), kind=kLoop, calls=%fused_computation.28 | loop fusion | bytes 393228 | tf_op jit(solution)/shard_map/dynamic_slice | solution.py:234
  1.6 3.0 %collective-permute-start = (bf16[128,256]{1,0:T(8,128)(2,1)S(1)}, bf16[128,256]{1,0:T(8,128)(2,1)S(1)}, u32[]{:S(2)}, u32[]{:S(2)}) collective-permute-start(bf16[128,256]{1,0:T(8,128)(2,1)S(1)} %pad_maximum_fusion.4), channel_id=1, source_target_pairs={{0,1},{1,0},{2,3},{3,2},{4,5},{5,4},{6,7},{7,6},{8,9},{9,8},{10,11... | collective-permute-start | bytes 196616 | tf_op jit(solution)/shard_map/ppermute | solution.py:202
  4.7 0.1 collective-permute-start.1
  5.4 0.8 %bitcast_dynamic-update-slice_fusion.1 = bf16[272,256]{1,0:T(8,128)(2,1)S(1)} fusion(bf16[1,64,1024]{2,1,0:T(8,128)(2,1)} %param.10, s32[]{:T(128)S(6)} %select_n.40), kind=kLoop, calls=%fused_computation.27 | loop fusion | bytes 65540
  6.2 0.9 %collective-permute-done = bf16[128,256]{1,0:T(8,128)(2,1)S(1)} collective-permute-done((bf16[128,256]{1,0:T(8,128)(2,1)S(1)}, bf16[128,256]{1,0:T(8,128)(2,1)S(1)}, u32[]{:S(2)}, u32[]{:S(2)}) %collective-permute-start) | collective-permute-done | bytes 65568 | tf_op jit(solution)/shard_map/ppermute | solution.py:202
  7.1 4.6 %collective-permute-start.2 = (bf16[256,256]{1,0:T(8,128)(2,1)S(1)}, bf16[256,256]{1,0:T(8,128)(2,1)S(1)}, u32[]{:S(2)}, u32[]{:S(2)}) collective-permute-start(bf16[256,256]{1,0:T(8,128)(2,1)S(1)} %pad_maximum_fusion.1.after_ref.refs_5_), channel_id=1, source_target_pairs={{0,6},{2,4},{4,2},{6,0},{1,7},{3,5},{5,3},{7,1},{8,14},{10,12},{12... | collective-permute-start | bytes 393224 | tf_op jit(solution)/shard_map/ppermute | solution.py:202
  11.7 0.0 collective-permute-start.5
  11.7 0.0 copy-done
  11.7 0.0 copy-start.1
  11.7 0.0 copy-start.3
  11.7 0.6 %turn.1.refs_2_ = bf16[4,128,1024]{2,1,0:T(8,128)(2,1)S(1)} custom-call(bf16[128,4096]{1,0:T(8,128)(2,1)S(1)} %bitcast.41, bf16[256,256]{1,0:T(8,128)(2,1)S(1)} %pad_maximum_fusion.1.after_ref.refs_5_), custom_call_target="tpu_custom_call" | custom-call | tf_op jit(solution)/shard_map/turn/pallas_call | solution.py:290
  12.3 0.0 copy-start.2
  12.3 0.0 collective-permute-done.1
  12.4 0.8 %bitcast_dynamic-update-slice_fusion = bf16[272,256]{1,0:T(8,128)(2,1)S(1)} fusion(bf16[272,256]{1,0:T(8,128)(2,1)S(1)} %slice_dynamic-update-slice_fusion.1, bf16[1,64,1024]{2,1,0:T(8,128)(2,1)} %param.11, s32[]{:T(128)S(6)} %select_n.40), kind=kLoop, calls=%fused_computation.26 | loop fusion | bytes 65540
  13.1 2.1 %collective-permute-done.2.refs_8_ = bf16[256,256]{1,0:T(8,128)(2,1)S(1)} collective-permute-done((bf16[256,256]{1,0:T(8,128)(2,1)S(1)}, bf16[256,256]{1,0:T(8,128)(2,1)S(1)}, u32[]{:S(2)}, u32[]{:S(2)}) %collective-permute-start.2) | collective-permute-done | bytes 131104 | tf_op jit(solution)/shard_map/ppermute | solution.py:202
  15.2 0.8 %collective-permute-start.6 = (bf16[256,256]{1,0:T(8,128)(2,1)S(1)}, bf16[256,256]{1,0:T(8,128)(2,1)S(1)}, u32[]{:S(2)}, u32[]{:S(2)}) collective-permute-start(bf16[256,256]{1,0:T(8,128)(2,1)S(1)} %collective-permute-done.2.refs_8_), channel_id=1, source_target_pairs={{0,2},{2,0},{4,6},{6,4},{1,3},{3,1},{5,7},{7,5},{8,10},{10,8},{12,... | collective-permute-start | bytes 393224 | tf_op jit(solution)/shard_map/ppermute | solution.py:202
  16.0 3.6 %collective-permute-start.4 = (bf16[272,256]{1,0:T(8,128)(2,1)S(1)}, bf16[272,256]{1,0:T(8,128)(2,1)S(1)}, u32[]{:S(2)}, u32[]{:S(2)}) collective-permute-start(bf16[272,256]{1,0:T(8,128)(2,1)S(1)} %constant_dynamic-update-slice_fusion.refs_5_), channel_id=1, source_target_pairs={{0,6},{2,4},{4,2},{6,0},{1,7},{3,5},{5,3},{7,1},{8,14},{10,12},{12... | collective-permute-start | bytes 417800 | tf_op jit(solution)/shard_map/ppermute | solution.py:202
  19.6 1.1 %collective-permute-start.3 = (bf16[272,256]{1,0:T(8,128)(2,1)S(1)}, bf16[272,256]{1,0:T(8,128)(2,1)S(1)}, u32[]{:S(2)}, u32[]{:S(2)}) collective-permute-start(bf16[272,256]{1,0:T(8,128)(2,1)S(1)} %constant_dynamic-update-slice_fusion.refs_5_), channel_id=1, source_target_pairs={{0,2},{2,0},{4,6},{6,4},{1,3},{3,1},{5,7},{7,5},{8,10},{10,8},{12,... | collective-permute-start | bytes 417800 | tf_op jit(solution)/shard_map/ppermute | solution.py:202
  20.7 0.0 collective-permute-done.5.refs_6_
  20.7 1.5 %collective-permute-done.6.refs_7_ = bf16[256,256]{1,0:T(8,128)(2,1)S(1)} collective-permute-done((bf16[256,256]{1,0:T(8,128)(2,1)S(1)}, bf16[256,256]{1,0:T(8,128)(2,1)S(1)}, u32[]{:S(2)}, u32[]{:S(2)}) %collective-permute-start.6) | collective-permute-done | bytes 131104 | tf_op jit(solution)/shard_map/ppermute | solution.py:202
  22.2 0.0 copy-done.1
  22.2 0.0 copy-done.3
  22.2 0.0 copy-done.2
  22.2 6.2 %attend_0.1 = (bf16[128,4096]{1,0:T(8,128)(2,1)}, bf16[128,2048]{1,0:T(8,128)(2,1)S(1)}, bf16[128,256]{1,0:T(8,128)(2,1)S(1)}, bf16[128,256]{1,0:T(8,128)(2,1)S(...) custom-call(s32[1]{0:T(128)} %bitcast.39.refs_0_, ...), custom_call_target="tpu_custom_call" | custom-call | flops 8053063680 | bytes 2097152 | tf_op jit(solution)/shard_map/attend_0/pallas_call | solution.py:320
  28.4 0.0 collective-permute-done.4
  28.5 1.2 %collective-permute-start.7 = (bf16[272,256]{1,0:T(8,128)(2,1)S(1)}, bf16[272,256]{1,0:T(8,128)(2,1)S(1)}, u32[]{:S(2)}, u32[]{:S(2)}) collective-permute-start(bf16[272,256]{1,0:T(8,128)(2,1)S(1)} %pad_maximum_fusion.refs_8_), channel_id=1, source_target_pairs={{0,2},{2,0},{4,6},{6,4},{1,3},{3,1},{5,7},{7,5},{8,10},{10,8},{12,... | collective-permute-start | bytes 417800 | tf_op jit(solution)/shard_map/ppermute | solution.py:202
  29.7 1.3 %collective-permute-start.10 = (bf16[256,256]{1,0:T(8,128)(2,1)S(1)}, bf16[256,256]{1,0:T(8,128)(2,1)S(1)}, u32[]{:S(2)}, u32[]{:S(2)}) collective-permute-start(bf16[256,256]{1,0:T(8,128)(2,1)S(1)} %get-tuple-element.32), channel_id=1, source_target_pairs={{0,6},{2,4},{4,2},{6,0},{1,7},{3,5},{5,3},{7,1},{8,14},{10,12},{12... | collective-permute-start | bytes 393224 | tf_op jit(solution)/shard_map/ppermute | solution.py:202
  31.0 1.0 %collective-permute-start.8 = (bf16[256,256]{1,0:T(8,128)(2,1)S(1)}, bf16[256,256]{1,0:T(8,128)(2,1)S(1)}, u32[]{:S(2)}, u32[]{:S(2)}) collective-permute-start(bf16[256,256]{1,0:T(8,128)(2,1)S(1)} %get-tuple-element.30), channel_id=1, source_target_pairs={{0,4},{2,6},{4,0},{6,2},{1,5},{3,7},{5,1},{7,3},{8,12},{10,14},{12... | collective-permute-start | bytes 393224 | tf_op jit(solution)/shard_map/ppermute | solution.py:202
  32.0 2.0 %collective-permute-start.9 = (bf16[256,256]{1,0:T(8,128)(2,1)S(1)}, bf16[256,256]{1,0:T(8,128)(2,1)S(1)}, u32[]{:S(2)}, u32[]{:S(2)}) collective-permute-start(bf16[256,256]{1,0:T(8,128)(2,1)S(1)} %get-tuple-element.31), channel_id=1, source_target_pairs={{0,2},{2,0},{4,6},{6,4},{1,3},{3,1},{5,7},{7,5},{8,10},{10,8},{12,... | collective-permute-start | bytes 393224 | tf_op jit(solution)/shard_map/ppermute | solution.py:202
  34.1 0.0 collective-permute-done.3.refs_6_
  34.1 0.8 %collective-permute-done.7.refs_7_ = bf16[272,256]{1,0:T(8,128)(2,1)S(1)} collective-permute-done((bf16[272,256]{1,0:T(8,128)(2,1)S(1)}, bf16[272,256]{1,0:T(8,128)(2,1)S(1)}, u32[]{:S(2)}, u32[]{:S(2)}) %collective-permute-start.7) | collective-permute-done | bytes 139296 | tf_op jit(solution)/shard_map/ppermute | solution.py:202
  34.9 6.2 %attend_1.1 = (bf16[128,4096]{1,0:T(8,128)(2,1)}, bf16[128,2048]{1,0:T(8,128)(2,1)S(1)}, bf16[128,256]{1,0:T(8,128)(2,1)S(1)}, bf16[128,256]{1,0:T(8,128)(2,1)S(...) custom-call(s32[1]{0:T(128)} %bitcast.40.refs_0_, ...), custom_call_target="tpu_custom_call", output_to_operand_aliasing={{0}: (9, {})} | custom-call | flops 8053063680 | bytes 2097152 | tf_op jit(solution)/shard_map/attend_1/pallas_call | solution.py:320
  41.1 3.8 %collective-permute-start.13 = (bf16[256,256]{1,0:T(8,128)(2,1)S(1)}, bf16[256,256]{1,0:T(8,128)(2,1)S(1)}, u32[]{:S(2)}, u32[]{:S(2)}) collective-permute-start(bf16[256,256]{1,0:T(8,128)(2,1)S(1)} %get-tuple-element.35), channel_id=1, source_target_pairs={{0,6},{2,4},{4,2},{6,0},{1,7},{3,5},{5,3},{7,1},{8,14},{10,12},{12... | collective-permute-start | bytes 393224 | tf_op jit(solution)/shard_map/ppermute | solution.py:202
  44.9 0.0 collective-permute-start.14
  44.9 0.0 collective-permute-done.10
  44.9 0.6 %collective-permute-start.15 = (bf16[256,256]{1,0:T(8,128)(2,1)S(1)}, bf16[256,256]{1,0:T(8,128)(2,1)S(1)}, u32[]{:S(2)}, u32[]{:S(2)}) collective-permute-start(bf16[256,256]{1,0:T(8,128)(2,1)S(1)} %get-tuple-element.37), channel_id=1, source_target_pairs={{0,2},{2,0},{4,6},{6,4},{1,3},{3,1},{5,7},{7,5},{8,10},{10,8},{12,... | collective-permute-start | bytes 393224 | tf_op jit(solution)/shard_map/ppermute | solution.py:202
  45.6 0.0 collective-permute-done.8
  45.6 0.0 collective-permute-done.9
  45.6 0.1 fusion.7
  45.7 0.1 collective-permute-start.11
  45.8 1.1 %collective-permute-done.11 = f32[8,128]{1,0:T(8,128)S(1)} collective-permute-done((f32[8,128]{1,0:T(8,128)S(1)}, f32[8,128]{1,0:T(8,128)S(1)}, u32[]{:S(2)}, u32[]{:S(2)}) %collective-permute-start.11) | collective-permute-done | bytes 4128 | tf_op jit(solution)/shard_map/ppermute | solution.py:202
  46.9 1.5 %collective-permute-start.12 = (f32[8,128]{1,0:T(8,128)S(1)}, f32[8,128]{1,0:T(8,128)S(1)}, u32[]{:S(2)}, u32[]{:S(2)}) collective-permute-start(f32[8,128]{1,0:T(8,128)S(1)} %add.89), channel_id=1, source_target_pairs={{0,16},{8,24},{16,0},{24,8},{1,17},{9,25},{17,1},{25,9},{2,18},{10... | collective-permute-start | bytes 12296 | tf_op jit(solution)/shard_map/ppermute | solution.py:202
  48.4 0.0 collective-permute-done.13
  48.4 2.5 %collective-permute-done.14 = bf16[256,256]{1,0:T(8,128)(2,1)S(1)} collective-permute-done((bf16[256,256]{1,0:T(8,128)(2,1)S(1)}, bf16[256,256]{1,0:T(8,128)(2,1)S(1)}, u32[]{:S(2)}, u32[]{:S(2)}) %collective-permute-start.14) | collective-permute-done | bytes 131104 | tf_op jit(solution)/shard_map/ppermute | solution.py:202
  50.9 0.5 collective-permute-done.15
  51.4 0.1 fusion.6
  51.5 1.2 %collective-permute-start.16 = (bf16[128,512]{1,0:T(8,128)(2,1)S(1)}, bf16[128,512]{1,0:T(8,128)(2,1)S(1)}, u32[]{:S(2)}, u32[]{:S(2)}) collective-permute-start(bf16[128,512]{1,0:T(8,128)(2,1)S(1)} %pad_maximum_fusion.2), channel_id=1, source_target_pairs={{0,1},{1,0},{2,3},{3,2},{4,5},{5,4},{6,7},{7,6},{8,9},{9,8},{10,11... | collective-permute-start | bytes 393224 | tf_op jit(solution)/shard_map/ppermute | solution.py:202
  52.7 0.0 collective-permute-done.12
  52.7 1.3 %scale.1 = (bf16[128,4096]{1,0:T(8,128)(2,1)}, bf16[128,512]{1,0:T(8,128)(2,1)}, bf16[128,512]{1,0:T(8,128)(2,1)}) custom-call(f32[8,128]{1,0:T(8,128)S(1)} %get-tuple-element.52.total_ref, bf16[128,2048]{1,0:T(8,128)(2,1)S(1)} %get-tuple-element.38.refs_0_, bf16[128,256]{1,0:T(8,128)(2,1)S(1)} %get-tuple-element.39.refs_1_, ...), custom_call_target="tpu_custom_call" | custom-call | flops 655360 | bytes 2621440 | tf_op jit(solution)/shard_map/scale/pallas_call | solution.py:339
  54.0 2.5 %collective-permute-done.16 = bf16[128,512]{1,0:T(8,128)(2,1)S(1)} collective-permute-done((bf16[128,512]{1,0:T(8,128)(2,1)S(1)}, bf16[128,512]{1,0:T(8,128)(2,1)S(1)}, u32[]{:S(2)}, u32[]{:S(2)}) %collective-permute-start.16) | collective-permute-done | bytes 131104 | tf_op jit(solution)/shard_map/ppermute | solution.py:202
  56.6 0.8 %multiply_convert_fusion = (bf16[1,64,1024]{2,1,0:T(8,128)(2,1)}, bf16[1,64,1024]{2,1,0:T(8,128)(2,1)}) fusion(bf16[1,64,512]{2,1,0:T(8,128)(2,1)S(1)} %select_bitcast_fusion, bf16[1,64,512]{2,1,0:T(8,128)(2,1)S(1)} %get-tuple-element.46, f32[1024]{0:T(1024)S(1)} %broadcast_bitcast_fusion, bf16[1,64,512]{2,1,0:T(8,128)(2,1)S(1)} %get-tuple-element.54, ...), kind=kLoop, calls=%fused_computation.6 | loop fusion | flops 786432 | bytes 528384 | tf_op jit(solution)/shard_map/convert_element_type | solution.py:388
  (20 shorter events, 0.2 us)
Async XLA Ops:
  0.6 11.0 %copy-start = (bf16[1,128,4096]{2,1,0:T(8,128)(2,1)S(1)}, bf16[1,128,4096]{2,1,0:T(8,128)(2,1)}, u32[]{:S(2)}) copy-start(bf16[1,128,4096]{2,1,0:T(8,128)(2,1)} %param.13) | copy-start | bytes 3145732
  1.6 5.4 %collective-permute-start = (bf16[128,256]{1,0:T(8,128)(2,1)S(1)}, bf16[128,256]{1,0:T(8,128)(2,1)S(1)}, u32[]{:S(2)}, u32[]{:S(2)}) collective-permute-start(bf16[128,256]{1,0:T(8,128)(2,1)S(1)} %pad_maximum_fusion.4), channel_id=1, source_target_pairs={{0,1},{1,0},{2,3},{3,2},{4,5},{5,4},{6,7},{7,6},{8,9},{9,8},{10,11... | collective-permute-start | bytes 196616 | tf_op jit(solution)/shard_map/ppermute | solution.py:202
  4.7 7.7 %collective-permute-start.1 = (bf16[128,256]{1,0:T(8,128)(2,1)S(1)}, bf16[128,256]{1,0:T(8,128)(2,1)S(1)}, u32[]{:S(2)}, u32[]{:S(2)}) collective-permute-start(bf16[128,256]{1,0:T(8,128)(2,1)S(1)} %pad_maximum_fusion.5), channel_id=1, source_target_pairs={{0,1},{1,0},{2,3},{3,2},{4,5},{5,4},{6,7},{7,6},{8,9},{9,8},{10,11... | collective-permute-start | bytes 196616 | tf_op jit(solution)/shard_map/ppermute | solution.py:202
  7.1 8.2 %collective-permute-start.2 = (bf16[256,256]{1,0:T(8,128)(2,1)S(1)}, bf16[256,256]{1,0:T(8,128)(2,1)S(1)}, u32[]{:S(2)}, u32[]{:S(2)}) collective-permute-start(bf16[256,256]{1,0:T(8,128)(2,1)S(1)} %pad_maximum_fusion.1.after_ref.refs_5_), channel_id=1, source_target_pairs={{0,6},{2,4},{4,2},{6,0},{1,7},{3,5},{5,3},{7,1},{8,14},{10,12},{12... | collective-permute-start | bytes 393224 | tf_op jit(solution)/shard_map/ppermute | solution.py:202
  11.7 9.0 %collective-permute-start.5 = (bf16[256,256]{1,0:T(8,128)(2,1)S(1)}, bf16[256,256]{1,0:T(8,128)(2,1)S(1)}, u32[]{:S(2)}, u32[]{:S(2)}) collective-permute-start(bf16[256,256]{1,0:T(8,128)(2,1)S(1)} %pad_maximum_fusion.1.after_ref.refs_5_), channel_id=1, source_target_pairs={{0,2},{2,0},{4,6},{6,4},{1,3},{3,1},{5,7},{7,5},{8,10},{10,8},{12,... | collective-permute-start | bytes 393224 | tf_op jit(solution)/shard_map/ppermute | solution.py:202
  11.7 10.5 %copy-start.1 = (bf16[1,128,4096]{2,1,0:T(8,128)(2,1)S(1)}, bf16[1,128,4096]{2,1,0:T(8,128)(2,1)}, u32[]{:S(2)}) copy-start(bf16[1,128,4096]{2,1,0:T(8,128)(2,1)} %param.7) | copy-start | bytes 3145732
  11.7 10.5 %copy-start.3 = (bf16[1,128,512]{2,1,0:T(8,128)(2,1)S(1)}, bf16[1,128,512]{2,1,0:T(8,128)(2,1)}, u32[]{:S(2)}) copy-start(bf16[1,128,512]{2,1,0:T(8,128)(2,1)} %param.9) | copy-start | bytes 393220
  12.3 9.9 %copy-start.2 = (bf16[1,128,512]{2,1,0:T(8,128)(2,1)S(1)}, bf16[1,128,512]{2,1,0:T(8,128)(2,1)}, u32[]{:S(2)}) copy-start(bf16[1,128,512]{2,1,0:T(8,128)(2,1)} %param.8) | copy-start | bytes 393220
  15.2 7.0 %collective-permute-start.6 = (bf16[256,256]{1,0:T(8,128)(2,1)S(1)}, bf16[256,256]{1,0:T(8,128)(2,1)S(1)}, u32[]{:S(2)}, u32[]{:S(2)}) collective-permute-start(bf16[256,256]{1,0:T(8,128)(2,1)S(1)} %collective-permute-done.2.refs_8_), channel_id=1, source_target_pairs={{0,2},{2,0},{4,6},{6,4},{1,3},{3,1},{5,7},{7,5},{8,10},{10,8},{12,... | collective-permute-start | bytes 393224 | tf_op jit(solution)/shard_map/ppermute | solution.py:202
  16.0 12.4 %collective-permute-start.4 = (bf16[272,256]{1,0:T(8,128)(2,1)S(1)}, bf16[272,256]{1,0:T(8,128)(2,1)S(1)}, u32[]{:S(2)}, u32[]{:S(2)}) collective-permute-start(bf16[272,256]{1,0:T(8,128)(2,1)S(1)} %constant_dynamic-update-slice_fusion.refs_5_), channel_id=1, source_target_pairs={{0,6},{2,4},{4,2},{6,0},{1,7},{3,5},{5,3},{7,1},{8,14},{10,12},{12... | collective-permute-start | bytes 417800 | tf_op jit(solution)/shard_map/ppermute | solution.py:202
  19.6 14.5 %collective-permute-start.3 = (bf16[272,256]{1,0:T(8,128)(2,1)S(1)}, bf16[272,256]{1,0:T(8,128)(2,1)S(1)}, u32[]{:S(2)}, u32[]{:S(2)}) collective-permute-start(bf16[272,256]{1,0:T(8,128)(2,1)S(1)} %constant_dynamic-update-slice_fusion.refs_5_), channel_id=1, source_target_pairs={{0,2},{2,0},{4,6},{6,4},{1,3},{3,1},{5,7},{7,5},{8,10},{10,8},{12,... | collective-permute-start | bytes 417800 | tf_op jit(solution)/shard_map/ppermute | solution.py:202
  28.5 6.4 %collective-permute-start.7 = (bf16[272,256]{1,0:T(8,128)(2,1)S(1)}, bf16[272,256]{1,0:T(8,128)(2,1)S(1)}, u32[]{:S(2)}, u32[]{:S(2)}) collective-permute-start(bf16[272,256]{1,0:T(8,128)(2,1)S(1)} %pad_maximum_fusion.refs_8_), channel_id=1, source_target_pairs={{0,2},{2,0},{4,6},{6,4},{1,3},{3,1},{5,7},{7,5},{8,10},{10,8},{12,... | collective-permute-start | bytes 417800 | tf_op jit(solution)/shard_map/ppermute | solution.py:202
  29.7 15.3 %collective-permute-start.10 = (bf16[256,256]{1,0:T(8,128)(2,1)S(1)}, bf16[256,256]{1,0:T(8,128)(2,1)S(1)}, u32[]{:S(2)}, u32[]{:S(2)}) collective-permute-start(bf16[256,256]{1,0:T(8,128)(2,1)S(1)} %get-tuple-element.32), channel_id=1, source_target_pairs={{0,6},{2,4},{4,2},{6,0},{1,7},{3,5},{5,3},{7,1},{8,14},{10,12},{12... | collective-permute-start | bytes 393224 | tf_op jit(solution)/shard_map/ppermute | solution.py:202
  31.0 14.6 %collective-permute-start.8 = (bf16[256,256]{1,0:T(8,128)(2,1)S(1)}, bf16[256,256]{1,0:T(8,128)(2,1)S(1)}, u32[]{:S(2)}, u32[]{:S(2)}) collective-permute-start(bf16[256,256]{1,0:T(8,128)(2,1)S(1)} %get-tuple-element.30), channel_id=1, source_target_pairs={{0,4},{2,6},{4,0},{6,2},{1,5},{3,7},{5,1},{7,3},{8,12},{10,14},{12... | collective-permute-start | bytes 393224 | tf_op jit(solution)/shard_map/ppermute | solution.py:202
  32.0 13.6 %collective-permute-start.9 = (bf16[256,256]{1,0:T(8,128)(2,1)S(1)}, bf16[256,256]{1,0:T(8,128)(2,1)S(1)}, u32[]{:S(2)}, u32[]{:S(2)}) collective-permute-start(bf16[256,256]{1,0:T(8,128)(2,1)S(1)} %get-tuple-element.31), channel_id=1, source_target_pairs={{0,2},{2,0},{4,6},{6,4},{1,3},{3,1},{5,7},{7,5},{8,10},{10,8},{12,... | collective-permute-start | bytes 393224 | tf_op jit(solution)/shard_map/ppermute | solution.py:202
  41.1 7.3 %collective-permute-start.13 = (bf16[256,256]{1,0:T(8,128)(2,1)S(1)}, bf16[256,256]{1,0:T(8,128)(2,1)S(1)}, u32[]{:S(2)}, u32[]{:S(2)}) collective-permute-start(bf16[256,256]{1,0:T(8,128)(2,1)S(1)} %get-tuple-element.35), channel_id=1, source_target_pairs={{0,6},{2,4},{4,2},{6,0},{1,7},{3,5},{5,3},{7,1},{8,14},{10,12},{12... | collective-permute-start | bytes 393224 | tf_op jit(solution)/shard_map/ppermute | solution.py:202
  44.9 6.0 %collective-permute-start.14 = (bf16[256,256]{1,0:T(8,128)(2,1)S(1)}, bf16[256,256]{1,0:T(8,128)(2,1)S(1)}, u32[]{:S(2)}, u32[]{:S(2)}) collective-permute-start(bf16[256,256]{1,0:T(8,128)(2,1)S(1)} %get-tuple-element.36), channel_id=1, source_target_pairs={{0,4},{2,6},{4,0},{6,2},{1,5},{3,7},{5,1},{7,3},{8,12},{10,14},{12... | collective-permute-start | bytes 393224 | tf_op jit(solution)/shard_map/ppermute | solution.py:202
  44.9 6.4 %collective-permute-start.15 = (bf16[256,256]{1,0:T(8,128)(2,1)S(1)}, bf16[256,256]{1,0:T(8,128)(2,1)S(1)}, u32[]{:S(2)}, u32[]{:S(2)}) collective-permute-start(bf16[256,256]{1,0:T(8,128)(2,1)S(1)} %get-tuple-element.37), channel_id=1, source_target_pairs={{0,2},{2,0},{4,6},{6,4},{1,3},{3,1},{5,7},{7,5},{8,10},{10,8},{12,... | collective-permute-start | bytes 393224 | tf_op jit(solution)/shard_map/ppermute | solution.py:202
  45.7 1.2 %collective-permute-start.11 = (f32[8,128]{1,0:T(8,128)S(1)}, f32[8,128]{1,0:T(8,128)S(1)}, u32[]{:S(2)}, u32[]{:S(2)}) collective-permute-start(f32[8,128]{1,0:T(8,128)S(1)} %fusion.5), channel_id=1, source_target_pairs={{0,8},{8,0},{16,24},{24,16},{1,9},{9,1},{17,25},{25,17},{2,10},{10... | collective-permute-start | bytes 12296 | tf_op jit(solution)/shard_map/ppermute | solution.py:202
  46.9 5.8 %collective-permute-start.12 = (f32[8,128]{1,0:T(8,128)S(1)}, f32[8,128]{1,0:T(8,128)S(1)}, u32[]{:S(2)}, u32[]{:S(2)}) collective-permute-start(f32[8,128]{1,0:T(8,128)S(1)} %add.89), channel_id=1, source_target_pairs={{0,16},{8,24},{16,0},{24,8},{1,17},{9,25},{17,1},{25,9},{2,18},{10... | collective-permute-start | bytes 12296 | tf_op jit(solution)/shard_map/ppermute | solution.py:202
  51.5 5.0 %collective-permute-start.16 = (bf16[128,512]{1,0:T(8,128)(2,1)S(1)}, bf16[128,512]{1,0:T(8,128)(2,1)S(1)}, u32[]{:S(2)}, u32[]{:S(2)}) collective-permute-start(bf16[128,512]{1,0:T(8,128)(2,1)S(1)} %pad_maximum_fusion.2), channel_id=1, source_target_pairs={{0,1},{1,0},{2,3},{3,2},{4,5},{5,4},{6,7},{7,6},{8,9},{9,8},{10,11... | collective-permute-start | bytes 393224 | tf_op jit(solution)/shard_map/ppermute | solution.py:202

commit v11 on v10

--- a/solution.py
+++ b/solution.py
@@ -25,15 +25,18 @@
     )
 
 
-def attend_kernel(n_slots, count, chunk, held, factor, *refs):
+def attend_kernel(pieces, count, chunk, held, factor, *refs):
     last = chunk + 1 == CHUNKS
     length_ref, q_ref, turned_ref, kown_ref, vown_ref = refs[:5]
-    slot_refs, refs = refs[5 : 5 + n_slots], refs[5 + n_slots + last :]
+    n_refs = sum(pieces)
+    piece_refs, refs = refs[5 : 5 + n_refs], refs[5 + n_refs + last :]
+    n_slots = len(pieces)
     out_hbm, dq_ref, dkown_ref, dvown_ref = refs[:4]
     term_refs, refs = refs[4 : 4 + n_slots], refs[4 + n_slots :]
     if last:
         total_ref, refs = refs[0], refs[1:]
-        totals = [ref[2 * held : 2 * held + 8, :HD].astype(jnp.float32) for ref in slot_refs]
+        extra = piece_refs[0].shape[0] - EXTRA
+        totals = [ref[extra : extra + 8, :HD].astype(jnp.float32) for ref in piece_refs]
         total_ref[...] = functools.reduce(jnp.add, totals)
     out_ref, s_ref, dp_ref, e_ref, ds_ref, dot_ref = refs[:6]
     keys_ref, keys_t_ref, values_ref, values_t_ref, out_sem = refs[6:]
@@ -52,12 +55,19 @@
 
     live = (lax.broadcasted_iota(jnp.int32, (1, width), 1) % rows) < length_ref[0]
 
-    def assemble(head, own_ref, slot_start, wide_ref, tall_ref):
+    sources = [
+        ref.at[at : at + 2 * held]
+        for ref in piece_refs
+        for at in range(0, ref.shape[0] - 2 * held + 1, 2 * held)
+    ]
+    parts = len(sources) // n_slots
+
+    def assemble(head, own_ref, start, wide_ref, tall_ref):
         here = slice(head * HD, (head + 1) * HD)
         wide_ref[head, :own] = own_ref[:, (first + head) * HD : (first + head + 1) * HD]
-        for i, ref in enumerate(slot_refs):
+        for i, ref in enumerate(sources):
             part = slice(own + i * held, own + (i + 1) * held)
-            wide_ref[head, part] = ref[slot_start : slot_start + held, here]
+            wide_ref[head, part] = ref[start : start + held, here]
         tall_ref[head] = wide_ref[head].T
 
     def place(head, pair):
@@ -147,8 +157,10 @@
             e_ref[head % 2], dot_ref[head % 2], NT, preferred_element_type=jnp.float32
         ).astype(jnp.bfloat16)
         dvown_ref[:, here] = dv[:own]
-        for i, ref in enumerate(term_refs):
-            ref[held:, here] = dv[own + i * held : own + (i + 1) * held]
+        for i in range(len(sources)):
+            row = i % parts * 2 * held + held
+            term = dv[own + i * held : own + (i + 1) * held]
+            term_refs[i // parts][row : row + held, here] = term
         dk = jnp.dot(
             ds_ref[head % 2],
             heads_down(q_ref, (first + head) * GROUP, GROUP),
@@ -156,8 +168,10 @@
         )
         dk = (dk * factor).astype(jnp.bfloat16)
         dkown_ref[:, here] = dk[:own]
-        for i, ref in enumerate(term_refs):
-            ref[:held, here] = dk[own + i * held : own + (i + 1) * held]
+        for i in range(len(sources)):
+            row = i % parts * 2 * held
+            term = dk[own + i * held : own + (i + 1) * held]
+            term_refs[i // parts][row : row + held, here] = term
 
     steps = [(head, pair) for head in range(count) for pair in range(pairs)]
     scores(*steps[0])
@@ -210,19 +224,6 @@
     return x
 
 
-def far_and_near(block):
-    size = lax.axis_size("response")
-    order = (3, 1) if size == 4 else range(1, size)
-    return {m: swap(block, "response", m) for m in order}
-
-
-def line_gather(block, sent):
-    size = lax.axis_size("response")
-    if size == 4:
-        sent = {**sent, 2: swap(sent[3], "response", 1)}
-    return [block] + [sent[m] for m in range(1, size)]
-
-
 def line_reduce(slots, order):
     terms = [swap(slots[m], "response", m) for m in order]
     return functools.reduce(jnp.add, [term.astype(jnp.float32) for term in [slots[0]] + terms])
@@ -235,28 +236,16 @@
 
 
 def tensor_gather(blocks, chunk):
-    parts = lax.axis_size("tensor")
     pieces = []
-    for m in range(parts):
+    for m in range(lax.axis_size("tensor")):
         piece = jnp.concatenate([own_columns(block, chunk, m) for block in blocks], axis=0)
         pieces.append(piece if m == 0 else swap(piece, "tensor", m))
-    rows = blocks[0].shape[0]
-    return jnp.concatenate(
-        [piece[i * rows : (i + 1) * rows] for i in range(len(blocks)) for piece in pieces], axis=0
-    )
-
-
-def tensor_spread(total, n_arrays):
-    parts = lax.axis_size("tensor")
-    rows = total.shape[0] // (n_arrays * parts)
-    pieces = []
-    for m in range(parts):
-        piece = jnp.concatenate(
-            [total[(i * parts + m) * rows : (i * parts + m + 1) * rows] for i in range(n_arrays)],
-            axis=0,
-        )
-        pieces.append(piece if m == 0 else swap(piece, "tensor", m))
     return pieces
+
+
+def tensor_spread(total):
+    pieces = jnp.split(total, lax.axis_size("tensor"), axis=0)
+    return [piece if m == 0 else swap(piece, "tensor", m) for m, piece in enumerate(pieces)]
 
 
 def whole_columns(chunk_pieces, array):
@@ -302,8 +291,11 @@
     rows = q.shape[0]
     count = k.shape[1] // (HD * CHUNKS)
     n_slots = len(slots)
+    pieces = [piece for slot in slots for piece in slot]
+    n_refs = len(pieces)
     last = chunk + 1 == CHUNKS
-    n_keys = rows + n_slots * held
+    parts = lax.axis_size("tensor")
+    n_keys = rows + n_slots * parts * held
     bf16 = jnp.bfloat16
     unit = 2 * n_keys * GROUP * rows * HD * count
     step_buffer = pltpu.VMEM((2, n_keys, PAIR * rows), jnp.float32)
@@ -315,14 +307,16 @@
     scratch += [pltpu.VMEM((2, HD, GROUP * rows), bf16), down, across, down, across]
     scratch += [pltpu.SemaphoreType.DMA((count,))]
     part = lambda x: jax.ShapeDtypeStruct((x.shape[0], x.shape[1] // CHUNKS), bf16)
-    terms = [jax.ShapeDtypeStruct((2 * held, count * HD), bf16)] * n_slots
+    terms = [jax.ShapeDtypeStruct((parts * 2 * held, count * HD), bf16)] * n_slots
     total = [jax.ShapeDtypeStruct((8, HD), jnp.float32)] * last
     return pl.pallas_call(
-        functools.partial(attend_kernel, n_slots, count, chunk, held, 1.0 / math.sqrt(HD)),
-        in_specs=[SMEM] + [VMEM] * (4 + n_slots) + [HBM] * last,
+        functools.partial(
+            attend_kernel, [len(slot) for slot in slots], count, chunk, held, 1.0 / math.sqrt(HD)
+        ),
+        in_specs=[SMEM] + [VMEM] * (4 + n_refs) + [HBM] * last,
         out_specs=[HBM] + [VMEM] * (3 + n_slots + last),
         out_shape=[like(q), part(q), part(k), part(v)] + terms + total,
-        input_output_aliases={5 + n_slots: 0} if last else {},
+        input_output_aliases={5 + n_refs: 0} if last else {},
         scratch_shapes=scratch,
         compiler_params=pltpu.CompilerParams(vmem_limit_bytes=VMEM_LIMIT),
         cost_estimate=pl.CostEstimate(
@@ -331,7 +325,7 @@
             transcendentals=count * n_keys * GROUP * rows,
         ),
         name=f"attend_{chunk}",
-    )(length, q, turned, k, v, *slots, *carried)
+    )(length, q, turned, k, v, *pieces, *carried)
 
 
 def scale_all(slots_all, total, chunk_grads, shapes):
@@ -359,18 +353,26 @@
     prefix = (prefix_keys[0], prefix_values[0])
     slots_all = q.shape[0] * lax.axis_size("prompt") * lax.axis_size("response")
     first, second = [tensor_gather(prefix, chunk) for chunk in range(CHUNKS)]
-    held = first.shape[0] // 2
-    sent = far_and_near(first)
-    slots = line_gather(first, sent)
-    length_rows = length[0].astype(second.dtype) + 0 * slots[-1][-EXTRA:]
-    second = jnp.concatenate([second, length_rows], axis=0)
-    sent = far_and_near(second)
-    turned = turn(do, first)
+    held = prefix[0].shape[0]
+    size = lax.axis_size("response")
+    line = size == 4
+    block = jnp.concatenate(first, axis=0)
+    if line:
+        far = [swap(piece, "response", 3) for piece in first]
+        near = swap(block, "response", 1)
+        slots = [first, [near], [swap(jnp.concatenate(far, axis=0), "response", 1)], far]
+    else:
+        slots = [first] + [[swap(block, "response", m)] for m in range(1, size)]
+    length_rows = length[0].astype(block.dtype) + 0 * slots[-1][-1][-EXTRA:]
+    second = jnp.concatenate([*second, length_rows], axis=0)
+    order = (3, 1) if line else range(1, size)
+    sent = {m: swap(second, "response", m) for m in order}
+    turned = turn(do, block)
     results = attend(0, held, slots, length, q, turned, k, v, [])
-    if len(slots) == 4:
-        far = sent[3]
-        sent[3] = jnp.concatenate([far[:-EXTRA] + 0 * results[4], far[-EXTRA:]], axis=0)
-    next_slots = line_gather(second, sent)
+    if line:
+        far = jnp.concatenate([sent[3][:-EXTRA] + 0 * results[4], sent[3][-EXTRA:]], axis=0)
+        sent[2] = swap(far, "response", 1)
+    next_slots = [[second]] + [[sent[m]] for m in range(1, size)]
     next_results = attend(1, held, next_slots, length, q, turned, k, v, results[:1])
     terms, next_terms = results[4:], next_results[4:-1]
     behind = 0 * next_results[3][:1].astype(jnp.float32)
@@ -383,7 +385,7 @@
         slots_all, total + 0 * sums[1][:8, :HD], [results[1:4], next_results[1:4]], [like(q), like(k), like(v)]
     )
     both = jnp.concatenate([terms.astype(jnp.bfloat16) for terms in sums], axis=1)
-    pieces = [tensor_spread(both, len(prefix))]
+    pieces = [tensor_spread(both)]
     grads = [whole_columns(pieces, array) for array in range(len(prefix))]
     grads = [(grad.astype(jnp.float32) * weight).astype(jnp.bfloat16) for grad in grads]
     return tuple(x[None] for x in (next_results[0], *scaled, *grads))

time: 57.6 us -> 59 us (1.024)
  waiting for transfers between devices: 12 us -> 17.1 us
  starting transfers between devices: 26 us -> 23.9 us
  local copies, waits for them, and re-layouts: 2.52 us -> 1.01 us
    ppermute x17 -> x18, waiting for transfers between devices: 12 us -> 17.1 us  [swap(): lax.ppermute(x, axis, [(i, i ^ by) for i in range(lax.axis_size(axis))])]
    ppermute x17 -> x18, starting transfers between devices: 26 us -> 23.9 us  [swap(): lax.ppermute(x, axis, [(i, i ^ by) for i in range(lax.axis_size(axis))])]
    unnamed x12 -> x8, local copies, waits for them, and re-layouts: 1.56 us -> 0.02 us
  transfers between devices with their start and end apart: 17 -> 18, of which waited for: 8 -> 6; matrix products, arithmetic and copies ran while one was open for 3% -> 0% of each run, Pallas kernels for 25% -> 24%
where the time goes in v11:
time: 59 us; the launch traced here: 58.9 us
  starting transfers between devices  23.9 us (41%)
  waiting for transfers between devices  17.1 us (29%)
  Pallas kernels  14.3 us (24%)
  between operations  1.57 us (3%)
  other arithmetic  1.07 us (2%)
  local copies, waits for them, and re-layouts  1.01 us (2%)
    ppermute x18, starting transfers between devices, swap(): lax.ppermute(x, axis, [(i, i ^ by) for i in range(lax.axis_size(axis))])  23.9 us
    ppermute x18, waiting for transfers between devices, swap(): lax.ppermute(x, axis, [(i, i ^ by) for i in range(lax.axis_size(axis))])  17.1 us
    pallas_call x2, Pallas kernels, attend(): pl.pallas_call(functools.partial(attend_kernel, [len(slot) for slot in sl...  12.4 us
    pallas_call x1, Pallas kernels, scale_all(): pl.pallas_call(functools.partial(scale_kernel, slots_all), in_specs=[VMEM...  1.27 us
  transfers between devices with their start and end apart: 18, of which 6 were waited for; matrix products, arithmetic and copies ran while one was open for 0% of the time, Pallas kernels for 24%

profile of v11, /device:TPU:0, one launch (start us, length us, event | category | flops | bytes accessed | tf_op | source)
XLA Modules:
  0.0 58.9 jit_solution(4612915144739396917)
XLA Ops:
  0.6 0.0 copy-start
  0.7 1.0 %dynamic-slice_bitcast_fusion.2 = (bf16[64,256]{1,0:T(8,128)(2,1)S(1)}, bf16[64,256]{1,0:T(8,128)(2,1)S(1)}, bf16[64,256]{1,0:T(8,128)(2,1)S(1)}, bf16[64,256]{1...) fusion(bf16[1,64,1024]{2,1,0:T(8,128)(2,1)} %param.11, ...), kind=kLoop, calls=%fused_computation.25 | loop fusion | bytes 524304 | tf_op jit(solution)/shard_map/dynamic_slice | solution.py:235
  1.7 3.0 %collective-permute-start = (bf16[128,256]{1,0:T(8,128)(2,1)S(1)}, bf16[128,256]{1,0:T(8,128)(2,1)S(1)}, u32[]{:S(2)}, u32[]{:S(2)}) collective-permute-start(bf16[128,256]{1,0:T(8,128)(2,1)S(1)} %pad_maximum_fusion.5), channel_id=1, source_target_pairs={{0,1},{1,0},{2,3},{3,2},{4,5},{5,4},{6,7},{7,6},{8,9},{9,8},{10,11... | collective-permute-start | bytes 196616 | tf_op jit(solution)/shard_map/ppermute | solution.py:216
  4.7 3.6 %collective-permute-start.6 = (bf16[128,256]{1,0:T(8,128)(2,1)S(1)}, bf16[128,256]{1,0:T(8,128)(2,1)S(1)}, u32[]{:S(2)}, u32[]{:S(2)}) collective-permute-start(bf16[128,256]{1,0:T(8,128)(2,1)S(1)} %pad_maximum_fusion.7.refs_5_), channel_id=1, source_target_pairs={{0,6},{2,4},{4,2},{6,0},{1,7},{3,5},{5,3},{7,1},{8,14},{10,12},{12... | collective-permute-start | bytes 196616 | tf_op jit(solution)/shard_map/ppermute | solution.py:216
  8.3 0.5 collective-permute-start.1
  9.5 0.0 collective-permute-done.refs_6_
  9.5 2.1 %collective-permute-start.2 = (bf16[128,256]{1,0:T(8,128)(2,1)S(1)}, bf16[128,256]{1,0:T(8,128)(2,1)S(1)}, u32[]{:S(2)}, u32[]{:S(2)}) collective-permute-start(bf16[128,256]{1,0:T(8,128)(2,1)S(1)} %collective-permute-done.refs_6_), channel_id=1, source_target_pairs={{0,6},{2,4},{4,2},{6,0},{1,7},{3,5},{5,3},{7,1},{8,14},{10,12},{12... | collective-permute-start | bytes 196616 | tf_op jit(solution)/shard_map/ppermute | solution.py:216
  11.6 0.1 collective-permute-start.5
  11.6 0.0 copy-done
  11.6 0.0 copy-start.1
  11.7 0.6 %turn.1.refs_2_ = bf16[4,128,1024]{2,1,0:T(8,128)(2,1)S(1)} custom-call(bf16[128,4096]{1,0:T(8,128)(2,1)S(1)} %bitcast.41, bf16[256,256]{1,0:T(8,128)(2,1)S(1)} %pad_maximum_fusion.2.after_ref), custom_call_target="tpu_custom_call" | custom-call | tf_op jit(solution)/shard_map/turn/pallas_call | solution.py:279
  12.3 0.0 collective-permute-done.6.refs_9_
  12.3 3.5 %collective-permute-done.2.refs_10_ = bf16[128,256]{1,0:T(8,128)(2,1)S(1)} collective-permute-done((bf16[128,256]{1,0:T(8,128)(2,1)S(1)}, bf16[128,256]{1,0:T(8,128)(2,1)S(1)}, u32[]{:S(2)}, u32[]{:S(2)}) %collective-permute-start.2) | collective-permute-done | bytes 65568 | tf_op jit(solution)/shard_map/ppermute | solution.py:216
  15.8 0.1 collective-permute-start.7
  15.9 0.0 collective-permute-done.1
  15.9 0.0 copy-start.2
  15.9 0.0 copy-start.3
  16.0 1.9 %collective-permute-start.4 = (bf16[272,256]{1,0:T(8,128)(2,1)S(1)}, bf16[272,256]{1,0:T(8,128)(2,1)S(1)}, u32[]{:S(2)}, u32[]{:S(2)}) collective-permute-start(bf16[272,256]{1,0:T(8,128)(2,1)S(1)} %pad_maximum_fusion.refs_5_), channel_id=1, source_target_pairs={{0,6},{2,4},{4,2},{6,0},{1,7},{3,5},{5,3},{7,1},{8,14},{10,12},{12... | collective-permute-start | bytes 417800 | tf_op jit(solution)/shard_map/ppermute | solution.py:216
  17.9 1.1 %collective-permute-start.3 = (bf16[272,256]{1,0:T(8,128)(2,1)S(1)}, bf16[272,256]{1,0:T(8,128)(2,1)S(1)}, u32[]{:S(2)}, u32[]{:S(2)}) collective-permute-start(bf16[272,256]{1,0:T(8,128)(2,1)S(1)} %pad_maximum_fusion.refs_5_), channel_id=1, source_target_pairs={{0,2},{2,0},{4,6},{6,4},{1,3},{3,1},{5,7},{7,5},{8,10},{10,8},{12,... | collective-permute-start | bytes 417800 | tf_op jit(solution)/shard_map/ppermute | solution.py:216
  19.0 0.0 collective-permute-done.5.refs_7_
  19.0 4.7 %collective-permute-done.7.refs_8_ = bf16[256,256]{1,0:T(8,128)(2,1)S(1)} collective-permute-done((bf16[256,256]{1,0:T(8,128)(2,1)S(1)}, bf16[256,256]{1,0:T(8,128)(2,1)S(1)}, u32[]{:S(2)}, u32[]{:S(2)}) %collective-permute-start.7) | collective-permute-done | bytes 131104 | tf_op jit(solution)/shard_map/ppermute | solution.py:216
  23.7 0.0 copy-done.1
  23.7 0.0 copy-done.2
  23.7 0.0 copy-done.3
  23.7 6.2 %attend_0.1 = (bf16[128,4096]{1,0:T(8,128)(2,1)}, bf16[128,2048]{1,0:T(8,128)(2,1)S(1)}, bf16[128,256]{1,0:T(8,128)(2,1)S(1)}, bf16[128,256]{1,0:T(8,128)(2,1)S(...) custom-call(s32[1]{0:T(128)} %bitcast.39.refs_0_, ...), custom_call_target="tpu_custom_call" | custom-call | flops 8053063680 | bytes 2097152 | tf_op jit(solution)/shard_map/attend_0/pallas_call | solution.py:312
  29.9 0.0 collective-permute-done.4.refs_8_
  30.0 0.1 collective-permute-start.8
  30.1 2.0 %collective-permute-start.10 = (bf16[256,256]{1,0:T(8,128)(2,1)S(1)}, bf16[256,256]{1,0:T(8,128)(2,1)S(1)}, u32[]{:S(2)}, u32[]{:S(2)}) collective-permute-start(bf16[256,256]{1,0:T(8,128)(2,1)S(1)} %get-tuple-element.31), channel_id=1, source_target_pairs={{0,2},{2,0},{4,6},{6,4},{1,3},{3,1},{5,7},{7,5},{8,10},{10,8},{12,... | collective-permute-start | bytes 393224 | tf_op jit(solution)/shard_map/ppermute | solution.py:216
  32.1 1.8 %collective-permute-start.11 = (bf16[256,256]{1,0:T(8,128)(2,1)S(1)}, bf16[256,256]{1,0:T(8,128)(2,1)S(1)}, u32[]{:S(2)}, u32[]{:S(2)}) collective-permute-start(bf16[256,256]{1,0:T(8,128)(2,1)S(1)} %get-tuple-element.32), channel_id=1, source_target_pairs={{0,6},{2,4},{4,2},{6,0},{1,7},{3,5},{5,3},{7,1},{8,14},{10,12},{12... | collective-permute-start | bytes 393224 | tf_op jit(solution)/shard_map/ppermute | solution.py:216
  33.8 0.0 collective-permute-start.9
  33.8 0.0 collective-permute-done.3.refs_6_
  33.8 2.4 %collective-permute-done.8.refs_7_ = bf16[272,256]{1,0:T(8,128)(2,1)S(1)} collective-permute-done((bf16[272,256]{1,0:T(8,128)(2,1)S(1)}, bf16[272,256]{1,0:T(8,128)(2,1)S(1)}, u32[]{:S(2)}, u32[]{:S(2)}) %collective-permute-start.8) | collective-permute-done | bytes 139296 | tf_op jit(solution)/shard_map/ppermute | solution.py:216
  36.3 6.2 %attend_1.1 = (bf16[128,4096]{1,0:T(8,128)(2,1)}, bf16[128,2048]{1,0:T(8,128)(2,1)S(1)}, bf16[128,256]{1,0:T(8,128)(2,1)S(1)}, bf16[128,256]{1,0:T(8,128)(2,1)S(...) custom-call(s32[1]{0:T(128)} %bitcast.40.refs_0_, ...), custom_call_target="tpu_custom_call", output_to_operand_aliasing={{0}: (9, {})} | custom-call | flops 8053063680 | bytes 2097152 | tf_op jit(solution)/shard_map/attend_1/pallas_call | solution.py:312
  42.5 2.0 %collective-permute-start.14 = (bf16[256,256]{1,0:T(8,128)(2,1)S(1)}, bf16[256,256]{1,0:T(8,128)(2,1)S(1)}, u32[]{:S(2)}, u32[]{:S(2)}) collective-permute-start(bf16[256,256]{1,0:T(8,128)(2,1)S(1)} %get-tuple-element.35), channel_id=1, source_target_pairs={{0,6},{2,4},{4,2},{6,0},{1,7},{3,5},{5,3},{7,1},{8,14},{10,12},{12... | collective-permute-start | bytes 393224 | tf_op jit(solution)/shard_map/ppermute | solution.py:216
  44.4 0.0 collective-permute-start.15
  44.4 0.0 collective-permute-done.10
  44.4 2.5 %collective-permute-start.16 = (bf16[256,256]{1,0:T(8,128)(2,1)S(1)}, bf16[256,256]{1,0:T(8,128)(2,1)S(1)}, u32[]{:S(2)}, u32[]{:S(2)}) collective-permute-start(bf16[256,256]{1,0:T(8,128)(2,1)S(1)} %get-tuple-element.37), channel_id=1, source_target_pairs={{0,2},{2,0},{4,6},{6,4},{1,3},{3,1},{5,7},{7,5},{8,10},{10,8},{12,... | collective-permute-start | bytes 393224 | tf_op jit(solution)/shard_map/ppermute | solution.py:216
  46.9 0.0 collective-permute-done.11
  46.9 0.0 collective-permute-done.9
  46.9 0.1 fusion.6
  47.0 0.1 collective-permute-start.12
  47.1 1.1 %collective-permute-done.12 = f32[8,128]{1,0:T(8,128)S(1)} collective-permute-done((f32[8,128]{1,0:T(8,128)S(1)}, f32[8,128]{1,0:T(8,128)S(1)}, u32[]{:S(2)}, u32[]{:S(2)}) %collective-permute-start.12) | collective-permute-done | bytes 4128 | tf_op jit(solution)/shard_map/ppermute | solution.py:216
  48.3 1.5 %collective-permute-start.13 = (f32[8,128]{1,0:T(8,128)S(1)}, f32[8,128]{1,0:T(8,128)S(1)}, u32[]{:S(2)}, u32[]{:S(2)}) collective-permute-start(f32[8,128]{1,0:T(8,128)S(1)} %add.89), channel_id=1, source_target_pairs={{0,16},{8,24},{16,0},{24,8},{1,17},{9,25},{17,1},{25,9},{2,18},{10... | collective-permute-start | bytes 12296 | tf_op jit(solution)/shard_map/ppermute | solution.py:216
  49.8 0.0 collective-permute-done.14
  49.8 3.2 %collective-permute-done.15 = bf16[256,256]{1,0:T(8,128)(2,1)S(1)} collective-permute-done((bf16[256,256]{1,0:T(8,128)(2,1)S(1)}, bf16[256,256]{1,0:T(8,128)(2,1)S(1)}, u32[]{:S(2)}, u32[]{:S(2)}) %collective-permute-start.15) | collective-permute-done | bytes 131104 | tf_op jit(solution)/shard_map/ppermute | solution.py:216
  52.9 0.0 collective-permute-done.16
  52.9 0.1 fusion.5
  53.0 1.6 %collective-permute-start.17 = (bf16[128,512]{1,0:T(8,128)(2,1)S(1)}, bf16[128,512]{1,0:T(8,128)(2,1)S(1)}, u32[]{:S(2)}, u32[]{:S(2)}) collective-permute-start(bf16[128,512]{1,0:T(8,128)(2,1)S(1)} %fusion), channel_id=1, source_target_pairs={{0,1},{1,0},{2,3},{3,2},{4,5},{5,4},{6,7},{7,6},{8,9},{9,8},{10,11... | collective-permute-start | bytes 393224 | tf_op jit(solution)/shard_map/ppermute | solution.py:216
  54.6 0.0 collective-permute-done.13
  54.7 1.3 %scale.1 = (bf16[128,4096]{1,0:T(8,128)(2,1)}, bf16[128,512]{1,0:T(8,128)(2,1)}, bf16[128,512]{1,0:T(8,128)(2,1)}) custom-call(f32[8,128]{1,0:T(8,128)S(1)} %get-tuple-element.52.total_ref, bf16[128,2048]{1,0:T(8,128)(2,1)S(1)} %get-tuple-element.38.refs_0_, bf16[128,256]{1,0:T(8,128)(2,1)S(1)} %get-tuple-element.39.refs_1_, ...), custom_call_target="tpu_custom_call" | custom-call | flops 655360 | bytes 2621440 | tf_op jit(solution)/shard_map/scale/pallas_call | solution.py:333
  55.9 2.1 %collective-permute-done.17 = bf16[128,512]{1,0:T(8,128)(2,1)S(1)} collective-permute-done((bf16[128,512]{1,0:T(8,128)(2,1)S(1)}, bf16[128,512]{1,0:T(8,128)(2,1)S(1)}, u32[]{:S(2)}, u32[]{:S(2)}) %collective-permute-start.17) | collective-permute-done | bytes 131104 | tf_op jit(solution)/shard_map/ppermute | solution.py:216
  58.1 0.8 %multiply_convert_fusion = (bf16[1,64,1024]{2,1,0:T(8,128)(2,1)}, bf16[1,64,1024]{2,1,0:T(8,128)(2,1)}) fusion(bf16[1,64,512]{2,1,0:T(8,128)(2,1)S(1)} %select_bitcast_fusion, bf16[1,64,512]{2,1,0:T(8,128)(2,1)S(1)} %get-tuple-element.46, f32[1024]{0:T(1024)S(1)} %broadcast_bitcast_fusion, bf16[1,64,512]{2,1,0:T(8,128)(2,1)S(1)} %get-tuple-element.54, ...), kind=kLoop, calls=%fused_computation.4 | loop fusion | flops 786432 | bytes 528384 | tf_op jit(solution)/shard_map/convert_element_type | solution.py:390
  (19 shorter events, 0.2 us)
Async XLA Ops:
  0.6 11.0 %copy-start = (bf16[1,128,4096]{2,1,0:T(8,128)(2,1)S(1)}, bf16[1,128,4096]{2,1,0:T(8,128)(2,1)}, u32[]{:S(2)}) copy-start(bf16[1,128,4096]{2,1,0:T(8,128)(2,1)} %param.13) | copy-start | bytes 3145732
  1.7 7.8 %collective-permute-start = (bf16[128,256]{1,0:T(8,128)(2,1)S(1)}, bf16[128,256]{1,0:T(8,128)(2,1)S(1)}, u32[]{:S(2)}, u32[]{:S(2)}) collective-permute-start(bf16[128,256]{1,0:T(8,128)(2,1)S(1)} %pad_maximum_fusion.5), channel_id=1, source_target_pairs={{0,1},{1,0},{2,3},{3,2},{4,5},{5,4},{6,7},{7,6},{8,9},{9,8},{10,11... | collective-permute-start | bytes 196616 | tf_op jit(solution)/shard_map/ppermute | solution.py:216
  4.7 7.6 %collective-permute-start.6 = (bf16[128,256]{1,0:T(8,128)(2,1)S(1)}, bf16[128,256]{1,0:T(8,128)(2,1)S(1)}, u32[]{:S(2)}, u32[]{:S(2)}) collective-permute-start(bf16[128,256]{1,0:T(8,128)(2,1)S(1)} %pad_maximum_fusion.7.refs_5_), channel_id=1, source_target_pairs={{0,6},{2,4},{4,2},{6,0},{1,7},{3,5},{5,3},{7,1},{8,14},{10,12},{12... | collective-permute-start | bytes 196616 | tf_op jit(solution)/shard_map/ppermute | solution.py:216
  8.3 7.6 %collective-permute-start.1 = (bf16[128,256]{1,0:T(8,128)(2,1)S(1)}, bf16[128,256]{1,0:T(8,128)(2,1)S(1)}, u32[]{:S(2)}, u32[]{:S(2)}) collective-permute-start(bf16[128,256]{1,0:T(8,128)(2,1)S(1)} %pad_maximum_fusion.6), channel_id=1, source_target_pairs={{0,1},{1,0},{2,3},{3,2},{4,5},{5,4},{6,7},{7,6},{8,9},{9,8},{10,11... | collective-permute-start | bytes 196616 | tf_op jit(solution)/shard_map/ppermute | solution.py:216
  9.5 6.3 %collective-permute-start.2 = (bf16[128,256]{1,0:T(8,128)(2,1)S(1)}, bf16[128,256]{1,0:T(8,128)(2,1)S(1)}, u32[]{:S(2)}, u32[]{:S(2)}) collective-permute-start(bf16[128,256]{1,0:T(8,128)(2,1)S(1)} %collective-permute-done.refs_6_), channel_id=1, source_target_pairs={{0,6},{2,4},{4,2},{6,0},{1,7},{3,5},{5,3},{7,1},{8,14},{10,12},{12... | collective-permute-start | bytes 196616 | tf_op jit(solution)/shard_map/ppermute | solution.py:216
  11.6 7.4 %collective-permute-start.5 = (bf16[256,256]{1,0:T(8,128)(2,1)S(1)}, bf16[256,256]{1,0:T(8,128)(2,1)S(1)}, u32[]{:S(2)}, u32[]{:S(2)}) collective-permute-start(bf16[256,256]{1,0:T(8,128)(2,1)S(1)} %pad_maximum_fusion.2.after_ref), channel_id=1, source_target_pairs={{0,2},{2,0},{4,6},{6,4},{1,3},{3,1},{5,7},{7,5},{8,10},{10,8},{12,... | collective-permute-start | bytes 393224 | tf_op jit(solution)/shard_map/ppermute | solution.py:216
  11.6 12.1 %copy-start.1 = (bf16[1,128,4096]{2,1,0:T(8,128)(2,1)S(1)}, bf16[1,128,4096]{2,1,0:T(8,128)(2,1)}, u32[]{:S(2)}) copy-start(bf16[1,128,4096]{2,1,0:T(8,128)(2,1)} %param.7) | copy-start | bytes 3145732
  15.8 7.9 %collective-permute-start.7 = (bf16[256,256]{1,0:T(8,128)(2,1)S(1)}, bf16[256,256]{1,0:T(8,128)(2,1)S(1)}, u32[]{:S(2)}, u32[]{:S(2)}) collective-permute-start(bf16[256,256]{1,0:T(8,128)(2,1)S(1)} %pad_maximum_fusion.3), channel_id=1, source_target_pairs={{0,2},{2,0},{4,6},{6,4},{1,3},{3,1},{5,7},{7,5},{8,10},{10,8},{12,... | collective-permute-start | bytes 393224 | tf_op jit(solution)/shard_map/ppermute | solution.py:216
  15.9 7.8 %copy-start.2 = (bf16[1,128,512]{2,1,0:T(8,128)(2,1)S(1)}, bf16[1,128,512]{2,1,0:T(8,128)(2,1)}, u32[]{:S(2)}) copy-start(bf16[1,128,512]{2,1,0:T(8,128)(2,1)} %param.8) | copy-start | bytes 393220
  15.9 7.8 %copy-start.3 = (bf16[1,128,512]{2,1,0:T(8,128)(2,1)S(1)}, bf16[1,128,512]{2,1,0:T(8,128)(2,1)}, u32[]{:S(2)}) copy-start(bf16[1,128,512]{2,1,0:T(8,128)(2,1)} %param.9) | copy-start | bytes 393220
  16.0 13.9 %collective-permute-start.4 = (bf16[272,256]{1,0:T(8,128)(2,1)S(1)}, bf16[272,256]{1,0:T(8,128)(2,1)S(1)}, u32[]{:S(2)}, u32[]{:S(2)}) collective-permute-start(bf16[272,256]{1,0:T(8,128)(2,1)S(1)} %pad_maximum_fusion.refs_5_), channel_id=1, source_target_pairs={{0,6},{2,4},{4,2},{6,0},{1,7},{3,5},{5,3},{7,1},{8,14},{10,12},{12... | collective-permute-start | bytes 417800 | tf_op jit(solution)/shard_map/ppermute | solution.py:216
  17.9 16.0 %collective-permute-start.3 = (bf16[272,256]{1,0:T(8,128)(2,1)S(1)}, bf16[272,256]{1,0:T(8,128)(2,1)S(1)}, u32[]{:S(2)}, u32[]{:S(2)}) collective-permute-start(bf16[272,256]{1,0:T(8,128)(2,1)S(1)} %pad_maximum_fusion.refs_5_), channel_id=1, source_target_pairs={{0,2},{2,0},{4,6},{6,4},{1,3},{3,1},{5,7},{7,5},{8,10},{10,8},{12,... | collective-permute-start | bytes 417800 | tf_op jit(solution)/shard_map/ppermute | solution.py:216
  30.0 6.3 %collective-permute-start.8 = (bf16[272,256]{1,0:T(8,128)(2,1)S(1)}, bf16[272,256]{1,0:T(8,128)(2,1)S(1)}, u32[]{:S(2)}, u32[]{:S(2)}) collective-permute-start(bf16[272,256]{1,0:T(8,128)(2,1)S(1)} %pad_maximum_fusion.1), channel_id=1, source_target_pairs={{0,2},{2,0},{4,6},{6,4},{1,3},{3,1},{5,7},{7,5},{8,10},{10,8},{12,... | collective-permute-start | bytes 417800 | tf_op jit(solution)/shard_map/ppermute | solution.py:216
  30.1 14.4 %collective-permute-start.10 = (bf16[256,256]{1,0:T(8,128)(2,1)S(1)}, bf16[256,256]{1,0:T(8,128)(2,1)S(1)}, u32[]{:S(2)}, u32[]{:S(2)}) collective-permute-start(bf16[256,256]{1,0:T(8,128)(2,1)S(1)} %get-tuple-element.31), channel_id=1, source_target_pairs={{0,2},{2,0},{4,6},{6,4},{1,3},{3,1},{5,7},{7,5},{8,10},{10,8},{12,... | collective-permute-start | bytes 393224 | tf_op jit(solution)/shard_map/ppermute | solution.py:216
  32.1 14.9 %collective-permute-start.11 = (bf16[256,256]{1,0:T(8,128)(2,1)S(1)}, bf16[256,256]{1,0:T(8,128)(2,1)S(1)}, u32[]{:S(2)}, u32[]{:S(2)}) collective-permute-start(bf16[256,256]{1,0:T(8,128)(2,1)S(1)} %get-tuple-element.32), channel_id=1, source_target_pairs={{0,6},{2,4},{4,2},{6,0},{1,7},{3,5},{5,3},{7,1},{8,14},{10,12},{12... | collective-permute-start | bytes 393224 | tf_op jit(solution)/shard_map/ppermute | solution.py:216
  33.8 13.1 %collective-permute-start.9 = (bf16[256,256]{1,0:T(8,128)(2,1)S(1)}, bf16[256,256]{1,0:T(8,128)(2,1)S(1)}, u32[]{:S(2)}, u32[]{:S(2)}) collective-permute-start(bf16[256,256]{1,0:T(8,128)(2,1)S(1)} %get-tuple-element.30), channel_id=1, source_target_pairs={{0,4},{2,6},{4,0},{6,2},{1,5},{3,7},{5,1},{7,3},{8,12},{10,14},{12... | collective-permute-start | bytes 393224 | tf_op jit(solution)/shard_map/ppermute | solution.py:216
  42.5 7.3 %collective-permute-start.14 = (bf16[256,256]{1,0:T(8,128)(2,1)S(1)}, bf16[256,256]{1,0:T(8,128)(2,1)S(1)}, u32[]{:S(2)}, u32[]{:S(2)}) collective-permute-start(bf16[256,256]{1,0:T(8,128)(2,1)S(1)} %get-tuple-element.35), channel_id=1, source_target_pairs={{0,6},{2,4},{4,2},{6,0},{1,7},{3,5},{5,3},{7,1},{8,14},{10,12},{12... | collective-permute-start | bytes 393224 | tf_op jit(solution)/shard_map/ppermute | solution.py:216
  44.4 8.5 %collective-permute-start.15 = (bf16[256,256]{1,0:T(8,128)(2,1)S(1)}, bf16[256,256]{1,0:T(8,128)(2,1)S(1)}, u32[]{:S(2)}, u32[]{:S(2)}) collective-permute-start(bf16[256,256]{1,0:T(8,128)(2,1)S(1)} %get-tuple-element.36), channel_id=1, source_target_pairs={{0,4},{2,6},{4,0},{6,2},{1,5},{3,7},{5,1},{7,3},{8,12},{10,14},{12... | collective-permute-start | bytes 393224 | tf_op jit(solution)/shard_map/ppermute | solution.py:216
  44.4 8.5 %collective-permute-start.16 = (bf16[256,256]{1,0:T(8,128)(2,1)S(1)}, bf16[256,256]{1,0:T(8,128)(2,1)S(1)}, u32[]{:S(2)}, u32[]{:S(2)}) collective-permute-start(bf16[256,256]{1,0:T(8,128)(2,1)S(1)} %get-tuple-element.37), channel_id=1, source_target_pairs={{0,2},{2,0},{4,6},{6,4},{1,3},{3,1},{5,7},{7,5},{8,10},{10,8},{12,... | collective-permute-start | bytes 393224 | tf_op jit(solution)/shard_map/ppermute | solution.py:216
  47.0 1.2 %collective-permute-start.12 = (f32[8,128]{1,0:T(8,128)S(1)}, f32[8,128]{1,0:T(8,128)S(1)}, u32[]{:S(2)}, u32[]{:S(2)}) collective-permute-start(f32[8,128]{1,0:T(8,128)S(1)} %fusion.4), channel_id=1, source_target_pairs={{0,8},{8,0},{16,24},{24,16},{1,9},{9,1},{17,25},{25,17},{2,10},{10... | collective-permute-start | bytes 12296 | tf_op jit(solution)/shard_map/ppermute | solution.py:216
  48.3 6.4 %collective-permute-start.13 = (f32[8,128]{1,0:T(8,128)S(1)}, f32[8,128]{1,0:T(8,128)S(1)}, u32[]{:S(2)}, u32[]{:S(2)}) collective-permute-start(f32[8,128]{1,0:T(8,128)S(1)} %add.89), channel_id=1, source_target_pairs={{0,16},{8,24},{16,0},{24,8},{1,17},{9,25},{17,1},{25,9},{2,18},{10... | collective-permute-start | bytes 12296 | tf_op jit(solution)/shard_map/ppermute | solution.py:216
  53.0 5.0 %collective-permute-start.17 = (bf16[128,512]{1,0:T(8,128)(2,1)S(1)}, bf16[128,512]{1,0:T(8,128)(2,1)S(1)}, u32[]{:S(2)}, u32[]{:S(2)}) collective-permute-start(bf16[128,512]{1,0:T(8,128)(2,1)S(1)} %fusion), channel_id=1, source_target_pairs={{0,1},{1,0},{2,3},{3,2},{4,5},{5,4},{6,7},{7,6},{8,9},{9,8},{10,11... | collective-permute-start | bytes 393224 | tf_op jit(solution)/shard_map/ppermute | solution.py:216

commit v12 on v10

--- a/solution.py
+++ b/solution.py
@@ -223,9 +223,9 @@
     return [block] + [sent[m] for m in range(1, size)]
 
 
-def line_reduce(slots, order):
-    terms = [swap(slots[m], "response", m) for m in order]
-    return functools.reduce(jnp.add, [term.astype(jnp.float32) for term in [slots[0]] + terms])
+def far_sum(slots, order):
+    terms = [slots[0]] + [swap(slots[m], "response", m) for m in order]
+    return functools.reduce(jnp.add, [term.astype(jnp.float32) for term in terms])
 
 
 def own_columns(block, chunk, by):
@@ -374,15 +374,17 @@
     next_results = attend(1, held, next_slots, length, q, turned, k, v, results[:1])
     terms, next_terms = results[4:], next_results[4:-1]
     behind = 0 * next_results[3][:1].astype(jnp.float32)
-    farthest_first = list(range(len(terms) - 1, 0, -1))
-    order = (2, 1, 3) if len(terms) == 4 else farthest_first
-    sums = [line_reduce(terms, order) + behind, line_reduce(next_terms, farthest_first)]
-    total = sum_over(next_results[-1] + 0 * sums[0][:8, :HD], "prompt")
+    order = list(range(len(terms) - 1, 1, -1))
+    sums = [far_sum(terms, order) + behind, far_sum(next_terms, order)]
+    nearest = jnp.concatenate([terms[1], next_terms[1]], axis=1)
+    near = swap(nearest, "response", 1)
+    total = sum_over(next_results[-1] + 0 * nearest[:8, :HD].astype(jnp.float32), "prompt")
     weight = jnp.tile(slots_all / total[:1], (1, prefix[0].shape[1] // HD))
     scaled = scale_all(
         slots_all, total + 0 * sums[1][:8, :HD], [results[1:4], next_results[1:4]], [like(q), like(k), like(v)]
     )
-    both = jnp.concatenate([terms.astype(jnp.bfloat16) for terms in sums], axis=1)
+    both = jnp.concatenate(sums, axis=1) + near.astype(jnp.float32)
+    both = both.astype(jnp.bfloat16)
     pieces = [tensor_spread(both, len(prefix))]
     grads = [whole_columns(pieces, array) for array in range(len(prefix))]
     grads = [(grad.astype(jnp.float32) * weight).astype(jnp.bfloat16) for grad in grads]

time: 57.6 us -> 64.6 us (1.12)
  waiting for transfers between devices: 12 us -> 17.6 us
  local copies, waits for them, and re-layouts: 2.52 us -> 4.96 us
  starting transfers between devices: 26 us -> 24 us
  Pallas kernels: 14.3 us -> 15.2 us
    ppermute x17 -> x16, waiting for transfers between devices: 12 us -> 17.6 us  [swap(): lax.ppermute(x, axis, [(i, i ^ by) for i in range(lax.axis_size(axis))])]
    unnamed x12 -> x20, local copies, waits for them, and re-layouts: 1.56 us -> 3.99 us
    ppermute x17 -> x16, starting transfers between devices: 26 us -> 24 us  [swap(): lax.ppermute(x, axis, [(i, i ^ by) for i in range(lax.axis_size(axis))])]
    pallas_call x2, Pallas kernels: 12.4 us -> 13.3 us  [attend(): pl.pallas_call(functools.partial(attend_kernel, n_slots, count, chunk, he...]
  transfers between devices with their start and end apart: 17 -> 16, of which waited for: 8 -> 8; matrix products, arithmetic and copies ran while one was open for 3% -> 3% of each run, Pallas kernels for 25% -> 24%
where the time goes in v12:
time: 64.6 us; the launch traced here: 64.4 us
  starting transfers between devices  24 us (37%)
  waiting for transfers between devices  17.6 us (27%)
  Pallas kernels  15.2 us (24%)
  local copies, waits for them, and re-layouts  4.96 us (8%)
  between operations  1.55 us (2%)
  other arithmetic  1.06 us (2%)
    ppermute x16, starting transfers between devices, swap(): lax.ppermute(x, axis, [(i, i ^ by) for i in range(lax.axis_size(axis))])  24 us
    ppermute x16, waiting for transfers between devices, swap(): lax.ppermute(x, axis, [(i, i ^ by) for i in range(lax.axis_size(axis))])  17.6 us
    pallas_call x2, Pallas kernels, attend(): pl.pallas_call(functools.partial(attend_kernel, n_slots, count, chunk, he...  13.3 us
    unnamed x20, local copies, waits for them, and re-layouts  3.99 us
  transfers between devices with their start and end apart: 16, of which 8 were waited for; matrix products, arithmetic and copies ran while one was open for 3% of the time, Pallas kernels for 24%

profile of v12, /device:TPU:0, one launch (start us, length us, event | category | flops | bytes accessed | tf_op | source)
XLA Modules:
  0.0 64.4 jit_solution(4327021473406523454)
XLA Ops:
  0.6 0.0 copy-start
  0.7 0.9 %dynamic-slice_bitcast_fusion = (bf16[64,256]{1,0:T(8,128)(2,1)S(1)}, bf16[64,256]{1,0:T(8,128)(2,1)S(1)}, bf16[64,256]{1,0:T(8,128)(2,1)S(1)}, bf16[64,256]{1,0...) fusion(bf16[1,64,1024]{2,1,0:T(8,128)(2,1)} %param.11, s32[]{:T(128)S(6)} %select_n.41, ...), kind=kLoop, calls=%fused_computation.21 | loop fusion | bytes 393228 | tf_op jit(solution)/shard_map/dynamic_slice | solution.py:234
  1.6 3.0 %collective-permute-start = (bf16[128,256]{1,0:T(8,128)(2,1)S(1)}, bf16[128,256]{1,0:T(8,128)(2,1)S(1)}, u32[]{:S(2)}, u32[]{:S(2)}) collective-permute-start(bf16[128,256]{1,0:T(8,128)(2,1)S(1)} %pad_maximum_fusion.4), channel_id=1, source_target_pairs={{0,1},{1,0},{2,3},{3,2},{4,5},{5,4},{6,7},{7,6},{8,9},{9,8},{10,11... | collective-permute-start | bytes 196616 | tf_op jit(solution)/shard_map/ppermute | solution.py:202
  4.7 0.1 collective-permute-start.1
  5.4 0.8 %bitcast_dynamic-update-slice_fusion.1 = bf16[272,256]{1,0:T(8,128)(2,1)S(1)} fusion(bf16[1,64,1024]{2,1,0:T(8,128)(2,1)} %param.10, s32[]{:T(128)S(6)} %select_n.40), kind=kLoop, calls=%fused_computation.20 | loop fusion | bytes 65540
  6.2 0.9 %collective-permute-done = bf16[128,256]{1,0:T(8,128)(2,1)S(1)} collective-permute-done((bf16[128,256]{1,0:T(8,128)(2,1)S(1)}, bf16[128,256]{1,0:T(8,128)(2,1)S(1)}, u32[]{:S(2)}, u32[]{:S(2)}) %collective-permute-start) | collective-permute-done | bytes 65568 | tf_op jit(solution)/shard_map/ppermute | solution.py:202
  7.1 4.6 %collective-permute-start.2 = (bf16[256,256]{1,0:T(8,128)(2,1)S(1)}, bf16[256,256]{1,0:T(8,128)(2,1)S(1)}, u32[]{:S(2)}, u32[]{:S(2)}) collective-permute-start(bf16[256,256]{1,0:T(8,128)(2,1)S(1)} %pad_maximum_fusion.2.after_ref.refs_5_), channel_id=1, source_target_pairs={{0,6},{2,4},{4,2},{6,0},{1,7},{3,5},{5,3},{7,1},{8,14},{10,12},{12... | collective-permute-start | bytes 393224 | tf_op jit(solution)/shard_map/ppermute | solution.py:202
  11.7 0.0 collective-permute-start.5
  11.7 0.0 copy-done
  11.7 0.0 copy-start.1
  11.7 0.0 copy-start.4
  11.7 0.6 turn.1.refs_2_
  12.3 0.0 copy-start.2
  12.3 0.0 collective-permute-done.1
  12.4 0.8 %bitcast_dynamic-update-slice_fusion = bf16[272,256]{1,0:T(8,128)(2,1)S(1)} fusion(bf16[272,256]{1,0:T(8,128)(2,1)S(1)} %slice_dynamic-update-slice_fusion.1, bf16[1,64,1024]{2,1,0:T(8,128)(2,1)} %param.11, s32[]{:T(128)S(6)} %select_n.40), kind=kLoop, calls=%fused_computation.19 | loop fusion | bytes 65540
  13.1 2.1 %collective-permute-done.2.refs_8_ = bf16[256,256]{1,0:T(8,128)(2,1)S(1)} collective-permute-done((bf16[256,256]{1,0:T(8,128)(2,1)S(1)}, bf16[256,256]{1,0:T(8,128)(2,1)S(1)}, u32[]{:S(2)}, u32[]{:S(2)}) %collective-permute-start.2) | collective-permute-done | bytes 131104 | tf_op jit(solution)/shard_map/ppermute | solution.py:202
  15.2 0.8 %collective-permute-start.6 = (bf16[256,256]{1,0:T(8,128)(2,1)S(1)}, bf16[256,256]{1,0:T(8,128)(2,1)S(1)}, u32[]{:S(2)}, u32[]{:S(2)}) collective-permute-start(bf16[256,256]{1,0:T(8,128)(2,1)S(1)} %collective-permute-done.2.refs_8_), channel_id=1, source_target_pairs={{0,2},{2,0},{4,6},{6,4},{1,3},{3,1},{5,7},{7,5},{8,10},{10,8},{12,... | collective-permute-start | bytes 393224 | tf_op jit(solution)/shard_map/ppermute | solution.py:202
  16.0 3.6 %collective-permute-start.4 = (bf16[272,256]{1,0:T(8,128)(2,1)S(1)}, bf16[272,256]{1,0:T(8,128)(2,1)S(1)}, u32[]{:S(2)}, u32[]{:S(2)}) collective-permute-start(bf16[272,256]{1,0:T(8,128)(2,1)S(1)} %constant_dynamic-update-slice_fusion.refs_5_), channel_id=1, source_target_pairs={{0,6},{2,4},{4,2},{6,0},{1,7},{3,5},{5,3},{7,1},{8,14},{10,12},{12... | collective-permute-start | bytes 417800 | tf_op jit(solution)/shard_map/ppermute | solution.py:202
  19.6 1.1 %collective-permute-start.3 = (bf16[272,256]{1,0:T(8,128)(2,1)S(1)}, bf16[272,256]{1,0:T(8,128)(2,1)S(1)}, u32[]{:S(2)}, u32[]{:S(2)}) collective-permute-start(bf16[272,256]{1,0:T(8,128)(2,1)S(1)} %constant_dynamic-update-slice_fusion.refs_5_), channel_id=1, source_target_pairs={{0,2},{2,0},{4,6},{6,4},{1,3},{3,1},{5,7},{7,5},{8,10},{10,8},{12,... | collective-permute-start | bytes 417800 | tf_op jit(solution)/shard_map/ppermute | solution.py:202
  20.7 0.0 collective-permute-done.5.refs_6_
  20.7 1.5 %collective-permute-done.6.refs_7_ = bf16[256,256]{1,0:T(8,128)(2,1)S(1)} collective-permute-done((bf16[256,256]{1,0:T(8,128)(2,1)S(1)}, bf16[256,256]{1,0:T(8,128)(2,1)S(1)}, u32[]{:S(2)}, u32[]{:S(2)}) %collective-permute-start.6) | collective-permute-done | bytes 131104 | tf_op jit(solution)/shard_map/ppermute | solution.py:202
  22.2 0.0 copy-done.1
  22.2 0.0 copy-done.4
  22.2 0.0 copy-done.2
  22.2 6.2 %attend_0.1 = (bf16[128,4096]{1,0:T(8,128)(2,1)}, bf16[128,2048]{1,0:T(8,128)(2,1)S(1)}, bf16[128,256]{1,0:T(8,128)(2,1)S(1)}, bf16[128,256]{1,0:T(8,128)(2,1)S(...) custom-call(s32[1]{0:T(128)} %bitcast.39.refs_0_, ...), custom_call_target="tpu_custom_call" | custom-call | flops 8053063680 | bytes 2097152 | tf_op jit(solution)/shard_map/attend_0/pallas_call | solution.py:320
  28.4 0.0 copy-start.6
  28.4 0.0 copy-start.7
  28.4 0.0 collective-permute-done.4
  28.5 0.6 copy-done.6
  29.1 0.0 copy-done.7
  29.1 1.2 %collective-permute-start.7 = (bf16[272,256]{1,0:T(8,128)(2,1)S(1)}, bf16[272,256]{1,0:T(8,128)(2,1)}, u32[]{:S(2)}, u32[]{:S(2)}) collective-permute-start(bf16[272,256]{1,0:T(8,128)(2,1)S(1)} %pad_maximum_fusion.1.refs_8_), channel_id=1, source_target_pairs={{0,2},{2,0},{4,6},{6,4},{1,3},{3,1},{5,7},{7,5},{8,10},{10,8},{12,... | collective-permute-start | bytes 417800 | tf_op jit(solution)/shard_map/ppermute | solution.py:202
  30.3 1.3 %collective-permute-start.12 = (bf16[256,256]{1,0:T(8,128)(2,1)}, bf16[256,256]{1,0:T(8,128)(2,1)S(1)}, u32[]{:S(2)}, u32[]{:S(2)}) collective-permute-start(bf16[256,256]{1,0:T(8,128)(2,1)} %copy-done.7), channel_id=1, source_target_pairs={{0,6},{2,4},{4,2},{6,0},{1,7},{3,5},{5,3},{7,1},{8,14},{10,12},{12... | collective-permute-start | bytes 393224 | tf_op jit(solution)/shard_map/ppermute | solution.py:202
  31.6 1.0 %collective-permute-start.13 = (bf16[256,256]{1,0:T(8,128)(2,1)}, bf16[256,256]{1,0:T(8,128)(2,1)S(1)}, u32[]{:S(2)}, u32[]{:S(2)}) collective-permute-start(bf16[256,256]{1,0:T(8,128)(2,1)} %copy-done.6), channel_id=1, source_target_pairs={{0,4},{2,6},{4,0},{6,2},{1,5},{3,7},{5,1},{7,3},{8,12},{10,14},{12... | collective-permute-start | bytes 393224 | tf_op jit(solution)/shard_map/ppermute | solution.py:202
  32.6 0.0 collective-permute-done.3.refs_6_
  32.6 3.1 %collective-permute-done.7.refs_7_ = bf16[272,256]{1,0:T(8,128)(2,1)} collective-permute-done((bf16[272,256]{1,0:T(8,128)(2,1)S(1)}, bf16[272,256]{1,0:T(8,128)(2,1)}, u32[]{:S(2)}, u32[]{:S(2)}) %collective-permute-start.7) | collective-permute-done | bytes 139296 | tf_op jit(solution)/shard_map/ppermute | solution.py:202
  35.7 0.0 copy-start.3
  35.7 0.9 %copy-done.3 = bf16[1,128,512]{2,1,0:T(8,128)(2,1)S(1)} copy-done((bf16[1,128,512]{2,1,0:T(8,128)(2,1)S(1)}, bf16[1,128,512]{2,1,0:T(8,128)(2,1)}, u32[]{:S(2)}) %copy-start.3) | copy-done | bytes 131096
  36.6 0.0 copy-start.5
  36.6 0.9 %copy-done.5 = bf16[1,128,512]{2,1,0:T(8,128)(2,1)S(1)} copy-done((bf16[1,128,512]{2,1,0:T(8,128)(2,1)S(1)}, bf16[1,128,512]{2,1,0:T(8,128)(2,1)}, u32[]{:S(2)}) %copy-start.5) | copy-done | bytes 131096
  37.5 7.1 %attend_1.1 = (bf16[128,4096]{1,0:T(8,128)(2,1)}, bf16[128,2048]{1,0:T(8,128)(2,1)S(1)}, bf16[128,256]{1,0:T(8,128)(2,1)S(1)}, bf16[128,256]{1,0:T(8,128)(2,1)S(...) custom-call(s32[1]{0:T(128)} %bitcast.40.refs_0_, ...), custom_call_target="tpu_custom_call", output_to_operand_aliasing={{0}: (9, {})} | custom-call | flops 8053063680 | bytes 2097152 | tf_op jit(solution)/shard_map/attend_1/pallas_call | solution.py:320
  44.6 0.1 collective-permute-start.14
  44.7 3.9 %collective-permute-start.10 = (bf16[256,256]{1,0:T(8,128)(2,1)S(1)}, bf16[256,256]{1,0:T(8,128)(2,1)S(1)}, u32[]{:S(2)}, u32[]{:S(2)}) collective-permute-start(bf16[256,256]{1,0:T(8,128)(2,1)S(1)} %get-tuple-element.32), channel_id=1, source_target_pairs={{0,6},{2,4},{4,2},{6,0},{1,7},{3,5},{5,3},{7,1},{8,14},{10,12},{12... | collective-permute-start | bytes 393224 | tf_op jit(solution)/shard_map/ppermute | solution.py:202
  48.6 0.5 collective-permute-start.11
  49.1 0.0 collective-permute-done.12
  49.1 0.1 collective-permute-start.8
  49.1 0.0 collective-permute-done.13
  49.2 0.1 add_add_fusion
  49.2 1.1 %collective-permute-done.8 = f32[8,128]{1,0:T(8,128)S(1)} collective-permute-done((f32[8,128]{1,0:T(8,128)S(1)}, f32[8,128]{1,0:T(8,128)S(1)}, u32[]{:S(2)}, u32[]{:S(2)}) %collective-permute-start.8) | collective-permute-done | bytes 4128 | tf_op jit(solution)/shard_map/ppermute | solution.py:202
  50.3 1.5 %collective-permute-start.9 = (f32[8,128]{1,0:T(8,128)S(1)}, f32[8,128]{1,0:T(8,128)S(1)}, u32[]{:S(2)}, u32[]{:S(2)}) collective-permute-start(f32[8,128]{1,0:T(8,128)S(1)} %add.80), channel_id=1, source_target_pairs={{0,16},{8,24},{16,0},{24,8},{1,17},{9,25},{17,1},{25,9},{2,18},{10... | collective-permute-start | bytes 12296 | tf_op jit(solution)/shard_map/ppermute | solution.py:202
  51.8 2.6 %collective-permute-done.10 = bf16[256,256]{1,0:T(8,128)(2,1)S(1)} collective-permute-done((bf16[256,256]{1,0:T(8,128)(2,1)S(1)}, bf16[256,256]{1,0:T(8,128)(2,1)S(1)}, u32[]{:S(2)}, u32[]{:S(2)}) %collective-permute-start.10) | collective-permute-done | bytes 131104 | tf_op jit(solution)/shard_map/ppermute | solution.py:202
  54.3 2.7 %collective-permute-done.11 = bf16[256,256]{1,0:T(8,128)(2,1)S(1)} collective-permute-done((bf16[256,256]{1,0:T(8,128)(2,1)S(1)}, bf16[256,256]{1,0:T(8,128)(2,1)S(1)}, u32[]{:S(2)}, u32[]{:S(2)}) %collective-permute-start.11) | collective-permute-done | bytes 131104 | tf_op jit(solution)/shard_map/ppermute | solution.py:202
  57.1 0.1 convert_add_fusion
  57.1 0.0 collective-permute-done.9
  57.1 1.3 %scale.1 = (bf16[128,4096]{1,0:T(8,128)(2,1)}, bf16[128,512]{1,0:T(8,128)(2,1)}, bf16[128,512]{1,0:T(8,128)(2,1)}) custom-call(f32[8,128]{1,0:T(8,128)S(1)} %get-tuple-element.46.total_ref, bf16[128,2048]{1,0:T(8,128)(2,1)S(1)} %get-tuple-element.34.refs_0_, bf16[128,256]{1,0:T(8,128)(2,1)S(1)} %get-tuple-element.35.refs_1_, ...), custom_call_target="tpu_custom_call" | custom-call | flops 655360 | bytes 2621440 | tf_op jit(solution)/shard_map/scale/pallas_call | solution.py:339
  58.4 0.0 collective-permute-done.14
  58.4 0.1 fusion
  58.5 1.4 %collective-permute-start.15 = (bf16[128,512]{1,0:T(8,128)(2,1)S(1)}, bf16[128,512]{1,0:T(8,128)(2,1)S(1)}, u32[]{:S(2)}, u32[]{:S(2)}) collective-permute-start(bf16[128,512]{1,0:T(8,128)(2,1)S(1)} %pad_maximum_fusion.3), channel_id=1, source_target_pairs={{0,1},{1,0},{2,3},{3,2},{4,5},{5,4},{6,7},{7,6},{8,9},{9,8},{10,11... | collective-permute-start | bytes 393224 | tf_op jit(solution)/shard_map/ppermute | solution.py:202
  59.9 3.6 %collective-permute-done.15 = bf16[128,512]{1,0:T(8,128)(2,1)S(1)} collective-permute-done((bf16[128,512]{1,0:T(8,128)(2,1)S(1)}, bf16[128,512]{1,0:T(8,128)(2,1)S(1)}, u32[]{:S(2)}, u32[]{:S(2)}) %collective-permute-start.15) | collective-permute-done | bytes 131104 | tf_op jit(solution)/shard_map/ppermute | solution.py:202
  63.6 0.8 %multiply_convert_fusion = (bf16[1,64,1024]{2,1,0:T(8,128)(2,1)}, bf16[1,64,1024]{2,1,0:T(8,128)(2,1)}) fusion(bf16[1,64,512]{2,1,0:T(8,128)(2,1)S(1)} %get-tuple-element.50, bf16[1,64,512]{2,1,0:T(8,128)(2,1)S(1)} %get-tuple-element.48, f32[1024]{0:T(1024)S(1)} %broadcast_bitcast_fusion, bf16[1,64,512]{2,1,0:T(8,128)(2,1)S(1)} %get-tuple-element.49, ...), kind=kLoop, calls=%fused_computation.3 | loop fusion | flops 786432 | bytes 528384 | tf_op jit(solution)/shard_map/convert_element_type | solution.py:390
  (20 shorter events, 0.2 us)
Async XLA Ops:
  0.6 11.0 %copy-start = (bf16[1,128,4096]{2,1,0:T(8,128)(2,1)S(1)}, bf16[1,128,4096]{2,1,0:T(8,128)(2,1)}, u32[]{:S(2)}) copy-start(bf16[1,128,4096]{2,1,0:T(8,128)(2,1)} %param.13) | copy-start | bytes 3145732
  1.6 5.4 %collective-permute-start = (bf16[128,256]{1,0:T(8,128)(2,1)S(1)}, bf16[128,256]{1,0:T(8,128)(2,1)S(1)}, u32[]{:S(2)}, u32[]{:S(2)}) collective-permute-start(bf16[128,256]{1,0:T(8,128)(2,1)S(1)} %pad_maximum_fusion.4), channel_id=1, source_target_pairs={{0,1},{1,0},{2,3},{3,2},{4,5},{5,4},{6,7},{7,6},{8,9},{9,8},{10,11... | collective-permute-start | bytes 196616 | tf_op jit(solution)/shard_map/ppermute | solution.py:202
  4.7 7.7 %collective-permute-start.1 = (bf16[128,256]{1,0:T(8,128)(2,1)S(1)}, bf16[128,256]{1,0:T(8,128)(2,1)S(1)}, u32[]{:S(2)}, u32[]{:S(2)}) collective-permute-start(bf16[128,256]{1,0:T(8,128)(2,1)S(1)} %pad_maximum_fusion.5), channel_id=1, source_target_pairs={{0,1},{1,0},{2,3},{3,2},{4,5},{5,4},{6,7},{7,6},{8,9},{9,8},{10,11... | collective-permute-start | bytes 196616 | tf_op jit(solution)/shard_map/ppermute | solution.py:202
  7.1 8.2 %collective-permute-start.2 = (bf16[256,256]{1,0:T(8,128)(2,1)S(1)}, bf16[256,256]{1,0:T(8,128)(2,1)S(1)}, u32[]{:S(2)}, u32[]{:S(2)}) collective-permute-start(bf16[256,256]{1,0:T(8,128)(2,1)S(1)} %pad_maximum_fusion.2.after_ref.refs_5_), channel_id=1, source_target_pairs={{0,6},{2,4},{4,2},{6,0},{1,7},{3,5},{5,3},{7,1},{8,14},{10,12},{12... | collective-permute-start | bytes 393224 | tf_op jit(solution)/shard_map/ppermute | solution.py:202
  11.7 9.0 %collective-permute-start.5 = (bf16[256,256]{1,0:T(8,128)(2,1)S(1)}, bf16[256,256]{1,0:T(8,128)(2,1)S(1)}, u32[]{:S(2)}, u32[]{:S(2)}) collective-permute-start(bf16[256,256]{1,0:T(8,128)(2,1)S(1)} %pad_maximum_fusion.2.after_ref.refs_5_), channel_id=1, source_target_pairs={{0,2},{2,0},{4,6},{6,4},{1,3},{3,1},{5,7},{7,5},{8,10},{10,8},{12,... | collective-permute-start | bytes 393224 | tf_op jit(solution)/shard_map/ppermute | solution.py:202
  11.7 10.5 %copy-start.1 = (bf16[1,128,4096]{2,1,0:T(8,128)(2,1)S(1)}, bf16[1,128,4096]{2,1,0:T(8,128)(2,1)}, u32[]{:S(2)}) copy-start(bf16[1,128,4096]{2,1,0:T(8,128)(2,1)} %param.7) | copy-start | bytes 3145732
  11.7 10.5 %copy-start.4 = (bf16[1,128,512]{2,1,0:T(8,128)(2,1)S(1)}, bf16[1,128,512]{2,1,0:T(8,128)(2,1)}, u32[]{:S(2)}) copy-start(bf16[1,128,512]{2,1,0:T(8,128)(2,1)} %param.9) | copy-start | bytes 393220
  12.3 9.9 %copy-start.2 = (bf16[1,128,512]{2,1,0:T(8,128)(2,1)S(1)}, bf16[1,128,512]{2,1,0:T(8,128)(2,1)}, u32[]{:S(2)}) copy-start(bf16[1,128,512]{2,1,0:T(8,128)(2,1)} %param.8) | copy-start | bytes 393220
  15.2 7.0 %collective-permute-start.6 = (bf16[256,256]{1,0:T(8,128)(2,1)S(1)}, bf16[256,256]{1,0:T(8,128)(2,1)S(1)}, u32[]{:S(2)}, u32[]{:S(2)}) collective-permute-start(bf16[256,256]{1,0:T(8,128)(2,1)S(1)} %collective-permute-done.2.refs_8_), channel_id=1, source_target_pairs={{0,2},{2,0},{4,6},{6,4},{1,3},{3,1},{5,7},{7,5},{8,10},{10,8},{12,... | collective-permute-start | bytes 393224 | tf_op jit(solution)/shard_map/ppermute | solution.py:202
  16.0 12.4 %collective-permute-start.4 = (bf16[272,256]{1,0:T(8,128)(2,1)S(1)}, bf16[272,256]{1,0:T(8,128)(2,1)S(1)}, u32[]{:S(2)}, u32[]{:S(2)}) collective-permute-start(bf16[272,256]{1,0:T(8,128)(2,1)S(1)} %constant_dynamic-update-slice_fusion.refs_5_), channel_id=1, source_target_pairs={{0,6},{2,4},{4,2},{6,0},{1,7},{3,5},{5,3},{7,1},{8,14},{10,12},{12... | collective-permute-start | bytes 417800 | tf_op jit(solution)/shard_map/ppermute | solution.py:202
  19.6 13.0 %collective-permute-start.3 = (bf16[272,256]{1,0:T(8,128)(2,1)S(1)}, bf16[272,256]{1,0:T(8,128)(2,1)S(1)}, u32[]{:S(2)}, u32[]{:S(2)}) collective-permute-start(bf16[272,256]{1,0:T(8,128)(2,1)S(1)} %constant_dynamic-update-slice_fusion.refs_5_), channel_id=1, source_target_pairs={{0,2},{2,0},{4,6},{6,4},{1,3},{3,1},{5,7},{7,5},{8,10},{10,8},{12,... | collective-permute-start | bytes 417800 | tf_op jit(solution)/shard_map/ppermute | solution.py:202
  28.4 0.7 %copy-start.6 = (bf16[256,256]{1,0:T(8,128)(2,1)}, bf16[256,256]{1,0:T(8,128)(2,1)S(1)}, u32[]{:S(2)}) copy-start(bf16[256,256]{1,0:T(8,128)(2,1)S(1)} %get-tuple-element.44) | copy-start | bytes 393220
  28.4 0.7 %copy-start.7 = (bf16[256,256]{1,0:T(8,128)(2,1)}, bf16[256,256]{1,0:T(8,128)(2,1)S(1)}, u32[]{:S(2)}) copy-start(bf16[256,256]{1,0:T(8,128)(2,1)S(1)} %get-tuple-element.43) | copy-start | bytes 393220
  29.1 6.6 %collective-permute-start.7 = (bf16[272,256]{1,0:T(8,128)(2,1)S(1)}, bf16[272,256]{1,0:T(8,128)(2,1)}, u32[]{:S(2)}, u32[]{:S(2)}) collective-permute-start(bf16[272,256]{1,0:T(8,128)(2,1)S(1)} %pad_maximum_fusion.1.refs_8_), channel_id=1, source_target_pairs={{0,2},{2,0},{4,6},{6,4},{1,3},{3,1},{5,7},{7,5},{8,10},{10,8},{12,... | collective-permute-start | bytes 417800 | tf_op jit(solution)/shard_map/ppermute | solution.py:202
  30.3 18.8 %collective-permute-start.12 = (bf16[256,256]{1,0:T(8,128)(2,1)}, bf16[256,256]{1,0:T(8,128)(2,1)S(1)}, u32[]{:S(2)}, u32[]{:S(2)}) collective-permute-start(bf16[256,256]{1,0:T(8,128)(2,1)} %copy-done.7), channel_id=1, source_target_pairs={{0,6},{2,4},{4,2},{6,0},{1,7},{3,5},{5,3},{7,1},{8,14},{10,12},{12... | collective-permute-start | bytes 393224 | tf_op jit(solution)/shard_map/ppermute | solution.py:202
  31.6 17.5 %collective-permute-start.13 = (bf16[256,256]{1,0:T(8,128)(2,1)}, bf16[256,256]{1,0:T(8,128)(2,1)S(1)}, u32[]{:S(2)}, u32[]{:S(2)}) collective-permute-start(bf16[256,256]{1,0:T(8,128)(2,1)} %copy-done.6), channel_id=1, source_target_pairs={{0,4},{2,6},{4,0},{6,2},{1,5},{3,7},{5,1},{7,3},{8,12},{10,14},{12... | collective-permute-start | bytes 393224 | tf_op jit(solution)/shard_map/ppermute | solution.py:202
  35.7 0.9 %copy-start.3 = (bf16[1,128,512]{2,1,0:T(8,128)(2,1)S(1)}, bf16[1,128,512]{2,1,0:T(8,128)(2,1)}, u32[]{:S(2)}) copy-start(bf16[1,128,512]{2,1,0:T(8,128)(2,1)} %param.8) | copy-start | bytes 393220
  36.6 0.9 %copy-start.5 = (bf16[1,128,512]{2,1,0:T(8,128)(2,1)S(1)}, bf16[1,128,512]{2,1,0:T(8,128)(2,1)}, u32[]{:S(2)}) copy-start(bf16[1,128,512]{2,1,0:T(8,128)(2,1)} %param.9) | copy-start | bytes 393220
  44.6 13.8 %collective-permute-start.14 = (bf16[256,512]{1,0:T(8,128)(2,1)S(1)}, bf16[256,512]{1,0:T(8,128)(2,1)S(1)}, u32[]{:S(2)}, u32[]{:S(2)}) collective-permute-start(bf16[256,512]{1,0:T(8,128)(2,1)S(1)} %pad_maximum_fusion), channel_id=1, source_target_pairs={{0,2},{2,0},{4,6},{6,4},{1,3},{3,1},{5,7},{7,5},{8,10},{10,8},{12,... | collective-permute-start | bytes 786440 | tf_op jit(solution)/shard_map/ppermute | solution.py:202
  44.7 9.6 %collective-permute-start.10 = (bf16[256,256]{1,0:T(8,128)(2,1)S(1)}, bf16[256,256]{1,0:T(8,128)(2,1)S(1)}, u32[]{:S(2)}, u32[]{:S(2)}) collective-permute-start(bf16[256,256]{1,0:T(8,128)(2,1)S(1)} %get-tuple-element.32), channel_id=1, source_target_pairs={{0,6},{2,4},{4,2},{6,0},{1,7},{3,5},{5,3},{7,1},{8,14},{10,12},{12... | collective-permute-start | bytes 393224 | tf_op jit(solution)/shard_map/ppermute | solution.py:202
  48.6 8.5 %collective-permute-start.11 = (bf16[256,256]{1,0:T(8,128)(2,1)S(1)}, bf16[256,256]{1,0:T(8,128)(2,1)S(1)}, u32[]{:S(2)}, u32[]{:S(2)}) collective-permute-start(bf16[256,256]{1,0:T(8,128)(2,1)S(1)} %get-tuple-element.33), channel_id=1, source_target_pairs={{0,4},{2,6},{4,0},{6,2},{1,5},{3,7},{5,1},{7,3},{8,12},{10,14},{12... | collective-permute-start | bytes 393224 | tf_op jit(solution)/shard_map/ppermute | solution.py:202
  49.1 1.2 %collective-permute-start.8 = (f32[8,128]{1,0:T(8,128)S(1)}, f32[8,128]{1,0:T(8,128)S(1)}, u32[]{:S(2)}, u32[]{:S(2)}) collective-permute-start(f32[8,128]{1,0:T(8,128)S(1)} %multiply_add_fusion), channel_id=1, source_target_pairs={{0,8},{8,0},{16,24},{24,16},{1,9},{9,1},{17,25},{25,17},{2,10},{10... | collective-permute-start | bytes 12296 | tf_op jit(solution)/shard_map/ppermute | solution.py:202
  50.3 6.8 %collective-permute-start.9 = (f32[8,128]{1,0:T(8,128)S(1)}, f32[8,128]{1,0:T(8,128)S(1)}, u32[]{:S(2)}, u32[]{:S(2)}) collective-permute-start(f32[8,128]{1,0:T(8,128)S(1)} %add.80), channel_id=1, source_target_pairs={{0,16},{8,24},{16,0},{24,8},{1,17},{9,25},{17,1},{25,9},{2,18},{10... | collective-permute-start | bytes 12296 | tf_op jit(solution)/shard_map/ppermute | solution.py:202
  58.5 5.0 %collective-permute-start.15 = (bf16[128,512]{1,0:T(8,128)(2,1)S(1)}, bf16[128,512]{1,0:T(8,128)(2,1)S(1)}, u32[]{:S(2)}, u32[]{:S(2)}) collective-permute-start(bf16[128,512]{1,0:T(8,128)(2,1)S(1)} %pad_maximum_fusion.3), channel_id=1, source_target_pairs={{0,1},{1,0},{2,3},{3,2},{4,5},{5,4},{6,7},{7,6},{8,9},{9,8},{10,11... | collective-permute-start | bytes 393224 | tf_op jit(solution)/shard_map/ppermute | solution.py:202

commit v13 on v12

--- a/solution.py
+++ b/solution.py
@@ -14,7 +14,6 @@
 CHUNKS = 2
 EXTRA = 16
 STEP = 64
-VMEM_LIMIT = 40 * 1024 * 1024
 SMALL_LIMIT = 8 * 1024 * 1024
 NT = (((1,), (1,)), ((), ()))
 
@@ -313,7 +312,7 @@
     across = pltpu.VMEM((count, HD, n_keys), bf16)
     scratch = [wide, step_buffer, step_buffer, head_buffer, head_buffer]
     scratch += [pltpu.VMEM((2, HD, GROUP * rows), bf16), down, across, down, across]
-    scratch += [pltpu.SemaphoreType.DMA((count,))]
+    in_buffers = sum(math.prod(x.shape) * jnp.dtype(x.dtype).itemsize for x in scratch)
     part = lambda x: jax.ShapeDtypeStruct((x.shape[0], x.shape[1] // CHUNKS), bf16)
     terms = [jax.ShapeDtypeStruct((2 * held, count * HD), bf16)] * n_slots
     total = [jax.ShapeDtypeStruct((8, HD), jnp.float32)] * last
@@ -323,8 +322,8 @@
         out_specs=[HBM] + [VMEM] * (3 + n_slots + last),
         out_shape=[like(q), part(q), part(k), part(v)] + terms + total,
         input_output_aliases={5 + n_slots: 0} if last else {},
-        scratch_shapes=scratch,
-        compiler_params=pltpu.CompilerParams(vmem_limit_bytes=VMEM_LIMIT),
+        scratch_shapes=scratch + [pltpu.SemaphoreType.DMA((count,))],
+        compiler_params=pltpu.CompilerParams(vmem_limit_bytes=in_buffers * 5 // 4 + SMALL_LIMIT // 2),
         cost_estimate=pl.CostEstimate(
             flops=24 * unit,
             bytes_accessed=8 * rows * GROUP * HD * count,

time: 64.6 us -> 64.6 us (level)
  no operation moved by 1% of the time
where the time goes in v13:
time: 64.6 us; the launch traced here: 64.4 us
  starting transfers between devices  24 us (37%)
  waiting for transfers between devices  17.6 us (27%)
  Pallas kernels  15.2 us (24%)
  local copies, waits for them, and re-layouts  4.96 us (8%)
  between operations  1.55 us (2%)
  other arithmetic  1.06 us (2%)
    ppermute x16, starting transfers between devices, swap(): lax.ppermute(x, axis, [(i, i ^ by) for i in range(lax.axis_size(axis))])  24 us
    ppermute x16, waiting for transfers between devices, swap(): lax.ppermute(x, axis, [(i, i ^ by) for i in range(lax.axis_size(axis))])  17.6 us
    pallas_call x2, Pallas kernels, attend(): pl.pallas_call(functools.partial(attend_kernel, n_slots, count, chunk, he...  13.3 us
    unnamed x20, local copies, waits for them, and re-layouts  3.99 us
  transfers between devices with their start and end apart: 16, of which 8 were waited for; matrix products, arithmetic and copies ran while one was open for 3% of the time, Pallas kernels for 24%

profile of v13, /device:TPU:0, one launch (start us, length us, event | category | flops | bytes accessed | tf_op | source)
XLA Modules:
  0.0 64.4 jit_solution(14001128899751142730)
XLA Ops:
  0.6 0.0 copy-start
  0.7 0.9 %dynamic-slice_bitcast_fusion = (bf16[64,256]{1,0:T(8,128)(2,1)S(1)}, bf16[64,256]{1,0:T(8,128)(2,1)S(1)}, bf16[64,256]{1,0:T(8,128)(2,1)S(1)}, bf16[64,256]{1,0...) fusion(bf16[1,64,1024]{2,1,0:T(8,128)(2,1)} %param.11, s32[]{:T(128)S(6)} %select_n.41, ...), kind=kLoop, calls=%fused_computation.21 | loop fusion | bytes 393228 | tf_op jit(solution)/shard_map/dynamic_slice | solution.py:233
  1.6 3.0 %collective-permute-start = (bf16[128,256]{1,0:T(8,128)(2,1)S(1)}, bf16[128,256]{1,0:T(8,128)(2,1)S(1)}, u32[]{:S(2)}, u32[]{:S(2)}) collective-permute-start(bf16[128,256]{1,0:T(8,128)(2,1)S(1)} %pad_maximum_fusion.4), channel_id=1, source_target_pairs={{0,1},{1,0},{2,3},{3,2},{4,5},{5,4},{6,7},{7,6},{8,9},{9,8},{10,11... | collective-permute-start | bytes 196616 | tf_op jit(solution)/shard_map/ppermute | solution.py:201
  4.7 0.1 collective-permute-start.1
  5.4 0.8 %bitcast_dynamic-update-slice_fusion.1 = bf16[272,256]{1,0:T(8,128)(2,1)S(1)} fusion(bf16[1,64,1024]{2,1,0:T(8,128)(2,1)} %param.10, s32[]{:T(128)S(6)} %select_n.40), kind=kLoop, calls=%fused_computation.20 | loop fusion | bytes 65540
  6.2 0.9 %collective-permute-done = bf16[128,256]{1,0:T(8,128)(2,1)S(1)} collective-permute-done((bf16[128,256]{1,0:T(8,128)(2,1)S(1)}, bf16[128,256]{1,0:T(8,128)(2,1)S(1)}, u32[]{:S(2)}, u32[]{:S(2)}) %collective-permute-start) | collective-permute-done | bytes 65568 | tf_op jit(solution)/shard_map/ppermute | solution.py:201
  7.1 4.6 %collective-permute-start.2 = (bf16[256,256]{1,0:T(8,128)(2,1)S(1)}, bf16[256,256]{1,0:T(8,128)(2,1)S(1)}, u32[]{:S(2)}, u32[]{:S(2)}) collective-permute-start(bf16[256,256]{1,0:T(8,128)(2,1)S(1)} %pad_maximum_fusion.2.after_ref.refs_5_), channel_id=1, source_target_pairs={{0,6},{2,4},{4,2},{6,0},{1,7},{3,5},{5,3},{7,1},{8,14},{10,12},{12... | collective-permute-start | bytes 393224 | tf_op jit(solution)/shard_map/ppermute | solution.py:201
  11.7 0.0 collective-permute-start.5
  11.7 0.0 copy-done
  11.7 0.0 copy-start.1
  11.7 0.0 copy-start.4
  11.7 0.6 turn.1.refs_2_
  12.3 0.0 copy-start.2
  12.3 0.0 collective-permute-done.1
  12.4 0.8 %bitcast_dynamic-update-slice_fusion = bf16[272,256]{1,0:T(8,128)(2,1)S(1)} fusion(bf16[272,256]{1,0:T(8,128)(2,1)S(1)} %slice_dynamic-update-slice_fusion.1, bf16[1,64,1024]{2,1,0:T(8,128)(2,1)} %param.11, s32[]{:T(128)S(6)} %select_n.40), kind=kLoop, calls=%fused_computation.19 | loop fusion | bytes 65540
  13.1 2.1 %collective-permute-done.2.refs_8_ = bf16[256,256]{1,0:T(8,128)(2,1)S(1)} collective-permute-done((bf16[256,256]{1,0:T(8,128)(2,1)S(1)}, bf16[256,256]{1,0:T(8,128)(2,1)S(1)}, u32[]{:S(2)}, u32[]{:S(2)}) %collective-permute-start.2) | collective-permute-done | bytes 131104 | tf_op jit(solution)/shard_map/ppermute | solution.py:201
  15.2 0.8 %collective-permute-start.6 = (bf16[256,256]{1,0:T(8,128)(2,1)S(1)}, bf16[256,256]{1,0:T(8,128)(2,1)S(1)}, u32[]{:S(2)}, u32[]{:S(2)}) collective-permute-start(bf16[256,256]{1,0:T(8,128)(2,1)S(1)} %collective-permute-done.2.refs_8_), channel_id=1, source_target_pairs={{0,2},{2,0},{4,6},{6,4},{1,3},{3,1},{5,7},{7,5},{8,10},{10,8},{12,... | collective-permute-start | bytes 393224 | tf_op jit(solution)/shard_map/ppermute | solution.py:201
  16.0 3.6 %collective-permute-start.4 = (bf16[272,256]{1,0:T(8,128)(2,1)S(1)}, bf16[272,256]{1,0:T(8,128)(2,1)S(1)}, u32[]{:S(2)}, u32[]{:S(2)}) collective-permute-start(bf16[272,256]{1,0:T(8,128)(2,1)S(1)} %constant_dynamic-update-slice_fusion.refs_5_), channel_id=1, source_target_pairs={{0,6},{2,4},{4,2},{6,0},{1,7},{3,5},{5,3},{7,1},{8,14},{10,12},{12... | collective-permute-start | bytes 417800 | tf_op jit(solution)/shard_map/ppermute | solution.py:201
  19.6 1.1 %collective-permute-start.3 = (bf16[272,256]{1,0:T(8,128)(2,1)S(1)}, bf16[272,256]{1,0:T(8,128)(2,1)S(1)}, u32[]{:S(2)}, u32[]{:S(2)}) collective-permute-start(bf16[272,256]{1,0:T(8,128)(2,1)S(1)} %constant_dynamic-update-slice_fusion.refs_5_), channel_id=1, source_target_pairs={{0,2},{2,0},{4,6},{6,4},{1,3},{3,1},{5,7},{7,5},{8,10},{10,8},{12,... | collective-permute-start | bytes 417800 | tf_op jit(solution)/shard_map/ppermute | solution.py:201
  20.7 0.0 collective-permute-done.5.refs_6_
  20.7 1.5 %collective-permute-done.6.refs_7_ = bf16[256,256]{1,0:T(8,128)(2,1)S(1)} collective-permute-done((bf16[256,256]{1,0:T(8,128)(2,1)S(1)}, bf16[256,256]{1,0:T(8,128)(2,1)S(1)}, u32[]{:S(2)}, u32[]{:S(2)}) %collective-permute-start.6) | collective-permute-done | bytes 131104 | tf_op jit(solution)/shard_map/ppermute | solution.py:201
  22.2 0.0 copy-done.1
  22.2 0.0 copy-done.4
  22.2 0.0 copy-done.2
  22.2 6.2 %attend_0.1 = (bf16[128,4096]{1,0:T(8,128)(2,1)}, bf16[128,2048]{1,0:T(8,128)(2,1)S(1)}, bf16[128,256]{1,0:T(8,128)(2,1)S(1)}, bf16[128,256]{1,0:T(8,128)(2,1)S(...) custom-call(s32[1]{0:T(128)} %bitcast.39.refs_0_, ...), custom_call_target="tpu_custom_call" | custom-call | flops 8053063680 | bytes 2097152 | tf_op jit(solution)/shard_map/attend_0/pallas_call | solution.py:319
  28.4 0.0 copy-start.6
  28.4 0.0 copy-start.7
  28.4 0.0 collective-permute-done.4
  28.5 0.6 copy-done.6
  29.1 0.0 copy-done.7
  29.1 1.2 %collective-permute-start.7 = (bf16[272,256]{1,0:T(8,128)(2,1)S(1)}, bf16[272,256]{1,0:T(8,128)(2,1)}, u32[]{:S(2)}, u32[]{:S(2)}) collective-permute-start(bf16[272,256]{1,0:T(8,128)(2,1)S(1)} %pad_maximum_fusion.1.refs_8_), channel_id=1, source_target_pairs={{0,2},{2,0},{4,6},{6,4},{1,3},{3,1},{5,7},{7,5},{8,10},{10,8},{12,... | collective-permute-start | bytes 417800 | tf_op jit(solution)/shard_map/ppermute | solution.py:201
  30.3 1.3 %collective-permute-start.12 = (bf16[256,256]{1,0:T(8,128)(2,1)}, bf16[256,256]{1,0:T(8,128)(2,1)S(1)}, u32[]{:S(2)}, u32[]{:S(2)}) collective-permute-start(bf16[256,256]{1,0:T(8,128)(2,1)} %copy-done.7), channel_id=1, source_target_pairs={{0,6},{2,4},{4,2},{6,0},{1,7},{3,5},{5,3},{7,1},{8,14},{10,12},{12... | collective-permute-start | bytes 393224 | tf_op jit(solution)/shard_map/ppermute | solution.py:201
  31.6 1.0 %collective-permute-start.13 = (bf16[256,256]{1,0:T(8,128)(2,1)}, bf16[256,256]{1,0:T(8,128)(2,1)S(1)}, u32[]{:S(2)}, u32[]{:S(2)}) collective-permute-start(bf16[256,256]{1,0:T(8,128)(2,1)} %copy-done.6), channel_id=1, source_target_pairs={{0,4},{2,6},{4,0},{6,2},{1,5},{3,7},{5,1},{7,3},{8,12},{10,14},{12... | collective-permute-start | bytes 393224 | tf_op jit(solution)/shard_map/ppermute | solution.py:201
  32.6 0.0 collective-permute-done.3.refs_6_
  32.6 3.1 %collective-permute-done.7.refs_7_ = bf16[272,256]{1,0:T(8,128)(2,1)} collective-permute-done((bf16[272,256]{1,0:T(8,128)(2,1)S(1)}, bf16[272,256]{1,0:T(8,128)(2,1)}, u32[]{:S(2)}, u32[]{:S(2)}) %collective-permute-start.7) | collective-permute-done | bytes 139296 | tf_op jit(solution)/shard_map/ppermute | solution.py:201
  35.7 0.0 copy-start.3
  35.7 0.9 %copy-done.3 = bf16[1,128,512]{2,1,0:T(8,128)(2,1)S(1)} copy-done((bf16[1,128,512]{2,1,0:T(8,128)(2,1)S(1)}, bf16[1,128,512]{2,1,0:T(8,128)(2,1)}, u32[]{:S(2)}) %copy-start.3) | copy-done | bytes 131096
  36.6 0.0 copy-start.5
  36.6 0.9 %copy-done.5 = bf16[1,128,512]{2,1,0:T(8,128)(2,1)S(1)} copy-done((bf16[1,128,512]{2,1,0:T(8,128)(2,1)S(1)}, bf16[1,128,512]{2,1,0:T(8,128)(2,1)}, u32[]{:S(2)}) %copy-start.5) | copy-done | bytes 131096
  37.5 7.1 %attend_1.1 = (bf16[128,4096]{1,0:T(8,128)(2,1)}, bf16[128,2048]{1,0:T(8,128)(2,1)S(1)}, bf16[128,256]{1,0:T(8,128)(2,1)S(1)}, bf16[128,256]{1,0:T(8,128)(2,1)S(...) custom-call(s32[1]{0:T(128)} %bitcast.40.refs_0_, ...), custom_call_target="tpu_custom_call", output_to_operand_aliasing={{0}: (9, {})} | custom-call | flops 8053063680 | bytes 2097152 | tf_op jit(solution)/shard_map/attend_1/pallas_call | solution.py:319
  44.6 0.1 collective-permute-start.14
  44.7 3.9 %collective-permute-start.10 = (bf16[256,256]{1,0:T(8,128)(2,1)S(1)}, bf16[256,256]{1,0:T(8,128)(2,1)S(1)}, u32[]{:S(2)}, u32[]{:S(2)}) collective-permute-start(bf16[256,256]{1,0:T(8,128)(2,1)S(1)} %get-tuple-element.32), channel_id=1, source_target_pairs={{0,6},{2,4},{4,2},{6,0},{1,7},{3,5},{5,3},{7,1},{8,14},{10,12},{12... | collective-permute-start | bytes 393224 | tf_op jit(solution)/shard_map/ppermute | solution.py:201
  48.6 0.5 collective-permute-start.11
  49.1 0.0 collective-permute-done.12
  49.1 0.1 collective-permute-start.8
  49.1 0.0 collective-permute-done.13
  49.2 0.1 add_add_fusion
  49.2 1.1 %collective-permute-done.8 = f32[8,128]{1,0:T(8,128)S(1)} collective-permute-done((f32[8,128]{1,0:T(8,128)S(1)}, f32[8,128]{1,0:T(8,128)S(1)}, u32[]{:S(2)}, u32[]{:S(2)}) %collective-permute-start.8) | collective-permute-done | bytes 4128 | tf_op jit(solution)/shard_map/ppermute | solution.py:201
  50.3 1.5 %collective-permute-start.9 = (f32[8,128]{1,0:T(8,128)S(1)}, f32[8,128]{1,0:T(8,128)S(1)}, u32[]{:S(2)}, u32[]{:S(2)}) collective-permute-start(f32[8,128]{1,0:T(8,128)S(1)} %add.80), channel_id=1, source_target_pairs={{0,16},{8,24},{16,0},{24,8},{1,17},{9,25},{17,1},{25,9},{2,18},{10... | collective-permute-start | bytes 12296 | tf_op jit(solution)/shard_map/ppermute | solution.py:201
  51.8 2.6 %collective-permute-done.10 = bf16[256,256]{1,0:T(8,128)(2,1)S(1)} collective-permute-done((bf16[256,256]{1,0:T(8,128)(2,1)S(1)}, bf16[256,256]{1,0:T(8,128)(2,1)S(1)}, u32[]{:S(2)}, u32[]{:S(2)}) %collective-permute-start.10) | collective-permute-done | bytes 131104 | tf_op jit(solution)/shard_map/ppermute | solution.py:201
  54.3 2.7 %collective-permute-done.11 = bf16[256,256]{1,0:T(8,128)(2,1)S(1)} collective-permute-done((bf16[256,256]{1,0:T(8,128)(2,1)S(1)}, bf16[256,256]{1,0:T(8,128)(2,1)S(1)}, u32[]{:S(2)}, u32[]{:S(2)}) %collective-permute-start.11) | collective-permute-done | bytes 131104 | tf_op jit(solution)/shard_map/ppermute | solution.py:201
  57.1 0.1 convert_add_fusion
  57.1 0.0 collective-permute-done.9
  57.1 1.3 %scale.1 = (bf16[128,4096]{1,0:T(8,128)(2,1)}, bf16[128,512]{1,0:T(8,128)(2,1)}, bf16[128,512]{1,0:T(8,128)(2,1)}) custom-call(f32[8,128]{1,0:T(8,128)S(1)} %get-tuple-element.46.total_ref, bf16[128,2048]{1,0:T(8,128)(2,1)S(1)} %get-tuple-element.34.refs_0_, bf16[128,256]{1,0:T(8,128)(2,1)S(1)} %get-tuple-element.35.refs_1_, ...), custom_call_target="tpu_custom_call" | custom-call | flops 655360 | bytes 2621440 | tf_op jit(solution)/shard_map/scale/pallas_call | solution.py:338
  58.4 0.0 collective-permute-done.14
  58.4 0.1 fusion
  58.5 1.4 %collective-permute-start.15 = (bf16[128,512]{1,0:T(8,128)(2,1)S(1)}, bf16[128,512]{1,0:T(8,128)(2,1)S(1)}, u32[]{:S(2)}, u32[]{:S(2)}) collective-permute-start(bf16[128,512]{1,0:T(8,128)(2,1)S(1)} %pad_maximum_fusion.3), channel_id=1, source_target_pairs={{0,1},{1,0},{2,3},{3,2},{4,5},{5,4},{6,7},{7,6},{8,9},{9,8},{10,11... | collective-permute-start | bytes 393224 | tf_op jit(solution)/shard_map/ppermute | solution.py:201
  59.9 3.6 %collective-permute-done.15 = bf16[128,512]{1,0:T(8,128)(2,1)S(1)} collective-permute-done((bf16[128,512]{1,0:T(8,128)(2,1)S(1)}, bf16[128,512]{1,0:T(8,128)(2,1)S(1)}, u32[]{:S(2)}, u32[]{:S(2)}) %collective-permute-start.15) | collective-permute-done | bytes 131104 | tf_op jit(solution)/shard_map/ppermute | solution.py:201
  63.6 0.8 %multiply_convert_fusion = (bf16[1,64,1024]{2,1,0:T(8,128)(2,1)}, bf16[1,64,1024]{2,1,0:T(8,128)(2,1)}) fusion(bf16[1,64,512]{2,1,0:T(8,128)(2,1)S(1)} %get-tuple-element.50, bf16[1,64,512]{2,1,0:T(8,128)(2,1)S(1)} %get-tuple-element.48, f32[1024]{0:T(1024)S(1)} %broadcast_bitcast_fusion, bf16[1,64,512]{2,1,0:T(8,128)(2,1)S(1)} %get-tuple-element.49, ...), kind=kLoop, calls=%fused_computation.3 | loop fusion | flops 786432 | bytes 528384 | tf_op jit(solution)/shard_map/convert_element_type | solution.py:389
  (20 shorter events, 0.2 us)
Async XLA Ops:
  0.6 11.0 %copy-start = (bf16[1,128,4096]{2,1,0:T(8,128)(2,1)S(1)}, bf16[1,128,4096]{2,1,0:T(8,128)(2,1)}, u32[]{:S(2)}) copy-start(bf16[1,128,4096]{2,1,0:T(8,128)(2,1)} %param.13) | copy-start | bytes 3145732
  1.6 5.4 %collective-permute-start = (bf16[128,256]{1,0:T(8,128)(2,1)S(1)}, bf16[128,256]{1,0:T(8,128)(2,1)S(1)}, u32[]{:S(2)}, u32[]{:S(2)}) collective-permute-start(bf16[128,256]{1,0:T(8,128)(2,1)S(1)} %pad_maximum_fusion.4), channel_id=1, source_target_pairs={{0,1},{1,0},{2,3},{3,2},{4,5},{5,4},{6,7},{7,6},{8,9},{9,8},{10,11... | collective-permute-start | bytes 196616 | tf_op jit(solution)/shard_map/ppermute | solution.py:201
  4.7 7.7 %collective-permute-start.1 = (bf16[128,256]{1,0:T(8,128)(2,1)S(1)}, bf16[128,256]{1,0:T(8,128)(2,1)S(1)}, u32[]{:S(2)}, u32[]{:S(2)}) collective-permute-start(bf16[128,256]{1,0:T(8,128)(2,1)S(1)} %pad_maximum_fusion.5), channel_id=1, source_target_pairs={{0,1},{1,0},{2,3},{3,2},{4,5},{5,4},{6,7},{7,6},{8,9},{9,8},{10,11... | collective-permute-start | bytes 196616 | tf_op jit(solution)/shard_map/ppermute | solution.py:201
  7.1 8.2 %collective-permute-start.2 = (bf16[256,256]{1,0:T(8,128)(2,1)S(1)}, bf16[256,256]{1,0:T(8,128)(2,1)S(1)}, u32[]{:S(2)}, u32[]{:S(2)}) collective-permute-start(bf16[256,256]{1,0:T(8,128)(2,1)S(1)} %pad_maximum_fusion.2.after_ref.refs_5_), channel_id=1, source_target_pairs={{0,6},{2,4},{4,2},{6,0},{1,7},{3,5},{5,3},{7,1},{8,14},{10,12},{12... | collective-permute-start | bytes 393224 | tf_op jit(solution)/shard_map/ppermute | solution.py:201
  11.7 9.0 %collective-permute-start.5 = (bf16[256,256]{1,0:T(8,128)(2,1)S(1)}, bf16[256,256]{1,0:T(8,128)(2,1)S(1)}, u32[]{:S(2)}, u32[]{:S(2)}) collective-permute-start(bf16[256,256]{1,0:T(8,128)(2,1)S(1)} %pad_maximum_fusion.2.after_ref.refs_5_), channel_id=1, source_target_pairs={{0,2},{2,0},{4,6},{6,4},{1,3},{3,1},{5,7},{7,5},{8,10},{10,8},{12,... | collective-permute-start | bytes 393224 | tf_op jit(solution)/shard_map/ppermute | solution.py:201
  11.7 10.5 %copy-start.1 = (bf16[1,128,4096]{2,1,0:T(8,128)(2,1)S(1)}, bf16[1,128,4096]{2,1,0:T(8,128)(2,1)}, u32[]{:S(2)}) copy-start(bf16[1,128,4096]{2,1,0:T(8,128)(2,1)} %param.7) | copy-start | bytes 3145732
  11.7 10.5 %copy-start.4 = (bf16[1,128,512]{2,1,0:T(8,128)(2,1)S(1)}, bf16[1,128,512]{2,1,0:T(8,128)(2,1)}, u32[]{:S(2)}) copy-start(bf16[1,128,512]{2,1,0:T(8,128)(2,1)} %param.9) | copy-start | bytes 393220
  12.3 9.9 %copy-start.2 = (bf16[1,128,512]{2,1,0:T(8,128)(2,1)S(1)}, bf16[1,128,512]{2,1,0:T(8,128)(2,1)}, u32[]{:S(2)}) copy-start(bf16[1,128,512]{2,1,0:T(8,128)(2,1)} %param.8) | copy-start | bytes 393220
  15.2 7.0 %collective-permute-start.6 = (bf16[256,256]{1,0:T(8,128)(2,1)S(1)}, bf16[256,256]{1,0:T(8,128)(2,1)S(1)}, u32[]{:S(2)}, u32[]{:S(2)}) collective-permute-start(bf16[256,256]{1,0:T(8,128)(2,1)S(1)} %collective-permute-done.2.refs_8_), channel_id=1, source_target_pairs={{0,2},{2,0},{4,6},{6,4},{1,3},{3,1},{5,7},{7,5},{8,10},{10,8},{12,... | collective-permute-start | bytes 393224 | tf_op jit(solution)/shard_map/ppermute | solution.py:201
  16.0 12.4 %collective-permute-start.4 = (bf16[272,256]{1,0:T(8,128)(2,1)S(1)}, bf16[272,256]{1,0:T(8,128)(2,1)S(1)}, u32[]{:S(2)}, u32[]{:S(2)}) collective-permute-start(bf16[272,256]{1,0:T(8,128)(2,1)S(1)} %constant_dynamic-update-slice_fusion.refs_5_), channel_id=1, source_target_pairs={{0,6},{2,4},{4,2},{6,0},{1,7},{3,5},{5,3},{7,1},{8,14},{10,12},{12... | collective-permute-start | bytes 417800 | tf_op jit(solution)/shard_map/ppermute | solution.py:201
  19.6 13.0 %collective-permute-start.3 = (bf16[272,256]{1,0:T(8,128)(2,1)S(1)}, bf16[272,256]{1,0:T(8,128)(2,1)S(1)}, u32[]{:S(2)}, u32[]{:S(2)}) collective-permute-start(bf16[272,256]{1,0:T(8,128)(2,1)S(1)} %constant_dynamic-update-slice_fusion.refs_5_), channel_id=1, source_target_pairs={{0,2},{2,0},{4,6},{6,4},{1,3},{3,1},{5,7},{7,5},{8,10},{10,8},{12,... | collective-permute-start | bytes 417800 | tf_op jit(solution)/shard_map/ppermute | solution.py:201
  28.4 0.7 %copy-start.6 = (bf16[256,256]{1,0:T(8,128)(2,1)}, bf16[256,256]{1,0:T(8,128)(2,1)S(1)}, u32[]{:S(2)}) copy-start(bf16[256,256]{1,0:T(8,128)(2,1)S(1)} %get-tuple-element.44) | copy-start | bytes 393220
  28.4 0.7 %copy-start.7 = (bf16[256,256]{1,0:T(8,128)(2,1)}, bf16[256,256]{1,0:T(8,128)(2,1)S(1)}, u32[]{:S(2)}) copy-start(bf16[256,256]{1,0:T(8,128)(2,1)S(1)} %get-tuple-element.43) | copy-start | bytes 393220
  29.1 6.6 %collective-permute-start.7 = (bf16[272,256]{1,0:T(8,128)(2,1)S(1)}, bf16[272,256]{1,0:T(8,128)(2,1)}, u32[]{:S(2)}, u32[]{:S(2)}) collective-permute-start(bf16[272,256]{1,0:T(8,128)(2,1)S(1)} %pad_maximum_fusion.1.refs_8_), channel_id=1, source_target_pairs={{0,2},{2,0},{4,6},{6,4},{1,3},{3,1},{5,7},{7,5},{8,10},{10,8},{12,... | collective-permute-start | bytes 417800 | tf_op jit(solution)/shard_map/ppermute | solution.py:201
  30.3 18.8 %collective-permute-start.12 = (bf16[256,256]{1,0:T(8,128)(2,1)}, bf16[256,256]{1,0:T(8,128)(2,1)S(1)}, u32[]{:S(2)}, u32[]{:S(2)}) collective-permute-start(bf16[256,256]{1,0:T(8,128)(2,1)} %copy-done.7), channel_id=1, source_target_pairs={{0,6},{2,4},{4,2},{6,0},{1,7},{3,5},{5,3},{7,1},{8,14},{10,12},{12... | collective-permute-start | bytes 393224 | tf_op jit(solution)/shard_map/ppermute | solution.py:201
  31.6 17.5 %collective-permute-start.13 = (bf16[256,256]{1,0:T(8,128)(2,1)}, bf16[256,256]{1,0:T(8,128)(2,1)S(1)}, u32[]{:S(2)}, u32[]{:S(2)}) collective-permute-start(bf16[256,256]{1,0:T(8,128)(2,1)} %copy-done.6), channel_id=1, source_target_pairs={{0,4},{2,6},{4,0},{6,2},{1,5},{3,7},{5,1},{7,3},{8,12},{10,14},{12... | collective-permute-start | bytes 393224 | tf_op jit(solution)/shard_map/ppermute | solution.py:201
  35.7 0.9 %copy-start.3 = (bf16[1,128,512]{2,1,0:T(8,128)(2,1)S(1)}, bf16[1,128,512]{2,1,0:T(8,128)(2,1)}, u32[]{:S(2)}) copy-start(bf16[1,128,512]{2,1,0:T(8,128)(2,1)} %param.8) | copy-start | bytes 393220
  36.6 0.9 %copy-start.5 = (bf16[1,128,512]{2,1,0:T(8,128)(2,1)S(1)}, bf16[1,128,512]{2,1,0:T(8,128)(2,1)}, u32[]{:S(2)}) copy-start(bf16[1,128,512]{2,1,0:T(8,128)(2,1)} %param.9) | copy-start | bytes 393220
  44.6 13.8 %collective-permute-start.14 = (bf16[256,512]{1,0:T(8,128)(2,1)S(1)}, bf16[256,512]{1,0:T(8,128)(2,1)S(1)}, u32[]{:S(2)}, u32[]{:S(2)}) collective-permute-start(bf16[256,512]{1,0:T(8,128)(2,1)S(1)} %pad_maximum_fusion), channel_id=1, source_target_pairs={{0,2},{2,0},{4,6},{6,4},{1,3},{3,1},{5,7},{7,5},{8,10},{10,8},{12,... | collective-permute-start | bytes 786440 | tf_op jit(solution)/shard_map/ppermute | solution.py:201
  44.7 9.6 %collective-permute-start.10 = (bf16[256,256]{1,0:T(8,128)(2,1)S(1)}, bf16[256,256]{1,0:T(8,128)(2,1)S(1)}, u32[]{:S(2)}, u32[]{:S(2)}) collective-permute-start(bf16[256,256]{1,0:T(8,128)(2,1)S(1)} %get-tuple-element.32), channel_id=1, source_target_pairs={{0,6},{2,4},{4,2},{6,0},{1,7},{3,5},{5,3},{7,1},{8,14},{10,12},{12... | collective-permute-start | bytes 393224 | tf_op jit(solution)/shard_map/ppermute | solution.py:201
  48.6 8.5 %collective-permute-start.11 = (bf16[256,256]{1,0:T(8,128)(2,1)S(1)}, bf16[256,256]{1,0:T(8,128)(2,1)S(1)}, u32[]{:S(2)}, u32[]{:S(2)}) collective-permute-start(bf16[256,256]{1,0:T(8,128)(2,1)S(1)} %get-tuple-element.33), channel_id=1, source_target_pairs={{0,4},{2,6},{4,0},{6,2},{1,5},{3,7},{5,1},{7,3},{8,12},{10,14},{12... | collective-permute-start | bytes 393224 | tf_op jit(solution)/shard_map/ppermute | solution.py:201
  49.1 1.2 %collective-permute-start.8 = (f32[8,128]{1,0:T(8,128)S(1)}, f32[8,128]{1,0:T(8,128)S(1)}, u32[]{:S(2)}, u32[]{:S(2)}) collective-permute-start(f32[8,128]{1,0:T(8,128)S(1)} %multiply_add_fusion), channel_id=1, source_target_pairs={{0,8},{8,0},{16,24},{24,16},{1,9},{9,1},{17,25},{25,17},{2,10},{10... | collective-permute-start | bytes 12296 | tf_op jit(solution)/shard_map/ppermute | solution.py:201
  50.3 6.8 %collective-permute-start.9 = (f32[8,128]{1,0:T(8,128)S(1)}, f32[8,128]{1,0:T(8,128)S(1)}, u32[]{:S(2)}, u32[]{:S(2)}) collective-permute-start(f32[8,128]{1,0:T(8,128)S(1)} %add.80), channel_id=1, source_target_pairs={{0,16},{8,24},{16,0},{24,8},{1,17},{9,25},{17,1},{25,9},{2,18},{10... | collective-permute-start | bytes 12296 | tf_op jit(solution)/shard_map/ppermute | solution.py:201
  58.5 5.0 %collective-permute-start.15 = (bf16[128,512]{1,0:T(8,128)(2,1)S(1)}, bf16[128,512]{1,0:T(8,128)(2,1)S(1)}, u32[]{:S(2)}, u32[]{:S(2)}) collective-permute-start(bf16[128,512]{1,0:T(8,128)(2,1)S(1)} %pad_maximum_fusion.3), channel_id=1, source_target_pairs={{0,1},{1,0},{2,3},{3,2},{4,5},{5,4},{6,7},{7,6},{8,9},{9,8},{10,11... | collective-permute-start | bytes 393224 | tf_op jit(solution)/shard_map/ppermute | solution.py:201

commit v14 on v10

--- a/solution.py
+++ b/solution.py
@@ -35,8 +35,8 @@
         total_ref, refs = refs[0], refs[1:]
         totals = [ref[2 * held : 2 * held + 8, :HD].astype(jnp.float32) for ref in slot_refs]
         total_ref[...] = functools.reduce(jnp.add, totals)
-    out_ref, s_ref, dp_ref, e_ref, ds_ref, dot_ref = refs[:6]
-    keys_ref, keys_t_ref, values_ref, values_t_ref, out_sem = refs[6:]
+    out_ref, s_ref, e_ref, ds_ref, dot_ref = refs[:5]
+    keys_ref, keys_t_ref, values_ref, values_t_ref, out_sem = refs[5:]
     first = chunk * count
     rows = q_ref.shape[0]
     own = kown_ref.shape[0]
@@ -63,31 +63,33 @@
     def place(head, pair):
         return slice(pair * width, (pair + 1) * width)
 
+    def fold(x):
+        return x.reshape(x.shape[0] // 8, 8, width)
+
     def scores(head, pair):
         if pair == 0:
             assemble(head, kown_ref, 0, keys_ref, keys_t_ref)
-        s_ref[pair % 2] = lax.dot_general(
+        s = lax.dot_general(
             keys_ref[head],
             heads_down(q_ref, (first + head) * GROUP + pair * PAIR, PAIR),
             NT,
             preferred_element_type=jnp.float32,
         )
-
-    def softmax(head, pair):
-        here = s_ref.at[pair % 2]
-        cols = place(head, pair)
-        fold = lambda x: x.reshape(x.shape[0] // 8, 8, width)
         top = jnp.full((8, width), -1e30, jnp.float32)
         for at in range(0, n_keys, STEP):
-            x = here[at : at + STEP]
+            x = s[at : at + STEP]
             if at < own:
                 key_pos = lax.broadcasted_iota(jnp.int32, x.shape, 0) + at
                 row_pos = lax.broadcasted_iota(jnp.int32, x.shape, 1) % rows
                 x = jnp.where(key_pos <= row_pos, x, -1e30)
-                here[at : at + STEP] = x
+            s_ref[pair % 2, at : at + STEP] = x
             top = jnp.maximum(top, jnp.max(fold(x), axis=0))
         top = jnp.max(top, axis=0, keepdims=True) * scale
-        top = jnp.broadcast_to(top, (8, width))
+        return jnp.broadcast_to(top, (8, width))
+
+    def softmax(head, pair, top):
+        here = s_ref.at[pair % 2]
+        cols = place(head, pair)
         total = jnp.zeros((8, width), jnp.float32)
         for at in range(0, n_keys, STEP):
             e = jnp.exp2(fold(here[at : at + STEP]) * scale - top)
@@ -104,7 +106,6 @@
         if pair == 0:
             assemble(head, vown_ref, held, values_ref, values_t_ref)
         grad = dot_ref[head % 2, :, cols]
-        dp_ref[pair % 2] = jnp.dot(values_ref[head], grad, preferred_element_type=jnp.float32)
         out = jnp.dot(
             values_t_ref[head], e_ref[head % 2, :, cols], preferred_element_type=jnp.float32
         )
@@ -117,11 +118,13 @@
 
     def score_grads(head, pair, centre):
         cols = place(head, pair)
-        here = dp_ref.at[pair % 2]
+        dp = jnp.dot(
+            values_ref[head], dot_ref[head % 2, :, cols], preferred_element_type=jnp.float32
+        )
         centre = jnp.broadcast_to(centre, (STEP, width))
         for at in range(0, n_keys, STEP):
             e = e_ref[head % 2, at : at + STEP, cols].astype(jnp.float32)
-            grad = e * (here[at : at + STEP] - centre)
+            grad = e * (dp[at : at + STEP] - centre)
             ds_ref[head % 2, at : at + STEP, cols] = grad.astype(jnp.bfloat16)
 
     def query_grads(head, pair):
@@ -160,14 +163,13 @@
             ref[:held, here] = dk[own + i * held : own + (i + 1) * held]
 
     steps = [(head, pair) for head in range(count) for pair in range(pairs)]
-    scores(*steps[0])
-    inverse = softmax(*steps[0])
+    inverse = softmax(*steps[0], scores(*steps[0]))
     for now, then in zip(steps, steps[1:] + [None]):
         if then:
-            scores(*then)
+            top = scores(*then)
         centre = attended(*now, inverse)
         if then:
-            inverse = softmax(*then)
+            inverse = softmax(*then, top)
         score_grads(*now, centre)
         query_grads(*now)
         if now[1] + 1 == pairs:
@@ -311,7 +313,7 @@
     wide = pltpu.VMEM((rows, count * GROUP * HD), bf16)
     down = pltpu.VMEM((count, n_keys, HD), bf16)
     across = pltpu.VMEM((count, HD, n_keys), bf16)
-    scratch = [wide, step_buffer, step_buffer, head_buffer, head_buffer]
+    scratch = [wide, step_buffer, head_buffer, head_buffer]
     scratch += [pltpu.VMEM((2, HD, GROUP * rows), bf16), down, across, down, across]
     scratch += [pltpu.SemaphoreType.DMA((count,))]
     part = lambda x: jax.ShapeDtypeStruct((x.shape[0], x.shape[1] // CHUNKS), bf16)

time: 57.6 us -> 58.1 us (level)
  transfers between devices with their start and end apart: 17 -> 17, of which waited for: 8 -> 8; matrix products, arithmetic and copies ran while one was open for 3% -> 3% of each run, Pallas kernels for 25% -> 26%
where the time goes in v14:
time: 58.1 us; the launch traced here: 57.8 us
  starting transfers between devices  26 us (45%)
  Pallas kernels  14.8 us (25%)
  waiting for transfers between devices  12 us (21%)
  local copies, waits for them, and re-layouts  2.52 us (4%)
  between operations  1.51 us (3%)
  other arithmetic  1.06 us (2%)
    ppermute x17, starting transfers between devices, swap(): lax.ppermute(x, axis, [(i, i ^ by) for i in range(lax.axis_size(axis))])  26 us
    pallas_call x2, Pallas kernels, attend(): pl.pallas_call(functools.partial(attend_kernel, n_slots, count, chunk, he...  12.9 us
    ppermute x17, waiting for transfers between devices, swap(): lax.ppermute(x, axis, [(i, i ^ by) for i in range(lax.axis_size(axis))])  12 us
    unnamed x12, local copies, waits for them, and re-layouts  1.56 us
    pallas_call x1, Pallas kernels, scale_all(): pl.pallas_call(functools.partial(scale_kernel, slots_all), in_specs=[VMEM...  1.27 us
  transfers between devices with their start and end apart: 17, of which 8 were waited for; matrix products, arithmetic and copies ran while one was open for 3% of the time, Pallas kernels for 26%

profile of v14, /device:TPU:0, one launch (start us, length us, event | category | flops | bytes accessed | tf_op | source)
XLA Modules:
  0.0 57.8 jit_solution(14305322170367705645)
XLA Ops:
  0.6 0.0 copy-start
  0.7 0.9 %dynamic-slice_bitcast_fusion = (bf16[64,256]{1,0:T(8,128)(2,1)S(1)}, bf16[64,256]{1,0:T(8,128)(2,1)S(1)}, bf16[64,256]{1,0:T(8,128)(2,1)S(1)}, bf16[64,256]{1,0...) fusion(bf16[1,64,1024]{2,1,0:T(8,128)(2,1)} %param.11, s32[]{:T(128)S(6)} %select_n.41, ...), kind=kLoop, calls=%fused_computation.28 | loop fusion | bytes 393228 | tf_op jit(solution)/shard_map/dynamic_slice | solution.py:236
  1.6 3.0 %collective-permute-start = (bf16[128,256]{1,0:T(8,128)(2,1)S(1)}, bf16[128,256]{1,0:T(8,128)(2,1)S(1)}, u32[]{:S(2)}, u32[]{:S(2)}) collective-permute-start(bf16[128,256]{1,0:T(8,128)(2,1)S(1)} %pad_maximum_fusion.4), channel_id=1, source_target_pairs={{0,1},{1,0},{2,3},{3,2},{4,5},{5,4},{6,7},{7,6},{8,9},{9,8},{10,11... | collective-permute-start | bytes 196616 | tf_op jit(solution)/shard_map/ppermute | solution.py:204
  4.7 0.1 collective-permute-start.1
  5.4 0.8 %bitcast_dynamic-update-slice_fusion.1 = bf16[272,256]{1,0:T(8,128)(2,1)S(1)} fusion(bf16[1,64,1024]{2,1,0:T(8,128)(2,1)} %param.10, s32[]{:T(128)S(6)} %select_n.40), kind=kLoop, calls=%fused_computation.27 | loop fusion | bytes 65540
  6.2 0.9 %collective-permute-done = bf16[128,256]{1,0:T(8,128)(2,1)S(1)} collective-permute-done((bf16[128,256]{1,0:T(8,128)(2,1)S(1)}, bf16[128,256]{1,0:T(8,128)(2,1)S(1)}, u32[]{:S(2)}, u32[]{:S(2)}) %collective-permute-start) | collective-permute-done | bytes 65568 | tf_op jit(solution)/shard_map/ppermute | solution.py:204
  7.1 4.6 %collective-permute-start.2 = (bf16[256,256]{1,0:T(8,128)(2,1)S(1)}, bf16[256,256]{1,0:T(8,128)(2,1)S(1)}, u32[]{:S(2)}, u32[]{:S(2)}) collective-permute-start(bf16[256,256]{1,0:T(8,128)(2,1)S(1)} %pad_maximum_fusion.1.after_ref.refs_5_), channel_id=1, source_target_pairs={{0,6},{2,4},{4,2},{6,0},{1,7},{3,5},{5,3},{7,1},{8,14},{10,12},{12... | collective-permute-start | bytes 393224 | tf_op jit(solution)/shard_map/ppermute | solution.py:204
  11.7 0.0 collective-permute-start.5
  11.7 0.0 copy-done
  11.7 0.0 copy-start.1
  11.7 0.0 copy-start.3
  11.7 0.6 %turn.1.refs_2_ = bf16[4,128,1024]{2,1,0:T(8,128)(2,1)S(1)} custom-call(bf16[128,4096]{1,0:T(8,128)(2,1)S(1)} %bitcast.41, bf16[256,256]{1,0:T(8,128)(2,1)S(1)} %pad_maximum_fusion.1.after_ref.refs_5_), custom_call_target="tpu_custom_call" | custom-call | tf_op jit(solution)/shard_map/turn/pallas_call | solution.py:292
  12.3 0.0 copy-start.2
  12.3 0.0 collective-permute-done.1
  12.4 0.8 %bitcast_dynamic-update-slice_fusion = bf16[272,256]{1,0:T(8,128)(2,1)S(1)} fusion(bf16[272,256]{1,0:T(8,128)(2,1)S(1)} %slice_dynamic-update-slice_fusion.1, bf16[1,64,1024]{2,1,0:T(8,128)(2,1)} %param.11, s32[]{:T(128)S(6)} %select_n.40), kind=kLoop, calls=%fused_computation.26 | loop fusion | bytes 65540
  13.1 2.1 %collective-permute-done.2.refs_8_ = bf16[256,256]{1,0:T(8,128)(2,1)S(1)} collective-permute-done((bf16[256,256]{1,0:T(8,128)(2,1)S(1)}, bf16[256,256]{1,0:T(8,128)(2,1)S(1)}, u32[]{:S(2)}, u32[]{:S(2)}) %collective-permute-start.2) | collective-permute-done | bytes 131104 | tf_op jit(solution)/shard_map/ppermute | solution.py:204
  15.2 0.8 %collective-permute-start.6 = (bf16[256,256]{1,0:T(8,128)(2,1)S(1)}, bf16[256,256]{1,0:T(8,128)(2,1)S(1)}, u32[]{:S(2)}, u32[]{:S(2)}) collective-permute-start(bf16[256,256]{1,0:T(8,128)(2,1)S(1)} %collective-permute-done.2.refs_8_), channel_id=1, source_target_pairs={{0,2},{2,0},{4,6},{6,4},{1,3},{3,1},{5,7},{7,5},{8,10},{10,8},{12,... | collective-permute-start | bytes 393224 | tf_op jit(solution)/shard_map/ppermute | solution.py:204
  16.0 3.6 %collective-permute-start.4 = (bf16[272,256]{1,0:T(8,128)(2,1)S(1)}, bf16[272,256]{1,0:T(8,128)(2,1)S(1)}, u32[]{:S(2)}, u32[]{:S(2)}) collective-permute-start(bf16[272,256]{1,0:T(8,128)(2,1)S(1)} %constant_dynamic-update-slice_fusion.refs_5_), channel_id=1, source_target_pairs={{0,6},{2,4},{4,2},{6,0},{1,7},{3,5},{5,3},{7,1},{8,14},{10,12},{12... | collective-permute-start | bytes 417800 | tf_op jit(solution)/shard_map/ppermute | solution.py:204
  19.6 1.1 %collective-permute-start.3 = (bf16[272,256]{1,0:T(8,128)(2,1)S(1)}, bf16[272,256]{1,0:T(8,128)(2,1)S(1)}, u32[]{:S(2)}, u32[]{:S(2)}) collective-permute-start(bf16[272,256]{1,0:T(8,128)(2,1)S(1)} %constant_dynamic-update-slice_fusion.refs_5_), channel_id=1, source_target_pairs={{0,2},{2,0},{4,6},{6,4},{1,3},{3,1},{5,7},{7,5},{8,10},{10,8},{12,... | collective-permute-start | bytes 417800 | tf_op jit(solution)/shard_map/ppermute | solution.py:204
  20.7 0.0 collective-permute-done.5.refs_6_
  20.7 1.5 %collective-permute-done.6.refs_7_ = bf16[256,256]{1,0:T(8,128)(2,1)S(1)} collective-permute-done((bf16[256,256]{1,0:T(8,128)(2,1)S(1)}, bf16[256,256]{1,0:T(8,128)(2,1)S(1)}, u32[]{:S(2)}, u32[]{:S(2)}) %collective-permute-start.6) | collective-permute-done | bytes 131104 | tf_op jit(solution)/shard_map/ppermute | solution.py:204
  22.2 0.0 copy-done.1
  22.2 0.0 copy-done.3
  22.2 0.0 copy-done.2
  22.2 6.5 %attend_0.1 = (bf16[128,4096]{1,0:T(8,128)(2,1)}, bf16[128,2048]{1,0:T(8,128)(2,1)S(1)}, bf16[128,256]{1,0:T(8,128)(2,1)S(1)}, bf16[128,256]{1,0:T(8,128)(2,1)S(...) custom-call(s32[1]{0:T(128)} %bitcast.39.refs_0_, ...), custom_call_target="tpu_custom_call" | custom-call | flops 8053063680 | bytes 2097152 | tf_op jit(solution)/shard_map/attend_0/pallas_call | solution.py:322
  28.7 0.0 collective-permute-done.4
  28.7 1.2 %collective-permute-start.7 = (bf16[272,256]{1,0:T(8,128)(2,1)S(1)}, bf16[272,256]{1,0:T(8,128)(2,1)S(1)}, u32[]{:S(2)}, u32[]{:S(2)}) collective-permute-start(bf16[272,256]{1,0:T(8,128)(2,1)S(1)} %pad_maximum_fusion.refs_8_), channel_id=1, source_target_pairs={{0,2},{2,0},{4,6},{6,4},{1,3},{3,1},{5,7},{7,5},{8,10},{10,8},{12,... | collective-permute-start | bytes 417800 | tf_op jit(solution)/shard_map/ppermute | solution.py:204
  29.9 1.3 %collective-permute-start.10 = (bf16[256,256]{1,0:T(8,128)(2,1)S(1)}, bf16[256,256]{1,0:T(8,128)(2,1)S(1)}, u32[]{:S(2)}, u32[]{:S(2)}) collective-permute-start(bf16[256,256]{1,0:T(8,128)(2,1)S(1)} %get-tuple-element.32), channel_id=1, source_target_pairs={{0,6},{2,4},{4,2},{6,0},{1,7},{3,5},{5,3},{7,1},{8,14},{10,12},{12... | collective-permute-start | bytes 393224 | tf_op jit(solution)/shard_map/ppermute | solution.py:204
  31.3 1.0 %collective-permute-start.8 = (bf16[256,256]{1,0:T(8,128)(2,1)S(1)}, bf16[256,256]{1,0:T(8,128)(2,1)S(1)}, u32[]{:S(2)}, u32[]{:S(2)}) collective-permute-start(bf16[256,256]{1,0:T(8,128)(2,1)S(1)} %get-tuple-element.30), channel_id=1, source_target_pairs={{0,4},{2,6},{4,0},{6,2},{1,5},{3,7},{5,1},{7,3},{8,12},{10,14},{12... | collective-permute-start | bytes 393224 | tf_op jit(solution)/shard_map/ppermute | solution.py:204
  32.3 2.1 %collective-permute-start.9 = (bf16[256,256]{1,0:T(8,128)(2,1)S(1)}, bf16[256,256]{1,0:T(8,128)(2,1)S(1)}, u32[]{:S(2)}, u32[]{:S(2)}) collective-permute-start(bf16[256,256]{1,0:T(8,128)(2,1)S(1)} %get-tuple-element.31), channel_id=1, source_target_pairs={{0,2},{2,0},{4,6},{6,4},{1,3},{3,1},{5,7},{7,5},{8,10},{10,8},{12,... | collective-permute-start | bytes 393224 | tf_op jit(solution)/shard_map/ppermute | solution.py:204
  34.3 0.0 collective-permute-done.3.refs_6_
  34.3 0.8 %collective-permute-done.7.refs_7_ = bf16[272,256]{1,0:T(8,128)(2,1)S(1)} collective-permute-done((bf16[272,256]{1,0:T(8,128)(2,1)S(1)}, bf16[272,256]{1,0:T(8,128)(2,1)S(1)}, u32[]{:S(2)}, u32[]{:S(2)}) %collective-permute-start.7) | collective-permute-done | bytes 139296 | tf_op jit(solution)/shard_map/ppermute | solution.py:204
  35.2 6.5 %attend_1.1 = (bf16[128,4096]{1,0:T(8,128)(2,1)}, bf16[128,2048]{1,0:T(8,128)(2,1)S(1)}, bf16[128,256]{1,0:T(8,128)(2,1)S(1)}, bf16[128,256]{1,0:T(8,128)(2,1)S(...) custom-call(s32[1]{0:T(128)} %bitcast.40.refs_0_, ...), custom_call_target="tpu_custom_call", output_to_operand_aliasing={{0}: (9, {})} | custom-call | flops 8053063680 | bytes 2097152 | tf_op jit(solution)/shard_map/attend_1/pallas_call | solution.py:322
  41.6 3.8 %collective-permute-start.13 = (bf16[256,256]{1,0:T(8,128)(2,1)S(1)}, bf16[256,256]{1,0:T(8,128)(2,1)S(1)}, u32[]{:S(2)}, u32[]{:S(2)}) collective-permute-start(bf16[256,256]{1,0:T(8,128)(2,1)S(1)} %get-tuple-element.35), channel_id=1, source_target_pairs={{0,6},{2,4},{4,2},{6,0},{1,7},{3,5},{5,3},{7,1},{8,14},{10,12},{12... | collective-permute-start | bytes 393224 | tf_op jit(solution)/shard_map/ppermute | solution.py:204
  45.4 0.0 collective-permute-start.14
  45.4 0.0 collective-permute-done.10
  45.4 0.7 %collective-permute-start.15 = (bf16[256,256]{1,0:T(8,128)(2,1)S(1)}, bf16[256,256]{1,0:T(8,128)(2,1)S(1)}, u32[]{:S(2)}, u32[]{:S(2)}) collective-permute-start(bf16[256,256]{1,0:T(8,128)(2,1)S(1)} %get-tuple-element.37), channel_id=1, source_target_pairs={{0,2},{2,0},{4,6},{6,4},{1,3},{3,1},{5,7},{7,5},{8,10},{10,8},{12,... | collective-permute-start | bytes 393224 | tf_op jit(solution)/shard_map/ppermute | solution.py:204
  46.1 0.0 collective-permute-done.8
  46.1 0.0 collective-permute-done.9
  46.1 0.1 fusion.7
  46.2 0.1 collective-permute-start.11
  46.3 1.1 %collective-permute-done.11 = f32[8,128]{1,0:T(8,128)S(1)} collective-permute-done((f32[8,128]{1,0:T(8,128)S(1)}, f32[8,128]{1,0:T(8,128)S(1)}, u32[]{:S(2)}, u32[]{:S(2)}) %collective-permute-start.11) | collective-permute-done | bytes 4128 | tf_op jit(solution)/shard_map/ppermute | solution.py:204
  47.4 1.5 %collective-permute-start.12 = (f32[8,128]{1,0:T(8,128)S(1)}, f32[8,128]{1,0:T(8,128)S(1)}, u32[]{:S(2)}, u32[]{:S(2)}) collective-permute-start(f32[8,128]{1,0:T(8,128)S(1)} %add.89), channel_id=1, source_target_pairs={{0,16},{8,24},{16,0},{24,8},{1,17},{9,25},{17,1},{25,9},{2,18},{10... | collective-permute-start | bytes 12296 | tf_op jit(solution)/shard_map/ppermute | solution.py:204
  48.9 0.0 collective-permute-done.13
  48.9 2.5 %collective-permute-done.14 = bf16[256,256]{1,0:T(8,128)(2,1)S(1)} collective-permute-done((bf16[256,256]{1,0:T(8,128)(2,1)S(1)}, bf16[256,256]{1,0:T(8,128)(2,1)S(1)}, u32[]{:S(2)}, u32[]{:S(2)}) %collective-permute-start.14) | collective-permute-done | bytes 131104 | tf_op jit(solution)/shard_map/ppermute | solution.py:204
  51.4 0.5 collective-permute-done.15
  51.9 0.1 fusion.6
  52.0 1.2 %collective-permute-start.16 = (bf16[128,512]{1,0:T(8,128)(2,1)S(1)}, bf16[128,512]{1,0:T(8,128)(2,1)S(1)}, u32[]{:S(2)}, u32[]{:S(2)}) collective-permute-start(bf16[128,512]{1,0:T(8,128)(2,1)S(1)} %pad_maximum_fusion.2), channel_id=1, source_target_pairs={{0,1},{1,0},{2,3},{3,2},{4,5},{5,4},{6,7},{7,6},{8,9},{9,8},{10,11... | collective-permute-start | bytes 393224 | tf_op jit(solution)/shard_map/ppermute | solution.py:204
  53.2 0.0 collective-permute-done.12
  53.2 1.3 %scale.1 = (bf16[128,4096]{1,0:T(8,128)(2,1)}, bf16[128,512]{1,0:T(8,128)(2,1)}, bf16[128,512]{1,0:T(8,128)(2,1)}) custom-call(f32[8,128]{1,0:T(8,128)S(1)} %get-tuple-element.52.total_ref, bf16[128,2048]{1,0:T(8,128)(2,1)S(1)} %get-tuple-element.38.refs_0_, bf16[128,256]{1,0:T(8,128)(2,1)S(1)} %get-tuple-element.39.refs_1_, ...), custom_call_target="tpu_custom_call" | custom-call | flops 655360 | bytes 2621440 | tf_op jit(solution)/shard_map/scale/pallas_call | solution.py:341
  54.5 2.5 %collective-permute-done.16 = bf16[128,512]{1,0:T(8,128)(2,1)S(1)} collective-permute-done((bf16[128,512]{1,0:T(8,128)(2,1)S(1)}, bf16[128,512]{1,0:T(8,128)(2,1)S(1)}, u32[]{:S(2)}, u32[]{:S(2)}) %collective-permute-start.16) | collective-permute-done | bytes 131104 | tf_op jit(solution)/shard_map/ppermute | solution.py:204
  57.1 0.8 %multiply_convert_fusion = (bf16[1,64,1024]{2,1,0:T(8,128)(2,1)}, bf16[1,64,1024]{2,1,0:T(8,128)(2,1)}) fusion(bf16[1,64,512]{2,1,0:T(8,128)(2,1)S(1)} %select_bitcast_fusion, bf16[1,64,512]{2,1,0:T(8,128)(2,1)S(1)} %get-tuple-element.46, f32[1024]{0:T(1024)S(1)} %broadcast_bitcast_fusion, bf16[1,64,512]{2,1,0:T(8,128)(2,1)S(1)} %get-tuple-element.54, ...), kind=kLoop, calls=%fused_computation.6 | loop fusion | flops 786432 | bytes 528384 | tf_op jit(solution)/shard_map/convert_element_type | solution.py:390
  (20 shorter events, 0.2 us)
Async XLA Ops:
  0.6 11.0 %copy-start = (bf16[1,128,4096]{2,1,0:T(8,128)(2,1)S(1)}, bf16[1,128,4096]{2,1,0:T(8,128)(2,1)}, u32[]{:S(2)}) copy-start(bf16[1,128,4096]{2,1,0:T(8,128)(2,1)} %param.13) | copy-start | bytes 3145732
  1.6 5.4 %collective-permute-start = (bf16[128,256]{1,0:T(8,128)(2,1)S(1)}, bf16[128,256]{1,0:T(8,128)(2,1)S(1)}, u32[]{:S(2)}, u32[]{:S(2)}) collective-permute-start(bf16[128,256]{1,0:T(8,128)(2,1)S(1)} %pad_maximum_fusion.4), channel_id=1, source_target_pairs={{0,1},{1,0},{2,3},{3,2},{4,5},{5,4},{6,7},{7,6},{8,9},{9,8},{10,11... | collective-permute-start | bytes 196616 | tf_op jit(solution)/shard_map/ppermute | solution.py:204
  4.7 7.7 %collective-permute-start.1 = (bf16[128,256]{1,0:T(8,128)(2,1)S(1)}, bf16[128,256]{1,0:T(8,128)(2,1)S(1)}, u32[]{:S(2)}, u32[]{:S(2)}) collective-permute-start(bf16[128,256]{1,0:T(8,128)(2,1)S(1)} %pad_maximum_fusion.5), channel_id=1, source_target_pairs={{0,1},{1,0},{2,3},{3,2},{4,5},{5,4},{6,7},{7,6},{8,9},{9,8},{10,11... | collective-permute-start | bytes 196616 | tf_op jit(solution)/shard_map/ppermute | solution.py:204
  7.1 8.2 %collective-permute-start.2 = (bf16[256,256]{1,0:T(8,128)(2,1)S(1)}, bf16[256,256]{1,0:T(8,128)(2,1)S(1)}, u32[]{:S(2)}, u32[]{:S(2)}) collective-permute-start(bf16[256,256]{1,0:T(8,128)(2,1)S(1)} %pad_maximum_fusion.1.after_ref.refs_5_), channel_id=1, source_target_pairs={{0,6},{2,4},{4,2},{6,0},{1,7},{3,5},{5,3},{7,1},{8,14},{10,12},{12... | collective-permute-start | bytes 393224 | tf_op jit(solution)/shard_map/ppermute | solution.py:204
  11.7 9.0 %collective-permute-start.5 = (bf16[256,256]{1,0:T(8,128)(2,1)S(1)}, bf16[256,256]{1,0:T(8,128)(2,1)S(1)}, u32[]{:S(2)}, u32[]{:S(2)}) collective-permute-start(bf16[256,256]{1,0:T(8,128)(2,1)S(1)} %pad_maximum_fusion.1.after_ref.refs_5_), channel_id=1, source_target_pairs={{0,2},{2,0},{4,6},{6,4},{1,3},{3,1},{5,7},{7,5},{8,10},{10,8},{12,... | collective-permute-start | bytes 393224 | tf_op jit(solution)/shard_map/ppermute | solution.py:204
  11.7 10.5 %copy-start.1 = (bf16[1,128,4096]{2,1,0:T(8,128)(2,1)S(1)}, bf16[1,128,4096]{2,1,0:T(8,128)(2,1)}, u32[]{:S(2)}) copy-start(bf16[1,128,4096]{2,1,0:T(8,128)(2,1)} %param.7) | copy-start | bytes 3145732
  11.7 10.5 %copy-start.3 = (bf16[1,128,512]{2,1,0:T(8,128)(2,1)S(1)}, bf16[1,128,512]{2,1,0:T(8,128)(2,1)}, u32[]{:S(2)}) copy-start(bf16[1,128,512]{2,1,0:T(8,128)(2,1)} %param.9) | copy-start | bytes 393220
  12.3 9.9 %copy-start.2 = (bf16[1,128,512]{2,1,0:T(8,128)(2,1)S(1)}, bf16[1,128,512]{2,1,0:T(8,128)(2,1)}, u32[]{:S(2)}) copy-start(bf16[1,128,512]{2,1,0:T(8,128)(2,1)} %param.8) | copy-start | bytes 393220
  15.2 7.0 %collective-permute-start.6 = (bf16[256,256]{1,0:T(8,128)(2,1)S(1)}, bf16[256,256]{1,0:T(8,128)(2,1)S(1)}, u32[]{:S(2)}, u32[]{:S(2)}) collective-permute-start(bf16[256,256]{1,0:T(8,128)(2,1)S(1)} %collective-permute-done.2.refs_8_), channel_id=1, source_target_pairs={{0,2},{2,0},{4,6},{6,4},{1,3},{3,1},{5,7},{7,5},{8,10},{10,8},{12,... | collective-permute-start | bytes 393224 | tf_op jit(solution)/shard_map/ppermute | solution.py:204
  16.0 12.6 %collective-permute-start.4 = (bf16[272,256]{1,0:T(8,128)(2,1)S(1)}, bf16[272,256]{1,0:T(8,128)(2,1)S(1)}, u32[]{:S(2)}, u32[]{:S(2)}) collective-permute-start(bf16[272,256]{1,0:T(8,128)(2,1)S(1)} %constant_dynamic-update-slice_fusion.refs_5_), channel_id=1, source_target_pairs={{0,6},{2,4},{4,2},{6,0},{1,7},{3,5},{5,3},{7,1},{8,14},{10,12},{12... | collective-permute-start | bytes 417800 | tf_op jit(solution)/shard_map/ppermute | solution.py:204
  19.6 14.7 %collective-permute-start.3 = (bf16[272,256]{1,0:T(8,128)(2,1)S(1)}, bf16[272,256]{1,0:T(8,128)(2,1)S(1)}, u32[]{:S(2)}, u32[]{:S(2)}) collective-permute-start(bf16[272,256]{1,0:T(8,128)(2,1)S(1)} %constant_dynamic-update-slice_fusion.refs_5_), channel_id=1, source_target_pairs={{0,2},{2,0},{4,6},{6,4},{1,3},{3,1},{5,7},{7,5},{8,10},{10,8},{12,... | collective-permute-start | bytes 417800 | tf_op jit(solution)/shard_map/ppermute | solution.py:204
  28.7 6.4 %collective-permute-start.7 = (bf16[272,256]{1,0:T(8,128)(2,1)S(1)}, bf16[272,256]{1,0:T(8,128)(2,1)S(1)}, u32[]{:S(2)}, u32[]{:S(2)}) collective-permute-start(bf16[272,256]{1,0:T(8,128)(2,1)S(1)} %pad_maximum_fusion.refs_8_), channel_id=1, source_target_pairs={{0,2},{2,0},{4,6},{6,4},{1,3},{3,1},{5,7},{7,5},{8,10},{10,8},{12,... | collective-permute-start | bytes 417800 | tf_op jit(solution)/shard_map/ppermute | solution.py:204
  29.9 15.5 %collective-permute-start.10 = (bf16[256,256]{1,0:T(8,128)(2,1)S(1)}, bf16[256,256]{1,0:T(8,128)(2,1)S(1)}, u32[]{:S(2)}, u32[]{:S(2)}) collective-permute-start(bf16[256,256]{1,0:T(8,128)(2,1)S(1)} %get-tuple-element.32), channel_id=1, source_target_pairs={{0,6},{2,4},{4,2},{6,0},{1,7},{3,5},{5,3},{7,1},{8,14},{10,12},{12... | collective-permute-start | bytes 393224 | tf_op jit(solution)/shard_map/ppermute | solution.py:204
  31.3 14.8 %collective-permute-start.8 = (bf16[256,256]{1,0:T(8,128)(2,1)S(1)}, bf16[256,256]{1,0:T(8,128)(2,1)S(1)}, u32[]{:S(2)}, u32[]{:S(2)}) collective-permute-start(bf16[256,256]{1,0:T(8,128)(2,1)S(1)} %get-tuple-element.30), channel_id=1, source_target_pairs={{0,4},{2,6},{4,0},{6,2},{1,5},{3,7},{5,1},{7,3},{8,12},{10,14},{12... | collective-permute-start | bytes 393224 | tf_op jit(solution)/shard_map/ppermute | solution.py:204
  32.3 13.8 %collective-permute-start.9 = (bf16[256,256]{1,0:T(8,128)(2,1)S(1)}, bf16[256,256]{1,0:T(8,128)(2,1)S(1)}, u32[]{:S(2)}, u32[]{:S(2)}) collective-permute-start(bf16[256,256]{1,0:T(8,128)(2,1)S(1)} %get-tuple-element.31), channel_id=1, source_target_pairs={{0,2},{2,0},{4,6},{6,4},{1,3},{3,1},{5,7},{7,5},{8,10},{10,8},{12,... | collective-permute-start | bytes 393224 | tf_op jit(solution)/shard_map/ppermute | solution.py:204
  41.6 7.3 %collective-permute-start.13 = (bf16[256,256]{1,0:T(8,128)(2,1)S(1)}, bf16[256,256]{1,0:T(8,128)(2,1)S(1)}, u32[]{:S(2)}, u32[]{:S(2)}) collective-permute-start(bf16[256,256]{1,0:T(8,128)(2,1)S(1)} %get-tuple-element.35), channel_id=1, source_target_pairs={{0,6},{2,4},{4,2},{6,0},{1,7},{3,5},{5,3},{7,1},{8,14},{10,12},{12... | collective-permute-start | bytes 393224 | tf_op jit(solution)/shard_map/ppermute | solution.py:204
  45.4 6.0 %collective-permute-start.14 = (bf16[256,256]{1,0:T(8,128)(2,1)S(1)}, bf16[256,256]{1,0:T(8,128)(2,1)S(1)}, u32[]{:S(2)}, u32[]{:S(2)}) collective-permute-start(bf16[256,256]{1,0:T(8,128)(2,1)S(1)} %get-tuple-element.36), channel_id=1, source_target_pairs={{0,4},{2,6},{4,0},{6,2},{1,5},{3,7},{5,1},{7,3},{8,12},{10,14},{12... | collective-permute-start | bytes 393224 | tf_op jit(solution)/shard_map/ppermute | solution.py:204
  45.4 6.4 %collective-permute-start.15 = (bf16[256,256]{1,0:T(8,128)(2,1)S(1)}, bf16[256,256]{1,0:T(8,128)(2,1)S(1)}, u32[]{:S(2)}, u32[]{:S(2)}) collective-permute-start(bf16[256,256]{1,0:T(8,128)(2,1)S(1)} %get-tuple-element.37), channel_id=1, source_target_pairs={{0,2},{2,0},{4,6},{6,4},{1,3},{3,1},{5,7},{7,5},{8,10},{10,8},{12,... | collective-permute-start | bytes 393224 | tf_op jit(solution)/shard_map/ppermute | solution.py:204
  46.2 1.2 %collective-permute-start.11 = (f32[8,128]{1,0:T(8,128)S(1)}, f32[8,128]{1,0:T(8,128)S(1)}, u32[]{:S(2)}, u32[]{:S(2)}) collective-permute-start(f32[8,128]{1,0:T(8,128)S(1)} %fusion.5), channel_id=1, source_target_pairs={{0,8},{8,0},{16,24},{24,16},{1,9},{9,1},{17,25},{25,17},{2,10},{10... | collective-permute-start | bytes 12296 | tf_op jit(solution)/shard_map/ppermute | solution.py:204
  47.4 5.8 %collective-permute-start.12 = (f32[8,128]{1,0:T(8,128)S(1)}, f32[8,128]{1,0:T(8,128)S(1)}, u32[]{:S(2)}, u32[]{:S(2)}) collective-permute-start(f32[8,128]{1,0:T(8,128)S(1)} %add.89), channel_id=1, source_target_pairs={{0,16},{8,24},{16,0},{24,8},{1,17},{9,25},{17,1},{25,9},{2,18},{10... | collective-permute-start | bytes 12296 | tf_op jit(solution)/shard_map/ppermute | solution.py:204
  52.0 5.0 %collective-permute-start.16 = (bf16[128,512]{1,0:T(8,128)(2,1)S(1)}, bf16[128,512]{1,0:T(8,128)(2,1)S(1)}, u32[]{:S(2)}, u32[]{:S(2)}) collective-permute-start(bf16[128,512]{1,0:T(8,128)(2,1)S(1)} %pad_maximum_fusion.2), channel_id=1, source_target_pairs={{0,1},{1,0},{2,3},{3,2},{4,5},{5,4},{6,7},{7,6},{8,9},{9,8},{10,11... | collective-permute-start | bytes 393224 | tf_op jit(solution)/shard_map/ppermute | solution.py:204

commit v15 on v10

--- a/solution.py
+++ b/solution.py
@@ -10,11 +10,10 @@
 
 HD = 128
 GROUP = 8
-PAIR = 2
+PAIR = 4
 CHUNKS = 2
 EXTRA = 16
 STEP = 64
-VMEM_LIMIT = 40 * 1024 * 1024
 SMALL_LIMIT = 8 * 1024 * 1024
 NT = (((1,), (1,)), ((), ()))
 
@@ -313,7 +312,7 @@
     across = pltpu.VMEM((count, HD, n_keys), bf16)
     scratch = [wide, step_buffer, step_buffer, head_buffer, head_buffer]
     scratch += [pltpu.VMEM((2, HD, GROUP * rows), bf16), down, across, down, across]
-    scratch += [pltpu.SemaphoreType.DMA((count,))]
+    in_buffers = sum(math.prod(x.shape) * jnp.dtype(x.dtype).itemsize for x in scratch)
     part = lambda x: jax.ShapeDtypeStruct((x.shape[0], x.shape[1] // CHUNKS), bf16)
     terms = [jax.ShapeDtypeStruct((2 * held, count * HD), bf16)] * n_slots
     total = [jax.ShapeDtypeStruct((8, HD), jnp.float32)] * last
@@ -323,8 +322,8 @@
         out_specs=[HBM] + [VMEM] * (3 + n_slots + last),
         out_shape=[like(q), part(q), part(k), part(v)] + terms + total,
         input_output_aliases={5 + n_slots: 0} if last else {},
-        scratch_shapes=scratch,
-        compiler_params=pltpu.CompilerParams(vmem_limit_bytes=VMEM_LIMIT),
+        scratch_shapes=scratch + [pltpu.SemaphoreType.DMA((count,))],
+        compiler_params=pltpu.CompilerParams(vmem_limit_bytes=in_buffers * 5 // 4 + SMALL_LIMIT // 2),
         cost_estimate=pl.CostEstimate(
             flops=24 * unit,
             bytes_accessed=8 * rows * GROUP * HD * count,

time: 57.6 us -> 58.8 us (1.021)
  Pallas kernels: 14.3 us -> 15.6 us
    pallas_call x2, Pallas kernels: 12.4 us -> 13.7 us  [attend(): pl.pallas_call(functools.partial(attend_kernel, n_slots, count, chunk, he...]
  transfers between devices with their start and end apart: 17 -> 17, of which waited for: 8 -> 8; matrix products, arithmetic and copies ran while one was open for 3% -> 3% of each run, Pallas kernels for 25% -> 27%
where the time goes in v15:
time: 58.8 us; the launch traced here: 58.6 us
  starting transfers between devices  26 us (44%)
  Pallas kernels  15.6 us (27%)
  waiting for transfers between devices  11.9 us (20%)
  local copies, waits for them, and re-layouts  2.52 us (4%)
  between operations  1.51 us (3%)
  other arithmetic  1.06 us (2%)
    ppermute x17, starting transfers between devices, swap(): lax.ppermute(x, axis, [(i, i ^ by) for i in range(lax.axis_size(axis))])  26 us
    pallas_call x2, Pallas kernels, attend(): pl.pallas_call(functools.partial(attend_kernel, n_slots, count, chunk, he...  13.7 us
    ppermute x17, waiting for transfers between devices, swap(): lax.ppermute(x, axis, [(i, i ^ by) for i in range(lax.axis_size(axis))])  11.9 us
    unnamed x12, local copies, waits for them, and re-layouts  1.56 us
    pallas_call x1, Pallas kernels, scale_all(): pl.pallas_call(functools.partial(scale_kernel, slots_all), in_specs=[VMEM...  1.27 us
  transfers between devices with their start and end apart: 17, of which 8 were waited for; matrix products, arithmetic and copies ran while one was open for 3% of the time, Pallas kernels for 27%

profile of v15, /device:TPU:0, one launch (start us, length us, event | category | flops | bytes accessed | tf_op | source)
XLA Modules:
  0.0 58.6 jit_solution(2490609189851901191)
XLA Ops:
  0.6 0.0 copy-start
  0.7 0.9 %dynamic-slice_bitcast_fusion = (bf16[64,256]{1,0:T(8,128)(2,1)S(1)}, bf16[64,256]{1,0:T(8,128)(2,1)S(1)}, bf16[64,256]{1,0:T(8,128)(2,1)S(1)}, bf16[64,256]{1,0...) fusion(bf16[1,64,1024]{2,1,0:T(8,128)(2,1)} %param.11, s32[]{:T(128)S(6)} %select_n.41, ...), kind=kLoop, calls=%fused_computation.28 | loop fusion | bytes 393228 | tf_op jit(solution)/shard_map/dynamic_slice | solution.py:233
  1.6 3.0 %collective-permute-start = (bf16[128,256]{1,0:T(8,128)(2,1)S(1)}, bf16[128,256]{1,0:T(8,128)(2,1)S(1)}, u32[]{:S(2)}, u32[]{:S(2)}) collective-permute-start(bf16[128,256]{1,0:T(8,128)(2,1)S(1)} %pad_maximum_fusion.4), channel_id=1, source_target_pairs={{0,1},{1,0},{2,3},{3,2},{4,5},{5,4},{6,7},{7,6},{8,9},{9,8},{10,11... | collective-permute-start | bytes 196616 | tf_op jit(solution)/shard_map/ppermute | solution.py:201
  4.7 0.1 collective-permute-start.1
  5.4 0.8 %bitcast_dynamic-update-slice_fusion.1 = bf16[272,256]{1,0:T(8,128)(2,1)S(1)} fusion(bf16[1,64,1024]{2,1,0:T(8,128)(2,1)} %param.10, s32[]{:T(128)S(6)} %select_n.40), kind=kLoop, calls=%fused_computation.27 | loop fusion | bytes 65540
  6.2 0.9 %collective-permute-done = bf16[128,256]{1,0:T(8,128)(2,1)S(1)} collective-permute-done((bf16[128,256]{1,0:T(8,128)(2,1)S(1)}, bf16[128,256]{1,0:T(8,128)(2,1)S(1)}, u32[]{:S(2)}, u32[]{:S(2)}) %collective-permute-start) | collective-permute-done | bytes 65568 | tf_op jit(solution)/shard_map/ppermute | solution.py:201
  7.1 4.6 %collective-permute-start.2 = (bf16[256,256]{1,0:T(8,128)(2,1)S(1)}, bf16[256,256]{1,0:T(8,128)(2,1)S(1)}, u32[]{:S(2)}, u32[]{:S(2)}) collective-permute-start(bf16[256,256]{1,0:T(8,128)(2,1)S(1)} %pad_maximum_fusion.1.after_ref.refs_5_), channel_id=1, source_target_pairs={{0,6},{2,4},{4,2},{6,0},{1,7},{3,5},{5,3},{7,1},{8,14},{10,12},{12... | collective-permute-start | bytes 393224 | tf_op jit(solution)/shard_map/ppermute | solution.py:201
  11.7 0.0 collective-permute-start.5
  11.7 0.0 copy-done
  11.7 0.0 copy-start.1
  11.7 0.0 copy-start.3
  11.7 0.6 %turn.1.refs_2_ = bf16[4,128,1024]{2,1,0:T(8,128)(2,1)S(1)} custom-call(bf16[128,4096]{1,0:T(8,128)(2,1)S(1)} %bitcast.41, bf16[256,256]{1,0:T(8,128)(2,1)S(1)} %pad_maximum_fusion.1.after_ref.refs_5_), custom_call_target="tpu_custom_call" | custom-call | tf_op jit(solution)/shard_map/turn/pallas_call | solution.py:289
  12.3 0.0 copy-start.2
  12.3 0.0 collective-permute-done.1
  12.4 0.8 %bitcast_dynamic-update-slice_fusion = bf16[272,256]{1,0:T(8,128)(2,1)S(1)} fusion(bf16[272,256]{1,0:T(8,128)(2,1)S(1)} %slice_dynamic-update-slice_fusion.1, bf16[1,64,1024]{2,1,0:T(8,128)(2,1)} %param.11, s32[]{:T(128)S(6)} %select_n.40), kind=kLoop, calls=%fused_computation.26 | loop fusion | bytes 65540
  13.1 2.1 %collective-permute-done.2.refs_8_ = bf16[256,256]{1,0:T(8,128)(2,1)S(1)} collective-permute-done((bf16[256,256]{1,0:T(8,128)(2,1)S(1)}, bf16[256,256]{1,0:T(8,128)(2,1)S(1)}, u32[]{:S(2)}, u32[]{:S(2)}) %collective-permute-start.2) | collective-permute-done | bytes 131104 | tf_op jit(solution)/shard_map/ppermute | solution.py:201
  15.2 0.8 %collective-permute-start.6 = (bf16[256,256]{1,0:T(8,128)(2,1)S(1)}, bf16[256,256]{1,0:T(8,128)(2,1)S(1)}, u32[]{:S(2)}, u32[]{:S(2)}) collective-permute-start(bf16[256,256]{1,0:T(8,128)(2,1)S(1)} %collective-permute-done.2.refs_8_), channel_id=1, source_target_pairs={{0,2},{2,0},{4,6},{6,4},{1,3},{3,1},{5,7},{7,5},{8,10},{10,8},{12,... | collective-permute-start | bytes 393224 | tf_op jit(solution)/shard_map/ppermute | solution.py:201
  16.0 3.6 %collective-permute-start.4 = (bf16[272,256]{1,0:T(8,128)(2,1)S(1)}, bf16[272,256]{1,0:T(8,128)(2,1)S(1)}, u32[]{:S(2)}, u32[]{:S(2)}) collective-permute-start(bf16[272,256]{1,0:T(8,128)(2,1)S(1)} %constant_dynamic-update-slice_fusion.refs_5_), channel_id=1, source_target_pairs={{0,6},{2,4},{4,2},{6,0},{1,7},{3,5},{5,3},{7,1},{8,14},{10,12},{12... | collective-permute-start | bytes 417800 | tf_op jit(solution)/shard_map/ppermute | solution.py:201
  19.6 1.1 %collective-permute-start.3 = (bf16[272,256]{1,0:T(8,128)(2,1)S(1)}, bf16[272,256]{1,0:T(8,128)(2,1)S(1)}, u32[]{:S(2)}, u32[]{:S(2)}) collective-permute-start(bf16[272,256]{1,0:T(8,128)(2,1)S(1)} %constant_dynamic-update-slice_fusion.refs_5_), channel_id=1, source_target_pairs={{0,2},{2,0},{4,6},{6,4},{1,3},{3,1},{5,7},{7,5},{8,10},{10,8},{12,... | collective-permute-start | bytes 417800 | tf_op jit(solution)/shard_map/ppermute | solution.py:201
  20.7 0.0 collective-permute-done.5.refs_6_
  20.7 1.5 %collective-permute-done.6.refs_7_ = bf16[256,256]{1,0:T(8,128)(2,1)S(1)} collective-permute-done((bf16[256,256]{1,0:T(8,128)(2,1)S(1)}, bf16[256,256]{1,0:T(8,128)(2,1)S(1)}, u32[]{:S(2)}, u32[]{:S(2)}) %collective-permute-start.6) | collective-permute-done | bytes 131104 | tf_op jit(solution)/shard_map/ppermute | solution.py:201
  22.2 0.0 copy-done.1
  22.2 0.0 copy-done.3
  22.2 0.0 copy-done.2
  22.2 6.9 %attend_0.1 = (bf16[128,4096]{1,0:T(8,128)(2,1)}, bf16[128,2048]{1,0:T(8,128)(2,1)S(1)}, bf16[128,256]{1,0:T(8,128)(2,1)S(1)}, bf16[128,256]{1,0:T(8,128)(2,1)S(...) custom-call(s32[1]{0:T(128)} %bitcast.39.refs_0_, ...), custom_call_target="tpu_custom_call" | custom-call | flops 8053063680 | bytes 2097152 | tf_op jit(solution)/shard_map/attend_0/pallas_call | solution.py:319
  29.1 0.0 collective-permute-done.4
  29.1 1.2 %collective-permute-start.7 = (bf16[272,256]{1,0:T(8,128)(2,1)S(1)}, bf16[272,256]{1,0:T(8,128)(2,1)S(1)}, u32[]{:S(2)}, u32[]{:S(2)}) collective-permute-start(bf16[272,256]{1,0:T(8,128)(2,1)S(1)} %pad_maximum_fusion.refs_8_), channel_id=1, source_target_pairs={{0,2},{2,0},{4,6},{6,4},{1,3},{3,1},{5,7},{7,5},{8,10},{10,8},{12,... | collective-permute-start | bytes 417800 | tf_op jit(solution)/shard_map/ppermute | solution.py:201
  30.3 1.3 %collective-permute-start.10 = (bf16[256,256]{1,0:T(8,128)(2,1)S(1)}, bf16[256,256]{1,0:T(8,128)(2,1)S(1)}, u32[]{:S(2)}, u32[]{:S(2)}) collective-permute-start(bf16[256,256]{1,0:T(8,128)(2,1)S(1)} %get-tuple-element.32), channel_id=1, source_target_pairs={{0,6},{2,4},{4,2},{6,0},{1,7},{3,5},{5,3},{7,1},{8,14},{10,12},{12... | collective-permute-start | bytes 393224 | tf_op jit(solution)/shard_map/ppermute | solution.py:201
  31.7 1.0 %collective-permute-start.8 = (bf16[256,256]{1,0:T(8,128)(2,1)S(1)}, bf16[256,256]{1,0:T(8,128)(2,1)S(1)}, u32[]{:S(2)}, u32[]{:S(2)}) collective-permute-start(bf16[256,256]{1,0:T(8,128)(2,1)S(1)} %get-tuple-element.30), channel_id=1, source_target_pairs={{0,4},{2,6},{4,0},{6,2},{1,5},{3,7},{5,1},{7,3},{8,12},{10,14},{12... | collective-permute-start | bytes 393224 | tf_op jit(solution)/shard_map/ppermute | solution.py:201
  32.7 2.0 %collective-permute-start.9 = (bf16[256,256]{1,0:T(8,128)(2,1)S(1)}, bf16[256,256]{1,0:T(8,128)(2,1)S(1)}, u32[]{:S(2)}, u32[]{:S(2)}) collective-permute-start(bf16[256,256]{1,0:T(8,128)(2,1)S(1)} %get-tuple-element.31), channel_id=1, source_target_pairs={{0,2},{2,0},{4,6},{6,4},{1,3},{3,1},{5,7},{7,5},{8,10},{10,8},{12,... | collective-permute-start | bytes 393224 | tf_op jit(solution)/shard_map/ppermute | solution.py:201
  34.7 0.0 collective-permute-done.3.refs_6_
  34.7 0.8 %collective-permute-done.7.refs_7_ = bf16[272,256]{1,0:T(8,128)(2,1)S(1)} collective-permute-done((bf16[272,256]{1,0:T(8,128)(2,1)S(1)}, bf16[272,256]{1,0:T(8,128)(2,1)S(1)}, u32[]{:S(2)}, u32[]{:S(2)}) %collective-permute-start.7) | collective-permute-done | bytes 139296 | tf_op jit(solution)/shard_map/ppermute | solution.py:201
  35.5 6.8 %attend_1.1 = (bf16[128,4096]{1,0:T(8,128)(2,1)}, bf16[128,2048]{1,0:T(8,128)(2,1)S(1)}, bf16[128,256]{1,0:T(8,128)(2,1)S(1)}, bf16[128,256]{1,0:T(8,128)(2,1)S(...) custom-call(s32[1]{0:T(128)} %bitcast.40.refs_0_, ...), custom_call_target="tpu_custom_call", output_to_operand_aliasing={{0}: (9, {})} | custom-call | flops 8053063680 | bytes 2097152 | tf_op jit(solution)/shard_map/attend_1/pallas_call | solution.py:319
  42.3 3.8 %collective-permute-start.13 = (bf16[256,256]{1,0:T(8,128)(2,1)S(1)}, bf16[256,256]{1,0:T(8,128)(2,1)S(1)}, u32[]{:S(2)}, u32[]{:S(2)}) collective-permute-start(bf16[256,256]{1,0:T(8,128)(2,1)S(1)} %get-tuple-element.35), channel_id=1, source_target_pairs={{0,6},{2,4},{4,2},{6,0},{1,7},{3,5},{5,3},{7,1},{8,14},{10,12},{12... | collective-permute-start | bytes 393224 | tf_op jit(solution)/shard_map/ppermute | solution.py:201
  46.2 0.0 collective-permute-start.14
  46.2 0.0 collective-permute-done.10
  46.2 0.6 %collective-permute-start.15 = (bf16[256,256]{1,0:T(8,128)(2,1)S(1)}, bf16[256,256]{1,0:T(8,128)(2,1)S(1)}, u32[]{:S(2)}, u32[]{:S(2)}) collective-permute-start(bf16[256,256]{1,0:T(8,128)(2,1)S(1)} %get-tuple-element.37), channel_id=1, source_target_pairs={{0,2},{2,0},{4,6},{6,4},{1,3},{3,1},{5,7},{7,5},{8,10},{10,8},{12,... | collective-permute-start | bytes 393224 | tf_op jit(solution)/shard_map/ppermute | solution.py:201
  46.8 0.0 collective-permute-done.8
  46.8 0.0 collective-permute-done.9
  46.8 0.1 fusion.7
  46.9 0.1 collective-permute-start.11
  47.0 1.1 %collective-permute-done.11 = f32[8,128]{1,0:T(8,128)S(1)} collective-permute-done((f32[8,128]{1,0:T(8,128)S(1)}, f32[8,128]{1,0:T(8,128)S(1)}, u32[]{:S(2)}, u32[]{:S(2)}) %collective-permute-start.11) | collective-permute-done | bytes 4128 | tf_op jit(solution)/shard_map/ppermute | solution.py:201
  48.2 1.5 %collective-permute-start.12 = (f32[8,128]{1,0:T(8,128)S(1)}, f32[8,128]{1,0:T(8,128)S(1)}, u32[]{:S(2)}, u32[]{:S(2)}) collective-permute-start(f32[8,128]{1,0:T(8,128)S(1)} %add.89), channel_id=1, source_target_pairs={{0,16},{8,24},{16,0},{24,8},{1,17},{9,25},{17,1},{25,9},{2,18},{10... | collective-permute-start | bytes 12296 | tf_op jit(solution)/shard_map/ppermute | solution.py:201
  49.7 0.0 collective-permute-done.13
  49.7 2.5 %collective-permute-done.14 = bf16[256,256]{1,0:T(8,128)(2,1)S(1)} collective-permute-done((bf16[256,256]{1,0:T(8,128)(2,1)S(1)}, bf16[256,256]{1,0:T(8,128)(2,1)S(1)}, u32[]{:S(2)}, u32[]{:S(2)}) %collective-permute-start.14) | collective-permute-done | bytes 131104 | tf_op jit(solution)/shard_map/ppermute | solution.py:201
  52.1 0.5 collective-permute-done.15
  52.6 0.1 fusion.6
  52.7 1.2 %collective-permute-start.16 = (bf16[128,512]{1,0:T(8,128)(2,1)S(1)}, bf16[128,512]{1,0:T(8,128)(2,1)S(1)}, u32[]{:S(2)}, u32[]{:S(2)}) collective-permute-start(bf16[128,512]{1,0:T(8,128)(2,1)S(1)} %pad_maximum_fusion.2), channel_id=1, source_target_pairs={{0,1},{1,0},{2,3},{3,2},{4,5},{5,4},{6,7},{7,6},{8,9},{9,8},{10,11... | collective-permute-start | bytes 393224 | tf_op jit(solution)/shard_map/ppermute | solution.py:201
  53.9 0.0 collective-permute-done.12
  54.0 1.3 %scale.1 = (bf16[128,4096]{1,0:T(8,128)(2,1)}, bf16[128,512]{1,0:T(8,128)(2,1)}, bf16[128,512]{1,0:T(8,128)(2,1)}) custom-call(f32[8,128]{1,0:T(8,128)S(1)} %get-tuple-element.52.total_ref, bf16[128,2048]{1,0:T(8,128)(2,1)S(1)} %get-tuple-element.38.refs_0_, bf16[128,256]{1,0:T(8,128)(2,1)S(1)} %get-tuple-element.39.refs_1_, ...), custom_call_target="tpu_custom_call" | custom-call | flops 655360 | bytes 2621440 | tf_op jit(solution)/shard_map/scale/pallas_call | solution.py:338
  55.2 2.5 %collective-permute-done.16 = bf16[128,512]{1,0:T(8,128)(2,1)S(1)} collective-permute-done((bf16[128,512]{1,0:T(8,128)(2,1)S(1)}, bf16[128,512]{1,0:T(8,128)(2,1)S(1)}, u32[]{:S(2)}, u32[]{:S(2)}) %collective-permute-start.16) | collective-permute-done | bytes 131104 | tf_op jit(solution)/shard_map/ppermute | solution.py:201
  57.8 0.8 %multiply_convert_fusion = (bf16[1,64,1024]{2,1,0:T(8,128)(2,1)}, bf16[1,64,1024]{2,1,0:T(8,128)(2,1)}) fusion(bf16[1,64,512]{2,1,0:T(8,128)(2,1)S(1)} %select_bitcast_fusion, bf16[1,64,512]{2,1,0:T(8,128)(2,1)S(1)} %get-tuple-element.46, f32[1024]{0:T(1024)S(1)} %broadcast_bitcast_fusion, bf16[1,64,512]{2,1,0:T(8,128)(2,1)S(1)} %get-tuple-element.54, ...), kind=kLoop, calls=%fused_computation.6 | loop fusion | flops 786432 | bytes 528384 | tf_op jit(solution)/shard_map/convert_element_type | solution.py:387
  (20 shorter events, 0.2 us)
Async XLA Ops:
  0.6 11.0 %copy-start = (bf16[1,128,4096]{2,1,0:T(8,128)(2,1)S(1)}, bf16[1,128,4096]{2,1,0:T(8,128)(2,1)}, u32[]{:S(2)}) copy-start(bf16[1,128,4096]{2,1,0:T(8,128)(2,1)} %param.13) | copy-start | bytes 3145732
  1.6 5.4 %collective-permute-start = (bf16[128,256]{1,0:T(8,128)(2,1)S(1)}, bf16[128,256]{1,0:T(8,128)(2,1)S(1)}, u32[]{:S(2)}, u32[]{:S(2)}) collective-permute-start(bf16[128,256]{1,0:T(8,128)(2,1)S(1)} %pad_maximum_fusion.4), channel_id=1, source_target_pairs={{0,1},{1,0},{2,3},{3,2},{4,5},{5,4},{6,7},{7,6},{8,9},{9,8},{10,11... | collective-permute-start | bytes 196616 | tf_op jit(solution)/shard_map/ppermute | solution.py:201
  4.7 7.7 %collective-permute-start.1 = (bf16[128,256]{1,0:T(8,128)(2,1)S(1)}, bf16[128,256]{1,0:T(8,128)(2,1)S(1)}, u32[]{:S(2)}, u32[]{:S(2)}) collective-permute-start(bf16[128,256]{1,0:T(8,128)(2,1)S(1)} %pad_maximum_fusion.5), channel_id=1, source_target_pairs={{0,1},{1,0},{2,3},{3,2},{4,5},{5,4},{6,7},{7,6},{8,9},{9,8},{10,11... | collective-permute-start | bytes 196616 | tf_op jit(solution)/shard_map/ppermute | solution.py:201
  7.1 8.2 %collective-permute-start.2 = (bf16[256,256]{1,0:T(8,128)(2,1)S(1)}, bf16[256,256]{1,0:T(8,128)(2,1)S(1)}, u32[]{:S(2)}, u32[]{:S(2)}) collective-permute-start(bf16[256,256]{1,0:T(8,128)(2,1)S(1)} %pad_maximum_fusion.1.after_ref.refs_5_), channel_id=1, source_target_pairs={{0,6},{2,4},{4,2},{6,0},{1,7},{3,5},{5,3},{7,1},{8,14},{10,12},{12... | collective-permute-start | bytes 393224 | tf_op jit(solution)/shard_map/ppermute | solution.py:201
  11.7 9.0 %collective-permute-start.5 = (bf16[256,256]{1,0:T(8,128)(2,1)S(1)}, bf16[256,256]{1,0:T(8,128)(2,1)S(1)}, u32[]{:S(2)}, u32[]{:S(2)}) collective-permute-start(bf16[256,256]{1,0:T(8,128)(2,1)S(1)} %pad_maximum_fusion.1.after_ref.refs_5_), channel_id=1, source_target_pairs={{0,2},{2,0},{4,6},{6,4},{1,3},{3,1},{5,7},{7,5},{8,10},{10,8},{12,... | collective-permute-start | bytes 393224 | tf_op jit(solution)/shard_map/ppermute | solution.py:201
  11.7 10.5 %copy-start.1 = (bf16[1,128,4096]{2,1,0:T(8,128)(2,1)S(1)}, bf16[1,128,4096]{2,1,0:T(8,128)(2,1)}, u32[]{:S(2)}) copy-start(bf16[1,128,4096]{2,1,0:T(8,128)(2,1)} %param.7) | copy-start | bytes 3145732
  11.7 10.5 %copy-start.3 = (bf16[1,128,512]{2,1,0:T(8,128)(2,1)S(1)}, bf16[1,128,512]{2,1,0:T(8,128)(2,1)}, u32[]{:S(2)}) copy-start(bf16[1,128,512]{2,1,0:T(8,128)(2,1)} %param.9) | copy-start | bytes 393220
  12.3 9.9 %copy-start.2 = (bf16[1,128,512]{2,1,0:T(8,128)(2,1)S(1)}, bf16[1,128,512]{2,1,0:T(8,128)(2,1)}, u32[]{:S(2)}) copy-start(bf16[1,128,512]{2,1,0:T(8,128)(2,1)} %param.8) | copy-start | bytes 393220
  15.2 7.0 %collective-permute-start.6 = (bf16[256,256]{1,0:T(8,128)(2,1)S(1)}, bf16[256,256]{1,0:T(8,128)(2,1)S(1)}, u32[]{:S(2)}, u32[]{:S(2)}) collective-permute-start(bf16[256,256]{1,0:T(8,128)(2,1)S(1)} %collective-permute-done.2.refs_8_), channel_id=1, source_target_pairs={{0,2},{2,0},{4,6},{6,4},{1,3},{3,1},{5,7},{7,5},{8,10},{10,8},{12,... | collective-permute-start | bytes 393224 | tf_op jit(solution)/shard_map/ppermute | solution.py:201
  16.0 13.0 %collective-permute-start.4 = (bf16[272,256]{1,0:T(8,128)(2,1)S(1)}, bf16[272,256]{1,0:T(8,128)(2,1)S(1)}, u32[]{:S(2)}, u32[]{:S(2)}) collective-permute-start(bf16[272,256]{1,0:T(8,128)(2,1)S(1)} %constant_dynamic-update-slice_fusion.refs_5_), channel_id=1, source_target_pairs={{0,6},{2,4},{4,2},{6,0},{1,7},{3,5},{5,3},{7,1},{8,14},{10,12},{12... | collective-permute-start | bytes 417800 | tf_op jit(solution)/shard_map/ppermute | solution.py:201
  19.6 15.1 %collective-permute-start.3 = (bf16[272,256]{1,0:T(8,128)(2,1)S(1)}, bf16[272,256]{1,0:T(8,128)(2,1)S(1)}, u32[]{:S(2)}, u32[]{:S(2)}) collective-permute-start(bf16[272,256]{1,0:T(8,128)(2,1)S(1)} %constant_dynamic-update-slice_fusion.refs_5_), channel_id=1, source_target_pairs={{0,2},{2,0},{4,6},{6,4},{1,3},{3,1},{5,7},{7,5},{8,10},{10,8},{12,... | collective-permute-start | bytes 417800 | tf_op jit(solution)/shard_map/ppermute | solution.py:201
  29.1 6.4 %collective-permute-start.7 = (bf16[272,256]{1,0:T(8,128)(2,1)S(1)}, bf16[272,256]{1,0:T(8,128)(2,1)S(1)}, u32[]{:S(2)}, u32[]{:S(2)}) collective-permute-start(bf16[272,256]{1,0:T(8,128)(2,1)S(1)} %pad_maximum_fusion.refs_8_), channel_id=1, source_target_pairs={{0,2},{2,0},{4,6},{6,4},{1,3},{3,1},{5,7},{7,5},{8,10},{10,8},{12,... | collective-permute-start | bytes 417800 | tf_op jit(solution)/shard_map/ppermute | solution.py:201
  30.3 15.8 %collective-permute-start.10 = (bf16[256,256]{1,0:T(8,128)(2,1)S(1)}, bf16[256,256]{1,0:T(8,128)(2,1)S(1)}, u32[]{:S(2)}, u32[]{:S(2)}) collective-permute-start(bf16[256,256]{1,0:T(8,128)(2,1)S(1)} %get-tuple-element.32), channel_id=1, source_target_pairs={{0,6},{2,4},{4,2},{6,0},{1,7},{3,5},{5,3},{7,1},{8,14},{10,12},{12... | collective-permute-start | bytes 393224 | tf_op jit(solution)/shard_map/ppermute | solution.py:201
  31.7 15.2 %collective-permute-start.8 = (bf16[256,256]{1,0:T(8,128)(2,1)S(1)}, bf16[256,256]{1,0:T(8,128)(2,1)S(1)}, u32[]{:S(2)}, u32[]{:S(2)}) collective-permute-start(bf16[256,256]{1,0:T(8,128)(2,1)S(1)} %get-tuple-element.30), channel_id=1, source_target_pairs={{0,4},{2,6},{4,0},{6,2},{1,5},{3,7},{5,1},{7,3},{8,12},{10,14},{12... | collective-permute-start | bytes 393224 | tf_op jit(solution)/shard_map/ppermute | solution.py:201
  32.7 14.1 %collective-permute-start.9 = (bf16[256,256]{1,0:T(8,128)(2,1)S(1)}, bf16[256,256]{1,0:T(8,128)(2,1)S(1)}, u32[]{:S(2)}, u32[]{:S(2)}) collective-permute-start(bf16[256,256]{1,0:T(8,128)(2,1)S(1)} %get-tuple-element.31), channel_id=1, source_target_pairs={{0,2},{2,0},{4,6},{6,4},{1,3},{3,1},{5,7},{7,5},{8,10},{10,8},{12,... | collective-permute-start | bytes 393224 | tf_op jit(solution)/shard_map/ppermute | solution.py:201
  42.3 7.3 %collective-permute-start.13 = (bf16[256,256]{1,0:T(8,128)(2,1)S(1)}, bf16[256,256]{1,0:T(8,128)(2,1)S(1)}, u32[]{:S(2)}, u32[]{:S(2)}) collective-permute-start(bf16[256,256]{1,0:T(8,128)(2,1)S(1)} %get-tuple-element.35), channel_id=1, source_target_pairs={{0,6},{2,4},{4,2},{6,0},{1,7},{3,5},{5,3},{7,1},{8,14},{10,12},{12... | collective-permute-start | bytes 393224 | tf_op jit(solution)/shard_map/ppermute | solution.py:201
  46.2 6.0 %collective-permute-start.14 = (bf16[256,256]{1,0:T(8,128)(2,1)S(1)}, bf16[256,256]{1,0:T(8,128)(2,1)S(1)}, u32[]{:S(2)}, u32[]{:S(2)}) collective-permute-start(bf16[256,256]{1,0:T(8,128)(2,1)S(1)} %get-tuple-element.36), channel_id=1, source_target_pairs={{0,4},{2,6},{4,0},{6,2},{1,5},{3,7},{5,1},{7,3},{8,12},{10,14},{12... | collective-permute-start | bytes 393224 | tf_op jit(solution)/shard_map/ppermute | solution.py:201
  46.2 6.4 %collective-permute-start.15 = (bf16[256,256]{1,0:T(8,128)(2,1)S(1)}, bf16[256,256]{1,0:T(8,128)(2,1)S(1)}, u32[]{:S(2)}, u32[]{:S(2)}) collective-permute-start(bf16[256,256]{1,0:T(8,128)(2,1)S(1)} %get-tuple-element.37), channel_id=1, source_target_pairs={{0,2},{2,0},{4,6},{6,4},{1,3},{3,1},{5,7},{7,5},{8,10},{10,8},{12,... | collective-permute-start | bytes 393224 | tf_op jit(solution)/shard_map/ppermute | solution.py:201
  46.9 1.2 %collective-permute-start.11 = (f32[8,128]{1,0:T(8,128)S(1)}, f32[8,128]{1,0:T(8,128)S(1)}, u32[]{:S(2)}, u32[]{:S(2)}) collective-permute-start(f32[8,128]{1,0:T(8,128)S(1)} %fusion.5), channel_id=1, source_target_pairs={{0,8},{8,0},{16,24},{24,16},{1,9},{9,1},{17,25},{25,17},{2,10},{10... | collective-permute-start | bytes 12296 | tf_op jit(solution)/shard_map/ppermute | solution.py:201
  48.2 5.8 %collective-permute-start.12 = (f32[8,128]{1,0:T(8,128)S(1)}, f32[8,128]{1,0:T(8,128)S(1)}, u32[]{:S(2)}, u32[]{:S(2)}) collective-permute-start(f32[8,128]{1,0:T(8,128)S(1)} %add.89), channel_id=1, source_target_pairs={{0,16},{8,24},{16,0},{24,8},{1,17},{9,25},{17,1},{25,9},{2,18},{10... | collective-permute-start | bytes 12296 | tf_op jit(solution)/shard_map/ppermute | solution.py:201
  52.7 5.0 %collective-permute-start.16 = (bf16[128,512]{1,0:T(8,128)(2,1)S(1)}, bf16[128,512]{1,0:T(8,128)(2,1)S(1)}, u32[]{:S(2)}, u32[]{:S(2)}) collective-permute-start(bf16[128,512]{1,0:T(8,128)(2,1)S(1)} %pad_maximum_fusion.2), channel_id=1, source_target_pairs={{0,1},{1,0},{2,3},{3,2},{4,5},{5,4},{6,7},{7,6},{8,9},{9,8},{10,11... | collective-permute-start | bytes 393224 | tf_op jit(solution)/shard_map/ppermute | solution.py:201

commit v16 on v10

--- a/solution.py
+++ b/solution.py
@@ -104,10 +104,10 @@
         if pair == 0:
             assemble(head, vown_ref, held, values_ref, values_t_ref)
         grad = dot_ref[head % 2, :, cols]
-        dp_ref[pair % 2] = jnp.dot(values_ref[head], grad, preferred_element_type=jnp.float32)
         out = jnp.dot(
             values_t_ref[head], e_ref[head % 2, :, cols], preferred_element_type=jnp.float32
         )
+        dp_ref[pair % 2] = jnp.dot(values_ref[head], grad, preferred_element_type=jnp.float32)
         out = out * inverse
         turned = out.astype(jnp.bfloat16).T
         for i in range(PAIR):
@@ -134,14 +134,7 @@
             at = head * GROUP + pair * PAIR + i
             dq_ref[:, at * HD : (at + 1) * HD] = turned[i * rows : (i + 1) * rows]
 
-    def key_grads(head):
-        copy = pltpu.make_async_copy(
-            out_ref.at[:, columns(head, GROUP * HD)],
-            out_hbm.at[:, columns(first + head, GROUP * HD)],
-            out_sem.at[head],
-        )
-        copy.start()
-        stores.append(copy)
+    def value_grads(head):
         here = slice(head * HD, (head + 1) * HD)
         dv = lax.dot_general(
             e_ref[head % 2], dot_ref[head % 2], NT, preferred_element_type=jnp.float32
@@ -149,6 +142,16 @@
         dvown_ref[:, here] = dv[:own]
         for i, ref in enumerate(term_refs):
             ref[held:, here] = dv[own + i * held : own + (i + 1) * held]
+
+    def key_grads(head):
+        copy = pltpu.make_async_copy(
+            out_ref.at[:, columns(head, GROUP * HD)],
+            out_hbm.at[:, columns(first + head, GROUP * HD)],
+            out_sem.at[head],
+        )
+        copy.start()
+        stores.append(copy)
+        here = slice(head * HD, (head + 1) * HD)
         dk = jnp.dot(
             ds_ref[head % 2],
             heads_down(q_ref, (first + head) * GROUP, GROUP),
@@ -166,6 +169,8 @@
         if then:
             scores(*then)
         centre = attended(*now, inverse)
+        if now[1] + 1 == pairs:
+            value_grads(now[0])
         if then:
             inverse = softmax(*then)
         score_grads(*now, centre)

time: 57.6 us -> 57.9 us (level)
  no operation moved by 1% of the time
where the time goes in v16:
time: 57.9 us; the launch traced here: 57.7 us
  starting transfers between devices  26 us (45%)
  Pallas kernels  14.6 us (25%)
  waiting for transfers between devices  12 us (21%)
  local copies, waits for them, and re-layouts  2.52 us (4%)
  between operations  1.51 us (3%)
  other arithmetic  1.06 us (2%)
    ppermute x17, starting transfers between devices, swap(): lax.ppermute(x, axis, [(i, i ^ by) for i in range(lax.axis_size(axis))])  26 us
    pallas_call x2, Pallas kernels, attend(): pl.pallas_call(functools.partial(attend_kernel, n_slots, count, chunk, he...  12.7 us
    ppermute x17, waiting for transfers between devices, swap(): lax.ppermute(x, axis, [(i, i ^ by) for i in range(lax.axis_size(axis))])  12 us
    unnamed x12, local copies, waits for them, and re-layouts  1.56 us
    pallas_call x1, Pallas kernels, scale_all(): pl.pallas_call(functools.partial(scale_kernel, slots_all), in_specs=[VMEM...  1.27 us
  transfers between devices with their start and end apart: 17, of which 8 were waited for; matrix products, arithmetic and copies ran while one was open for 3% of the time, Pallas kernels for 25%

profile of v16, /device:TPU:0, one launch (start us, length us, event | category | flops | bytes accessed | tf_op | source)
XLA Modules:
  0.0 57.7 jit_solution(1262541625622608743)
XLA Ops:
  0.6 0.0 copy-start
  0.7 0.9 %dynamic-slice_bitcast_fusion = (bf16[64,256]{1,0:T(8,128)(2,1)S(1)}, bf16[64,256]{1,0:T(8,128)(2,1)S(1)}, bf16[64,256]{1,0:T(8,128)(2,1)S(1)}, bf16[64,256]{1,0...) fusion(bf16[1,64,1024]{2,1,0:T(8,128)(2,1)} %param.11, s32[]{:T(128)S(6)} %select_n.41, ...), kind=kLoop, calls=%fused_computation.28 | loop fusion | bytes 393228 | tf_op jit(solution)/shard_map/dynamic_slice | solution.py:239
  1.6 3.0 %collective-permute-start = (bf16[128,256]{1,0:T(8,128)(2,1)S(1)}, bf16[128,256]{1,0:T(8,128)(2,1)S(1)}, u32[]{:S(2)}, u32[]{:S(2)}) collective-permute-start(bf16[128,256]{1,0:T(8,128)(2,1)S(1)} %pad_maximum_fusion.4), channel_id=1, source_target_pairs={{0,1},{1,0},{2,3},{3,2},{4,5},{5,4},{6,7},{7,6},{8,9},{9,8},{10,11... | collective-permute-start | bytes 196616 | tf_op jit(solution)/shard_map/ppermute | solution.py:207
  4.7 0.1 collective-permute-start.1
  5.4 0.8 %bitcast_dynamic-update-slice_fusion.1 = bf16[272,256]{1,0:T(8,128)(2,1)S(1)} fusion(bf16[1,64,1024]{2,1,0:T(8,128)(2,1)} %param.10, s32[]{:T(128)S(6)} %select_n.40), kind=kLoop, calls=%fused_computation.27 | loop fusion | bytes 65540
  6.2 0.9 %collective-permute-done = bf16[128,256]{1,0:T(8,128)(2,1)S(1)} collective-permute-done((bf16[128,256]{1,0:T(8,128)(2,1)S(1)}, bf16[128,256]{1,0:T(8,128)(2,1)S(1)}, u32[]{:S(2)}, u32[]{:S(2)}) %collective-permute-start) | collective-permute-done | bytes 65568 | tf_op jit(solution)/shard_map/ppermute | solution.py:207
  7.1 4.6 %collective-permute-start.2 = (bf16[256,256]{1,0:T(8,128)(2,1)S(1)}, bf16[256,256]{1,0:T(8,128)(2,1)S(1)}, u32[]{:S(2)}, u32[]{:S(2)}) collective-permute-start(bf16[256,256]{1,0:T(8,128)(2,1)S(1)} %pad_maximum_fusion.1.after_ref.refs_5_), channel_id=1, source_target_pairs={{0,6},{2,4},{4,2},{6,0},{1,7},{3,5},{5,3},{7,1},{8,14},{10,12},{12... | collective-permute-start | bytes 393224 | tf_op jit(solution)/shard_map/ppermute | solution.py:207
  11.7 0.0 collective-permute-start.5
  11.7 0.0 copy-done
  11.7 0.0 copy-start.1
  11.7 0.0 copy-start.3
  11.7 0.6 %turn.1.refs_2_ = bf16[4,128,1024]{2,1,0:T(8,128)(2,1)S(1)} custom-call(bf16[128,4096]{1,0:T(8,128)(2,1)S(1)} %bitcast.41, bf16[256,256]{1,0:T(8,128)(2,1)S(1)} %pad_maximum_fusion.1.after_ref.refs_5_), custom_call_target="tpu_custom_call" | custom-call | tf_op jit(solution)/shard_map/turn/pallas_call | solution.py:295
  12.3 0.0 copy-start.2
  12.3 0.0 collective-permute-done.1
  12.4 0.8 %bitcast_dynamic-update-slice_fusion = bf16[272,256]{1,0:T(8,128)(2,1)S(1)} fusion(bf16[272,256]{1,0:T(8,128)(2,1)S(1)} %slice_dynamic-update-slice_fusion.1, bf16[1,64,1024]{2,1,0:T(8,128)(2,1)} %param.11, s32[]{:T(128)S(6)} %select_n.40), kind=kLoop, calls=%fused_computation.26 | loop fusion | bytes 65540
  13.1 2.1 %collective-permute-done.2.refs_8_ = bf16[256,256]{1,0:T(8,128)(2,1)S(1)} collective-permute-done((bf16[256,256]{1,0:T(8,128)(2,1)S(1)}, bf16[256,256]{1,0:T(8,128)(2,1)S(1)}, u32[]{:S(2)}, u32[]{:S(2)}) %collective-permute-start.2) | collective-permute-done | bytes 131104 | tf_op jit(solution)/shard_map/ppermute | solution.py:207
  15.2 0.8 %collective-permute-start.6 = (bf16[256,256]{1,0:T(8,128)(2,1)S(1)}, bf16[256,256]{1,0:T(8,128)(2,1)S(1)}, u32[]{:S(2)}, u32[]{:S(2)}) collective-permute-start(bf16[256,256]{1,0:T(8,128)(2,1)S(1)} %collective-permute-done.2.refs_8_), channel_id=1, source_target_pairs={{0,2},{2,0},{4,6},{6,4},{1,3},{3,1},{5,7},{7,5},{8,10},{10,8},{12,... | collective-permute-start | bytes 393224 | tf_op jit(solution)/shard_map/ppermute | solution.py:207
  16.0 3.6 %collective-permute-start.4 = (bf16[272,256]{1,0:T(8,128)(2,1)S(1)}, bf16[272,256]{1,0:T(8,128)(2,1)S(1)}, u32[]{:S(2)}, u32[]{:S(2)}) collective-permute-start(bf16[272,256]{1,0:T(8,128)(2,1)S(1)} %constant_dynamic-update-slice_fusion.refs_5_), channel_id=1, source_target_pairs={{0,6},{2,4},{4,2},{6,0},{1,7},{3,5},{5,3},{7,1},{8,14},{10,12},{12... | collective-permute-start | bytes 417800 | tf_op jit(solution)/shard_map/ppermute | solution.py:207
  19.6 1.1 %collective-permute-start.3 = (bf16[272,256]{1,0:T(8,128)(2,1)S(1)}, bf16[272,256]{1,0:T(8,128)(2,1)S(1)}, u32[]{:S(2)}, u32[]{:S(2)}) collective-permute-start(bf16[272,256]{1,0:T(8,128)(2,1)S(1)} %constant_dynamic-update-slice_fusion.refs_5_), channel_id=1, source_target_pairs={{0,2},{2,0},{4,6},{6,4},{1,3},{3,1},{5,7},{7,5},{8,10},{10,8},{12,... | collective-permute-start | bytes 417800 | tf_op jit(solution)/shard_map/ppermute | solution.py:207
  20.7 0.0 collective-permute-done.5.refs_6_
  20.7 1.5 %collective-permute-done.6.refs_7_ = bf16[256,256]{1,0:T(8,128)(2,1)S(1)} collective-permute-done((bf16[256,256]{1,0:T(8,128)(2,1)S(1)}, bf16[256,256]{1,0:T(8,128)(2,1)S(1)}, u32[]{:S(2)}, u32[]{:S(2)}) %collective-permute-start.6) | collective-permute-done | bytes 131104 | tf_op jit(solution)/shard_map/ppermute | solution.py:207
  22.2 0.0 copy-done.1
  22.2 0.0 copy-done.3
  22.2 0.0 copy-done.2
  22.2 6.4 %attend_0.1 = (bf16[128,4096]{1,0:T(8,128)(2,1)}, bf16[128,2048]{1,0:T(8,128)(2,1)S(1)}, bf16[128,256]{1,0:T(8,128)(2,1)S(1)}, bf16[128,256]{1,0:T(8,128)(2,1)S(...) custom-call(s32[1]{0:T(128)} %bitcast.39.refs_0_, ...), custom_call_target="tpu_custom_call" | custom-call | flops 8053063680 | bytes 2097152 | tf_op jit(solution)/shard_map/attend_0/pallas_call | solution.py:325
  28.6 0.0 collective-permute-done.4
  28.6 1.2 %collective-permute-start.7 = (bf16[272,256]{1,0:T(8,128)(2,1)S(1)}, bf16[272,256]{1,0:T(8,128)(2,1)S(1)}, u32[]{:S(2)}, u32[]{:S(2)}) collective-permute-start(bf16[272,256]{1,0:T(8,128)(2,1)S(1)} %pad_maximum_fusion.refs_8_), channel_id=1, source_target_pairs={{0,2},{2,0},{4,6},{6,4},{1,3},{3,1},{5,7},{7,5},{8,10},{10,8},{12,... | collective-permute-start | bytes 417800 | tf_op jit(solution)/shard_map/ppermute | solution.py:207
  29.9 1.3 %collective-permute-start.10 = (bf16[256,256]{1,0:T(8,128)(2,1)S(1)}, bf16[256,256]{1,0:T(8,128)(2,1)S(1)}, u32[]{:S(2)}, u32[]{:S(2)}) collective-permute-start(bf16[256,256]{1,0:T(8,128)(2,1)S(1)} %get-tuple-element.32), channel_id=1, source_target_pairs={{0,6},{2,4},{4,2},{6,0},{1,7},{3,5},{5,3},{7,1},{8,14},{10,12},{12... | collective-permute-start | bytes 393224 | tf_op jit(solution)/shard_map/ppermute | solution.py:207
  31.2 1.0 %collective-permute-start.8 = (bf16[256,256]{1,0:T(8,128)(2,1)S(1)}, bf16[256,256]{1,0:T(8,128)(2,1)S(1)}, u32[]{:S(2)}, u32[]{:S(2)}) collective-permute-start(bf16[256,256]{1,0:T(8,128)(2,1)S(1)} %get-tuple-element.30), channel_id=1, source_target_pairs={{0,4},{2,6},{4,0},{6,2},{1,5},{3,7},{5,1},{7,3},{8,12},{10,14},{12... | collective-permute-start | bytes 393224 | tf_op jit(solution)/shard_map/ppermute | solution.py:207
  32.2 2.1 %collective-permute-start.9 = (bf16[256,256]{1,0:T(8,128)(2,1)S(1)}, bf16[256,256]{1,0:T(8,128)(2,1)S(1)}, u32[]{:S(2)}, u32[]{:S(2)}) collective-permute-start(bf16[256,256]{1,0:T(8,128)(2,1)S(1)} %get-tuple-element.31), channel_id=1, source_target_pairs={{0,2},{2,0},{4,6},{6,4},{1,3},{3,1},{5,7},{7,5},{8,10},{10,8},{12,... | collective-permute-start | bytes 393224 | tf_op jit(solution)/shard_map/ppermute | solution.py:207
  34.3 0.0 collective-permute-done.3.refs_6_
  34.3 0.8 %collective-permute-done.7.refs_7_ = bf16[272,256]{1,0:T(8,128)(2,1)S(1)} collective-permute-done((bf16[272,256]{1,0:T(8,128)(2,1)S(1)}, bf16[272,256]{1,0:T(8,128)(2,1)S(1)}, u32[]{:S(2)}, u32[]{:S(2)}) %collective-permute-start.7) | collective-permute-done | bytes 139296 | tf_op jit(solution)/shard_map/ppermute | solution.py:207
  35.1 6.4 %attend_1.1 = (bf16[128,4096]{1,0:T(8,128)(2,1)}, bf16[128,2048]{1,0:T(8,128)(2,1)S(1)}, bf16[128,256]{1,0:T(8,128)(2,1)S(1)}, bf16[128,256]{1,0:T(8,128)(2,1)S(...) custom-call(s32[1]{0:T(128)} %bitcast.40.refs_0_, ...), custom_call_target="tpu_custom_call", output_to_operand_aliasing={{0}: (9, {})} | custom-call | flops 8053063680 | bytes 2097152 | tf_op jit(solution)/shard_map/attend_1/pallas_call | solution.py:325
  41.4 3.8 %collective-permute-start.13 = (bf16[256,256]{1,0:T(8,128)(2,1)S(1)}, bf16[256,256]{1,0:T(8,128)(2,1)S(1)}, u32[]{:S(2)}, u32[]{:S(2)}) collective-permute-start(bf16[256,256]{1,0:T(8,128)(2,1)S(1)} %get-tuple-element.35), channel_id=1, source_target_pairs={{0,6},{2,4},{4,2},{6,0},{1,7},{3,5},{5,3},{7,1},{8,14},{10,12},{12... | collective-permute-start | bytes 393224 | tf_op jit(solution)/shard_map/ppermute | solution.py:207
  45.3 0.0 collective-permute-start.14
  45.3 0.0 collective-permute-done.10
  45.3 0.6 %collective-permute-start.15 = (bf16[256,256]{1,0:T(8,128)(2,1)S(1)}, bf16[256,256]{1,0:T(8,128)(2,1)S(1)}, u32[]{:S(2)}, u32[]{:S(2)}) collective-permute-start(bf16[256,256]{1,0:T(8,128)(2,1)S(1)} %get-tuple-element.37), channel_id=1, source_target_pairs={{0,2},{2,0},{4,6},{6,4},{1,3},{3,1},{5,7},{7,5},{8,10},{10,8},{12,... | collective-permute-start | bytes 393224 | tf_op jit(solution)/shard_map/ppermute | solution.py:207
  45.9 0.0 collective-permute-done.8
  45.9 0.0 collective-permute-done.9
  45.9 0.1 fusion.7
  46.0 0.1 collective-permute-start.11
  46.1 1.1 %collective-permute-done.11 = f32[8,128]{1,0:T(8,128)S(1)} collective-permute-done((f32[8,128]{1,0:T(8,128)S(1)}, f32[8,128]{1,0:T(8,128)S(1)}, u32[]{:S(2)}, u32[]{:S(2)}) %collective-permute-start.11) | collective-permute-done | bytes 4128 | tf_op jit(solution)/shard_map/ppermute | solution.py:207
  47.3 1.5 %collective-permute-start.12 = (f32[8,128]{1,0:T(8,128)S(1)}, f32[8,128]{1,0:T(8,128)S(1)}, u32[]{:S(2)}, u32[]{:S(2)}) collective-permute-start(f32[8,128]{1,0:T(8,128)S(1)} %add.89), channel_id=1, source_target_pairs={{0,16},{8,24},{16,0},{24,8},{1,17},{9,25},{17,1},{25,9},{2,18},{10... | collective-permute-start | bytes 12296 | tf_op jit(solution)/shard_map/ppermute | solution.py:207
  48.7 0.0 collective-permute-done.13
  48.7 2.5 %collective-permute-done.14 = bf16[256,256]{1,0:T(8,128)(2,1)S(1)} collective-permute-done((bf16[256,256]{1,0:T(8,128)(2,1)S(1)}, bf16[256,256]{1,0:T(8,128)(2,1)S(1)}, u32[]{:S(2)}, u32[]{:S(2)}) %collective-permute-start.14) | collective-permute-done | bytes 131104 | tf_op jit(solution)/shard_map/ppermute | solution.py:207
  51.2 0.5 collective-permute-done.15
  51.7 0.1 fusion.6
  51.8 1.2 %collective-permute-start.16 = (bf16[128,512]{1,0:T(8,128)(2,1)S(1)}, bf16[128,512]{1,0:T(8,128)(2,1)S(1)}, u32[]{:S(2)}, u32[]{:S(2)}) collective-permute-start(bf16[128,512]{1,0:T(8,128)(2,1)S(1)} %pad_maximum_fusion.2), channel_id=1, source_target_pairs={{0,1},{1,0},{2,3},{3,2},{4,5},{5,4},{6,7},{7,6},{8,9},{9,8},{10,11... | collective-permute-start | bytes 393224 | tf_op jit(solution)/shard_map/ppermute | solution.py:207
  53.0 0.0 collective-permute-done.12
  53.0 1.3 %scale.1 = (bf16[128,4096]{1,0:T(8,128)(2,1)}, bf16[128,512]{1,0:T(8,128)(2,1)}, bf16[128,512]{1,0:T(8,128)(2,1)}) custom-call(f32[8,128]{1,0:T(8,128)S(1)} %get-tuple-element.52.total_ref, bf16[128,2048]{1,0:T(8,128)(2,1)S(1)} %get-tuple-element.38.refs_0_, bf16[128,256]{1,0:T(8,128)(2,1)S(1)} %get-tuple-element.39.refs_1_, ...), custom_call_target="tpu_custom_call" | custom-call | flops 655360 | bytes 2621440 | tf_op jit(solution)/shard_map/scale/pallas_call | solution.py:344
  54.3 2.5 %collective-permute-done.16 = bf16[128,512]{1,0:T(8,128)(2,1)S(1)} collective-permute-done((bf16[128,512]{1,0:T(8,128)(2,1)S(1)}, bf16[128,512]{1,0:T(8,128)(2,1)S(1)}, u32[]{:S(2)}, u32[]{:S(2)}) %collective-permute-start.16) | collective-permute-done | bytes 131104 | tf_op jit(solution)/shard_map/ppermute | solution.py:207
  56.9 0.8 %multiply_convert_fusion = (bf16[1,64,1024]{2,1,0:T(8,128)(2,1)}, bf16[1,64,1024]{2,1,0:T(8,128)(2,1)}) fusion(bf16[1,64,512]{2,1,0:T(8,128)(2,1)S(1)} %select_bitcast_fusion, bf16[1,64,512]{2,1,0:T(8,128)(2,1)S(1)} %get-tuple-element.46, f32[1024]{0:T(1024)S(1)} %broadcast_bitcast_fusion, bf16[1,64,512]{2,1,0:T(8,128)(2,1)S(1)} %get-tuple-element.54, ...), kind=kLoop, calls=%fused_computation.6 | loop fusion | flops 786432 | bytes 528384 | tf_op jit(solution)/shard_map/convert_element_type | solution.py:393
  (20 shorter events, 0.2 us)
Async XLA Ops:
  0.6 11.0 %copy-start = (bf16[1,128,4096]{2,1,0:T(8,128)(2,1)S(1)}, bf16[1,128,4096]{2,1,0:T(8,128)(2,1)}, u32[]{:S(2)}) copy-start(bf16[1,128,4096]{2,1,0:T(8,128)(2,1)} %param.13) | copy-start | bytes 3145732
  1.6 5.4 %collective-permute-start = (bf16[128,256]{1,0:T(8,128)(2,1)S(1)}, bf16[128,256]{1,0:T(8,128)(2,1)S(1)}, u32[]{:S(2)}, u32[]{:S(2)}) collective-permute-start(bf16[128,256]{1,0:T(8,128)(2,1)S(1)} %pad_maximum_fusion.4), channel_id=1, source_target_pairs={{0,1},{1,0},{2,3},{3,2},{4,5},{5,4},{6,7},{7,6},{8,9},{9,8},{10,11... | collective-permute-start | bytes 196616 | tf_op jit(solution)/shard_map/ppermute | solution.py:207
  4.7 7.7 %collective-permute-start.1 = (bf16[128,256]{1,0:T(8,128)(2,1)S(1)}, bf16[128,256]{1,0:T(8,128)(2,1)S(1)}, u32[]{:S(2)}, u32[]{:S(2)}) collective-permute-start(bf16[128,256]{1,0:T(8,128)(2,1)S(1)} %pad_maximum_fusion.5), channel_id=1, source_target_pairs={{0,1},{1,0},{2,3},{3,2},{4,5},{5,4},{6,7},{7,6},{8,9},{9,8},{10,11... | collective-permute-start | bytes 196616 | tf_op jit(solution)/shard_map/ppermute | solution.py:207
  7.1 8.2 %collective-permute-start.2 = (bf16[256,256]{1,0:T(8,128)(2,1)S(1)}, bf16[256,256]{1,0:T(8,128)(2,1)S(1)}, u32[]{:S(2)}, u32[]{:S(2)}) collective-permute-start(bf16[256,256]{1,0:T(8,128)(2,1)S(1)} %pad_maximum_fusion.1.after_ref.refs_5_), channel_id=1, source_target_pairs={{0,6},{2,4},{4,2},{6,0},{1,7},{3,5},{5,3},{7,1},{8,14},{10,12},{12... | collective-permute-start | bytes 393224 | tf_op jit(solution)/shard_map/ppermute | solution.py:207
  11.7 9.0 %collective-permute-start.5 = (bf16[256,256]{1,0:T(8,128)(2,1)S(1)}, bf16[256,256]{1,0:T(8,128)(2,1)S(1)}, u32[]{:S(2)}, u32[]{:S(2)}) collective-permute-start(bf16[256,256]{1,0:T(8,128)(2,1)S(1)} %pad_maximum_fusion.1.after_ref.refs_5_), channel_id=1, source_target_pairs={{0,2},{2,0},{4,6},{6,4},{1,3},{3,1},{5,7},{7,5},{8,10},{10,8},{12,... | collective-permute-start | bytes 393224 | tf_op jit(solution)/shard_map/ppermute | solution.py:207
  11.7 10.5 %copy-start.1 = (bf16[1,128,4096]{2,1,0:T(8,128)(2,1)S(1)}, bf16[1,128,4096]{2,1,0:T(8,128)(2,1)}, u32[]{:S(2)}) copy-start(bf16[1,128,4096]{2,1,0:T(8,128)(2,1)} %param.7) | copy-start | bytes 3145732
  11.7 10.5 %copy-start.3 = (bf16[1,128,512]{2,1,0:T(8,128)(2,1)S(1)}, bf16[1,128,512]{2,1,0:T(8,128)(2,1)}, u32[]{:S(2)}) copy-start(bf16[1,128,512]{2,1,0:T(8,128)(2,1)} %param.9) | copy-start | bytes 393220
  12.3 9.9 %copy-start.2 = (bf16[1,128,512]{2,1,0:T(8,128)(2,1)S(1)}, bf16[1,128,512]{2,1,0:T(8,128)(2,1)}, u32[]{:S(2)}) copy-start(bf16[1,128,512]{2,1,0:T(8,128)(2,1)} %param.8) | copy-start | bytes 393220
  15.2 7.0 %collective-permute-start.6 = (bf16[256,256]{1,0:T(8,128)(2,1)S(1)}, bf16[256,256]{1,0:T(8,128)(2,1)S(1)}, u32[]{:S(2)}, u32[]{:S(2)}) collective-permute-start(bf16[256,256]{1,0:T(8,128)(2,1)S(1)} %collective-permute-done.2.refs_8_), channel_id=1, source_target_pairs={{0,2},{2,0},{4,6},{6,4},{1,3},{3,1},{5,7},{7,5},{8,10},{10,8},{12,... | collective-permute-start | bytes 393224 | tf_op jit(solution)/shard_map/ppermute | solution.py:207
  16.0 12.5 %collective-permute-start.4 = (bf16[272,256]{1,0:T(8,128)(2,1)S(1)}, bf16[272,256]{1,0:T(8,128)(2,1)S(1)}, u32[]{:S(2)}, u32[]{:S(2)}) collective-permute-start(bf16[272,256]{1,0:T(8,128)(2,1)S(1)} %constant_dynamic-update-slice_fusion.refs_5_), channel_id=1, source_target_pairs={{0,6},{2,4},{4,2},{6,0},{1,7},{3,5},{5,3},{7,1},{8,14},{10,12},{12... | collective-permute-start | bytes 417800 | tf_op jit(solution)/shard_map/ppermute | solution.py:207
  19.6 14.7 %collective-permute-start.3 = (bf16[272,256]{1,0:T(8,128)(2,1)S(1)}, bf16[272,256]{1,0:T(8,128)(2,1)S(1)}, u32[]{:S(2)}, u32[]{:S(2)}) collective-permute-start(bf16[272,256]{1,0:T(8,128)(2,1)S(1)} %constant_dynamic-update-slice_fusion.refs_5_), channel_id=1, source_target_pairs={{0,2},{2,0},{4,6},{6,4},{1,3},{3,1},{5,7},{7,5},{8,10},{10,8},{12,... | collective-permute-start | bytes 417800 | tf_op jit(solution)/shard_map/ppermute | solution.py:207
  28.6 6.4 %collective-permute-start.7 = (bf16[272,256]{1,0:T(8,128)(2,1)S(1)}, bf16[272,256]{1,0:T(8,128)(2,1)S(1)}, u32[]{:S(2)}, u32[]{:S(2)}) collective-permute-start(bf16[272,256]{1,0:T(8,128)(2,1)S(1)} %pad_maximum_fusion.refs_8_), channel_id=1, source_target_pairs={{0,2},{2,0},{4,6},{6,4},{1,3},{3,1},{5,7},{7,5},{8,10},{10,8},{12,... | collective-permute-start | bytes 417800 | tf_op jit(solution)/shard_map/ppermute | solution.py:207
  29.9 15.4 %collective-permute-start.10 = (bf16[256,256]{1,0:T(8,128)(2,1)S(1)}, bf16[256,256]{1,0:T(8,128)(2,1)S(1)}, u32[]{:S(2)}, u32[]{:S(2)}) collective-permute-start(bf16[256,256]{1,0:T(8,128)(2,1)S(1)} %get-tuple-element.32), channel_id=1, source_target_pairs={{0,6},{2,4},{4,2},{6,0},{1,7},{3,5},{5,3},{7,1},{8,14},{10,12},{12... | collective-permute-start | bytes 393224 | tf_op jit(solution)/shard_map/ppermute | solution.py:207
  31.2 14.7 %collective-permute-start.8 = (bf16[256,256]{1,0:T(8,128)(2,1)S(1)}, bf16[256,256]{1,0:T(8,128)(2,1)S(1)}, u32[]{:S(2)}, u32[]{:S(2)}) collective-permute-start(bf16[256,256]{1,0:T(8,128)(2,1)S(1)} %get-tuple-element.30), channel_id=1, source_target_pairs={{0,4},{2,6},{4,0},{6,2},{1,5},{3,7},{5,1},{7,3},{8,12},{10,14},{12... | collective-permute-start | bytes 393224 | tf_op jit(solution)/shard_map/ppermute | solution.py:207
  32.2 13.7 %collective-permute-start.9 = (bf16[256,256]{1,0:T(8,128)(2,1)S(1)}, bf16[256,256]{1,0:T(8,128)(2,1)S(1)}, u32[]{:S(2)}, u32[]{:S(2)}) collective-permute-start(bf16[256,256]{1,0:T(8,128)(2,1)S(1)} %get-tuple-element.31), channel_id=1, source_target_pairs={{0,2},{2,0},{4,6},{6,4},{1,3},{3,1},{5,7},{7,5},{8,10},{10,8},{12,... | collective-permute-start | bytes 393224 | tf_op jit(solution)/shard_map/ppermute | solution.py:207
  41.4 7.3 %collective-permute-start.13 = (bf16[256,256]{1,0:T(8,128)(2,1)S(1)}, bf16[256,256]{1,0:T(8,128)(2,1)S(1)}, u32[]{:S(2)}, u32[]{:S(2)}) collective-permute-start(bf16[256,256]{1,0:T(8,128)(2,1)S(1)} %get-tuple-element.35), channel_id=1, source_target_pairs={{0,6},{2,4},{4,2},{6,0},{1,7},{3,5},{5,3},{7,1},{8,14},{10,12},{12... | collective-permute-start | bytes 393224 | tf_op jit(solution)/shard_map/ppermute | solution.py:207
  45.3 6.0 %collective-permute-start.14 = (bf16[256,256]{1,0:T(8,128)(2,1)S(1)}, bf16[256,256]{1,0:T(8,128)(2,1)S(1)}, u32[]{:S(2)}, u32[]{:S(2)}) collective-permute-start(bf16[256,256]{1,0:T(8,128)(2,1)S(1)} %get-tuple-element.36), channel_id=1, source_target_pairs={{0,4},{2,6},{4,0},{6,2},{1,5},{3,7},{5,1},{7,3},{8,12},{10,14},{12... | collective-permute-start | bytes 393224 | tf_op jit(solution)/shard_map/ppermute | solution.py:207
  45.3 6.4 %collective-permute-start.15 = (bf16[256,256]{1,0:T(8,128)(2,1)S(1)}, bf16[256,256]{1,0:T(8,128)(2,1)S(1)}, u32[]{:S(2)}, u32[]{:S(2)}) collective-permute-start(bf16[256,256]{1,0:T(8,128)(2,1)S(1)} %get-tuple-element.37), channel_id=1, source_target_pairs={{0,2},{2,0},{4,6},{6,4},{1,3},{3,1},{5,7},{7,5},{8,10},{10,8},{12,... | collective-permute-start | bytes 393224 | tf_op jit(solution)/shard_map/ppermute | solution.py:207
  46.0 1.2 %collective-permute-start.11 = (f32[8,128]{1,0:T(8,128)S(1)}, f32[8,128]{1,0:T(8,128)S(1)}, u32[]{:S(2)}, u32[]{:S(2)}) collective-permute-start(f32[8,128]{1,0:T(8,128)S(1)} %fusion.5), channel_id=1, source_target_pairs={{0,8},{8,0},{16,24},{24,16},{1,9},{9,1},{17,25},{25,17},{2,10},{10... | collective-permute-start | bytes 12296 | tf_op jit(solution)/shard_map/ppermute | solution.py:207
  47.3 5.8 %collective-permute-start.12 = (f32[8,128]{1,0:T(8,128)S(1)}, f32[8,128]{1,0:T(8,128)S(1)}, u32[]{:S(2)}, u32[]{:S(2)}) collective-permute-start(f32[8,128]{1,0:T(8,128)S(1)} %add.89), channel_id=1, source_target_pairs={{0,16},{8,24},{16,0},{24,8},{1,17},{9,25},{17,1},{25,9},{2,18},{10... | collective-permute-start | bytes 12296 | tf_op jit(solution)/shard_map/ppermute | solution.py:207
  51.8 5.0 %collective-permute-start.16 = (bf16[128,512]{1,0:T(8,128)(2,1)S(1)}, bf16[128,512]{1,0:T(8,128)(2,1)S(1)}, u32[]{:S(2)}, u32[]{:S(2)}) collective-permute-start(bf16[128,512]{1,0:T(8,128)(2,1)S(1)} %pad_maximum_fusion.2), channel_id=1, source_target_pairs={{0,1},{1,0},{2,3},{3,2},{4,5},{5,4},{6,7},{7,6},{8,9},{9,8},{10,11... | collective-permute-start | bytes 393224 | tf_op jit(solution)/shard_map/ppermute | solution.py:207
